TPU v7x, 32 devices: a whole 2x2x4 slice. The times are simulated.
32 devices in a mesh: dp: 8 (over y, x, core), seq: 4 (over z).
Axes of the slice: x: 2, y: 2, z: 4, core: 2. Of those that a mesh axis runs over, the one named last changes fastest.
Arguments:
- tokens: bfloat16 [64, 512, 768], P('dp', 'seq'), may hold values from -6 to 6
- cotangent: bfloat16 [64, 512, 768], P('dp', 'seq'), may hold values from -6 to 6
- lengths: int32 [64, 4], P('dp'), may hold values from 1 to 448, 512 in all within a row
- packed_weight: float32 [768, 2304], P(('dp', 'seq')), may hold values from -0.21875 to 0.21875
- query_bias: float32 [768], P(('dp', 'seq')), may hold values from -3 to 3
- value_bias: float32 [768], P(('dp', 'seq')), may hold values from -3 to 3
- output_weight: float32 [768, 768], P(('dp', 'seq')), may hold values from -2.5 to 2.5
- output_bias: float32 [768], P(('dp', 'seq')), may hold values from -3 to 3
- first_gain: float32 [768], P(('dp', 'seq')), may hold values from 0.25 to 1.75
- first_shift: float32 [768], P(('dp', 'seq')), may hold values from -2 to 2
- inner_weight: float32 [768, 3072], P(('dp', 'seq')), may hold values from -0.21875 to 0.21875
- inner_bias: float32 [3072], P(('dp', 'seq')), may hold values from -3 to 3
- outer_weight: float32 [3072, 768], P(('dp', 'seq')), may hold values from -0.109375 to 0.109375
- outer_bias: float32 [768], P(('dp', 'seq')), may hold values from -3 to 3
- second_gain: float32 [768], P(('dp', 'seq')), may hold values from 0.25 to 1.75
- second_shift: float32 [768], P(('dp', 'seq')), may hold values from -2 to 2
Outputs:
- output: bfloat16 [64, 512, 768], P('dp', 'seq')
- tokens_grad: float32 [64, 512, 768], P('dp', 'seq')
- packed_weight_grad: float32 [768, 2304], P(('dp', 'seq'))
- query_bias_grad: float32 [768], P(('dp', 'seq'))
- value_bias_grad: float32 [768], P(('dp', 'seq'))
- output_weight_grad: float32 [768, 768], P(('dp', 'seq'))
- output_bias_grad: float32 [768], P(('dp', 'seq'))
- first_gain_grad: float32 [768], P(('dp', 'seq'))
- first_shift_grad: float32 [768], P(('dp', 'seq'))
- inner_weight_grad: float32 [768, 3072], P(('dp', 'seq'))
- inner_bias_grad: float32 [3072], P(('dp', 'seq'))
- outer_weight_grad: float32 [3072, 768], P(('dp', 'seq'))
- outer_bias_grad: float32 [768], P(('dp', 'seq'))
- second_gain_grad: float32 [768], P(('dp', 'seq'))
- second_shift_grad: float32 [768], P(('dp', 'seq'))
Inputs may be any that keep to these rules, and one draw needn't show every extreme that they name: Each row's 4 lengths add up to 512, and in every row the longest is exactly 448.
All inputs are finite; a program needn't handle non-finite values.
Results may differ from a plain program's by a relative error of at most 0.014.
The roundings to bfloat16 on the way count: a program that leaves them out, or rounds other values in their place, can miss the bound.
Values may be sent and summed in bfloat16 or wider, within the bound.
No kernel may reach another device: no remote copies, remote signals or barrier semaphores. Data moves between devices by JAX's collectives and lax.ppermute only.
A program may use at most 192 MiB of HBM per device.

v0:
```python
from functools import partial

import jax
import jax.numpy as jnp
from jax import lax
from jax.sharding import PartitionSpec as P

HEAD_DIM = 64


EPSILON = 1e-06


def narrow(value):
    return value.astype(jnp.bfloat16)


def widen(value):
    return value.astype(jnp.float32)


def pair_labels(lengths, length):
    bounds = jnp.cumsum(lengths, axis=-1)[..., :-1]
    places = jnp.arange(length, dtype=jnp.int32)
    return jnp.sum((places[None, :, None] >= bounds[:, None, :]).astype(jnp.int32), axis=-1)


def normalize(summed, gain, shift):
    average = jnp.mean(summed, axis=-1, keepdims=True)
    centred = summed - average
    variance = jnp.mean(centred * centred, axis=-1, keepdims=True)
    inverse = lax.rsqrt(variance + EPSILON)
    normed = centred * inverse
    return (normed * gain + shift, normed, inverse)


def normalize_back(upstream, normed, inverse, gain):
    scaled = upstream * gain
    first_mean = jnp.mean(scaled, axis=-1, keepdims=True)
    second_mean = jnp.mean(scaled * normed, axis=-1, keepdims=True)
    result = inverse * (scaled - first_mean - normed * second_mean)
    return (result, jnp.sum(upstream * normed, axis=0), jnp.sum(upstream, axis=0))


def masked_scores(query_rows, key_rows, labels):
    scale = query_rows.shape[-1] ** (-0.5)
    scores = (
        jnp.einsum("qhd,khd->hqk", query_rows, key_rows, preferred_element_type=jnp.float32) * scale
    )
    allowed = labels[:, None] == labels[None, :]
    return jnp.where(allowed[None], scores, -1e30)


def attend_forward(pieces):
    packed, labels = pieces
    query_rows, key_rows, value_rows = (packed[:, 0], packed[:, 1], packed[:, 2])
    scores = masked_scores(query_rows, key_rows, labels)
    highest = jnp.max(scores, axis=-1, keepdims=True)
    raised = jnp.exp(scores - highest)
    summed = jnp.sum(raised, axis=-1, keepdims=True)
    softmaxed = raised / summed
    context = jnp.einsum(
        "hqk,khd->qhd", narrow(softmaxed), value_rows, preferred_element_type=jnp.float32
    )
    return (narrow(context), (highest + jnp.log(summed))[..., 0])


def attend_backward(pieces):
    packed, labels, log_total, upstream = pieces
    query_rows, key_rows, value_rows = (packed[:, 0], packed[:, 1], packed[:, 2])
    scale = query_rows.shape[-1] ** (-0.5)
    scores = masked_scores(query_rows, key_rows, labels)
    softmaxed = jnp.exp(scores - log_total[..., None])
    value_grad = jnp.einsum(
        "hqk,qhd->khd", narrow(softmaxed), upstream, preferred_element_type=jnp.float32
    )
    prob_grad = jnp.einsum("qhd,khd->hqk", upstream, value_rows, preferred_element_type=jnp.float32)
    weighted = jnp.sum(softmaxed * prob_grad, axis=-1, keepdims=True)
    score_grad = narrow(softmaxed * (prob_grad - weighted))
    query_grad = (
        jnp.einsum("hqk,khd->qhd", score_grad, key_rows, preferred_element_type=jnp.float32) * scale
    )
    key_grad = (
        jnp.einsum("hqk,qhd->khd", score_grad, query_rows, preferred_element_type=jnp.float32)
        * scale
    )
    return narrow(jnp.stack([query_grad, key_grad, value_grad], axis=1))


def shards(
    tokens,
    cotangent,
    lengths,
    packed_weight,
    query_bias,
    value_bias,
    output_weight,
    output_bias,
    first_gain,
    first_shift,
    inner_weight,
    inner_bias,
    outer_weight,
    outer_bias,
    second_gain,
    second_shift,
):
    row_count, local_length, width = tokens.shape
    heads_all = width // HEAD_DIM
    attention_set = (
        lax.all_gather(narrow(packed_weight), ("dp", "seq"), axis=0, tiled=True),
        lax.all_gather(narrow(query_bias), ("dp", "seq"), axis=0, tiled=True),
        lax.all_gather(narrow(value_bias), ("dp", "seq"), axis=0, tiled=True),
        lax.all_gather(narrow(output_weight), ("dp", "seq"), axis=0, tiled=True),
        lax.all_gather(narrow(output_bias), ("dp", "seq"), axis=0, tiled=True),
        lax.all_gather(narrow(first_gain), ("dp", "seq"), axis=0, tiled=True),
        lax.all_gather(narrow(first_shift), ("dp", "seq"), axis=0, tiled=True),
    )
    (
        whole_packed,
        whole_query,
        whole_value,
        whole_output,
        whole_outbias,
        whole_gain_one,
        whole_shift_one,
    ) = attention_set
    flat = tokens.reshape(-1, width)
    middle = jnp.zeros((width,), jnp.float32)
    bias_row = jnp.concatenate([widen(whole_query), middle, widen(whole_value)])
    mixed = jnp.dot(flat, whole_packed, preferred_element_type=jnp.float32) + bias_row
    packed = narrow(mixed).reshape(row_count, local_length, 3, heads_all, HEAD_DIM)
    spread_rows = lax.all_to_all(packed, "seq", split_axis=3, concat_axis=1, tiled=True)
    labels = pair_labels(lengths, spread_rows.shape[1])
    context_heads, log_totals = lax.map(attend_forward, (spread_rows, labels))
    context = lax.all_to_all(context_heads, "seq", split_axis=1, concat_axis=2, tiled=True).reshape(
        -1, width
    )
    projected = jnp.dot(context, whole_output, preferred_element_type=jnp.float32) + widen(
        whole_outbias
    )
    hidden, first_normed, first_inverse = normalize(
        widen(flat) + projected, widen(whole_gain_one), widen(whole_shift_one)
    )
    hidden_low = narrow(hidden)
    feedforward_set = (
        lax.all_gather(narrow(inner_weight), ("dp", "seq"), axis=0, tiled=True),
        lax.all_gather(narrow(inner_bias), ("dp", "seq"), axis=0, tiled=True),
        lax.all_gather(narrow(outer_weight), ("dp", "seq"), axis=0, tiled=True),
        lax.all_gather(narrow(outer_bias), ("dp", "seq"), axis=0, tiled=True),
        lax.all_gather(narrow(second_gain), ("dp", "seq"), axis=0, tiled=True),
        lax.all_gather(narrow(second_shift), ("dp", "seq"), axis=0, tiled=True),
    )
    whole_inner, whole_innerbias, whole_outer, whole_outerbias, whole_gain_two, whole_shift_two = (
        feedforward_set
    )
    inner = jnp.dot(hidden_low, whole_inner, preferred_element_type=jnp.float32) + widen(
        whole_innerbias
    )
    active = narrow(jax.nn.gelu(inner, approximate=False))
    branch = jnp.dot(active, whole_outer, preferred_element_type=jnp.float32) + widen(
        whole_outerbias
    )
    result, second_normed, second_inverse = normalize(
        hidden + branch, widen(whole_gain_two), widen(whole_shift_two)
    )
    output = narrow(result).reshape(row_count, local_length, width)
    back_inner, back_innerbias, back_outer, back_outerbias, back_gain_two, back_shift_two = (
        feedforward_set
    )
    upstream = widen(cotangent).reshape(-1, width)
    second_up, second_gain_grad, second_shift_grad = normalize_back(
        upstream, second_normed, second_inverse, widen(back_gain_two)
    )
    branch_grad = narrow(second_up)
    outer_weight_grad = jnp.einsum(
        "tf,td->fd", active, branch_grad, preferred_element_type=jnp.float32
    )
    outer_bias_grad = jnp.sum(widen(branch_grad), axis=0)
    active_grad = jnp.einsum(
        "td,fd->tf", branch_grad, back_outer, preferred_element_type=jnp.float32
    )
    gelu_pull = jax.vjp(partial(jax.nn.gelu, approximate=False), inner)[1]
    inner_grad = narrow(gelu_pull(active_grad)[0])
    inner_weight_grad = jnp.einsum(
        "td,tf->df", hidden_low, inner_grad, preferred_element_type=jnp.float32
    )
    inner_bias_grad = jnp.sum(widen(inner_grad), axis=0)
    hidden_grad = second_up + jnp.einsum(
        "tf,df->td", inner_grad, back_inner, preferred_element_type=jnp.float32
    )
    feed_shares = (
        lax.psum_scatter(inner_weight_grad, ("dp", "seq"), scatter_dimension=0, tiled=True),
        lax.psum_scatter(inner_bias_grad, ("dp", "seq"), scatter_dimension=0, tiled=True),
        lax.psum_scatter(outer_weight_grad, ("dp", "seq"), scatter_dimension=0, tiled=True),
        lax.psum_scatter(outer_bias_grad, ("dp", "seq"), scatter_dimension=0, tiled=True),
        lax.psum_scatter(second_gain_grad, ("dp", "seq"), scatter_dimension=0, tiled=True),
        lax.psum_scatter(second_shift_grad, ("dp", "seq"), scatter_dimension=0, tiled=True),
    )
    (
        back_packed,
        back_query,
        back_value,
        back_output,
        back_outbias,
        back_gain_one,
        back_shift_one,
    ) = attention_set
    first_up, first_gain_grad, first_shift_grad = normalize_back(
        hidden_grad, first_normed, first_inverse, widen(back_gain_one)
    )
    projected_grad = narrow(first_up)
    output_weight_grad = jnp.einsum(
        "td,te->de", context, projected_grad, preferred_element_type=jnp.float32
    )
    output_bias_grad = jnp.sum(widen(projected_grad), axis=0)
    context_grad = narrow(
        jnp.einsum("te,de->td", projected_grad, back_output, preferred_element_type=jnp.float32)
    )
    context_grad = context_grad.reshape(row_count, local_length, heads_all, HEAD_DIM)
    context_grad_heads = lax.all_to_all(
        context_grad, "seq", split_axis=2, concat_axis=1, tiled=True
    )
    packed_grad_heads = lax.map(
        attend_backward, (spread_rows, labels, log_totals, context_grad_heads)
    )
    packed_grad = lax.all_to_all(
        packed_grad_heads, "seq", split_axis=1, concat_axis=3, tiled=True
    ).reshape(-1, 3 * width)
    packed_weight_grad = jnp.einsum(
        "td,tc->dc", flat, packed_grad, preferred_element_type=jnp.float32
    )
    column_sums = jnp.sum(widen(packed_grad), axis=0)
    query_bias_grad = column_sums[:width]
    value_bias_grad = column_sums[2 * width :]
    tokens_grad = first_up + jnp.einsum(
        "tc,dc->td", packed_grad, back_packed, preferred_element_type=jnp.float32
    )
    attention_shares = (
        lax.psum_scatter(packed_weight_grad, ("dp", "seq"), scatter_dimension=0, tiled=True),
        lax.psum_scatter(query_bias_grad, ("dp", "seq"), scatter_dimension=0, tiled=True),
        lax.psum_scatter(value_bias_grad, ("dp", "seq"), scatter_dimension=0, tiled=True),
        lax.psum_scatter(output_weight_grad, ("dp", "seq"), scatter_dimension=0, tiled=True),
        lax.psum_scatter(output_bias_grad, ("dp", "seq"), scatter_dimension=0, tiled=True),
        lax.psum_scatter(first_gain_grad, ("dp", "seq"), scatter_dimension=0, tiled=True),
        lax.psum_scatter(first_shift_grad, ("dp", "seq"), scatter_dimension=0, tiled=True),
    )
    return (
        output,
        tokens_grad.reshape(row_count, local_length, width),
        attention_shares[0],
        attention_shares[1],
        attention_shares[2],
        attention_shares[3],
        attention_shares[4],
        attention_shares[5],
        attention_shares[6],
        feed_shares[0],
        feed_shares[1],
        feed_shares[2],
        feed_shares[3],
        feed_shares[4],
        feed_shares[5],
    )


def solution(mesh):
    return jax.shard_map(
        shards,
        mesh=mesh,
        in_specs=(
            P("dp", "seq", None),
            P("dp", "seq", None),
            P("dp", None),
            P(("dp", "seq"), None),
            P(("dp", "seq")),
            P(("dp", "seq")),
            P(("dp", "seq"), None),
            P(("dp", "seq")),
            P(("dp", "seq")),
            P(("dp", "seq")),
            P(("dp", "seq"), None),
            P(("dp", "seq")),
            P(("dp", "seq"), None),
            P(("dp", "seq")),
            P(("dp", "seq")),
            P(("dp", "seq")),
        ),
        out_specs=(
            P("dp", "seq", None),
            P("dp", "seq", None),
            P(("dp", "seq"), None),
            P(("dp", "seq")),
            P(("dp", "seq")),
            P(("dp", "seq"), None),
            P(("dp", "seq")),
            P(("dp", "seq")),
            P(("dp", "seq")),
            P(("dp", "seq"), None),
            P(("dp", "seq")),
            P(("dp", "seq"), None),
            P(("dp", "seq")),
            P(("dp", "seq")),
            P(("dp", "seq")),
        ),
        check_vma=False,
    )
```

profile of v0, /device:TPU:0, one launch (start us, length us, event | category | flops | bytes accessed | tf_op | source)
XLA Modules:
  0.0 994.1 jit_solution(3279969328286213736)
XLA Ops:
  16.6 42.7 %all-reduce.19 = (bf16[768]{0:T(1024)(128)(2,1)S(1)}, bf16[768]{0:T(1024)(128)(2,1)S(1)}, bf16[768]{0:T(1024)(128)(2,1)S(1)}, bf16[768]{0:T(1024)(128)(2,1)S(1)}...) all-reduce(bf16[768]{0:T(1024)(128)(2,1)S(1)} %dynamic-update-slice, ...), channel_id=1, replica_groups=mesh['dp'=8,'seq'=4] {'dp','seq'}, use_global_device_ids=true, to_apply=%add.2 | all-reduce | flops 9216 | bytes 36864
  59.4 15.0 %all-gather.5.cloned.1.call-done = bf16[768,2304]{1,0:T(8,128)(2,1)} async-done(((bf16[24,2304]{1,0:T(8,128)(2,1)}), bf16[768,2304]{1,0:T(8,128)(2,1)}) %all-gather.5.cloned.1.call-update) | async-done | bytes 3538960 | tf_op jit(solution)/shard_map/all_gather | solution.py:111
  74.4 8.4 add_convert_fusion.1
  82.8 6.7 copy.103
  95.6 5.1 all-to-all-start
  102.6 105.6 %all-to-all-done = bf16[8,128,3,12,64]{1,0,4,2,3:T(8,128)(2,1)} async-done(((bf16[8,128,3,12,64]{1,0,4,2,3:T(8,128)(2,1)}), bf16[8,128,3,12,64]{1,0,4,2,3:T(8,128)(2,1)}, u32[]{:S(2)}, u32[]{:S(2)}) %all-to-all-start) | async-done | bytes 4718624 | tf_op jit(solution)/shard_map/all_to_all | solution.py:133
  208.2 8.1 copy.106
  216.3 8.1 all_to_all.51
  224.4 36.3 %while.22 = (s32[]{:T(128)}, bf16[8,512,3,64]{1,3,2,0:T(8,128)(2,1)S(1)}, f32[8,3,512]{2,1,0:T(4,128)}, bf16[8,512,3,3,64]{1,4,3,2,0:T(8,128)(2,1)}, s32[8,512]{1,0:T(8,128)S(1)}, /*index=5*/s32[]{:T(128)}) while((s32[]{:T(128)}, bf16[8,512,3,64]{1,3,2,0:T(8,128)(2,1)S(1)}, f32[8,3,512]{2,1,0:T(4,128)}, bf16[8,512,3,3,64]{1,4,3,2,0:T(8,128)(2,1)}, ...), condition=%wide.region_5.6_spmd, body=%wide.region_2.5_spmd.sunk | while | flops 211122688 | bytes 12513873 | solution.py:135
  264.1 5.2 reshape.282
  269.3 4.5 all-to-all-start.1
  275.9 47.2 %all-to-all-done.1 = bf16[4,2,98304]{2,1,0:T(2,128)(2,1)} async-done(((bf16[4,2,98304]{2,1,0:T(2,128)(2,1)}), bf16[4,2,98304]{2,1,0:T(2,128)(2,1)}, u32[]{:S(2)}, u32[]{:S(2)}) %all-to-all-start.1) | async-done | bytes 1572896 | tf_op jit(solution)/shard_map/all_to_all | solution.py:136
  335.1 35.8 %multiply_convert_fusion.1 = (bf16[1024,3072]{1,0:T(8,128)(2,1)}, f32[1024,3072]{1,0:T(8,128)}, f32[1024,3072]{1,0:T(8,128)}) fusion(f32[3072]{0:T(1024)S(1)} %convert_element_type.155, bf16[768,3072]{1,0:T(8,128)(2,1)} %all-gather.9.cloned.1.call-done, f32[1024,768]{1,0:T(8,128)S(1)} %get-tuple-element.230, f32[768]{0:T(1024)S(1)} %convert_element_type.151, ...), kind=kOutput, calls=%fused_computation.51 | convolution fusion | flops 5043388416 | bytes 39348224 | tf_op jit(solution)/shard_map/dot_general | solution.py:157
  371.0 8.8 fusion.68
  386.6 18.7 %convert_reduce_fusion = (f32[3072]{0:T(1024)S(1)}, bf16[1024,3072]{1,0:T(8,128)(2,1)}) fusion(f32[1024,3072]{1,0:T(8,128)} %get-tuple-element.221, bf16[3072,768]{1,0:T(8,128)(2,1)} %all-gather.11.cloned.1.call-done, f32[1024,768]{1,0:T(8,128)} %get-tuple-element.217, f32[1024,3072]{1,0:T(8,128)} %get-tuple-element.231, f32[3072]{0:T(1024)S(1)} %convert_element_type.155), kind=kOutput, calls=%fused_computation.49 | convolution fusion | flops 4886098944 | bytes 39346176 | tf_op jit(solution)/shard_map/td,fd->tf/dot_general | solution.py:180
  405.3 10.0 %multiply_reduce_fusion.1 = (f32[768]{0:T(1024)S(1)}, f32[1024]{0:T(1024)S(1)}, f32[1024]{0:T(1024)S(1)}, f32[768]{0:T(1024)S(1)}, f32[1024,768]{1,0:T(8,128)S(1)}) fusion(f32[1024,768]{1,0:T(8,128)S(1)} %get-tuple-element.230, f32[1024]{0:T(1024)S(1)} %add_rsqrt_fusion.1, f32[1024]{0:T(1024)S(1)} %broadcast_multiply_fusion.4, ...), kind=kOutput, calls=%fused_computation.85 | convolution fusion | flops 4839698432 | bytes 20472832 | tf_op jit(solution)/shard_map/tf,df->td/dot_general | solution.py:189
  421.0 10.9 %fusion.60 = f32[768,3072]{1,0:T(8,128)} fusion(bf16[1024,3072]{1,0:T(8,128)(2,1)} %get-tuple-element.236, f32[1024,768]{1,0:T(8,128)S(1)} %get-tuple-element.230, f32[768]{0:T(1024)S(1)} %convert_element_type.151, f32[768]{0:T(1024)S(1)} %convert_element_type.149, f32[1024]{0:T(1024)S(1)} %add_rsqrt_fusion.1, f32[1024]{0:T(1024)S(1)} %broadcast_multiply_fusion.4), kind=kOutput, calls=%fused_computation.123 | convolution fusion | flops 4835770368 | bytes 18888704 | tf_op jit(solution)/shard_map/td,tf->df/dot_general | solution.py:185
  444.7 10.4 %fusion.57 = f32[3072,768]{1,0:T(8,128)} fusion(bf16[1024,3072]{1,0:T(8,128)(2,1)} %get-tuple-element.220, f32[1024,768]{1,0:T(8,128)} %get-tuple-element.217), kind=kOutput, calls=%fused_computation.120 | convolution fusion | flops 4832624640 | bytes 18874368 | tf_op jit(solution)/shard_map/tf,td->fd/dot_general | solution.py:176
  455.2 33.0 %all-to-all-done.2 = bf16[8,128,12,64]{1,0,3,2:T(8,128)(2,1)S(1)} async-done(((bf16[8,128,12,64]{1,0,3,2:T(8,128)(2,1)}), bf16[8,128,12,64]{1,0,3,2:T(8,128)(2,1)S(1)}, u32[]{:S(2)}, u32[]{:S(2)}) %all-to-all-start.2) | async-done | bytes 1572896 | tf_op jit(solution)/shard_map/all_to_all | solution.py:221
  490.3 62.9 %while.23 = (s32[]{:T(128)}, bf16[8,512,3,3,64]{1,4,3,2,0:T(8,128)(2,1)}, bf16[8,512,3,3,64]{1,4,3,2,0:T(8,128)(2,1)}, s32[8,512]{1,0:T(8,128)}, f32[8,3,512]{2,...) while((s32[]{:T(128)}, bf16[8,512,3,3,64]{1,4,3,2,0:T(8,128)(2,1)}, ...), condition=%wide.region_16.17_spmd, body=%wide.region_14.16_spmd.sunk | while | flops 512915968 | bytes 28482144 | solution.py:224
  553.2 11.7 %copy.112 = bf16[8,512,3,3,64]{4,0,3,2,1:T(8,128)(2,1)} copy(bf16[8,512,3,3,64]{1,4,3,2,0:T(8,128)(2,1)} %get-tuple-element.77) | data formatting | bytes 9437184 | tf_op jit(solution)/shard_map/while | solution.py:224
  564.9 10.6 %reshape.284 = bf16[4,2,294912]{2,1,0:T(2,128)(2,1)} reshape(bf16[512,3,3,8,64]{4,3,2,1,0:T(8,128)(2,1)} %bitcast.197) | data formatting | bytes 9437184
  575.5 154.6 %all_to_all.66 = bf16[4,2,294912]{2,1,0:T(2,128)(2,1)} all-to-all(bf16[4,2,294912]{2,1,0:T(2,128)(2,1)} %reshape.284), channel_id=1, replica_groups=mesh['dp'=8,'seq'=4] {'seq'}, dimensions={0} | all-to-all | bytes 9437184 | tf_op jit(solution)/shard_map/all_to_all | solution.py:227
  730.2 10.2 %reshape.285 = bf16[512,3,3,8,64]{4,3,2,1,0:T(8,128)(2,1)} reshape(bf16[4,2,294912]{2,1,0:T(2,128)(2,1)} %all_to_all.66) | data formatting | bytes 9437184
  740.4 11.6 %copy.113 = bf16[8,4,128,3,3,64]{2,0,5,4,1,3:T(8,128)(2,1)} copy(bf16[8,4,128,3,3,64]{5,0,4,3,2,1:T(8,128)(2,1)} %bitcast.198) | data formatting | bytes 9437184 | tf_op jit(solution)/shard_map/all_to_all | solution.py:227
  752.0 8.3 convolution_bitcast_fusion
  760.3 8.3 copy.121
  768.7 6.6 convert_reduce_fusion.1
  775.5 42.1 %all-reduce.18 = (f32[768]{0:T(1024)S(1)}, f32[768]{0:T(1024)S(1)}, f32[768]{0:T(1024)S(1)}, f32[768]{0:T(1024)S(1)}, f32[768]{0:T(1024)S(1)}, /*index=5*/f32[30...) all-reduce(f32[768]{0:T(1024)S(1)} %slice.35, ...), channel_id=3, replica_groups=mesh['dp'=8,'seq'=4] {'dp','seq'}, use_global_device_ids=true, to_apply=%region_19.20.clone | all-reduce | flops 9216 | bytes 73728
  822.8 9.1 fusion.47
  831.9 29.8 %reduce-scatter.11.cloned.1.call-done = f32[96,768]{1,0:T(8,128)} async-done(((f32[3072,768]{1,0:T(8,128)}), f32[96,768]{1,0:T(8,128)}) %reduce-scatter.11.cloned.1.call-update) | async-done | bytes 294928 | tf_op jit(solution)/shard_map/reduce_scatter | solution.py:195
  861.8 125.3 %reduce-scatter.13.cloned.1.call-done = f32[24,2304]{1,0:T(8,128)} async-done(((f32[768,2304]{1,0:T(8,128)}), f32[24,2304]{1,0:T(8,128)}) %reduce-scatter.13.cloned.1.call-update) | async-done | bytes 221200
  (280 shorter events, 166.2 us)
Async XLA Ops:
  7.2 67.2 %all-gather.5.cloned.1.call-start = ((), (), s32[]{:S(2)}) async-start(), calls=%async_computation.8 | async-start | bytes 3649536 | tf_op jit(solution)/shard_map/all_gather | solution.py:111
  95.6 5.1 copy-start.9
  95.6 6.2 copy-start.6
  95.6 6.9 copy-start.13
  95.6 112.6 %all-to-all-start = ((bf16[8,128,3,12,64]{1,0,4,2,3:T(8,128)(2,1)}), bf16[8,128,3,12,64]{1,0,4,2,3:T(8,128)(2,1)}, u32[]{:S(2)}, u32[]{:S(2)}) async-start(bf16[8,128,3,12,64]{1,0,4,2,3:T(8,128)(2,1)} %copy.104), calls=%async_computation | async-start | bytes 9437184 | tf_op jit(solution)/shard_map/all_to_all | solution.py:133
  100.6 230.0 %all-gather.7.cloned.1.call-start = ((), (), s32[]{:S(2)}) async-start(), calls=%async_computation.9 | async-start | bytes 1216512 | tf_op jit(solution)/shard_map/all_gather | solution.py:114
  101.4 233.7 %all-gather.9.cloned.1.call-start = ((), (), s32[]{:S(2)}) async-start(), calls=%async_computation.10 | async-start | bytes 4866048 | tf_op jit(solution)/shard_map/all_gather | solution.py:147
  260.7 3.5 copy-start.8
  264.1 9.7 copy-start.7
  264.1 10.5 %copy-start = (bf16[8,128,768]{2,1,0:T(8,128)(2,1)S(1)}, bf16[8,128,768]{2,1,0:T(8,128)(2,1)}, u32[]{:S(2)}) copy-start(bf16[8,128,768]{2,1,0:T(8,128)(2,1)} %param.21) | copy-start | bytes 4718596
  269.3 53.8 %all-to-all-start.1 = ((bf16[4,2,98304]{2,1,0:T(2,128)(2,1)}), bf16[4,2,98304]{2,1,0:T(2,128)(2,1)}, u32[]{:S(2)}, u32[]{:S(2)}) async-start(bf16[4,2,98304]{2,1,0:T(2,128)(2,1)} %reshape.282), calls=%async_computation.1 | async-start | bytes 3145728 | tf_op jit(solution)/shard_map/all_to_all | solution.py:136
  273.8 97.2 %all-gather.11.cloned.1.call-start = ((), (), s32[]{:S(2)}) async-start(), calls=%async_computation.11 | async-start | bytes 4866048 | tf_op jit(solution)/shard_map/all_gather | solution.py:149
  274.5 557.4 %reduce-scatter.7.cloned.1.call-start = ((), (), s32[]{:S(2)}) async-start(), calls=%async_computation.12 | async-start | bytes 2433024 | tf_op jit(solution)/shard_map/reduce_scatter | solution.py:243
  379.8 1.4 copy-start.1
  415.3 2.8 copy-start.5
  416.5 1.6 copy-start.2
  421.0 410.9 %reduce-scatter.9.cloned.1.call-start = ((), (), s32[]{:S(2)}) async-start(), calls=%async_computation.13 | async-start | bytes 9732096 | tf_op jit(solution)/shard_map/reduce_scatter | solution.py:193
  431.9 1.9 copy-start.3
  441.0 47.2 %all-to-all-start.2 = ((bf16[8,128,12,64]{1,0,3,2:T(8,128)(2,1)}), bf16[8,128,12,64]{1,0,3,2:T(8,128)(2,1)S(1)}, u32[]{:S(2)}, u32[]{:S(2)}) async-start(bf16[8,128,12,64]{1,0,3,2:T(8,128)(2,1)} %bitcast.57), calls=%async_computation.2 | async-start | bytes 3145728 | tf_op jit(solution)/shard_map/all_to_all | solution.py:221
  444.6 417.2 %reduce-scatter.11.cloned.1.call-start = ((), (), s32[]{:S(2)}) async-start(), calls=%async_computation.14 | async-start | bytes 9732096 | tf_op jit(solution)/shard_map/reduce_scatter | solution.py:195
  455.1 531.9 %reduce-scatter.13.cloned.1.call-start = ((), (), s32[]{:S(2)}) async-start(), calls=%async_computation.15 | async-start | bytes 7299072
  740.4 11.6 %copy-start.14 = (bf16[8,128,768]{2,1,0:T(8,128)(2,1)S(1)}, bf16[8,128,768]{2,1,0:T(8,128)(2,1)}, u32[]{:S(2)}) copy-start(bf16[8,128,768]{2,1,0:T(8,128)(2,1)} %param.20) | copy-start | bytes 4718596
  768.6 6.8 copy-start.10
  768.7 6.8 copy-start.11
  768.7 6.8 copy-start.12
  768.7 54.2 %copy-start.4 = (f32[1024,768]{1,0:T(8,128)S(1)}, f32[1024,768]{1,0:T(8,128)}, u32[]{:S(2)}) copy-start(f32[1024,768]{1,0:T(8,128)} %copy-done.2) | copy-start | bytes 9437188
Sparse Core Ops, SparseCore 0:
  11.4 62.9 all-gather.4
  104.8 120.2 all-gather.6
  228.5 73.8 all-gather.8
  305.6 64.9 all-gather.10
  421.1 102.5 reduce-scatter.6
  531.0 188.1 reduce-scatter.8
  725.7 136.0 reduce-scatter.10
  869.0 118.0 reduce-scatter.12
where the time goes:
time: 1000 us; the launch traced here: 994 us
  waiting for transfers between devices  356 us (36%)
  blocking collectives  239 us (24%)
  matrix products  173 us (17%)
  local copies, waits for them, and re-layouts  144 us (14%)
  other arithmetic  52.7 us (5%)
  between operations  14.8 us (1%)
  starting transfers between devices  13.7 us (1%)
    all_to_all x1, blocking collectives, shards(): lax.all_to_all(packed_grad_heads, 'seq', split_axis=1, concat_axis=3, til...  155 us
    unnamed x9, waiting for transfers between devices  125 us
    all_to_all x1, waiting for transfers between devices, shards(): lax.all_to_all(packed, 'seq', split_axis=3, concat_axis=1, tiled=True)  106 us
    unnamed x2, blocking collectives  84.8 us
    unnamed x64, local copies, waits for them, and re-layouts  55.3 us
    all_to_all x1, waiting for transfers between devices, shards(): lax.all_to_all(context_heads, 'seq', split_axis=1, concat_axis=2, tiled=T...  47.2 us
    dot_general x1, matrix products, shards(): jnp.dot(hidden_low, whole_inner, preferred_element_type=jnp.float32)  35.8 us
    all_to_all x1, waiting for transfers between devices, shards(): lax.all_to_all(context_grad, 'seq', split_axis=2, concat_axis=1, tiled=True)  33 us
  transfers between devices with their start and end apart: 11, of which 6 were waited for; matrix products, arithmetic and copies ran while one was open for 29% of the time, Pallas kernels for 0%

commit v1 on v0

v1 whole, which is shorter than its diff:
```python
from functools import partial

import jax
import jax.numpy as jnp
from jax import lax
from jax.sharding import PartitionSpec as P

HEAD_DIM = 64


EPSILON = 1e-06
AXES = ("dp", "seq")


def narrow(value):
    return value.astype(jnp.bfloat16)


def widen(value):
    return value.astype(jnp.float32)


def normalize(summed, gain, shift):
    average = jnp.mean(summed, axis=-1, keepdims=True)
    centred = summed - average
    variance = jnp.mean(centred * centred, axis=-1, keepdims=True)
    inverse = lax.rsqrt(variance + EPSILON)
    normed = centred * inverse
    return (normed * gain + shift, normed, inverse)


def normalize_back(upstream, normed, inverse, gain):
    scaled = upstream * gain
    first_mean = jnp.mean(scaled, axis=-1, keepdims=True)
    second_mean = jnp.mean(scaled * normed, axis=-1, keepdims=True)
    result = inverse * (scaled - first_mean - normed * second_mean)
    return (result, jnp.sum(upstream * normed, axis=0), jnp.sum(upstream, axis=0))


def masked_scores(query_rows, key_rows, labels):
    scale = query_rows.shape[-1] ** (-0.5)
    scores = (
        jnp.einsum("qhd,khd->hqk", query_rows, key_rows, preferred_element_type=jnp.float32) * scale
    )
    allowed = labels[:, None] == labels[None, :]
    return jnp.where(allowed[None], scores, -1e30)


def attend_forward(pieces):
    packed, labels = pieces
    query_rows, key_rows, value_rows = (packed[:, 0], packed[:, 1], packed[:, 2])
    scores = masked_scores(query_rows, key_rows, labels)
    highest = jnp.max(scores, axis=-1, keepdims=True)
    raised = jnp.exp(scores - highest)
    summed = jnp.sum(raised, axis=-1, keepdims=True)
    softmaxed = raised / summed
    context = jnp.einsum(
        "hqk,khd->qhd", narrow(softmaxed), value_rows, preferred_element_type=jnp.float32
    )
    return (narrow(context), (highest + jnp.log(summed))[..., 0])


def attend_backward(pieces):
    packed, labels, log_total, upstream = pieces
    query_rows, key_rows, value_rows = (packed[:, 0], packed[:, 1], packed[:, 2])
    scale = query_rows.shape[-1] ** (-0.5)
    scores = masked_scores(query_rows, key_rows, labels)
    softmaxed = jnp.exp(scores - log_total[..., None])
    value_grad = jnp.einsum(
        "hqk,qhd->khd", narrow(softmaxed), upstream, preferred_element_type=jnp.float32
    )
    prob_grad = jnp.einsum("qhd,khd->hqk", upstream, value_rows, preferred_element_type=jnp.float32)
    weighted = jnp.sum(softmaxed * prob_grad, axis=-1, keepdims=True)
    score_grad = narrow(softmaxed * (prob_grad - weighted))
    query_grad = (
        jnp.einsum("hqk,khd->qhd", score_grad, key_rows, preferred_element_type=jnp.float32) * scale
    )
    key_grad = (
        jnp.einsum("hqk,qhd->khd", score_grad, query_rows, preferred_element_type=jnp.float32)
        * scale
    )
    return narrow(jnp.stack([query_grad, key_grad, value_grad], axis=1))


def block_at(blocks, index, axis=0):
    return lax.dynamic_index_in_dim(blocks, index, axis, keepdims=False)


class Links:
    def __init__(self, mesh):
        self.dp, self.seq = mesh.shape["dp"], mesh.shape["seq"]
        self.bits = self.dp.bit_length() - 1
        assert self.dp == 1 << self.bits

    def along(self, value, step):
        pairs = [
            (d * self.seq + s, d * self.seq + (s + step) % self.seq)
            for d in range(self.dp)
            for s in range(self.seq)
        ]
        return lax.ppermute(value, AXES, pairs)

    def across(self, value, bit):
        pairs = [
            (d * self.seq + s, (d ^ (1 << bit)) * self.seq + s)
            for d in range(self.dp)
            for s in range(self.seq)
        ]
        return lax.ppermute(value, AXES, pairs)

    def digit(self, bit):
        return (lax.axis_index("dp") >> bit) & 1

    def orders(self):
        upward = list(range(1, self.bits))
        return upward, upward[::-1]

    def gather(self, shard, order):
        place = lax.axis_index("seq")
        held = jnp.zeros((self.seq,) + shard.shape, shard.dtype)
        held = lax.dynamic_update_index_in_dim(held, shard, place, 0)
        for step in range(1, self.seq):
            held = lax.dynamic_update_index_in_dim(
                held, self.along(shard, step), (place - step) % self.seq, 0
            )
        done = []
        for bit in order + [0]:
            axis = sum(other > bit for other in done)
            other = self.across(held, bit)
            mine = self.digit(bit)
            whole = jnp.zeros(held.shape[:axis] + (2,) + held.shape[axis:], held.dtype)
            whole = lax.dynamic_update_index_in_dim(whole, held, mine, axis)
            held = lax.dynamic_update_index_in_dim(whole, other, 1 - mine, axis)
            done.append(bit)
        return held.reshape(self.dp * self.seq * shard.shape[0], *shard.shape[1:])

    def reduce(self, whole, order):
        rows = whole.shape[0] // (self.dp * self.seq)
        held = whole.reshape((2,) * self.bits + (self.seq, rows) + whole.shape[1:])
        left = list(range(self.bits))[::-1]
        for bit in [0] + order:
            axis = left.index(bit)
            mine = self.digit(bit)
            other = self.across(block_at(held, 1 - mine, axis), bit)
            held = narrow(widen(block_at(held, mine, axis)) + widen(other))
            left.remove(bit)
        place = lax.axis_index("seq")
        total = widen(block_at(held, place))
        for step in range(1, self.seq):
            sent = block_at(held, (place + step) % self.seq)
            total = total + widen(self.along(sent, step))
        return total

    def to_rows(self, value):
        place = lax.axis_index("seq")
        blocks = value.reshape(self.seq, value.shape[0] // self.seq, *value.shape[1:])
        pieces = [block_at(blocks, place)]
        for step in range(1, self.seq):
            pieces.append(self.along(block_at(blocks, (place + step) % self.seq), step))
        return jnp.stack(pieces)

    def from_rows(self, value):
        place = lax.axis_index("seq")
        blocks = jnp.zeros_like(value)
        for step in range(self.seq):
            piece = value[step]
            if step:
                piece = self.along(piece, -step)
            blocks = lax.dynamic_update_index_in_dim(blocks, piece, (place + step) % self.seq, 0)
        return blocks.reshape(self.seq * value.shape[1], *value.shape[2:])


def columns(vectors, rows):
    block = jnp.concatenate([vector.reshape(rows, -1) for vector in vectors], axis=1)
    return jnp.pad(block, ((0, 0), (0, 128 - block.shape[1])))


def shards(
    links,
    tokens,
    cotangent,
    lengths,
    packed_weight,
    query_bias,
    value_bias,
    output_weight,
    output_bias,
    first_gain,
    first_shift,
    inner_weight,
    inner_bias,
    outer_weight,
    outer_bias,
    second_gain,
    second_shift,
):
    row_count, local_length, width = tokens.shape
    heads_all = width // HEAD_DIM
    seq = links.seq
    place = lax.axis_index("seq")
    rows = row_count // seq
    length = seq * local_length
    small = packed_weight.shape[0]
    first_order, second_order = links.orders()

    tokens_mine = links.to_rows(tokens)
    attention_vectors = columns(
        [narrow(v) for v in (query_bias, value_bias, output_bias, first_gain, first_shift)], small
    )
    half_one = links.gather(narrow(packed_weight[:, : 2 * width]), first_order)
    half_two = links.gather(
        jnp.concatenate(
            [narrow(packed_weight[:, 2 * width :]), narrow(output_weight), attention_vectors], axis=1
        ),
        second_order,
    )
    whole_packed = jnp.concatenate([half_one, half_two[:, :width]], axis=1)
    whole_output = half_two[:, width : 2 * width]
    vectors = widen(half_two[:, 2 * width : 2 * width + 8].T)
    whole_query, whole_value, whole_outbias, gain_one, shift_one = (vectors[i] for i in range(5))

    feed_vectors = columns(
        [narrow(v) for v in (outer_bias, second_gain, second_shift, inner_bias)], small
    )
    feed_one = links.gather(
        jnp.concatenate([narrow(inner_weight), feed_vectors], axis=1), first_order
    )
    whole_outer = links.gather(narrow(outer_weight), second_order)
    whole_inner = feed_one[:, : inner_weight.shape[1]]
    feed_rows = feed_one[:, inner_weight.shape[1] :]
    vectors = widen(feed_rows[:, :3].T)
    whole_outerbias, gain_two, shift_two = (vectors[i] for i in range(3))
    whole_innerbias = widen(feed_rows[:, 3 : 3 + inner_weight.shape[1] // width]).reshape(-1)

    starts = (place - jnp.arange(seq, dtype=jnp.int32)) % seq * local_length
    places = (starts[:, None] + jnp.arange(local_length, dtype=jnp.int32)[None]).reshape(-1)
    mine = lax.dynamic_slice_in_dim(lengths, place * rows, rows, 0)
    bounds = jnp.cumsum(mine, axis=-1)[..., :-1]
    labels = jnp.sum((places[None, :, None] >= bounds[:, None, :]).astype(jnp.int32), axis=-1)

    flat = tokens_mine.reshape(-1, width)
    middle = jnp.zeros((width,), jnp.float32)
    bias_row = jnp.concatenate([whole_query, middle, whole_value])
    mixed = jnp.dot(flat, whole_packed, preferred_element_type=jnp.float32) + bias_row
    packed = narrow(mixed).reshape(seq, rows, local_length, 3, heads_all, HEAD_DIM)
    spread_rows = packed.swapaxes(0, 1).reshape(rows, length, 3, heads_all, HEAD_DIM)
    context_rows, log_totals = lax.map(attend_forward, (spread_rows, labels))
    context = (
        context_rows.reshape(rows, seq, local_length, width).swapaxes(0, 1).reshape(-1, width)
    )
    projected = jnp.dot(context, whole_output, preferred_element_type=jnp.float32) + whole_outbias
    hidden, first_normed, first_inverse = normalize(widen(flat) + projected, gain_one, shift_one)
    hidden_low = narrow(hidden)
    inner = (
        jnp.dot(hidden_low, whole_inner, preferred_element_type=jnp.float32) + whole_innerbias
    )
    active = narrow(jax.nn.gelu(inner, approximate=False))
    branch = jnp.dot(active, whole_outer, preferred_element_type=jnp.float32) + whole_outerbias
    result, second_normed, second_inverse = normalize(hidden + branch, gain_two, shift_two)
    output = links.from_rows(narrow(result).reshape(seq, rows, local_length, width))

    upstream = widen(links.to_rows(cotangent)).reshape(-1, width)
    second_up, second_gain_grad, second_shift_grad = normalize_back(
        upstream, second_normed, second_inverse, gain_two
    )
    branch_grad = narrow(second_up)
    outer_weight_grad = narrow(
        jnp.einsum("tf,td->fd", active, branch_grad, preferred_element_type=jnp.float32)
    )
    outer_bias_grad = jnp.sum(widen(branch_grad), axis=0)
    active_grad = jnp.einsum(
        "td,fd->tf", branch_grad, whole_outer, preferred_element_type=jnp.float32
    )
    gelu_pull = jax.vjp(partial(jax.nn.gelu, approximate=False), inner)[1]
    inner_grad = narrow(gelu_pull(active_grad)[0])
    inner_weight_grad = narrow(
        jnp.einsum("td,tf->df", hidden_low, inner_grad, preferred_element_type=jnp.float32)
    )
    inner_bias_grad = jnp.sum(widen(inner_grad), axis=0)
    hidden_grad = second_up + jnp.einsum(
        "tf,df->td", inner_grad, whole_inner, preferred_element_type=jnp.float32
    )
    feed_sums = columns(
        [
            narrow(v)
            for v in (outer_bias_grad, second_gain_grad, second_shift_grad, inner_bias_grad)
        ],
        width,
    )
    feed_share = links.reduce(
        jnp.concatenate([inner_weight_grad, feed_sums], axis=1), first_order
    )
    outer_share = links.reduce(outer_weight_grad, second_order)

    first_up, first_gain_grad, first_shift_grad = normalize_back(
        hidden_grad, first_normed, first_inverse, gain_one
    )
    projected_grad = narrow(first_up)
    output_weight_grad = narrow(
        jnp.einsum("td,te->de", context, projected_grad, preferred_element_type=jnp.float32)
    )
    output_bias_grad = jnp.sum(widen(projected_grad), axis=0)
    context_grad = narrow(
        jnp.einsum("te,de->td", projected_grad, whole_output, preferred_element_type=jnp.float32)
    )
    context_grad_rows = (
        context_grad.reshape(seq, rows, local_length, width)
        .swapaxes(0, 1)
        .reshape(rows, length, heads_all, HEAD_DIM)
    )
    packed_grad_rows = lax.map(
        attend_backward, (spread_rows, labels, log_totals, context_grad_rows)
    )
    packed_grad = (
        packed_grad_rows.reshape(rows, seq, local_length, 3 * width)
        .swapaxes(0, 1)
        .reshape(-1, 3 * width)
    )
    packed_weight_grad = narrow(
        jnp.einsum("td,tc->dc", flat, packed_grad, preferred_element_type=jnp.float32)
    )
    column_sums = jnp.sum(widen(packed_grad), axis=0)
    tokens_grad = first_up + jnp.einsum(
        "tc,dc->td", packed_grad, whole_packed, preferred_element_type=jnp.float32
    )
    tokens_grad = widen(
        links.from_rows(narrow(tokens_grad).reshape(seq, rows, local_length, width))
    )
    attention_sums = columns(
        [
            narrow(v)
            for v in (
                column_sums[:width],
                column_sums[2 * width :],
                output_bias_grad,
                first_gain_grad,
                first_shift_grad,
            )
        ],
        width,
    )
    one_share = links.reduce(packed_weight_grad[:, : 2 * width], first_order)
    two_share = links.reduce(
        jnp.concatenate(
            [packed_weight_grad[:, 2 * width :], output_weight_grad, attention_sums], axis=1
        ),
        second_order,
    )
    feed = inner_weight.shape[1]
    wide = feed // width
    return (
        output,
        tokens_grad,
        jnp.concatenate([one_share, two_share[:, :width]], axis=1),
        two_share[:, 2 * width],
        two_share[:, 2 * width + 1],
        two_share[:, width : 2 * width],
        two_share[:, 2 * width + 2],
        two_share[:, 2 * width + 3],
        two_share[:, 2 * width + 4],
        feed_share[:, :feed],
        feed_share[:, feed + 3 : feed + 3 + wide].reshape(-1),
        outer_share,
        feed_share[:, feed],
        feed_share[:, feed + 1],
        feed_share[:, feed + 2],
    )


def solution(mesh):
    split = P(AXES)
    split_rows = P(AXES, None)
    packed_rows = P("dp", "seq", None)
    return jax.shard_map(
        partial(shards, Links(mesh)),
        mesh=mesh,
        in_specs=(
            packed_rows,
            packed_rows,
            P("dp", None),
            split_rows,
            split,
            split,
            split_rows,
            split,
            split,
            split,
            split_rows,
            split,
            split_rows,
            split,
            split,
            split,
        ),
        out_specs=(
            packed_rows,
            packed_rows,
            split_rows,
            split,
            split,
            split_rows,
            split,
            split,
            split,
            split_rows,
            split,
            split_rows,
            split,
            split,
            split,
        ),
        check_vma=False,
    )
```

time: 1000 us -> 658 us (0.66)
  blocking collectives: 239 us -> 0 us
  waiting for transfers between devices: 356 us -> 164 us
  starting transfers between devices: 13.7 us -> 127 us
  between operations: 14.8 us -> 2.4 us
  matrix products: 173 us -> 162 us
    all_to_all x3 -> x0, waiting for transfers between devices: 186 us -> none  [the longest x1 106 us: shards(): lax.all_to_all(packed, 'seq', split_axis=3, concat_axis=1, tiled=True)]
    ppermute x0 -> x60, waiting for transfers between devices: none -> 164 us  [the longest x24 82.7 us: across(): return lax.ppermute(value, AXES, pairs)]
    all_to_all x1 -> x0, blocking collectives: 155 us -> none  [shards(): lax.all_to_all(packed_grad_heads, 'seq', split_axis=1, concat_axis=3, til...]
    ppermute x0 -> x60, starting transfers between devices: none -> 127 us  [the longest x36 107 us: along(): return lax.ppermute(value, AXES, pairs)]
    unnamed x9 -> x0, waiting for transfers between devices: 125 us -> none
    unnamed x2 -> x0, blocking collectives: 84.8 us -> none
    unnamed x64 -> x135, local copies, waits for them, and re-layouts: 55.3 us -> 10.1 us
    reshape x1 -> x16, local copies, waits for them, and re-layouts: 2.48 us -> 39.7 us  [the longest x2 16.3 us: shards(): packed_grad_rows.reshape(rows, seq, local_length, 3 * width).swapaxes(0, 1)]
  transfers between devices with their start and end apart: 11 -> 60, of which waited for: 6 -> 24; matrix products, arithmetic and copies ran while one was open for 29% -> 23% of each run, Pallas kernels for 0% -> 0%
where the time goes in v1:
time: 658 us; the launch traced here: 653 us
  waiting for transfers between devices  164 us (25%)
  matrix products  162 us (25%)
  local copies, waits for them, and re-layouts  136 us (21%)
  starting transfers between devices  127 us (19%)
  other arithmetic  60.1 us (9%)
    ppermute x36, starting transfers between devices, along(): return lax.ppermute(value, AXES, pairs)  107 us
    ppermute x24, waiting for transfers between devices, across(): return lax.ppermute(value, AXES, pairs)  82.7 us
    ppermute x36, waiting for transfers between devices, along(): return lax.ppermute(value, AXES, pairs)  81.3 us
    dot_general x1, matrix products, shards(): jnp.dot(hidden_low, whole_inner, preferred_element_type=jnp.float32)  36.5 us
    convert_element_type x17, other arithmetic, narrow(): return value.astype(jnp.bfloat16)  22.1 us
    ppermute x24, starting transfers between devices, across(): return lax.ppermute(value, AXES, pairs)  20.2 us
    dot_general x1, matrix products, shards(): jnp.einsum('td,fd->tf', branch_grad, whole_outer, preferred_element_type=...  19.8 us
    reshape x2, local copies, waits for them, and re-layouts, shards(): packed_grad_rows.reshape(rows, seq, local_length, 3 * width).swapaxes(0, 1)  16.3 us
  transfers between devices with their start and end apart: 60, of which 24 were waited for; matrix products, arithmetic and copies ran while one was open for 23% of the time, Pallas kernels for 0%

profile of v1, /device:TPU:0, one launch (start us, length us, event | category | flops | bytes accessed | tf_op | source)
XLA Modules:
  0.0 652.5 jit_solution(7546110237661441440)
XLA Ops:
  55.9 15.1 %collective-permute-start.1 = (bf16[2,128,768]{1,2,0:T(8,128)(2,1)}, bf16[2,128,768]{1,2,0:T(8,128)(2,1)S(1)}, u32[]{:S(2)}, u32[]{:S(2)}) collective-permute-start(bf16[2,128,768]{1,2,0:T(8,128)(2,1)} %get-tuple-element.154), channel_id=1, source_target_pairs={{0,2},{1,3},{2,0},{3,1},{4,6},{5,7},{6,4},{7,5},{8,10},{9,11},{10,... | collective-permute-start | bytes 1179656 | tf_op jit(solution)/shard_map/ppermute | solution.py:101
  87.7 7.1 %collective-permute-done.1 = bf16[2,128,768]{1,2,0:T(8,128)(2,1)S(1)} collective-permute-done((bf16[2,128,768]{1,2,0:T(8,128)(2,1)}, bf16[2,128,768]{1,2,0:T(8,128)(2,1)S(1)}, u32[]{:S(2)}, u32[]{:S(2)}) %collective-permute-start.1) | collective-permute-done | bytes 393248 | tf_op jit(solution)/shard_map/ppermute | solution.py:101
  101.5 17.7 %collective-permute-done.31 = bf16[2,128,768]{2,1,0:T(8,128)(2,1)S(1)} collective-permute-done((bf16[2,128,768]{2,1,0:T(8,128)(2,1)}, bf16[2,128,768]{2,1,0:T(8,128)(2,1)S(1)}, u32[]{:S(2)}, u32[]{:S(2)}) %collective-permute-start.31) | collective-permute-done | bytes 393248 | tf_op jit(solution)/shard_map/ppermute | solution.py:101
  140.7 18.1 %collective-permute-done.25 = bf16[2,4,96,768]{3,2,1,0:T(8,128)(2,1)S(1)} collective-permute-done((bf16[2,4,96,768]{3,2,1,0:T(8,128)(2,1)S(1)}, bf16[2,4,96,768]{3,2,1,0:T(8,128)(2,1)S(1)}, u32[]{:S(2)}, u32[]{:S(2)}) %collective-permute-start.25) | collective-permute-done | bytes 1179680 | tf_op jit(solution)/shard_map/ppermute | solution.py:109
  179.8 6.6 %copy.173 = bf16[1024,2304]{0,1:T(8,128)(2,1)} copy(bf16[1024,2304]{1,0:T(8,128)(2,1)} %add_convert_fusion.1) | data formatting | bytes 9437184 | tf_op jit(solution)/shard_map/convert_element_type | solution.py:16
  186.4 8.7 %reshape.455 = bf16[4,2,128,3,12,64]{2,1,0,5,4,3:T(2,128)(2,1)} reshape(bf16[1024,2304]{0,1:T(8,128)(2,1)} %copy.173) | data formatting | bytes 9437184 | tf_op jit(solution)/shard_map/reshape | solution.py:245
  195.1 6.8 %copy.174 = bf16[2,4,128,3,12,64]{2,1,5,4,3,0:T(4,128)(2,1)} copy(bf16[2,4,128,3,12,64]{2,0,1,5,4,3:T(2,128)(2,1)} %bitcast.438) | data formatting | bytes 9437184 | tf_op jit(solution)/shard_map/transpose | solution.py:246
  202.0 8.0 %reshape.456 = bf16[2,512,3,12,64]{1,4,3,2,0:T(8,128)(2,1)} reshape(bf16[2,4,128,3,12,64]{2,1,5,4,3,0:T(4,128)(2,1)} %copy.174) | data formatting | bytes 9437184 | tf_op jit(solution)/shard_map/reshape | solution.py:246
  210.0 22.6 %while.22 = (s32[]{:T(128)}, bf16[2,512,12,64]{1,3,2,0:T(8,128)(2,1)}, f32[2,12,512]{2,1,0:T(8,128)S(1)}, bf16[2,512,3,12,64]{1,4,3,2,0:T(8,128)(2,1)}, s32[2,512]{1,0:T(2,128)S(1)}, /*index=5*/s32[]{:T(128)}) while((s32[]{:T(128)}, bf16[2,512,12,64]{1,3,2,0:T(8,128)(2,1)}, f32[2,12,512]{2,1,0:T(8,128)S(1)}, ...), condition=%wide.region_5.6_spmd, body=%wide.region_2.5_spmd.sunk | while | flops 843704320 | bytes 46905936 | solution.py:247
  253.3 36.5 %multiply_convert_fusion.3 = (bf16[1024,3072]{1,0:T(8,128)(2,1)S(1)}, f32[1024,3072]{1,0:T(8,128)}, f32[1024,3072]{1,0:T(8,128)}) fusion(f32[3072]{0:T(1024)} %reshape.481, bf16[768,3200]{1,0:T(8,128)(2,1)} %bitcast.459, f32[1024,768]{1,0:T(8,128)S(1)} %get-tuple-element.173, f32[768]{0:T(1024)} %get-tuple-element.88, f32[768]{0:T(1024)S(1)} %copy-done.49, ...), kind=kOutput, calls=%fused_computation.52 | convolution fusion | flops 5043388416 | bytes 39349248 | tf_op jit(solution)/shard_map/dot_general | solution.py:255
  289.9 7.8 %fusion.113 = (f32[1024]{0:T(1024)S(1)}, f32[1024,768]{1,0:T(8,128)S(1)}) fusion(f32[768]{0:T(1024)S(1)} %get-tuple-element.86, bf16[1024,3072]{1,0:T(8,128)(2,1)S(1)} %get-tuple-element.130, bf16[3072,768]{1,0:T(8,128)(2,1)} %bitcast.91, f32[768]{0:T(1024)S(1)} %copy-done.55, f32[768]{0:T(1024)S(1)} %copy-done.49, f32[1024]{0:T(1024)S(1)} %add_rsqrt_fusion.1, ...), kind=kOutput, calls=%fused_computation.316 | convolution fusion | flops 4837342208 | bytes 17323008 | tf_op jit(solution)/shard_map/dot_general | solution.py:258
  305.4 6.9 %convolution_convert_fusion = bf16[3072,768]{1,0:T(8,128)(2,1)} fusion(bf16[1024,3072]{1,0:T(8,128)(2,1)S(1)} %get-tuple-element.130, f32[1024,768]{1,0:T(8,128)S(1)} %get-tuple-element.123), kind=kOutput, calls=%fused_computation.70 | convolution fusion | flops 4834983936 | bytes 14155776 | tf_op jit(solution)/shard_map/tf,td->fd/dot_general | solution.py:268
  312.3 19.8 %fusion.114 = (bf16[3072]{0:T(1024)(128)(2,1)}, bf16[1024,3072]{1,0:T(8,128)(2,1)}) fusion(f32[1024,3072]{1,0:T(8,128)} %get-tuple-element.131, bf16[3072,768]{1,0:T(8,128)(2,1)} %bitcast.91, f32[1024,768]{1,0:T(8,128)} %copy-done.22, f32[1024,3072]{1,0:T(8,128)} %get-tuple-element.174, f32[3072]{0:T(1024)S(1)} %copy-done.50), kind=kOutput, calls=%fused_computation.317 | convolution fusion | flops 4882953216 | bytes 39340032 | tf_op jit(solution)/shard_map/td,fd->tf/dot_general | solution.py:271
  332.1 10.0 %convolution_convert_fusion.1 = bf16[768,3072]{1,0:T(8,128)(2,1)} fusion(bf16[1024,3072]{1,0:T(8,128)(2,1)} %get-tuple-element.179, f32[1024,768]{1,0:T(8,128)S(1)} %get-tuple-element.173, f32[768]{0:T(1024)S(1)} %copy-done.55, f32[768]{0:T(1024)S(1)} %copy-done.49, f32[1024]{0:T(1024)S(1)} %add_rsqrt_fusion.1, f32[1024]{0:T(1024)S(1)} %broadcast_multiply_fusion.5), kind=kOutput, calls=%fused_computation.71 | convolution fusion | flops 4838129664 | bytes 14170112 | tf_op jit(solution)/shard_map/td,tf->df/dot_general | solution.py:277
  342.1 8.9 %multiply_reduce_fusion.1 = (bf16[768]{0:T(1024)(128)(2,1)}, f32[1024]{0:T(1024)S(1)}, f32[1024]{0:T(1024)S(1)}, bf16[768]{0:T(1024)(128)(2,1)}, f32[1024,768]{1,0:T(8,128)S(1)}) fusion(f32[1024,768]{1,0:T(8,128)S(1)} %get-tuple-element.173, f32[1024]{0:T(1024)S(1)} %add_rsqrt_fusion.1, f32[1024]{0:T(1024)S(1)} %broadcast_multiply_fusion.5, ...), kind=kOutput, calls=%fused_computation.93 | convolution fusion | flops 4839698432 | bytes 20469760 | tf_op jit(solution)/shard_map/tf,df->td/dot_general | solution.py:280
  361.2 50.2 %while.23 = (s32[]{:T(128)}, bf16[2,512,3,12,64]{1,4,3,2,0:T(8,128)(2,1)}, bf16[2,512,3,12,64]{1,4,3,2,0:T(8,128)(2,1)}, s32[2,512]{1,0:T(2,128)S(1)}, f32[2,12,...) while((s32[]{:T(128)}, bf16[2,512,3,12,64]{1,4,3,2,0:T(8,128)(2,1)}, ...), condition=%wide.region_16.17_spmd, body=%wide.region_14.16_spmd.sunk | while | flops 2069751808 | bytes 112917088 | solution.py:311
  365.1 6.8 %multiply_reduce_fusion.7 = (f32[12,512]{1,0:T(8,128)S(1)}, f32[12,512,512]{1,2,0:T(8,128)}) fusion(f32[12,512,512]{1,2,0:T(8,128)S(1)} %fusion.145, f32[12,512]{1,0:T(8,128)S(1)} %dynamic-slice_bitcast_fusion.36, pred[512,512]{0,1:T(8,128)(4,1)S(1)} %broadcast_compare_fusion.5, bf16[512,3,12,64]{0,3,2,1:T(8,128)(2,1)S(1)} %dynamic-slice_bitcast_fusion.35, ...), kind=kOutput, calls=%fused_computation.20.clone.1 | convolution fusion | flops 418375680 | bytes 27058180 | tf_op jit(solution)/shard_map/while/body/eval_jaxpr/qhd,khd->hqk/dot_general | solution.py:72
  371.9 6.6 %multiply_convert_fusion.5 = bf16[12,512,512]{1,2,0:T(8,128)(2,1)S(1)} fusion(f32[12,512,512]{1,2,0:T(8,128)} %get-tuple-element.258, f32[12,512,512]{1,2,0:T(8,128)S(1)} %fusion.145, f32[12,512]{1,0:T(8,128)S(1)} %get-tuple-element.259, f32[12,512]{1,0:T(8,128)S(1)} %dynamic-slice_bitcast_fusion.36, pred[512,512]{0,1:T(8,128)(4,1)S(1)} %broadcast_compare_fusion.5), kind=kLoop, calls=%fused_computation.19.clone.1 | loop fusion | flops 18874368 | bytes 31768576 | tf_op jit(solution)/shard_map/while/body/eval_jaxpr/convert_element_type | solution.py:16
  390.2 6.8 %multiply_reduce_fusion.7 = (f32[12,512]{1,0:T(8,128)S(1)}, f32[12,512,512]{1,2,0:T(8,128)}) fusion(f32[12,512,512]{1,2,0:T(8,128)S(1)} %fusion.145, f32[12,512]{1,0:T(8,128)S(1)} %dynamic-slice_bitcast_fusion.36, pred[512,512]{0,1:T(8,128)(4,1)S(1)} %broadcast_compare_fusion.5, bf16[512,3,12,64]{0,3,2,1:T(8,128)(2,1)S(1)} %dynamic-slice_bitcast_fusion.35, ...), kind=kOutput, calls=%fused_computation.20.clone.1 | convolution fusion | flops 418375680 | bytes 27058180 | tf_op jit(solution)/shard_map/while/body/eval_jaxpr/qhd,khd->hqk/dot_general | solution.py:72
  397.0 6.6 %multiply_convert_fusion.5 = bf16[12,512,512]{1,2,0:T(8,128)(2,1)S(1)} fusion(f32[12,512,512]{1,2,0:T(8,128)} %get-tuple-element.258, f32[12,512,512]{1,2,0:T(8,128)S(1)} %fusion.145, f32[12,512]{1,0:T(8,128)S(1)} %get-tuple-element.259, f32[12,512]{1,0:T(8,128)S(1)} %dynamic-slice_bitcast_fusion.36, pred[512,512]{0,1:T(8,128)(4,1)S(1)} %broadcast_compare_fusion.5), kind=kLoop, calls=%fused_computation.19.clone.1 | loop fusion | flops 18874368 | bytes 31768576 | tf_op jit(solution)/shard_map/while/body/eval_jaxpr/convert_element_type | solution.py:16
  411.4 7.7 %reshape.469 = bf16[2,4,128,2304]{2,1,3,0:T(4,128)(2,1)} reshape(bf16[2,512,3,12,64]{1,4,3,2,0:T(8,128)(2,1)} %get-tuple-element.77) | data formatting | bytes 9437184 | tf_op jit(solution)/shard_map/reshape | solution.py:315
  419.1 8.6 %copy.183 = bf16[2,4,128,2304]{3,2,0,1:T(8,128)(2,1)} copy(bf16[2,4,128,2304]{2,1,3,0:T(4,128)(2,1)} %reshape.469) | data formatting | bytes 9437184 | tf_op jit(solution)/shard_map/reshape | solution.py:315
  455.2 8.2 %add_convert_fusion.2 = bf16[1024,768]{1,0:T(8,128)(2,1)S(1)} fusion(f32[1024,768]{1,0:T(8,128)} %copy-done.20, bf16[1024,2304]{1,0:T(8,128)(2,1)} %bitcast.467, bf16[768,768]{1,0:T(8,128)(2,1)} %copy-done.33, bf16[768,1536]{1,0:T(8,128)(2,1)} %bitcast.469), kind=kOutput, calls=%fused_computation.94 | convolution fusion | flops 3632529408 | bytes 12976128 | tf_op jit(solution)/shard_map/tc,dc->td/dot_general | solution.py:323
  463.5 7.8 %collective-permute-start.33 = (bf16[2,128,768]{2,1,0:T(8,128)(2,1)S(1)}, bf16[2,128,768]{2,1,0:T(8,128)(2,1)S(1)}, u32[]{:S(2)}, u32[]{:S(2)}) collective-permute-start(bf16[2,128,768]{2,1,0:T(8,128)(2,1)S(1)} %bitcast.491), channel_id=1, source_target_pairs={{0,3},{1,0},{2,1},{3,2},{4,7},{5,4},{6,5},{7,6},{8,11},{9,8},{10,9... | collective-permute-start | bytes 1179656 | tf_op jit(solution)/shard_map/ppermute | solution.py:101
  480.9 19.3 %collective-permute-start.35 = (bf16[2,128,768]{2,1,0:T(8,128)(2,1)S(1)}, bf16[2,128,768]{2,1,0:T(8,128)(2,1)S(1)}, u32[]{:S(2)}, u32[]{:S(2)}) collective-permute-start(bf16[2,128,768]{2,1,0:T(8,128)(2,1)S(1)} %bitcast.488), channel_id=1, source_target_pairs={{0,1},{1,2},{2,3},{3,0},{4,5},{5,6},{6,7},{7,4},{8,9},{9,10},{10,1... | collective-permute-start | bytes 1179656 | tf_op jit(solution)/shard_map/ppermute | solution.py:101
  500.2 7.3 %collective-permute-done.34 = bf16[2,128,768]{2,1,0:T(8,128)(2,1)S(1)} collective-permute-done((bf16[2,128,768]{2,1,0:T(8,128)(2,1)S(1)}, bf16[2,128,768]{2,1,0:T(8,128)(2,1)S(1)}, u32[]{:S(2)}, u32[]{:S(2)}) %collective-permute-start.34) | collective-permute-done | bytes 393248 | tf_op jit(solution)/shard_map/ppermute | solution.py:101
  508.7 9.8 %collective-permute-done.27 = bf16[2,128,768]{2,1,0:T(8,128)(2,1)S(1)} collective-permute-done((bf16[2,128,768]{2,1,0:T(8,128)(2,1)S(1)}, bf16[2,128,768]{2,1,0:T(8,128)(2,1)S(1)}, u32[]{:S(2)}, u32[]{:S(2)}) %collective-permute-start.27) | collective-permute-done | bytes 393248 | tf_op jit(solution)/shard_map/ppermute | solution.py:101
  518.5 16.2 %collective-permute-start.29 = (bf16[2,128,768]{2,1,0:T(8,128)(2,1)S(1)}, bf16[2,128,768]{2,1,0:T(8,128)(2,1)S(1)}, u32[]{:S(2)}, u32[]{:S(2)}) collective-permute-start(bf16[2,128,768]{2,1,0:T(8,128)(2,1)S(1)} %bitcast.486), channel_id=1, source_target_pairs={{0,1},{1,2},{2,3},{3,0},{4,5},{5,6},{6,7},{7,4},{8,9},{9,10},{10,1... | collective-permute-start | bytes 1179656 | tf_op jit(solution)/shard_map/ppermute | solution.py:101
  549.6 12.3 %collective-permute-done.37 = bf16[2,4,24,1536]{3,2,1,0:T(8,128)(2,1)S(1)} collective-permute-done((bf16[2,4,24,1536]{3,2,1,0:T(8,128)(2,1)S(1)}, bf16[2,4,24,1536]{3,2,1,0:T(8,128)(2,1)S(1)}, u32[]{:S(2)}, u32[]{:S(2)}) %collective-permute-start.37) | collective-permute-done | bytes 589856 | tf_op jit(solution)/shard_map/ppermute | solution.py:109
  589.6 20.9 %collective-permute-done.55 = bf16[2,4,96,768]{3,2,1,0:T(8,128)(2,1)S(1)} collective-permute-done((bf16[2,4,96,768]{3,2,1,0:T(8,128)(2,1)S(1)}, bf16[2,4,96,768]{3,2,1,0:T(8,128)(2,1)S(1)}, u32[]{:S(2)}, u32[]{:S(2)}) %collective-permute-start.55) | collective-permute-done | bytes 1179680 | tf_op jit(solution)/shard_map/ppermute | solution.py:109
  616.6 8.7 %collective-permute-done.56 = bf16[4,96,768]{2,1,0:T(8,128)(2,1)S(1)} collective-permute-done((bf16[4,96,768]{2,1,0:T(8,128)(2,1)S(1)}, bf16[4,96,768]{2,1,0:T(8,128)(2,1)S(1)}, u32[]{:S(2)}, u32[]{:S(2)}) %collective-permute-start.56) | collective-permute-done | bytes 589856 | tf_op jit(solution)/shard_map/ppermute | solution.py:109
  643.5 6.5 collective-permute-done.52
  (475 shorter events, 311.4 us)
Async XLA Ops:
  4.8 29.1 %collective-permute-start.9 = (bf16[24,1664]{1,0:T(8,128)(2,1)S(1)}, bf16[24,1664]{1,0:T(8,128)(2,1)S(1)}, u32[]{:S(2)}, u32[]{:S(2)}) collective-permute-start(bf16[24,1664]{1,0:T(8,128)(2,1)S(1)} %fusion.86), channel_id=1, source_target_pairs={{0,1},{1,2},{2,3},{3,0},{4,5},{5,6},{6,7},{7,4},{8,9},{9,10},{10,1... | collective-permute-start | bytes 239624 | tf_op jit(solution)/shard_map/ppermute | solution.py:101
  7.8 30.6 %collective-permute-start.10 = (bf16[24,1664]{1,0:T(8,128)(2,1)S(1)}, bf16[24,1664]{1,0:T(8,128)(2,1)S(1)}, u32[]{:S(2)}, u32[]{:S(2)}) collective-permute-start(bf16[24,1664]{1,0:T(8,128)(2,1)S(1)} %fusion.86), channel_id=1, source_target_pairs={{0,2},{1,3},{2,0},{3,1},{4,6},{5,7},{6,4},{7,5},{8,10},{9,11},{10,... | collective-permute-start | bytes 239624 | tf_op jit(solution)/shard_map/ppermute | solution.py:101
  10.4 28.6 %collective-permute-start.11 = (bf16[24,1664]{1,0:T(8,128)(2,1)S(1)}, bf16[24,1664]{1,0:T(8,128)(2,1)S(1)}, u32[]{:S(2)}, u32[]{:S(2)}) collective-permute-start(bf16[24,1664]{1,0:T(8,128)(2,1)S(1)} %fusion.86), channel_id=1, source_target_pairs={{0,3},{1,0},{2,1},{3,2},{4,7},{5,4},{6,5},{7,6},{8,11},{9,8},{10,9... | collective-permute-start | bytes 239624 | tf_op jit(solution)/shard_map/ppermute | solution.py:101
  26.3 46.7 %collective-permute-start.15 = (bf16[24,3200]{1,0:T(8,128)(2,1)}, bf16[24,3200]{1,0:T(8,128)(2,1)S(1)}, u32[]{:S(2)}, u32[]{:S(2)}) collective-permute-start(bf16[24,3200]{1,0:T(8,128)(2,1)} %pad_maximum_fusion.9), channel_id=1, source_target_pairs={{0,1},{1,2},{2,3},{3,0},{4,5},{5,6},{6,7},{7,4},{8,9},{9,10},{10,1... | collective-permute-start | bytes 460808 | tf_op jit(solution)/shard_map/ppermute | solution.py:101
  28.3 48.2 %collective-permute-start.16 = (bf16[24,3200]{1,0:T(8,128)(2,1)}, bf16[24,3200]{1,0:T(8,128)(2,1)S(1)}, u32[]{:S(2)}, u32[]{:S(2)}) collective-permute-start(bf16[24,3200]{1,0:T(8,128)(2,1)} %pad_maximum_fusion.9), channel_id=1, source_target_pairs={{0,2},{1,3},{2,0},{3,1},{4,6},{5,7},{6,4},{7,5},{8,10},{9,11},{10,... | collective-permute-start | bytes 460808 | tf_op jit(solution)/shard_map/ppermute | solution.py:101
  33.9 42.7 %collective-permute-start.17 = (bf16[24,3200]{1,0:T(8,128)(2,1)}, bf16[24,3200]{1,0:T(8,128)(2,1)S(1)}, u32[]{:S(2)}, u32[]{:S(2)}) collective-permute-start(bf16[24,3200]{1,0:T(8,128)(2,1)} %pad_maximum_fusion.9), channel_id=1, source_target_pairs={{0,3},{1,0},{2,1},{3,2},{4,7},{5,4},{6,5},{7,6},{8,11},{9,8},{10,9... | collective-permute-start | bytes 460808 | tf_op jit(solution)/shard_map/ppermute | solution.py:101
  53.3 30.6 %collective-permute-start = (bf16[2,128,768]{1,2,0:T(8,128)(2,1)S(1)}, bf16[2,128,768]{1,2,0:T(8,128)(2,1)S(1)}, u32[]{:S(2)}, u32[]{:S(2)}) collective-permute-start(bf16[2,128,768]{1,2,0:T(8,128)(2,1)S(1)} %copy-done.44), channel_id=1, source_target_pairs={{0,1},{1,2},{2,3},{3,0},{4,5},{5,6},{6,7},{7,4},{8,9},{9,10},{10,1... | collective-permute-start | bytes 1179656 | tf_op jit(solution)/shard_map/ppermute | solution.py:101
  55.9 38.8 %collective-permute-start.1 = (bf16[2,128,768]{1,2,0:T(8,128)(2,1)}, bf16[2,128,768]{1,2,0:T(8,128)(2,1)S(1)}, u32[]{:S(2)}, u32[]{:S(2)}) collective-permute-start(bf16[2,128,768]{1,2,0:T(8,128)(2,1)} %get-tuple-element.154), channel_id=1, source_target_pairs={{0,2},{1,3},{2,0},{3,1},{4,6},{5,7},{6,4},{7,5},{8,10},{9,11},{10,... | collective-permute-start | bytes 1179656 | tf_op jit(solution)/shard_map/ppermute | solution.py:101
  73.0 23.3 %collective-permute-start.2 = (bf16[2,128,768]{1,2,0:T(8,128)(2,1)S(1)}, bf16[2,128,768]{1,2,0:T(8,128)(2,1)S(1)}, u32[]{:S(2)}, u32[]{:S(2)}) collective-permute-start(bf16[2,128,768]{1,2,0:T(8,128)(2,1)S(1)} %copy-done.43), channel_id=1, source_target_pairs={{0,3},{1,0},{2,1},{3,2},{4,7},{5,4},{6,5},{7,6},{8,11},{9,8},{10,9... | collective-permute-start | bytes 1179656 | tf_op jit(solution)/shard_map/ppermute | solution.py:101
  76.4 23.5 %collective-permute-start.30 = (bf16[2,128,768]{2,1,0:T(8,128)(2,1)}, bf16[2,128,768]{2,1,0:T(8,128)(2,1)S(1)}, u32[]{:S(2)}, u32[]{:S(2)}) collective-permute-start(bf16[2,128,768]{2,1,0:T(8,128)(2,1)} %get-tuple-element.147), channel_id=1, source_target_pairs={{0,1},{1,2},{2,3},{3,0},{4,5},{5,6},{6,7},{7,4},{8,9},{9,10},{10,1... | collective-permute-start | bytes 1179656 | tf_op jit(solution)/shard_map/ppermute | solution.py:101
  83.3 35.9 %collective-permute-start.31 = (bf16[2,128,768]{2,1,0:T(8,128)(2,1)}, bf16[2,128,768]{2,1,0:T(8,128)(2,1)S(1)}, u32[]{:S(2)}, u32[]{:S(2)}) collective-permute-start(bf16[2,128,768]{2,1,0:T(8,128)(2,1)} %get-tuple-element.146), channel_id=1, source_target_pairs={{0,2},{1,3},{2,0},{3,1},{4,6},{5,7},{6,4},{7,5},{8,10},{9,11},{10,... | collective-permute-start | bytes 1179656 | tf_op jit(solution)/shard_map/ppermute | solution.py:101
  83.9 36.9 %collective-permute-start.32 = (bf16[2,128,768]{2,1,0:T(8,128)(2,1)}, bf16[2,128,768]{2,1,0:T(8,128)(2,1)S(1)}, u32[]{:S(2)}, u32[]{:S(2)}) collective-permute-start(bf16[2,128,768]{2,1,0:T(8,128)(2,1)} %get-tuple-element.145), channel_id=1, source_target_pairs={{0,3},{1,0},{2,1},{3,2},{4,7},{5,4},{6,5},{7,6},{8,11},{9,8},{10,9... | collective-permute-start | bytes 1179656 | tf_op jit(solution)/shard_map/ppermute | solution.py:101
  94.8 27.0 %collective-permute-start.12 = (bf16[4,24,1664]{2,1,0:T(8,128)(2,1)}, bf16[4,24,1664]{2,1,0:T(8,128)(2,1)}, u32[]{:S(2)}, u32[]{:S(2)}) collective-permute-start(bf16[4,24,1664]{2,1,0:T(8,128)(2,1)} %bitcast_dynamic-update-slice_fusion.39), channel_id=1, source_target_pairs={{0,16},{1,17},{2,18},{3,19},{4,20},{5,21},{6,22},{7,23},{8,24},{9,... | collective-permute-start | bytes 958472 | tf_op jit(solution)/shard_map/ppermute | solution.py:109
  96.3 28.2 %collective-permute-start.24 = (bf16[4,96,768]{2,1,0:T(8,128)(2,1)}, bf16[4,96,768]{2,1,0:T(8,128)(2,1)}, u32[]{:S(2)}, u32[]{:S(2)}) collective-permute-start(bf16[4,96,768]{2,1,0:T(8,128)(2,1)} %bitcast_dynamic-update-slice_fusion.35), channel_id=1, source_target_pairs={{0,16},{1,17},{2,18},{3,19},{4,20},{5,21},{6,22},{7,23},{8,24},{9,... | collective-permute-start | bytes 1769480 | tf_op jit(solution)/shard_map/ppermute | solution.py:109
  100.0 29.2 %collective-permute-start.18 = (bf16[4,24,3200]{2,1,0:T(8,128)(2,1)}, bf16[4,24,3200]{2,1,0:T(8,128)(2,1)}, u32[]{:S(2)}, u32[]{:S(2)}) collective-permute-start(bf16[4,24,3200]{2,1,0:T(8,128)(2,1)} %copy-done.24), channel_id=1, source_target_pairs={{0,8},{1,9},{2,10},{3,11},{4,12},{5,13},{6,14},{7,15},{8,0},{9,1},... | collective-permute-start | bytes 1843208 | tf_op jit(solution)/shard_map/ppermute | solution.py:109
  122.8 17.4 %collective-permute-start.13 = (bf16[2,4,24,1664]{3,2,1,0:T(8,128)(2,1)S(1)}, bf16[2,4,24,1664]{3,2,1,0:T(8,128)(2,1)S(1)}, u32[]{:S(2)}, u32[]{:S(2)}) collective-permute-start(bf16[2,4,24,1664]{3,2,1,0:T(8,128)(2,1)S(1)} %bitcast_dynamic-update-slice_fusion.27), channel_id=1, source_target_pairs={{0,8},{1,9},{2,10},{3,11},{4,12},{5,13},{6,14},{7,15},{8,0},{9,1},... | collective-permute-start | bytes 1916936 | tf_op jit(solution)/shard_map/ppermute | solution.py:109
  125.8 33.1 %collective-permute-start.25 = (bf16[2,4,96,768]{3,2,1,0:T(8,128)(2,1)S(1)}, bf16[2,4,96,768]{3,2,1,0:T(8,128)(2,1)S(1)}, u32[]{:S(2)}, u32[]{:S(2)}) collective-permute-start(bf16[2,4,96,768]{3,2,1,0:T(8,128)(2,1)S(1)} %bitcast_dynamic-update-slice_fusion.17), channel_id=1, source_target_pairs={{0,8},{1,9},{2,10},{3,11},{4,12},{5,13},{6,14},{7,15},{8,0},{9,1},... | collective-permute-start | bytes 3538952 | tf_op jit(solution)/shard_map/ppermute | solution.py:109
  130.4 35.6 %collective-permute-start.19 = (bf16[2,4,24,3200]{3,2,1,0:T(8,128)(2,1)S(1)}, bf16[2,4,24,3200]{3,2,1,0:T(8,128)(2,1)S(1)}, u32[]{:S(2)}, u32[]{:S(2)}) collective-permute-start(bf16[2,4,24,3200]{3,2,1,0:T(8,128)(2,1)S(1)} %bitcast_dynamic-update-slice_fusion.15), channel_id=1, source_target_pairs={{0,16},{1,17},{2,18},{3,19},{4,20},{5,21},{6,22},{7,23},{8,24},{9,... | collective-permute-start | bytes 3686408 | tf_op jit(solution)/shard_map/ppermute | solution.py:109
  134.8 35.2 %collective-permute-start.8 = (bf16[2,2,4,24,1536]{4,3,2,1,0:T(8,128)(2,1)S(1)}, bf16[2,2,4,24,1536]{4,3,2,1,0:T(8,128)(2,1)S(1)}, u32[]{:S(2)}, u32[]{:S(2)}) collective-permute-start(bf16[2,2,4,24,1536]{4,3,2,1,0:T(8,128)(2,1)S(1)} %bitcast_dynamic-update-slice_fusion.19), channel_id=1, source_target_pairs={{0,4},{1,5},{2,6},{3,7},{4,0},{5,1},{6,2},{7,3},{8,12},{9,13},{10,... | collective-permute-start | bytes 3538952 | tf_op jit(solution)/shard_map/ppermute | solution.py:109
  140.3 29.9 %collective-permute-start.14 = (bf16[2,2,4,24,1664]{4,3,2,1,0:T(8,128)(2,1)S(1)}, bf16[2,2,4,24,1664]{4,3,2,1,0:T(8,128)(2,1)S(1)}, u32[]{:S(2)}, u32[]{:S(2)}) collective-permute-start(bf16[2,2,4,24,1664]{4,3,2,1,0:T(8,128)(2,1)S(1)} %bitcast_dynamic-update-slice_fusion.14), channel_id=1, source_target_pairs={{0,4},{1,5},{2,6},{3,7},{4,0},{5,1},{6,2},{7,3},{8,12},{9,13},{10,... | collective-permute-start | bytes 3833864 | tf_op jit(solution)/shard_map/ppermute | solution.py:109
  160.0 81.6 %collective-permute-start.26 = (bf16[2,2,4,96,768]{4,3,2,1,0:T(8,128)(2,1)}, bf16[2,2,4,96,768]{4,3,2,1,0:T(8,128)(2,1)}, u32[]{:S(2)}, u32[]{:S(2)}) collective-permute-start(bf16[2,2,4,96,768]{4,3,2,1,0:T(8,128)(2,1)} %bitcast_dynamic-update-slice_fusion.11), channel_id=1, source_target_pairs={{0,4},{1,5},{2,6},{3,7},{4,0},{5,1},{6,2},{7,3},{8,12},{9,13},{10,... | collective-permute-start | bytes 7077896 | tf_op jit(solution)/shard_map/ppermute | solution.py:109
  167.1 77.8 %collective-permute-start.20 = (bf16[2,2,4,24,3200]{4,3,2,1,0:T(8,128)(2,1)}, bf16[2,2,4,24,3200]{4,3,2,1,0:T(8,128)(2,1)}, u32[]{:S(2)}, u32[]{:S(2)}) collective-permute-start(bf16[2,2,4,24,3200]{4,3,2,1,0:T(8,128)(2,1)} %bitcast_dynamic-update-slice_fusion.7), channel_id=1, source_target_pairs={{0,4},{1,5},{2,6},{3,7},{4,0},{5,1},{6,2},{7,3},{8,12},{9,13},{10,... | collective-permute-start | bytes 7372808 | tf_op jit(solution)/shard_map/ppermute | solution.py:109
  441.8 133.3 %collective-permute-start.54 = (bf16[2,2,4,96,768]{4,3,2,1,0:T(8,128)(2,1)}, bf16[2,2,4,96,768]{4,3,2,1,0:T(8,128)(2,1)}, u32[]{:S(2)}, u32[]{:S(2)}) collective-permute-start(bf16[2,2,4,96,768]{4,3,2,1,0:T(8,128)(2,1)} %dynamic-slice_bitcast_fusion.3), channel_id=1, source_target_pairs={{0,4},{1,5},{2,6},{3,7},{4,0},{5,1},{6,2},{7,3},{8,12},{9,13},{10,... | collective-permute-start | bytes 7077896 | tf_op jit(solution)/shard_map/ppermute | solution.py:109
  448.0 130.5 %collective-permute-start.48 = (bf16[2,2,4,24,3200]{4,3,2,0,1:T(8,128)(2,1)}, bf16[2,2,4,24,3200]{4,3,2,0,1:T(8,128)(2,1)}, u32[]{:S(2)}, u32[]{:S(2)}) collective-permute-start(bf16[2,2,4,24,3200]{4,3,2,0,1:T(8,128)(2,1)} %bitcast.390), channel_id=1, source_target_pairs={{0,4},{1,5},{2,6},{3,7},{4,0},{5,1},{6,2},{7,3},{8,12},{9,13},{10,... | collective-permute-start | bytes 7372808 | tf_op jit(solution)/shard_map/ppermute | solution.py:109
  451.3 93.2 %collective-permute-start.36 = (bf16[2,2,4,24,1536]{4,3,2,0,1:T(8,128)(2,1)}, bf16[2,2,4,24,1536]{4,3,2,0,1:T(8,128)(2,1)}, u32[]{:S(2)}, u32[]{:S(2)}) collective-permute-start(bf16[2,2,4,24,1536]{4,3,2,0,1:T(8,128)(2,1)} %bitcast.391), channel_id=1, source_target_pairs={{0,4},{1,5},{2,6},{3,7},{4,0},{5,1},{6,2},{7,3},{8,12},{9,13},{10,... | collective-permute-start | bytes 3538952 | tf_op jit(solution)/shard_map/ppermute | solution.py:109
  471.4 36.1 %collective-permute-start.34 = (bf16[2,128,768]{2,1,0:T(8,128)(2,1)S(1)}, bf16[2,128,768]{2,1,0:T(8,128)(2,1)S(1)}, u32[]{:S(2)}, u32[]{:S(2)}) collective-permute-start(bf16[2,128,768]{2,1,0:T(8,128)(2,1)S(1)} %bitcast.490), channel_id=1, source_target_pairs={{0,2},{1,3},{2,0},{3,1},{4,6},{5,7},{6,4},{7,5},{8,10},{9,11},{10,... | collective-permute-start | bytes 1179656 | tf_op jit(solution)/shard_map/ppermute | solution.py:101
  480.9 26.6 %collective-permute-start.35 = (bf16[2,128,768]{2,1,0:T(8,128)(2,1)S(1)}, bf16[2,128,768]{2,1,0:T(8,128)(2,1)S(1)}, u32[]{:S(2)}, u32[]{:S(2)}) collective-permute-start(bf16[2,128,768]{2,1,0:T(8,128)(2,1)S(1)} %bitcast.488), channel_id=1, source_target_pairs={{0,1},{1,2},{2,3},{3,0},{4,5},{5,6},{6,7},{7,4},{8,9},{9,10},{10,1... | collective-permute-start | bytes 1179656 | tf_op jit(solution)/shard_map/ppermute | solution.py:101
  507.5 33.3 %collective-permute-start.28 = (bf16[2,128,768]{2,1,0:T(8,128)(2,1)S(1)}, bf16[2,128,768]{2,1,0:T(8,128)(2,1)S(1)}, u32[]{:S(2)}, u32[]{:S(2)}) collective-permute-start(bf16[2,128,768]{2,1,0:T(8,128)(2,1)S(1)} %bitcast.487), channel_id=1, source_target_pairs={{0,2},{1,3},{2,0},{3,1},{4,6},{5,7},{6,4},{7,5},{8,10},{9,11},{10,... | collective-permute-start | bytes 1179656 | tf_op jit(solution)/shard_map/ppermute | solution.py:101
  518.5 23.1 %collective-permute-start.29 = (bf16[2,128,768]{2,1,0:T(8,128)(2,1)S(1)}, bf16[2,128,768]{2,1,0:T(8,128)(2,1)S(1)}, u32[]{:S(2)}, u32[]{:S(2)}) collective-permute-start(bf16[2,128,768]{2,1,0:T(8,128)(2,1)S(1)} %bitcast.486), channel_id=1, source_target_pairs={{0,1},{1,2},{2,3},{3,0},{4,5},{5,6},{6,7},{7,4},{8,9},{9,10},{10,1... | collective-permute-start | bytes 1179656 | tf_op jit(solution)/shard_map/ppermute | solution.py:101
  585.2 25.2 %collective-permute-start.55 = (bf16[2,4,96,768]{3,2,1,0:T(8,128)(2,1)S(1)}, bf16[2,4,96,768]{3,2,1,0:T(8,128)(2,1)S(1)}, u32[]{:S(2)}, u32[]{:S(2)}) collective-permute-start(bf16[2,4,96,768]{3,2,1,0:T(8,128)(2,1)S(1)} %dynamic-slice_bitcast_fusion.6), channel_id=1, source_target_pairs={{0,16},{1,17},{2,18},{3,19},{4,20},{5,21},{6,22},{7,23},{8,24},{9,... | collective-permute-start | bytes 3538952 | tf_op jit(solution)/shard_map/ppermute | solution.py:109
  586.7 28.8 %collective-permute-start.49 = (bf16[2,4,24,3200]{3,2,1,0:T(8,128)(2,1)S(1)}, bf16[2,4,24,3200]{3,2,1,0:T(8,128)(2,1)S(1)}, u32[]{:S(2)}, u32[]{:S(2)}) collective-permute-start(bf16[2,4,24,3200]{3,2,1,0:T(8,128)(2,1)S(1)} %dynamic-slice_bitcast_fusion.5), channel_id=1, source_target_pairs={{0,8},{1,9},{2,10},{3,11},{4,12},{5,13},{6,14},{7,15},{8,0},{9,1},... | collective-permute-start | bytes 3686408 | tf_op jit(solution)/shard_map/ppermute | solution.py:109
  630.3 19.8 %collective-permute-start.52 = (bf16[24,3200]{1,0:T(8,128)(2,1)S(1)}, bf16[24,3200]{1,0:T(8,128)(2,1)S(1)}, u32[]{:S(2)}, u32[]{:S(2)}) collective-permute-start(bf16[24,3200]{1,0:T(8,128)(2,1)S(1)} %get-tuple-element.158), channel_id=1, source_target_pairs={{0,2},{1,3},{2,0},{3,1},{4,6},{5,7},{6,4},{7,5},{8,10},{9,11},{10,... | collective-permute-start | bytes 460808 | tf_op jit(solution)/shard_map/ppermute | solution.py:101
  (97 other events, 1012.8 us)

commit v2 on v1

v2 whole, which is shorter than its diff:
```python
from functools import partial
import math

import jax
import jax.numpy as jnp
from jax import lax
from jax.experimental import pallas as pl
from jax.experimental.pallas import tpu as pltpu
from jax.sharding import PartitionSpec as P

HEAD_DIM = 64
LANES = 128
EPSILON = 1e-06
AXES = ("dp", "seq")
BF16, F32 = jnp.bfloat16, jnp.float32

NN = (((1,), (0,)), ((), ()))
NT = (((1,), (1,)), ((), ()))
TN = (((0,), (0,)), ((), ()))


def narrow(value):
    return value.astype(BF16)


def widen(value):
    return value.astype(F32)


def after(value, *others):
    return lax.optimization_barrier((value,) + others)[0]


def dot(left, right, dims=NN):
    return lax.dot_general(left, right, dims, preferred_element_type=F32)


def shape(dims, dtype=BF16):
    return jax.ShapeDtypeStruct(dims, dtype)


def whole_block(dims):
    return pl.BlockSpec(dims, lambda *_: (0,) * len(dims))


def row_sum(value):
    return jnp.sum(value, axis=0, keepdims=True)


def kernel(body, name, flops, touched, **options):
    return pl.pallas_call(
        body,
        name=name,
        compiler_params=pltpu.CompilerParams(vmem_limit_bytes=60 << 20),
        cost_estimate=pl.CostEstimate(flops=flops, bytes_accessed=touched, transcendentals=0),
        **options,
    )


def project_body(tokens, first, second, vectors, packed, rows):
    part = pl.program_id(0)
    turned = widen(vectors[...]).T

    @pl.when(part == 0)
    def _():
        rows[...] = turned[:8]
        packed[...] = narrow(dot(tokens[...], first[...]) + turned[0:1])

    @pl.when(part == 1)
    def _():
        packed[...] = narrow(dot(tokens[...], first[...]))

    @pl.when(part == 2)
    def _():
        packed[...] = narrow(dot(tokens[...], second[...]) + turned[1:2])


def project(tokens, first, second):
    count, width = tokens.shape
    square = (width, width)
    return kernel(
        project_body,
        "project",
        6 * count * width * width,
        8 * count * width,
        grid=(3,),
        in_specs=[
            whole_block(tokens.shape),
            pl.BlockSpec(square, lambda i: (0, jnp.minimum(i, 1))),
            pl.BlockSpec(square, lambda i: (0, 0)),
            pl.BlockSpec((width, LANES), lambda i: (0, 2 * width // LANES)),
        ],
        out_specs=[pl.BlockSpec((count, width), lambda i: (0, i)), whole_block((8, width))],
        out_shape=[shape((count, 3 * width)), shape((8, width), F32)],
    )(tokens, first, second, first)


def attend_body(labels_down, labels_along, query, key, value, context, probs, bias):
    @pl.when(pl.program_id(1) == 0)
    def _():
        bias[...] = jnp.where(labels_down[0] == labels_along[0], 0.0, -1e30)

    lane = lax.broadcasted_iota(jnp.int32, (1, LANES), 1)
    keys, values = key[0], value[0]
    queries = query[0] * BF16(HEAD_DIM**-0.5)
    parts = []
    for head in range(2):
        mine = (lane >= HEAD_DIM) == bool(head)
        scores = dot(jnp.where(mine, queries, BF16(0)), keys, NT) + bias[...]
        raised = jnp.exp(scores - jnp.max(scores, axis=-1, keepdims=True))
        total = jnp.sum(raised, axis=-1, keepdims=True)
        low = narrow(raised * (1.0 / total))
        probs[0, head] = low
        parts.append(dot(low, values))
    context[0] = narrow(jnp.where(lane < HEAD_DIM, parts[0], parts[1]))


def head_pair(length, offset):
    return pl.BlockSpec((1, length, LANES), lambda r, p: (r, 0, offset + p))


def attend(packed, labels):
    rows, length, _ = packed.shape
    width = packed.shape[2] // 3
    pairs = width // LANES
    return kernel(
        attend_body,
        "attend",
        rows * pairs * 16 * length * length * LANES,
        rows * pairs * 8 * length * length,
        grid=(rows, pairs),
        in_specs=[
            pl.BlockSpec((1, length, 1), lambda r, p: (r, 0, 0)),
            pl.BlockSpec((1, 1, length), lambda r, p: (r, 0, 0)),
            head_pair(length, 0),
            head_pair(length, pairs),
            head_pair(length, 2 * pairs),
        ],
        out_specs=[
            head_pair(length, 0),
            pl.BlockSpec((1, 2, length, length), lambda r, p: (r, p, 0, 0)),
        ],
        out_shape=[shape((rows, length, width)), shape((rows, 2 * pairs, length, length))],
        scratch_shapes=[pltpu.VMEM((length, length), F32)],
    )(labels[:, :, None], labels[:, None, :], packed, packed, packed)


def attend_back_body(query, key, value, upstream, probs, grads, sums):
    pair, pairs = pl.program_id(1), pl.num_programs(1)
    lane = lax.broadcasted_iota(jnp.int32, (1, LANES), 1)
    scale = BF16(HEAD_DIM**-0.5)
    queries, keys, values, up = query[0] * scale, key[0], value[0], upstream[0]
    scaled_keys = keys * scale
    query_parts, key_grad, value_grad = [], 0.0, 0.0
    for head in range(2):
        mine = (lane >= HEAD_DIM) == bool(head)
        up_mine = jnp.where(mine, up, BF16(0))
        queries_mine = jnp.where(mine, queries, BF16(0))
        low = probs[0, head]
        prob_grad = dot(up_mine, values, NT)
        softmaxed = widen(low)
        weighted = jnp.sum(softmaxed * prob_grad, axis=-1, keepdims=True)
        score_grad = narrow(softmaxed * (prob_grad - weighted))
        query_parts.append(dot(score_grad, scaled_keys))
        key_grad = key_grad + dot(queries_mine, score_grad, TN)
        value_grad = value_grad + dot(up_mine, low, TN)
    query_grad = jnp.where(lane < HEAD_DIM, query_parts[0], query_parts[1])
    for part, grad in enumerate((query_grad, key_grad.T, value_grad.T)):
        at = pl.ds(pl.multiple_of((part * pairs + pair) * LANES, LANES), LANES)
        rounded = narrow(grad)
        grads[0, :, at] = rounded
        sums[0, :, at] = row_sum(widen(rounded))


def attend_back(packed, probs, upstream):
    rows, length, wide = packed.shape
    pairs = wide // 3 // LANES
    return kernel(
        attend_back_body,
        "attend_back",
        rows * pairs * 16 * length * length * LANES,
        rows * pairs * 8 * length * length,
        grid=(rows, pairs),
        in_specs=[
            head_pair(length, 0),
            head_pair(length, pairs),
            head_pair(length, 2 * pairs),
            head_pair(length, 0),
            pl.BlockSpec((1, 2, length, length), lambda r, p: (r, p, 0, 0)),
        ],
        out_specs=[
            pl.BlockSpec((1, length, wide), lambda r, p: (r, 0, 0)),
            pl.BlockSpec((1, 1, wide), lambda r, p: (r, 0, 0)),
        ],
        out_shape=[shape((rows, length, wide)), shape((rows, 1, wide), F32)],
    )(packed, packed, packed, upstream, probs)


def normed_of(summed):
    centred = summed - jnp.mean(summed, axis=-1, keepdims=True)
    variance = jnp.mean(centred * centred, axis=-1, keepdims=True)
    inverse = lax.rsqrt(variance + EPSILON)
    return centred * inverse, inverse


def norm_back(upstream, normed, inverse, gain):
    scaled = upstream * gain
    first_mean = jnp.mean(scaled, axis=-1, keepdims=True)
    second_mean = jnp.mean(scaled * normed, axis=-1, keepdims=True)
    return inverse * (scaled - first_mean - normed * second_mean)


def settle_body(context, weight, tokens, rows, normed, inverse, low):
    summed = widen(tokens[...]) + dot(context[...], weight[...]) + rows[2:3]
    normed[...], inverse[...] = normed_of(summed)
    low[...] = narrow(normed[...] * rows[3:4] + rows[4:5])


def settle(context, second, tokens, rows):
    count, width = context.shape
    block = count // 4
    tall = pl.BlockSpec((block, width), lambda i: (i, 0))
    return kernel(
        settle_body,
        "settle",
        2 * count * width * width,
        10 * count * width,
        grid=(4,),
        in_specs=[
            tall,
            pl.BlockSpec((width, width), lambda i: (0, 1)),
            tall,
            whole_block(rows.shape),
        ],
        out_specs=[tall, pl.BlockSpec((block, 1), lambda i: (i, 0)), tall],
        out_shape=[shape((count, width), F32), shape((count, 1), F32), shape((count, width))],
    )(context, second, tokens, rows)


def feed_body(
    low, inner_weight, inner_bias, outer_weight, normed_one, rows_one, rows_two,
    active, slope, normed_two, inverse_two, *pieces_and_branch,
):
    pieces, branch = pieces_and_branch[:-1], pieces_and_branch[-1]
    step, steps = pl.program_id(0), pl.num_programs(0)
    inner = dot(low[...], inner_weight[...]) + inner_bias[...]
    share = 0.5 * (1.0 + lax.erf(inner * math.sqrt(0.5)))
    raised = jnp.exp(-0.5 * inner * inner) * (1.0 / math.sqrt(2.0 * math.pi))
    acted = narrow(inner * share)
    active[...] = acted
    slope[...] = narrow(share + inner * raised)
    part = dot(acted, outer_weight[...])

    @pl.when(step == 0)
    def _():
        branch[...] = part

    @pl.when(step > 0)
    def _():
        branch[...] += part

    @pl.when(step == steps - 1)
    def _():
        hidden = normed_one[...] * rows_one[3:4] + rows_one[4:5]
        normed_two[...], inverse_two[...] = normed_of(hidden + branch[...] + rows_two[0:1])
        result = narrow(normed_two[...] * rows_two[1:2] + rows_two[2:3])
        rows, places, width = pieces[0].shape
        result = result.reshape(rows, len(pieces), places, width)
        for index, piece in enumerate(pieces):
            piece[...] = result[:, index]


def feed(low, inner_weight, inner_bias, outer_weight, normed_one, rows_one, rows_two, piece, seq):
    count, width = low.shape
    wide = outer_weight.shape[0]
    block = 512
    all_of = whole_block((count, width))
    across = pl.BlockSpec((count, block), lambda f: (0, f))
    return kernel(
        feed_body,
        "feed",
        4 * count * width * wide,
        12 * count * wide,
        grid=(wide // block,),
        in_specs=[
            all_of,
            pl.BlockSpec((width, block), lambda f: (0, f)),
            pl.BlockSpec((1, block), lambda f: (0, f)),
            pl.BlockSpec((block, width), lambda f: (f, 0)),
            all_of,
            whole_block(rows_one.shape),
            whole_block(rows_two.shape),
        ],
        out_specs=[across, across, all_of, whole_block((count, 1))] + [whole_block(piece)] * seq,
        out_shape=[
            shape((count, wide)),
            shape((count, wide)),
            shape((count, width), F32),
            shape((count, 1), F32),
        ]
        + [shape(piece)] * seq,
        scratch_shapes=[pltpu.VMEM((count, width), F32)],
    )(low, inner_weight, inner_bias, outer_weight, normed_one, rows_one, rows_two)


def feed_back_body(
    cotangent, normed_two, inverse_two, rows_two, low, inner_weight, outer_weight, active, slope,
    inner_grad_out, inner_bias_out, outer_grad_out, hidden_grad, sums, up,
):
    step = pl.program_id(0)

    @pl.when(step == 0)
    def _():
        upstream = widen(cotangent[...])
        normed = normed_two[...]
        hidden_grad[...] = norm_back(upstream, normed, inverse_two[...], rows_two[1:2])
        up[...] = narrow(hidden_grad[...])
        sums[0:1] = row_sum(widen(up[...]))
        sums[1:2] = row_sum(upstream * normed)
        sums[2:3] = row_sum(upstream)
        sums[3:8] = jnp.zeros_like(sums[3:8])

    inner_grad = narrow(dot(up[...], outer_weight[...], NT) * widen(slope[...]))
    inner_bias_out[...] = row_sum(widen(inner_grad))
    outer_grad_out[...] = narrow(dot(active[...], up[...], TN))
    inner_grad_out[...] = narrow(dot(low[...], inner_grad, TN))
    hidden_grad[...] += dot(inner_grad, inner_weight[...], NT)


def feed_back(cotangent, normed_two, inverse_two, rows_two, low, inner_weight, outer_weight, active, slope):
    count, width = low.shape
    wide = outer_weight.shape[0]
    block = 512
    all_of = whole_block((count, width))
    across = pl.BlockSpec((count, block), lambda f: (0, f))
    right = pl.BlockSpec((width, block), lambda f: (0, f))
    down = pl.BlockSpec((block, width), lambda f: (f, 0))
    return kernel(
        feed_back_body,
        "feed_back",
        8 * count * width * wide,
        12 * count * wide,
        grid=(wide // block,),
        in_specs=[
            all_of,
            all_of,
            whole_block((count, 1)),
            whole_block(rows_two.shape),
            all_of,
            right,
            down,
            across,
            across,
        ],
        out_specs=[
            right,
            pl.BlockSpec((1, block), lambda f: (0, f)),
            down,
            all_of,
            whole_block((8, width)),
        ],
        out_shape=[
            shape((width, wide)),
            shape((1, wide), F32),
            shape((wide, width)),
            shape((count, width), F32),
            shape((8, width), F32),
        ],
        scratch_shapes=[pltpu.VMEM((count, width), BF16)],
    )(cotangent, normed_two, inverse_two, rows_two, low, inner_weight, outer_weight, active, slope)


def settle_back_body(
    hidden_grad, normed, inverse, rows, context, weight,
    first_up, context_grad, weight_grad, sums, total,
):
    step, steps = pl.program_id(0), pl.num_programs(0)

    @pl.when(step == 0)
    def _():
        sums[...] = jnp.zeros_like(sums)
        total[...] = jnp.zeros_like(total)

    upstream = hidden_grad[...]
    up = norm_back(upstream, normed[...], inverse[...], rows[3:4])
    first_up[...] = up
    low = narrow(up)
    context_grad[...] = narrow(dot(low, weight[...], NT))
    total[...] += dot(context[...], low, TN)
    sums[0:1] += row_sum(widen(low))
    sums[1:2] += row_sum(upstream * normed[...])
    sums[2:3] += row_sum(upstream)

    @pl.when(step == steps - 1)
    def _():
        weight_grad[...] = narrow(total[...])


def settle_back(hidden_grad, normed, inverse, rows, context, second):
    count, width = context.shape
    block = count // 2
    tall = pl.BlockSpec((block, width), lambda i: (i, 0))
    return kernel(
        settle_back_body,
        "settle_back",
        4 * count * width * width,
        16 * count * width,
        grid=(2,),
        in_specs=[
            tall,
            tall,
            pl.BlockSpec((block, 1), lambda i: (i, 0)),
            whole_block(rows.shape),
            tall,
            pl.BlockSpec((width, width), lambda i: (0, 1)),
        ],
        out_specs=[tall, tall, whole_block((width, width)), whole_block((8, width))],
        out_shape=[
            shape((count, width), F32),
            shape((count, width)),
            shape((width, width)),
            shape((8, width), F32),
        ],
        scratch_shapes=[pltpu.VMEM((width, width), F32)],
    )(hidden_grad, normed, inverse, rows, context, second)


def project_back_body(packed_grad, tokens, first, second, first_up, weight_grad, *pieces_and_total):
    pieces, total = pieces_and_total[:-1], pieces_and_total[-1]
    part = pl.program_id(0)
    grad = packed_grad[...]
    weight_grad[...] = narrow(dot(tokens[...], grad, TN))

    @pl.when(part == 0)
    def _():
        total[...] = first_up[...] + dot(grad, first[...], NT)

    @pl.when(part == 1)
    def _():
        total[...] += dot(grad, first[...], NT)

    @pl.when(part == 2)
    def _():
        result = narrow(total[...] + dot(grad, second[...], NT))
        rows, places, width = pieces[0].shape
        result = result.reshape(rows, len(pieces), places, width)
        for index, piece in enumerate(pieces):
            piece[...] = result[:, index]


def project_back(packed_grad, tokens, first, second, first_up, piece, seq):
    count, width = tokens.shape
    square = (width, width)
    return kernel(
        project_back_body,
        "project_back",
        12 * count * width * width,
        12 * count * width,
        grid=(3,),
        in_specs=[
            pl.BlockSpec((count, width), lambda i: (0, i)),
            whole_block(tokens.shape),
            pl.BlockSpec(square, lambda i: (0, jnp.minimum(i, 1))),
            pl.BlockSpec(square, lambda i: (0, 0)),
            whole_block(tokens.shape),
        ],
        out_specs=[pl.BlockSpec(square, lambda i: (0, i))] + [whole_block(piece)] * seq,
        out_shape=[shape((width, 3 * width))] + [shape(piece)] * seq,
        scratch_shapes=[pltpu.VMEM((count, width), F32)],
    )(packed_grad, tokens, first, second, first_up)


def block_at(blocks, index, axis=0):
    return lax.dynamic_index_in_dim(blocks, index, axis, keepdims=False)


class Links:
    def __init__(self, mesh):
        self.dp, self.seq = mesh.shape["dp"], mesh.shape["seq"]
        self.bits = self.dp.bit_length() - 1
        assert self.dp == 1 << self.bits
        upward = list(range(1, self.bits))
        self.orders = (upward, upward[::-1])

    def along(self, value, step):
        pairs = [
            (d * self.seq + s, d * self.seq + (s + step) % self.seq)
            for d in range(self.dp)
            for s in range(self.seq)
        ]
        return lax.ppermute(value, AXES, pairs)

    def across(self, value, bit):
        pairs = [
            (d * self.seq + s, (d ^ (1 << bit)) * self.seq + s)
            for d in range(self.dp)
            for s in range(self.seq)
        ]
        return lax.ppermute(value, AXES, pairs)

    def digit(self, bit):
        return (lax.axis_index("dp") >> bit) & 1

    def gather_seq(self, shard):
        place = lax.axis_index("seq")
        held = jnp.zeros((self.seq,) + shard.shape, shard.dtype)
        held = lax.dynamic_update_index_in_dim(held, shard, place, 0)
        for step in range(1, self.seq):
            held = lax.dynamic_update_index_in_dim(
                held, self.along(shard, step), (place - step) % self.seq, 0
            )
        return held

    def gather_digit(self, held, bit, done):
        axis = sum(other > bit for other in done)
        other = self.across(held, bit)
        mine = self.digit(bit)
        return jnp.where(
            mine == 0, jnp.stack([held, other], axis=axis), jnp.stack([other, held], axis=axis)
        )

    def flat(self, held):
        return held.reshape(-1, held.shape[-1])

    def spread(self, whole):
        rows = whole.shape[0] // (self.dp * self.seq)
        return whole.reshape((2,) * self.bits + (self.seq, rows) + whole.shape[1:])

    def reduce_digit(self, held, bit, done):
        axis = sum(1 for other in range(bit + 1, self.bits) if other not in done)
        mine = self.digit(bit)
        other = self.across(block_at(held, 1 - mine, axis), bit)
        return narrow(widen(block_at(held, mine, axis)) + widen(other))

    def reduce_seq(self, held):
        place = lax.axis_index("seq")
        total = widen(block_at(held, place))
        for step in range(1, self.seq):
            sent = block_at(held, (place + step) % self.seq)
            total = total + widen(self.along(sent, step))
        return total

    def to_rows(self, value, *others):
        place = lax.axis_index("seq")
        blocks = value.reshape(self.seq, value.shape[0] // self.seq, *value.shape[1:])
        pieces = [block_at(blocks, place)]
        sent = [block_at(blocks, (place + step) % self.seq) for step in range(1, self.seq)]
        if others:
            sent = [after(piece, *others) for piece in sent]
        for step in range(1, self.seq):
            pieces.append(self.along(sent[step - 1], step))
        return jnp.concatenate(pieces, axis=1)

    def from_rows(self, pieces):
        return [pieces[0]] + [self.along(pieces[step], -step) for step in range(1, self.seq)]

    def placed(self, pieces):
        place = lax.axis_index("seq")
        blocks = jnp.zeros((self.seq,) + pieces[0].shape, pieces[0].dtype)
        for step, piece in enumerate(pieces):
            blocks = lax.dynamic_update_index_in_dim(blocks, piece, (place + step) % self.seq, 0)
        return blocks.reshape(self.seq * pieces[0].shape[0], *pieces[0].shape[1:])


def columns(vectors, rows):
    block = jnp.concatenate([vector.reshape(rows, -1) for vector in vectors], axis=1)
    return jnp.pad(block, ((0, 0), (0, LANES - block.shape[1])))


def shards(
    links,
    tokens,
    cotangent,
    lengths,
    packed_weight,
    query_bias,
    value_bias,
    output_weight,
    output_bias,
    first_gain,
    first_shift,
    inner_weight,
    inner_bias,
    outer_weight,
    outer_bias,
    second_gain,
    second_shift,
):
    row_count, local_length, width = tokens.shape
    seq = links.seq
    place = lax.axis_index("seq")
    rows = row_count // seq
    length = seq * local_length
    small = packed_weight.shape[0]
    feed_width = inner_weight.shape[1]
    wide = feed_width // width
    piece = (rows, local_length, width)
    order_a, order_b = links.orders

    attention_vectors = columns(
        [narrow(v) for v in (query_bias, value_bias, output_bias, first_gain, first_shift)], small
    )
    attention_shard = jnp.concatenate(
        [
            narrow(packed_weight[:, : 2 * width]),
            attention_vectors,
            narrow(packed_weight[:, 2 * width :]),
            narrow(output_weight),
        ],
        axis=1,
    )
    cut = 2 * width + LANES
    held = links.gather_seq(attention_shard)
    tokens_mine = links.to_rows(tokens, held)
    first, second = held[..., :cut], held[..., cut:]
    for index in range(links.bits - 1):
        first = links.gather_digit(first, order_a[index], order_a[:index])
        second = links.gather_digit(second, order_b[index], order_b[:index])
        if index == 0:
            feed_shard = jnp.concatenate(
                [
                    narrow(inner_weight),
                    columns(
                        [narrow(v) for v in (outer_bias, second_gain, second_shift, inner_bias)],
                        small,
                    ),
                ],
                axis=1,
            )
            feed_shard, outer_shard = after(feed_shard, first), after(narrow(outer_weight), first)
            feed_first = links.gather_seq(feed_shard)
            feed_second = links.gather_seq(outer_shard)
    first = links.flat(links.gather_digit(first, 0, order_a))
    second = links.flat(links.gather_digit(second, 0, order_b))

    starts = (place - jnp.arange(seq, dtype=jnp.int32)) % seq * local_length
    places = (starts[:, None] + jnp.arange(local_length, dtype=jnp.int32)[None]).reshape(-1)
    mine = lax.dynamic_slice_in_dim(lengths, place * rows, rows, 0)
    bounds = jnp.cumsum(mine, axis=-1)[..., :-1]
    labels = jnp.sum((places[None, :, None] >= bounds[:, None, :]).astype(jnp.int32), axis=-1)

    flat = tokens_mine.reshape(-1, width)
    feed_first = links.gather_digit(feed_first, order_a[0], [])
    feed_second = links.gather_digit(feed_second, order_b[0], [])
    flat = after(flat, feed_first, feed_second)
    packed, rows_one = project(flat, first, second)
    packed = packed.reshape(rows, length, 3 * width)
    cotangent_mine = links.to_rows(cotangent, packed).reshape(-1, width)
    feed_first, feed_second = after(feed_first, packed), after(feed_second, packed)
    for index in range(1, links.bits - 1):
        feed_first = links.gather_digit(feed_first, order_a[index], order_a[:index])
        feed_second = links.gather_digit(feed_second, order_b[index], order_b[:index])
    context, probs = attend(packed, labels)
    context = context.reshape(-1, width)
    normed_one, inverse_one, low = settle(context, second, flat, rows_one)
    feed_first, feed_second = after(feed_first, low), after(feed_second, low)
    feed_first = links.flat(links.gather_digit(feed_first, 0, order_a))
    feed_second = links.flat(links.gather_digit(feed_second, 0, order_b))
    feed_vectors = widen(feed_first[:, feed_width:])
    rows_two = feed_vectors[:, :8].T
    inner_row = feed_vectors[:, 3 : 3 + wide].reshape(1, -1)

    active, slope, normed_two, inverse_two, *pieces = feed(
        low, feed_first, inner_row, feed_second, normed_one, rows_one, rows_two, piece, seq
    )
    output = links.placed(links.from_rows(pieces))

    inner_grad, inner_bias_grad, outer_grad, hidden_grad, feed_sums = feed_back(
        cotangent_mine, normed_two, inverse_two, rows_two, low, feed_first, feed_second, active, slope
    )
    feed_columns = columns(
        [narrow(v) for v in (feed_sums[0], feed_sums[1], feed_sums[2], inner_bias_grad)], width
    )
    feed_first = links.reduce_digit(
        links.spread(jnp.concatenate([inner_grad, feed_columns], axis=1)), 0, []
    )
    feed_second = links.reduce_digit(links.spread(outer_grad), 0, [])

    first_up, context_grad, output_grad, attention_sums = settle_back(
        hidden_grad, normed_one, inverse_one, rows_one, context, second
    )
    context_grad = after(context_grad, feed_first, feed_second, output)
    packed_grad, packed_sums = attend_back(
        packed, probs, context_grad.reshape(rows, length, width)
    )
    feed_first = links.reduce_digit(feed_first, order_a[0], [0])
    feed_second = links.reduce_digit(feed_second, order_b[0], [0])
    packed_grad = after(packed_grad, feed_first, feed_second)
    packed_weight_grad, *pieces = project_back(
        packed_grad.reshape(-1, 3 * width), flat, first, second, first_up, piece, seq
    )
    pieces = links.from_rows(pieces)
    for index in range(1, links.bits - 1):
        feed_first = links.reduce_digit(feed_first, order_a[index], [0] + order_a[:index])
        feed_second = links.reduce_digit(feed_second, order_b[index], [0] + order_b[:index])

    packed_sums = jnp.sum(packed_sums, axis=(0, 1))
    attention_columns = columns(
        [
            narrow(v)
            for v in (
                packed_sums[:width],
                packed_sums[2 * width :],
                attention_sums[0],
                attention_sums[1],
                attention_sums[2],
            )
        ],
        width,
    )
    first = links.spread(
        jnp.concatenate([packed_weight_grad[:, : 2 * width], attention_columns], axis=1)
    )
    second = links.spread(
        jnp.concatenate([packed_weight_grad[:, 2 * width :], output_grad], axis=1)
    )
    order_a, order_b = [0] + order_a, [0] + order_b
    for index in range(links.bits):
        first = links.reduce_digit(first, order_a[index], order_a[:index])
        second = links.reduce_digit(second, order_b[index], order_b[:index])
    feed_first, feed_second = links.reduce_seq(feed_first), links.reduce_seq(feed_second)
    tokens_grad = widen(links.placed(pieces))
    first, second = links.reduce_seq(first), links.reduce_seq(second)
    return (
        output,
        tokens_grad,
        jnp.concatenate([first[:, : 2 * width], second[:, :width]], axis=1),
        first[:, 2 * width],
        first[:, 2 * width + 1],
        second[:, width:],
        first[:, 2 * width + 2],
        first[:, 2 * width + 3],
        first[:, 2 * width + 4],
        feed_first[:, :feed_width],
        feed_first[:, feed_width + 3 : feed_width + 3 + wide].reshape(-1),
        feed_second,
        feed_first[:, feed_width],
        feed_first[:, feed_width + 1],
        feed_first[:, feed_width + 2],
    )


def solution(mesh):
    split = P(AXES)
    split_rows = P(AXES, None)
    packed_rows = P("dp", "seq", None)
    return jax.shard_map(
        partial(shards, Links(mesh)),
        mesh=mesh,
        in_specs=(
            packed_rows,
            packed_rows,
            P("dp", None),
            split_rows,
            split,
            split,
            split_rows,
            split,
            split,
            split,
            split_rows,
            split,
            split_rows,
            split,
            split,
            split,
        ),
        out_specs=(
            packed_rows,
            packed_rows,
            split_rows,
            split,
            split,
            split_rows,
            split,
            split,
            split,
            split_rows,
            split,
            split_rows,
            split,
            split,
            split,
        ),
        check_vma=False,
    )
```

time: 658 us -> 491 us (0.75)
  matrix products: 162 us -> 0 us
  Pallas kernels: 0 us -> 129 us
  local copies, waits for them, and re-layouts: 136 us -> 35.4 us
  starting transfers between devices: 127 us -> 101 us
    dot_general x26 -> x0, matrix products: 162 us -> none  [the longest x1 36.5 us: shards(): jnp.dot(hidden_low, whole_inner, preferred_element_type=jnp.float32)]
    pallas_call x0 -> x8, Pallas kernels: none -> 129 us  [the longest x1 28.7 us: feed_back(): kernel(feed_back_body, 'feed_back', 8 * count * width * wide, 12 * count...]
    ppermute x36 -> x33, waiting for transfers between devices: 81.3 us -> 133 us  [along(): return lax.ppermute(value, AXES, pairs)]
    ppermute x24, waiting for transfers between devices: 82.7 us -> 33.8 us  [across(): return lax.ppermute(value, AXES, pairs)]
    reshape x7 -> x2, local copies, waits for them, and re-layouts: 38.5 us -> 1.46 us  [the longest x1 0.85 us: shards(): inner_row = feed_vectors[:, 3:3 + wide].reshape(1, -1)]
    dynamic_update_slice x45 -> x19, local copies, waits for them, and re-layouts: 31.9 us -> 0.46 us  [the longest x8 0.25 us: placed(): lax.dynamic_update_index_in_dim(blocks, piece, (place + step) % self.seq, 0)]
    ppermute x36 -> x33, starting transfers between devices: 107 us -> 79.7 us  [along(): return lax.ppermute(value, AXES, pairs)]
    select_n x0 -> x16, other arithmetic: none -> 20.2 us  [gather_digit(): jnp.where(mine == 0, jnp.stack([held, other], axis=axis), jnp.stack([othe...]
  transfers between devices with their start and end apart: 60 -> 57, of which waited for: 24 -> 27; matrix products, arithmetic and copies ran while one was open for 23% -> 14% of each run, Pallas kernels for 0% -> 14%
where the time goes in v2:
time: 491 us; the launch traced here: 488 us
  waiting for transfers between devices  167 us (34%)
  Pallas kernels  129 us (26%)
  starting transfers between devices  101 us (21%)
  other arithmetic  55 us (11%)
  local copies, waits for them, and re-layouts  35.4 us (7%)
    ppermute x33, waiting for transfers between devices, along(): return lax.ppermute(value, AXES, pairs)  133 us
    ppermute x33, starting transfers between devices, along(): return lax.ppermute(value, AXES, pairs)  79.7 us
    ppermute x24, waiting for transfers between devices, across(): return lax.ppermute(value, AXES, pairs)  33.8 us
    pallas_call x1, Pallas kernels, feed_back(): kernel(feed_back_body, 'feed_back', 8 * count * width * wide, 12 * count...  28.7 us
    pallas_call x1, Pallas kernels, feed(): kernel(feed_body, 'feed', 4 * count * width * wide, 12 * count * wide, gr...  22.7 us
    pallas_call x1, Pallas kernels, attend_back(): kernel(attend_back_body, 'attend_back', rows * pairs * 16 * length * leng...  21.1 us
    ppermute x24, starting transfers between devices, across(): return lax.ppermute(value, AXES, pairs)  20.8 us
    select_n x16, other arithmetic, gather_digit(): jnp.where(mine == 0, jnp.stack([held, other], axis=axis), jnp.stack([othe...  20.2 us
  transfers between devices with their start and end apart: 57, of which 27 were waited for; matrix products, arithmetic and copies ran while one was open for 14% of the time, Pallas kernels for 14%

profile of v2, /device:TPU:0, one launch (start us, length us, event | category | flops | bytes accessed | tf_op | source)
XLA Modules:
  0.0 488.2 jit_solution(17128975633703859210)
XLA Ops:
  15.6 5.1 %collective-permute-done.1 = bf16[24,3200]{1,0:T(8,128)(2,1)S(1)} collective-permute-done((bf16[24,3200]{1,0:T(8,128)(2,1)S(1)}, bf16[24,3200]{1,0:T(8,128)(2,1)S(1)}, u32[]{:S(2)}, u32[]{:S(2)}) %collective-permute-start.1) | collective-permute-done | bytes 153632 | tf_op jit(solution)/shard_map/ppermute | solution.py:491
  24.0 3.7 collective-permute-start.3
  33.7 5.3 %collective-permute-done.3 = bf16[2,128,768]{2,1,0:T(8,128)(2,1)S(1)} collective-permute-done((bf16[2,128,768]{2,1,0:T(8,128)(2,1)S(1)}, bf16[2,128,768]{2,1,0:T(8,128)(2,1)S(1)}, u32[]{:S(2)}, u32[]{:S(2)}) %collective-permute-start.3) | collective-permute-done | bytes 393248 | tf_op jit(solution)/shard_map/ppermute | solution.py:491
  39.8 15.3 %collective-permute-done.4 = bf16[2,128,768]{2,1,0:T(8,128)(2,1)S(1)} collective-permute-done((bf16[2,128,768]{2,1,0:T(8,128)(2,1)S(1)}, bf16[2,128,768]{2,1,0:T(8,128)(2,1)S(1)}, u32[]{:S(2)}, u32[]{:S(2)}) %collective-permute-start.4) | collective-permute-done | bytes 393248 | tf_op jit(solution)/shard_map/ppermute | solution.py:491
  55.1 13.4 %collective-permute-start.13 = (bf16[96,768]{1,0:T(8,128)(2,1)S(1)}, bf16[96,768]{1,0:T(8,128)(2,1)S(1)}, u32[]{:S(2)}, u32[]{:S(2)}) collective-permute-start(bf16[96,768]{1,0:T(8,128)(2,1)S(1)} %convert_element_type.345), channel_id=1, source_target_pairs={{0,3},{1,0},{2,1},{3,2},{4,7},{5,4},{6,5},{7,6},{8,11},{9,8},{10,9... | collective-permute-start | bytes 442376 | tf_op jit(solution)/shard_map/ppermute | solution.py:491
  72.9 8.4 %collective-permute-start.9 = (bf16[24,3200]{1,0:T(8,128)(2,1)S(1)}, bf16[24,3200]{1,0:T(8,128)(2,1)S(1)}, u32[]{:S(2)}, u32[]{:S(2)}) collective-permute-start(bf16[24,3200]{1,0:T(8,128)(2,1)S(1)} %fusion.33), channel_id=1, source_target_pairs={{0,3},{1,0},{2,1},{3,2},{4,7},{5,4},{6,5},{7,6},{8,11},{9,8},{10,9... | collective-permute-start | bytes 460808 | tf_op jit(solution)/shard_map/ppermute | solution.py:491
  87.6 4.7 collective-permute-done.14
  92.5 6.6 %collective-permute-done.10 = bf16[4,24,3200]{2,1,0:T(8,128)(2,1)S(1)} collective-permute-done((bf16[4,24,3200]{2,1,0:T(8,128)(2,1)S(1)}, bf16[4,24,3200]{2,1,0:T(8,128)(2,1)S(1)}, u32[]{:S(2)}, u32[]{:S(2)}) %collective-permute-start.10) | collective-permute-done | bytes 614432 | tf_op jit(solution)/shard_map/ppermute | solution.py:499
  103.4 7.9 %project.1 = (bf16[1024,2304]{1,0:T(8,128)(2,1)}, f32[8,768]{1,0:T(8,128)}) custom-call(bf16[1024,768]{1,0:T(8,128)(2,1)} %bitcast.267, bf16[768,1664]{1,0:T(8,128)(2,1)} %bitcast.287, bf16[768,1536]{1,0:T(8,128)(2,1)} %bitcast.256, bf16[768,1664]{1,0:T(8,128)(2,1)} %bitcast.288), custom_call_target="tpu_custom_call" | custom-call | flops 3623878656 | bytes 6291456 | tf_op jit(solution)/shard_map/project/pallas_call | solution.py:81
  114.3 18.8 %attend.1 = (bf16[2,512,768]{2,1,0:T(8,128)(2,1)}, bf16[2,12,512,512]{3,2,1,0:T(8,128)(2,1)}) custom-call(s32[2,512,1]{2,1,0:T(8,128)} %copy.120.labels_down, s32[2,1,512]{2,1,0:T(1,128)} %broadcast_in_dim.76.labels_along, bf16[2,512,2304]{2,1,0:T(8,128)(2,1)} %bitcast.250, bf16[2,512,2304]{2,1,0:T(8,128)(2,1)} %bitcast.251, bf16[2,512,2304]{2,1,0:T(8,128)(2,1)} %bitcast.252), custom_call_target="tpu_custom_call" | custom-call | flops 6442450944 | bytes 25165824 | tf_op jit(solution)/shard_map/attend/pallas_call | solution.py:126
  133.1 6.4 %settle.1 = (f32[1024,768]{1,0:T(8,128)}, f32[1024,1]{1,0:T(8,128)}, bf16[1024,768]{1,0:T(8,128)(2,1)}) custom-call(bf16[1024,768]{1,0:T(8,128)(2,1)} %bitcast.265, bf16[768,1536]{1,0:T(8,128)(2,1)} %bitcast.257, bf16[1024,768]{1,0:T(8,128)(2,1)} %bitcast.268, f32[8,768]{1,0:T(8,128)} %get-tuple-element.69.rows.rows_one), custom_call_target="tpu_custom_call" | custom-call | flops 1207959552 | bytes 7864320 | tf_op jit(solution)/shard_map/settle/pallas_call | solution.py:223
  139.5 3.6 maximum_select_fusion.5
  147.0 4.5 collective-permute-start.27
  154.1 8.9 %collective-permute-done.27 = bf16[2,128,768]{2,1,0:T(8,128)(2,1)S(1)} collective-permute-done((bf16[2,128,768]{2,1,0:T(8,128)(2,1)}, bf16[2,128,768]{2,1,0:T(8,128)(2,1)S(1)}, u32[]{:S(2)}, u32[]{:S(2)}) %collective-permute-start.27) | collective-permute-done | bytes 393248 | tf_op jit(solution)/shard_map/ppermute | solution.py:491
  162.9 16.3 %collective-permute-done.28 = bf16[2,128,768]{2,1,0:T(8,128)(2,1)} collective-permute-done((bf16[2,128,768]{2,1,0:T(8,128)(2,1)}, bf16[2,128,768]{2,1,0:T(8,128)(2,1)}, u32[]{:S(2)}, u32[]{:S(2)}) %collective-permute-start.28) | collective-permute-done | bytes 393248 | tf_op jit(solution)/shard_map/ppermute | solution.py:491
  181.7 6.8 %maximum_select_fusion.1 = bf16[2,2,2,4,96,768]{5,4,3,2,1,0:T(8,128)(2,1)} fusion(bf16[2,2,1,4,96,768]{5,4,3,2,1,0:T(8,128)(2,1)} %bitcast.60, bf16[2,2,1,4,96,768]{5,4,3,2,1,0:T(8,128)(2,1)} %bitcast.59, pred[]{:T(512)S(6)} %eq.58), kind=kLoop, calls=%fused_computation.6 | loop fusion | flops 7077888 | bytes 9437185 | tf_op jit(solution)/shard_map/jit(_where)/select_n | solution.py:518
  196.6 22.7 %feed.1 = (bf16[1024,3072]{1,0:T(8,128)(2,1)}, bf16[1024,3072]{1,0:T(8,128)(2,1)}, f32[1024,768]{1,0:T(8,128)}, f32[1024,1]{1,0:T(8,128)}, bf16[2,128,768]{2,1,0...) custom-call(bf16[1024,768]{1,0:T(8,128)(2,1)} %get-tuple-element.70.low, ...), custom_call_target="tpu_custom_call" | custom-call | flops 9663676416 | bytes 37748736 | tf_op jit(solution)/shard_map/feed/pallas_call | solution.py:279
  219.4 28.7 %feed_back.1 = (bf16[768,3072]{1,0:T(8,128)(2,1)}, f32[1,3072]{1,0:T(1,128)}, bf16[3072,768]{1,0:T(8,128)(2,1)}, f32[1024,768]{1,0:T(8,128)}, f32[8,768]{1,0:T(8,128)}) custom-call(bf16[1024,768]{1,0:T(8,128)(2,1)} %bitcast.295, f32[1024,768]{1,0:T(8,128)} %get-tuple-element.83.normed_two, f32[1024,1]{1,0:T(8,128)} %get-tuple-element.84.inverse_two, ...), custom_call_target="tpu_custom_call" | custom-call | flops 19327352832 | bytes 37748736 | tf_op jit(solution)/shard_map/feed_back/pallas_call | solution.py:338
  258.2 9.5 %collective-permute-start.24 = (bf16[2,128,768]{2,1,0:T(8,128)(2,1)}, bf16[2,128,768]{2,1,0:T(8,128)(2,1)S(1)}, u32[]{:S(2)}, u32[]{:S(2)}) collective-permute-start(bf16[2,128,768]{2,1,0:T(8,128)(2,1)} %get-tuple-element.77), channel_id=1, source_target_pairs={{0,3},{1,0},{2,1},{3,2},{4,7},{5,4},{6,5},{7,6},{8,11},{9,8},{10,9... | collective-permute-start | bytes 1179656 | tf_op jit(solution)/shard_map/ppermute | solution.py:491
  268.6 9.6 %settle_back.1 = (f32[1024,768]{1,0:T(8,128)}, bf16[1024,768]{1,0:T(8,128)(2,1)}, bf16[768,768]{1,0:T(8,128)(2,1)}, f32[8,768]{1,0:T(8,128)}) custom-call(f32[1024,768]{1,0:T(8,128)} %get-tuple-element.87.hidden_grad, f32[1024,768]{1,0:T(8,128)} %get-tuple-element.75.normed_one.normed, f32[1024,1]{1,0:T(8,128)} %get-tuple-element.88.inverse, ...), custom_call_target="tpu_custom_call" | custom-call | flops 2415919104 | bytes 12582912 | tf_op jit(solution)/shard_map/settle_back/pallas_call | solution.py:403
  279.3 23.8 %collective-permute-done.25 = bf16[2,128,768]{2,1,0:T(8,128)(2,1)S(1)} collective-permute-done((bf16[2,128,768]{2,1,0:T(8,128)(2,1)}, bf16[2,128,768]{2,1,0:T(8,128)(2,1)S(1)}, u32[]{:S(2)}, u32[]{:S(2)}) %collective-permute-start.25) | collective-permute-done | bytes 393248 | tf_op jit(solution)/shard_map/ppermute | solution.py:491
  316.1 21.1 %attend_back.1 = (bf16[2,512,2304]{2,1,0:T(8,128)(2,1)}, f32[2,1,2304]{2,1,0:T(1,128)}) custom-call(bf16[2,512,2304]{2,1,0:T(8,128)(2,1)} %bitcast.253, bf16[2,512,2304]{2,1,0:T(8,128)(2,1)} %bitcast.254, bf16[2,512,2304]{2,1,0:T(8,128)(2,1)} %bitcast.255, bf16[2,512,768]{2,1,0:T(8,128)(2,1)} %bitcast.294, bf16[2,12,512,512]{3,2,1,0:T(8,128)(2,1)} %get-tuple-element.95.probs), custom_call_target="tpu_custom_call" | custom-call | flops 6442450944 | bytes 25165824 | tf_op jit(solution)/shard_map/attend_back/pallas_call | solution.py:178
  346.3 13.7 %project_back.1 = (bf16[768,2304]{1,0:T(8,128)(2,1)}, bf16[2,128,768]{2,1,0:T(8,128)(2,1)}, bf16[2,128,768]{2,1,0:T(8,128)(2,1)}, bf16[2,128,768]{2,1,0:T(8,128)(2,1)}, bf16[2,128,768]{2,1,0:T(8,128)(2,1)}) custom-call(bf16[1024,2304]{1,0:T(8,128)(2,1)} %bitcast.305, bf16[1024,768]{1,0:T(8,128)(2,1)} %bitcast.269, bf16[768,1664]{1,0:T(8,128)(2,1)} %bitcast.289, ...), custom_call_target="tpu_custom_call" | custom-call | flops 7247757312 | bytes 9437184 | tf_op jit(solution)/shard_map/project_back/pallas_call | solution.py:454
  369.9 10.0 %collective-permute-done.34 = bf16[2,128,768]{2,1,0:T(8,128)(2,1)S(1)} collective-permute-done((bf16[2,128,768]{2,1,0:T(8,128)(2,1)S(1)}, bf16[2,128,768]{2,1,0:T(8,128)(2,1)S(1)}, u32[]{:S(2)}, u32[]{:S(2)}) %collective-permute-start.34) | collective-permute-done | bytes 393248 | tf_op jit(solution)/shard_map/ppermute | solution.py:491
  379.9 23.4 %collective-permute-done.35 = bf16[2,128,768]{2,1,0:T(8,128)(2,1)S(1)} collective-permute-done((bf16[2,128,768]{2,1,0:T(8,128)(2,1)S(1)}, bf16[2,128,768]{2,1,0:T(8,128)(2,1)S(1)}, u32[]{:S(2)}, u32[]{:S(2)}) %collective-permute-start.35) | collective-permute-done | bytes 393248 | tf_op jit(solution)/shard_map/ppermute | solution.py:491
  411.8 3.7 collective-permute-done.54
  415.5 4.1 collective-permute-start.50
  421.6 4.9 collective-permute-start.52
  427.3 6.6 %collective-permute-done.51 = bf16[24,3200]{1,0:T(8,128)(2,1)S(1)} collective-permute-done((bf16[24,3200]{1,0:T(8,128)(2,1)S(1)}, bf16[24,3200]{1,0:T(8,128)(2,1)S(1)}, u32[]{:S(2)}, u32[]{:S(2)}) %collective-permute-start.51) | collective-permute-done | bytes 153632 | tf_op jit(solution)/shard_map/ppermute | solution.py:491
  446.0 10.2 %collective-permute-done.44 = bf16[2,4,24,1536]{3,2,1,0:T(8,128)(2,1)S(1)} collective-permute-done((bf16[2,4,24,1536]{3,2,1,0:T(8,128)(2,1)S(1)}, bf16[2,4,24,1536]{3,2,1,0:T(8,128)(2,1)S(1)}, u32[]{:S(2)}, u32[]{:S(2)}) %collective-permute-start.44) | collective-permute-done | bytes 589856 | tf_op jit(solution)/shard_map/ppermute | solution.py:499
  461.4 5.2 %collective-permute-done.45 = bf16[4,24,1536]{2,1,0:T(8,128)(2,1)S(1)} collective-permute-done((bf16[4,24,1536]{2,1,0:T(8,128)(2,1)S(1)}, bf16[4,24,1536]{2,1,0:T(8,128)(2,1)S(1)}, u32[]{:S(2)}, u32[]{:S(2)}) %collective-permute-start.45) | collective-permute-done | bytes 294944 | tf_op jit(solution)/shard_map/ppermute | solution.py:499
  475.0 3.7 collective-permute-done.39
  (288 shorter events, 149.7 us)
Async XLA Ops:
  24.0 15.0 %collective-permute-start.3 = (bf16[2,128,768]{2,1,0:T(8,128)(2,1)S(1)}, bf16[2,128,768]{2,1,0:T(8,128)(2,1)S(1)}, u32[]{:S(2)}, u32[]{:S(2)}) collective-permute-start(bf16[2,128,768]{2,1,0:T(8,128)(2,1)S(1)} %get-tuple-element.61), channel_id=1, source_target_pairs={{0,1},{1,2},{2,3},{3,0},{4,5},{5,6},{6,7},{7,4},{8,9},{9,10},{10,1... | collective-permute-start | bytes 1179656 | tf_op jit(solution)/shard_map/ppermute | solution.py:491
  27.7 27.4 %collective-permute-start.4 = (bf16[2,128,768]{2,1,0:T(8,128)(2,1)S(1)}, bf16[2,128,768]{2,1,0:T(8,128)(2,1)S(1)}, u32[]{:S(2)}, u32[]{:S(2)}) collective-permute-start(bf16[2,128,768]{2,1,0:T(8,128)(2,1)S(1)} %get-tuple-element.62), channel_id=1, source_target_pairs={{0,2},{1,3},{2,0},{3,1},{4,6},{5,7},{6,4},{7,5},{8,10},{9,11},{10,... | collective-permute-start | bytes 1179656 | tf_op jit(solution)/shard_map/ppermute | solution.py:491
  29.4 25.7 %collective-permute-start.5 = (bf16[2,128,768]{2,1,0:T(8,128)(2,1)S(1)}, bf16[2,128,768]{2,1,0:T(8,128)(2,1)S(1)}, u32[]{:S(2)}, u32[]{:S(2)}) collective-permute-start(bf16[2,128,768]{2,1,0:T(8,128)(2,1)S(1)} %get-tuple-element.63), channel_id=1, source_target_pairs={{0,3},{1,0},{2,1},{3,2},{4,7},{5,4},{6,5},{7,6},{8,11},{9,8},{10,9... | collective-permute-start | bytes 1179656 | tf_op jit(solution)/shard_map/ppermute | solution.py:491
  30.2 55.8 %collective-permute-start.18 = (bf16[2,4,24,1536]{3,2,1,0:T(8,128)(2,1)S(1)}, bf16[2,4,24,1536]{3,2,1,0:T(8,128)(2,1)S(1)}, u32[]{:S(2)}, u32[]{:S(2)}) collective-permute-start(bf16[2,4,24,1536]{3,2,1,0:T(8,128)(2,1)S(1)} %maximum_select_fusion.14), channel_id=1, source_target_pairs={{0,8},{1,9},{2,10},{3,11},{4,12},{5,13},{6,14},{7,15},{8,0},{9,1},... | collective-permute-start | bytes 1769480 | tf_op jit(solution)/shard_map/ppermute | solution.py:499
  31.7 54.8 %collective-permute-start.15 = (bf16[2,4,24,1664]{3,2,1,0:T(8,128)(2,1)S(1)}, bf16[2,4,24,1664]{3,2,1,0:T(8,128)(2,1)S(1)}, u32[]{:S(2)}, u32[]{:S(2)}) collective-permute-start(bf16[2,4,24,1664]{3,2,1,0:T(8,128)(2,1)S(1)} %maximum_select_fusion.11), channel_id=1, source_target_pairs={{0,16},{1,17},{2,18},{3,19},{4,20},{5,21},{6,22},{7,23},{8,24},{9,... | collective-permute-start | bytes 1916936 | tf_op jit(solution)/shard_map/ppermute | solution.py:499
  39.0 30.8 %collective-permute-start.11 = (bf16[96,768]{1,0:T(8,128)(2,1)S(1)}, bf16[96,768]{1,0:T(8,128)(2,1)S(1)}, u32[]{:S(2)}, u32[]{:S(2)}) collective-permute-start(bf16[96,768]{1,0:T(8,128)(2,1)S(1)} %convert_element_type.345), channel_id=1, source_target_pairs={{0,1},{1,2},{2,3},{3,0},{4,5},{5,6},{6,7},{7,4},{8,9},{9,10},{10,1... | collective-permute-start | bytes 442376 | tf_op jit(solution)/shard_map/ppermute | solution.py:491
  55.1 15.3 %collective-permute-start.12 = (bf16[96,768]{1,0:T(8,128)(2,1)S(1)}, bf16[96,768]{1,0:T(8,128)(2,1)S(1)}, u32[]{:S(2)}, u32[]{:S(2)}) collective-permute-start(bf16[96,768]{1,0:T(8,128)(2,1)S(1)} %convert_element_type.345), channel_id=1, source_target_pairs={{0,2},{1,3},{2,0},{3,1},{4,6},{5,7},{6,4},{7,5},{8,10},{9,11},{10,... | collective-permute-start | bytes 442376 | tf_op jit(solution)/shard_map/ppermute | solution.py:491
  55.1 17.8 %collective-permute-start.13 = (bf16[96,768]{1,0:T(8,128)(2,1)S(1)}, bf16[96,768]{1,0:T(8,128)(2,1)S(1)}, u32[]{:S(2)}, u32[]{:S(2)}) collective-permute-start(bf16[96,768]{1,0:T(8,128)(2,1)S(1)} %convert_element_type.345), channel_id=1, source_target_pairs={{0,3},{1,0},{2,1},{3,2},{4,7},{5,4},{6,5},{7,6},{8,11},{9,8},{10,9... | collective-permute-start | bytes 442376 | tf_op jit(solution)/shard_map/ppermute | solution.py:491
  70.3 14.6 %collective-permute-start.8 = (bf16[24,3200]{1,0:T(8,128)(2,1)S(1)}, bf16[24,3200]{1,0:T(8,128)(2,1)S(1)}, u32[]{:S(2)}, u32[]{:S(2)}) collective-permute-start(bf16[24,3200]{1,0:T(8,128)(2,1)S(1)} %fusion.33), channel_id=1, source_target_pairs={{0,2},{1,3},{2,0},{3,1},{4,6},{5,7},{6,4},{7,5},{8,10},{9,11},{10,... | collective-permute-start | bytes 460808 | tf_op jit(solution)/shard_map/ppermute | solution.py:491
  111.3 28.2 %collective-permute-start.22 = (bf16[2,4,96,768]{3,2,1,0:T(8,128)(2,1)S(1)}, bf16[2,4,96,768]{3,2,1,0:T(8,128)(2,1)}, u32[]{:S(2)}, u32[]{:S(2)}) collective-permute-start(bf16[2,4,96,768]{3,2,1,0:T(8,128)(2,1)S(1)} %maximum_select_fusion.9), channel_id=1, source_target_pairs={{0,8},{1,9},{2,10},{3,11},{4,12},{5,13},{6,14},{7,15},{8,0},{9,1},... | collective-permute-start | bytes 3538952 | tf_op jit(solution)/shard_map/ppermute | solution.py:499
  112.0 31.2 %collective-permute-start.20 = (bf16[2,4,24,3200]{3,2,1,0:T(8,128)(2,1)S(1)}, bf16[2,4,24,3200]{3,2,1,0:T(8,128)(2,1)}, u32[]{:S(2)}, u32[]{:S(2)}) collective-permute-start(bf16[2,4,24,3200]{3,2,1,0:T(8,128)(2,1)S(1)} %maximum_select_fusion.8), channel_id=1, source_target_pairs={{0,16},{1,17},{2,18},{3,19},{4,20},{5,21},{6,22},{7,23},{8,24},{9,... | collective-permute-start | bytes 3686408 | tf_op jit(solution)/shard_map/ppermute | solution.py:499
  143.1 38.6 %collective-permute-start.23 = (bf16[2,2,4,96,768]{4,3,2,1,0:T(8,128)(2,1)}, bf16[2,2,4,96,768]{4,3,2,1,0:T(8,128)(2,1)}, u32[]{:S(2)}, u32[]{:S(2)}) collective-permute-start(bf16[2,2,4,96,768]{4,3,2,1,0:T(8,128)(2,1)} %maximum_select_fusion.5), channel_id=1, source_target_pairs={{0,4},{1,5},{2,6},{3,7},{4,0},{5,1},{6,2},{7,3},{8,12},{9,13},{10,... | collective-permute-start | bytes 7077896 | tf_op jit(solution)/shard_map/ppermute | solution.py:499
  145.4 43.1 %collective-permute-start.21 = (bf16[2,2,4,24,3200]{4,3,2,1,0:T(8,128)(2,1)S(1)}, bf16[2,2,4,24,3200]{4,3,2,1,0:T(8,128)(2,1)}, u32[]{:S(2)}, u32[]{:S(2)}) collective-permute-start(bf16[2,2,4,24,3200]{4,3,2,1,0:T(8,128)(2,1)S(1)} %maximum_select_fusion.3), channel_id=1, source_target_pairs={{0,4},{1,5},{2,6},{3,7},{4,0},{5,1},{6,2},{7,3},{8,12},{9,13},{10,... | collective-permute-start | bytes 7372808 | tf_op jit(solution)/shard_map/ppermute | solution.py:499
  147.0 16.0 %collective-permute-start.27 = (bf16[2,128,768]{2,1,0:T(8,128)(2,1)}, bf16[2,128,768]{2,1,0:T(8,128)(2,1)S(1)}, u32[]{:S(2)}, u32[]{:S(2)}) collective-permute-start(bf16[2,128,768]{2,1,0:T(8,128)(2,1)} %get-tuple-element.80), channel_id=1, source_target_pairs={{0,1},{1,2},{2,3},{3,0},{4,5},{5,6},{6,7},{7,4},{8,9},{9,10},{10,1... | collective-permute-start | bytes 1179656 | tf_op jit(solution)/shard_map/ppermute | solution.py:491
  151.5 27.8 %collective-permute-start.28 = (bf16[2,128,768]{2,1,0:T(8,128)(2,1)}, bf16[2,128,768]{2,1,0:T(8,128)(2,1)}, u32[]{:S(2)}, u32[]{:S(2)}) collective-permute-start(bf16[2,128,768]{2,1,0:T(8,128)(2,1)} %get-tuple-element.81), channel_id=1, source_target_pairs={{0,2},{1,3},{2,0},{3,1},{4,6},{5,7},{6,4},{7,5},{8,10},{9,11},{10,... | collective-permute-start | bytes 1179656 | tf_op jit(solution)/shard_map/ppermute | solution.py:491
  153.2 26.1 %collective-permute-start.29 = (bf16[2,128,768]{2,1,0:T(8,128)(2,1)}, bf16[2,128,768]{2,1,0:T(8,128)(2,1)}, u32[]{:S(2)}, u32[]{:S(2)}) collective-permute-start(bf16[2,128,768]{2,1,0:T(8,128)(2,1)} %get-tuple-element.82), channel_id=1, source_target_pairs={{0,3},{1,0},{2,1},{3,2},{4,7},{5,4},{6,5},{7,6},{8,11},{9,8},{10,9... | collective-permute-start | bytes 1179656 | tf_op jit(solution)/shard_map/ppermute | solution.py:491
  251.3 51.9 %collective-permute-start.31 = (bf16[2,2,4,96,768]{4,3,2,1,0:T(8,128)(2,1)}, bf16[2,2,4,96,768]{4,3,2,1,0:T(8,128)(2,1)}, u32[]{:S(2)}, u32[]{:S(2)}) collective-permute-start(bf16[2,2,4,96,768]{4,3,2,1,0:T(8,128)(2,1)} %dynamic-slice_bitcast_fusion), channel_id=1, source_target_pairs={{0,4},{1,5},{2,6},{3,7},{4,0},{5,1},{6,2},{7,3},{8,12},{9,13},{10,... | collective-permute-start | bytes 7077896 | tf_op jit(solution)/shard_map/ppermute | solution.py:499
  257.7 51.8 %collective-permute-start.30 = (bf16[2,2,4,24,3200]{4,3,2,0,1:T(8,128)(2,1)}, bf16[2,2,4,24,3200]{4,3,2,0,1:T(8,128)(2,1)}, u32[]{:S(2)}, u32[]{:S(2)}) collective-permute-start(bf16[2,2,4,24,3200]{4,3,2,0,1:T(8,128)(2,1)} %bitcast.247), channel_id=1, source_target_pairs={{0,4},{1,5},{2,6},{3,7},{4,0},{5,1},{6,2},{7,3},{8,12},{9,13},{10,... | collective-permute-start | bytes 7372808 | tf_op jit(solution)/shard_map/ppermute | solution.py:499
  258.2 21.0 %collective-permute-start.24 = (bf16[2,128,768]{2,1,0:T(8,128)(2,1)}, bf16[2,128,768]{2,1,0:T(8,128)(2,1)S(1)}, u32[]{:S(2)}, u32[]{:S(2)}) collective-permute-start(bf16[2,128,768]{2,1,0:T(8,128)(2,1)} %get-tuple-element.77), channel_id=1, source_target_pairs={{0,3},{1,0},{2,1},{3,2},{4,7},{5,4},{6,5},{7,6},{8,11},{9,8},{10,9... | collective-permute-start | bytes 1179656 | tf_op jit(solution)/shard_map/ppermute | solution.py:491
  267.7 35.4 %collective-permute-start.25 = (bf16[2,128,768]{2,1,0:T(8,128)(2,1)}, bf16[2,128,768]{2,1,0:T(8,128)(2,1)S(1)}, u32[]{:S(2)}, u32[]{:S(2)}) collective-permute-start(bf16[2,128,768]{2,1,0:T(8,128)(2,1)} %get-tuple-element.78), channel_id=1, source_target_pairs={{0,2},{1,3},{2,0},{3,1},{4,6},{5,7},{6,4},{7,5},{8,10},{9,11},{10,... | collective-permute-start | bytes 1179656 | tf_op jit(solution)/shard_map/ppermute | solution.py:491
  268.6 34.5 %collective-permute-start.26 = (bf16[2,128,768]{2,1,0:T(8,128)(2,1)}, bf16[2,128,768]{2,1,0:T(8,128)(2,1)S(1)}, u32[]{:S(2)}, u32[]{:S(2)}) collective-permute-start(bf16[2,128,768]{2,1,0:T(8,128)(2,1)} %get-tuple-element.79), channel_id=1, source_target_pairs={{0,1},{1,2},{2,3},{3,0},{4,5},{5,6},{6,7},{7,4},{8,9},{9,10},{10,1... | collective-permute-start | bytes 1179656 | tf_op jit(solution)/shard_map/ppermute | solution.py:491
  308.1 30.8 %collective-permute-start.33 = (bf16[2,4,96,768]{3,2,1,0:T(8,128)(2,1)}, bf16[2,4,96,768]{3,2,1,0:T(8,128)(2,1)}, u32[]{:S(2)}, u32[]{:S(2)}) collective-permute-start(bf16[2,4,96,768]{3,2,1,0:T(8,128)(2,1)} %dynamic-slice_bitcast_fusion.3), channel_id=1, source_target_pairs={{0,16},{1,17},{2,18},{3,19},{4,20},{5,21},{6,22},{7,23},{8,24},{9,... | collective-permute-start | bytes 3538952 | tf_op jit(solution)/shard_map/ppermute | solution.py:499
  314.6 28.1 %collective-permute-start.32 = (bf16[2,4,24,3200]{3,2,1,0:T(8,128)(2,1)}, bf16[2,4,24,3200]{3,2,1,0:T(8,128)(2,1)}, u32[]{:S(2)}, u32[]{:S(2)}) collective-permute-start(bf16[2,4,24,3200]{3,2,1,0:T(8,128)(2,1)} %dynamic-slice_bitcast_fusion.1), channel_id=1, source_target_pairs={{0,8},{1,9},{2,10},{3,11},{4,12},{5,13},{6,14},{7,15},{8,0},{9,1},... | collective-permute-start | bytes 3686408 | tf_op jit(solution)/shard_map/ppermute | solution.py:499
  341.5 64.0 %collective-permute-start.53 = (bf16[4,96,768]{2,1,0:T(8,128)(2,1)}, bf16[4,96,768]{2,1,0:T(8,128)(2,1)}, u32[]{:S(2)}, u32[]{:S(2)}) collective-permute-start(bf16[4,96,768]{2,1,0:T(8,128)(2,1)} %dynamic-slice_bitcast_fusion.6), channel_id=1, source_target_pairs={{0,8},{1,9},{2,10},{3,11},{4,12},{5,13},{6,14},{7,15},{8,0},{9,1},... | collective-permute-start | bytes 1769480 | tf_op jit(solution)/shard_map/ppermute | solution.py:499
  363.3 45.4 %collective-permute-start.49 = (bf16[4,24,3200]{2,1,0:T(8,128)(2,1)}, bf16[4,24,3200]{2,1,0:T(8,128)(2,1)S(1)}, u32[]{:S(2)}, u32[]{:S(2)}) collective-permute-start(bf16[4,24,3200]{2,1,0:T(8,128)(2,1)} %dynamic-slice_bitcast_fusion.5), channel_id=1, source_target_pairs={{0,16},{1,17},{2,18},{3,19},{4,20},{5,21},{6,22},{7,23},{8,24},{9,... | collective-permute-start | bytes 1843208 | tf_op jit(solution)/shard_map/ppermute | solution.py:499
  366.9 75.1 %collective-permute-start.37 = (bf16[2,2,4,24,1664]{4,3,2,0,1:T(8,128)(2,1)}, bf16[2,2,4,24,1664]{4,3,2,0,1:T(8,128)(2,1)}, u32[]{:S(2)}, u32[]{:S(2)}) collective-permute-start(bf16[2,2,4,24,1664]{4,3,2,0,1:T(8,128)(2,1)} %bitcast.248), channel_id=1, source_target_pairs={{0,4},{1,5},{2,6},{3,7},{4,0},{5,1},{6,2},{7,3},{8,12},{9,13},{10,... | collective-permute-start | bytes 3833864 | tf_op jit(solution)/shard_map/ppermute | solution.py:499
  367.2 36.1 %collective-permute-start.35 = (bf16[2,128,768]{2,1,0:T(8,128)(2,1)S(1)}, bf16[2,128,768]{2,1,0:T(8,128)(2,1)S(1)}, u32[]{:S(2)}, u32[]{:S(2)}) collective-permute-start(bf16[2,128,768]{2,1,0:T(8,128)(2,1)S(1)} %copy-done.23), channel_id=1, source_target_pairs={{0,2},{1,3},{2,0},{3,1},{4,6},{5,7},{6,4},{7,5},{8,10},{9,11},{10,... | collective-permute-start | bytes 1179656 | tf_op jit(solution)/shard_map/ppermute | solution.py:491
  379.9 23.5 %collective-permute-start.36 = (bf16[2,128,768]{2,1,0:T(8,128)(2,1)S(1)}, bf16[2,128,768]{2,1,0:T(8,128)(2,1)S(1)}, u32[]{:S(2)}, u32[]{:S(2)}) collective-permute-start(bf16[2,128,768]{2,1,0:T(8,128)(2,1)S(1)} %copy-done.22), channel_id=1, source_target_pairs={{0,1},{1,2},{2,3},{3,0},{4,5},{5,6},{6,7},{7,4},{8,9},{9,10},{10,1... | collective-permute-start | bytes 1179656 | tf_op jit(solution)/shard_map/ppermute | solution.py:491
  403.3 35.7 %collective-permute-start.43 = (bf16[2,2,4,24,1536]{4,3,2,1,0:T(8,128)(2,1)}, bf16[2,2,4,24,1536]{4,3,2,1,0:T(8,128)(2,1)}, u32[]{:S(2)}, u32[]{:S(2)}) collective-permute-start(bf16[2,2,4,24,1536]{4,3,2,1,0:T(8,128)(2,1)} %dynamic-slice_bitcast_fusion.2), channel_id=1, source_target_pairs={{0,4},{1,5},{2,6},{3,7},{4,0},{5,1},{6,2},{7,3},{8,12},{9,13},{10,... | collective-permute-start | bytes 3538952 | tf_op jit(solution)/shard_map/ppermute | solution.py:499
  421.6 15.2 %collective-permute-start.52 = (bf16[24,3200]{1,0:T(8,128)(2,1)S(1)}, bf16[24,3200]{1,0:T(8,128)(2,1)S(1)}, u32[]{:S(2)}, u32[]{:S(2)}) collective-permute-start(bf16[24,3200]{1,0:T(8,128)(2,1)S(1)} %get-tuple-element.130), channel_id=1, source_target_pairs={{0,3},{1,0},{2,1},{3,2},{4,7},{5,4},{6,5},{7,6},{8,11},{9,8},{10,9... | collective-permute-start | bytes 460808 | tf_op jit(solution)/shard_map/ppermute | solution.py:491
  440.9 15.3 %collective-permute-start.44 = (bf16[2,4,24,1536]{3,2,1,0:T(8,128)(2,1)S(1)}, bf16[2,4,24,1536]{3,2,1,0:T(8,128)(2,1)S(1)}, u32[]{:S(2)}, u32[]{:S(2)}) collective-permute-start(bf16[2,4,24,1536]{3,2,1,0:T(8,128)(2,1)S(1)} %dynamic-slice_bitcast_fusion.7), channel_id=1, source_target_pairs={{0,16},{1,17},{2,18},{3,19},{4,20},{5,21},{6,22},{7,23},{8,24},{9,... | collective-permute-start | bytes 1769480 | tf_op jit(solution)/shard_map/ppermute | solution.py:499
  443.8 17.4 %collective-permute-start.38 = (bf16[2,4,24,1664]{3,2,1,0:T(8,128)(2,1)S(1)}, bf16[2,4,24,1664]{3,2,1,0:T(8,128)(2,1)S(1)}, u32[]{:S(2)}, u32[]{:S(2)}) collective-permute-start(bf16[2,4,24,1664]{3,2,1,0:T(8,128)(2,1)S(1)} %dynamic-slice_bitcast_fusion.4), channel_id=1, source_target_pairs={{0,8},{1,9},{2,10},{3,11},{4,12},{5,13},{6,14},{7,15},{8,0},{9,1},... | collective-permute-start | bytes 1916936 | tf_op jit(solution)/shard_map/ppermute | solution.py:499
  (50 other events, 507.4 us)

commit v3 on v2

v3 whole, which is shorter than its diff:
```python
from functools import partial
import math

import jax
import jax.numpy as jnp
from jax import lax
from jax.experimental import pallas as pl
from jax.experimental.pallas import tpu as pltpu
from jax.sharding import PartitionSpec as P

HEAD_DIM = 64
LANES = 128
STEPS = 4
EPSILON = 1e-06
AXES = ("dp", "seq")
BF16, F32 = jnp.bfloat16, jnp.float32

NN = (((1,), (0,)), ((), ()))
NT = (((1,), (1,)), ((), ()))
TN = (((0,), (0,)), ((), ()))


def narrow(value):
    return value.astype(BF16)


def widen(value):
    return value.astype(F32)


def after(value, *others):
    return lax.optimization_barrier((value,) + others)[0]


def dot(left, right, dims=NN):
    return lax.dot_general(left, right, dims, preferred_element_type=F32)


def shape(dims, dtype=BF16):
    return jax.ShapeDtypeStruct(dims, dtype)


def like(value):
    return jax.ShapeDtypeStruct(value.shape, value.dtype)


def fixed(dims, *index):
    at = tuple(index) or (0,) * len(dims)
    return pl.BlockSpec(dims, lambda *_: at)


SCALARS = pl.BlockSpec(memory_space=pltpu.SMEM)
ANYWHERE = pl.BlockSpec(memory_space=pl.ANY)


def row_sum(value):
    return jnp.sum(value, axis=0, keepdims=True)


def kernel(body, name, flops, touched, **options):
    return pl.pallas_call(
        body,
        name=name,
        compiler_params=pltpu.CompilerParams(vmem_limit_bytes=60 << 20),
        cost_estimate=pl.CostEstimate(flops=flops, bytes_accessed=touched, transcendentals=0),
        **options,
    )


def unite(target, own, other, side):
    count, rows = own.shape[:2]
    for index in range(count):
        for half, value in ((side, own), (1 - side, other)):
            start = pl.multiple_of((2 * index + half) * rows, rows)
            target[pl.ds(start, rows), :] = value[index]


def divide(source, keep, send, side, columns):
    count, rows = keep.shape[:2]
    for index in range(count):
        for half, target in ((side, keep), (1 - side, send)):
            start = pl.multiple_of((2 * index + half) * rows, rows)
            target[index, :, columns] = source[pl.ds(start, rows), :]


def as_columns(rows):
    width = rows[0].shape[1]
    padding = jnp.zeros((LANES - len(rows), width), F32)
    return jnp.concatenate(list(rows) + [padding], axis=0).T


def project_body(
    spots, tokens, own_first, other_first, own_second, other_second, own_vectors, other_vectors,
    packed, rows, weight, vectors,
):
    part, side = pl.program_id(0), spots[1]

    @pl.when(part == 0)
    def _():
        unite(vectors, own_vectors, other_vectors, side)
        rows[...] = widen(vectors[...]).T[:8]

    @pl.when(part < 2)
    def _():
        unite(weight, own_first, other_first, side)

    @pl.when(part == 2)
    def _():
        unite(weight, own_second, other_second, side)

    query, value = rows[0:1], rows[1:2]
    bias = jnp.where(part == 0, query, jnp.where(part == 2, value, jnp.zeros_like(query)))
    packed[...] = narrow(dot(tokens[...], weight[...]) + bias)


def project(spots, tokens, first, second):
    count, width = tokens.shape
    parts, rows, _ = first[0].shape
    pick = pl.BlockSpec((parts, rows, width), lambda i: (0, 0, jnp.minimum(i, 1)))
    value = fixed((parts, rows, width))
    vectors = fixed((parts, rows, LANES), 0, 0, 2 * width // LANES)
    return kernel(
        project_body,
        "project",
        6 * count * width * width,
        8 * count * width,
        grid=(3,),
        in_specs=[SCALARS, fixed(tokens.shape), pick, pick, value, value, vectors, vectors],
        out_specs=[pl.BlockSpec((count, width), lambda i: (0, i)), fixed((8, width))],
        out_shape=[shape((count, 3 * width)), shape((8, width), F32)],
        scratch_shapes=[pltpu.VMEM((width, width), BF16), pltpu.VMEM((width, LANES), BF16)],
    )(spots, tokens, *first, *second, *first)


def pair_labels(places, lengths, row):
    label, bound = jnp.zeros_like(places), 0
    for pair in range(lengths.shape[1] - 1):
        bound = bound + lengths[row, pair]
        label = label + (places >= bound).astype(jnp.int32)
    return label


def row_of(block):
    return block[...].reshape(-1, block.shape[-1])


def attend_body(spots, lengths, query, key, value, context, probs, bias):
    length = bias.shape[0]

    @pl.when(pl.program_id(1) == 0)
    def _():
        row = spots[0] * pl.num_programs(0) + pl.program_id(0)
        down = pair_labels(lax.broadcasted_iota(jnp.int32, (length, 1), 0), lengths, row)
        along = pair_labels(lax.broadcasted_iota(jnp.int32, (1, length), 1), lengths, row)
        bias[...] = jnp.where(down == along, 0.0, -1e30)

    lane = lax.broadcasted_iota(jnp.int32, (1, LANES), 1)
    keys, values = row_of(key), row_of(value)
    queries = row_of(query) * BF16(HEAD_DIM**-0.5)
    parts = []
    for head in range(2):
        mine = (lane >= HEAD_DIM) == bool(head)
        scores = dot(jnp.where(mine, queries, BF16(0)), keys, NT) + bias[...]
        raised = jnp.exp(scores - jnp.max(scores, axis=-1, keepdims=True))
        total = jnp.sum(raised, axis=-1, keepdims=True)
        low = narrow(raised * (1.0 / total))
        probs[0, head] = low
        parts.append(dot(low, values))
    result = narrow(jnp.where(lane < HEAD_DIM, parts[0], parts[1]))
    context[...] = result.reshape(context.shape)


def head_pair(seq, places, offset):
    return pl.BlockSpec((seq, 1, places, LANES), lambda r, p: (0, r, 0, offset + p))


def attend(spots, lengths, packed):
    seq, rows, places, wide = packed.shape
    length, pairs = seq * places, wide // 3 // LANES
    return kernel(
        attend_body,
        "attend",
        rows * pairs * 16 * length * length * LANES,
        rows * pairs * 8 * length * length,
        grid=(rows, pairs),
        in_specs=[
            SCALARS,
            SCALARS,
            head_pair(seq, places, 0),
            head_pair(seq, places, pairs),
            head_pair(seq, places, 2 * pairs),
        ],
        out_specs=[
            head_pair(seq, places, 0),
            pl.BlockSpec((1, 2, length, length), lambda r, p: (r, p, 0, 0)),
        ],
        out_shape=[shape((seq, rows, places, wide // 3)), shape((rows, 2 * pairs, length, length))],
        scratch_shapes=[pltpu.VMEM((length, length), F32)],
    )(spots, lengths, packed, packed, packed)


def attend_back_body(query, key, value, upstream, probs, grads, sums):
    pair, pairs = pl.program_id(1), pl.num_programs(1)
    lane = lax.broadcasted_iota(jnp.int32, (1, LANES), 1)
    scale = BF16(HEAD_DIM**-0.5)
    queries, keys, values, up = row_of(query) * scale, row_of(key), row_of(value), row_of(upstream)
    scaled_keys = keys * scale
    query_parts, key_grad, value_grad = [], 0.0, 0.0
    for head in range(2):
        mine = (lane >= HEAD_DIM) == bool(head)
        up_mine = jnp.where(mine, up, BF16(0))
        queries_mine = jnp.where(mine, queries, BF16(0))
        low = probs[0, head]
        prob_grad = dot(up_mine, values, NT)
        softmaxed = widen(low)
        weighted = jnp.sum(softmaxed * prob_grad, axis=-1, keepdims=True)
        score_grad = narrow(softmaxed * (prob_grad - weighted))
        query_parts.append(dot(score_grad, scaled_keys))
        key_grad = key_grad + dot(queries_mine, score_grad, TN)
        value_grad = value_grad + dot(up_mine, low, TN)
    query_grad = jnp.where(lane < HEAD_DIM, query_parts[0], query_parts[1])
    for part, grad in enumerate((query_grad, key_grad.T, value_grad.T)):
        at = pl.ds(pl.multiple_of((part * pairs + pair) * LANES, LANES), LANES)
        rounded = narrow(grad)
        grads[:, :, :, at] = rounded.reshape(grads.shape[:3] + (LANES,))
        sums[0, :, at] = row_sum(widen(rounded))


def attend_back(packed, probs, upstream):
    seq, rows, places, wide = packed.shape
    length, pairs = seq * places, wide // 3 // LANES
    return kernel(
        attend_back_body,
        "attend_back",
        rows * pairs * 16 * length * length * LANES,
        rows * pairs * 8 * length * length,
        grid=(rows, pairs),
        in_specs=[
            head_pair(seq, places, 0),
            head_pair(seq, places, pairs),
            head_pair(seq, places, 2 * pairs),
            head_pair(seq, places, 0),
            pl.BlockSpec((1, 2, length, length), lambda r, p: (r, p, 0, 0)),
        ],
        out_specs=[
            pl.BlockSpec((seq, 1, places, wide), lambda r, p: (0, r, 0, 0)),
            pl.BlockSpec((1, 1, wide), lambda r, p: (r, 0, 0)),
        ],
        out_shape=[shape(packed.shape), shape((rows, 1, wide), F32)],
    )(packed, packed, packed, upstream, probs)


def normed_of(summed):
    centred = summed - jnp.mean(summed, axis=-1, keepdims=True)
    variance = jnp.mean(centred * centred, axis=-1, keepdims=True)
    inverse = lax.rsqrt(variance + EPSILON)
    return centred * inverse, inverse


def norm_back(upstream, normed, inverse, gain):
    scaled = upstream * gain
    first_mean = jnp.mean(scaled, axis=-1, keepdims=True)
    second_mean = jnp.mean(scaled * normed, axis=-1, keepdims=True)
    return inverse * (scaled - first_mean - normed * second_mean)


def settle_body(spots, context, own, other, tokens, rows, normed, inverse, low, weight):
    @pl.when(pl.program_id(0) == 0)
    def _():
        unite(weight, own, other, spots[1])

    summed = widen(tokens[...]) + dot(context[...], weight[...]) + rows[2:3]
    normed[...], inverse[...] = normed_of(summed)
    low[...] = narrow(normed[...] * rows[3:4] + rows[4:5])


def settle(spots, context, second, tokens, rows):
    count, width = context.shape
    block = count // 4
    tall = pl.BlockSpec((block, width), lambda i: (i, 0))
    half = fixed(second[0].shape[:2] + (width,), 0, 0, 1)
    return kernel(
        settle_body,
        "settle",
        2 * count * width * width,
        10 * count * width,
        grid=(4,),
        in_specs=[SCALARS, tall, half, half, tall, fixed(rows.shape)],
        out_specs=[tall, pl.BlockSpec((block, 1), lambda i: (i, 0)), tall],
        out_shape=[shape((count, width), F32), shape((count, 1), F32), shape((count, width))],
        scratch_shapes=[pltpu.VMEM((width, width), BF16)],
    )(spots, context, *second, tokens, rows)


def spread_mask(rows, per, column):
    down = lax.broadcasted_iota(jnp.int32, (rows, rows * per), 0)
    along = lax.broadcasted_iota(jnp.int32, (rows, rows * per), 1)
    return along == down * per + column


def feed_body(
    spots, low, own_inner, other_inner, own_outer, other_outer, own_vectors, other_vectors,
    normed_one, rows_one,
    active, slope, normed_two, inverse_two, rows_two, output,
    branch, inner_weight, outer_weight, vectors,
):
    step, steps, side = pl.program_id(0), pl.num_programs(0), spots[1]

    @pl.when(step == 0)
    def _():
        unite(vectors, own_vectors, other_vectors, side)
        rows_two[...] = widen(vectors[...]).T[:8]

    unite(inner_weight, own_inner, other_inner, side)
    unite(outer_weight, own_outer, other_outer, side)
    block = inner_weight.shape[1]
    share_rows = vectors.shape[0] // STEPS
    per = block // share_rows
    own_rows = vectors[pl.ds(pl.multiple_of(step * share_rows, share_rows), share_rows), :]
    bias = 0.0
    for column in range(per):
        value = widen(own_rows[:, 3 + column : 4 + column])
        bias = bias + jnp.where(spread_mask(share_rows, per, column), value, 0.0)
    inner = dot(low[...], inner_weight[...]) + row_sum(bias)
    share = 0.5 * (1.0 + lax.erf(inner * math.sqrt(0.5)))
    raised = jnp.exp(-0.5 * inner * inner) * (1.0 / math.sqrt(2.0 * math.pi))
    acted = narrow(inner * share)
    active[...] = acted
    slope[...] = narrow(share + inner * raised)
    part = dot(acted, outer_weight[...])

    @pl.when(step == 0)
    def _():
        branch[...] = part

    @pl.when(step > 0)
    def _():
        branch[...] += part

    @pl.when(step == steps - 1)
    def _():
        hidden = normed_one[...] * rows_one[3:4] + rows_one[4:5]
        normed_two[...], inverse_two[...] = normed_of(hidden + branch[...] + rows_two[0:1])
        output[...] = narrow(normed_two[...] * rows_two[1:2] + rows_two[2:3])


def feed_specs(width, inner, outer):
    parts, rows, _ = inner[0].shape
    block = outer[0].shape[0] * outer[0].shape[1] * 2 // STEPS
    right = pl.BlockSpec((parts, rows, block), lambda f: (0, 0, f))
    down = pl.BlockSpec((outer[0].shape[0] // STEPS, outer[0].shape[1], width), lambda f: (f, 0, 0))
    return block, right, down


def feed(spots, low, inner, outer, normed_one, rows_one):
    count, width = low.shape
    block, right, down = feed_specs(width, inner, outer)
    wide = block * STEPS
    all_of = fixed((count, width))
    across = pl.BlockSpec((count, block), lambda f: (0, f))
    vectors = fixed(inner[0].shape[:2] + (LANES,), 0, 0, wide // LANES)
    return kernel(
        feed_body,
        "feed",
        4 * count * width * wide,
        12 * count * wide,
        grid=(STEPS,),
        in_specs=[SCALARS, all_of, right, right, down, down, vectors, vectors, all_of]
        + [fixed(rows_one.shape)],
        out_specs=[across, across, all_of, fixed((count, 1)), fixed((8, width)), all_of],
        out_shape=[
            shape((count, wide)),
            shape((count, wide)),
            shape((count, width), F32),
            shape((count, 1), F32),
            shape((8, width), F32),
            shape((count, width)),
        ],
        scratch_shapes=[
            pltpu.VMEM((count, width), F32),
            pltpu.VMEM((width, block), BF16),
            pltpu.VMEM((block, width), BF16),
            pltpu.VMEM((width, LANES), BF16),
        ],
    )(spots, low, *inner, *outer, *inner, normed_one, rows_one)


def feed_back_body(
    spots, cotangent, normed_two, inverse_two, rows_two, low,
    own_inner, other_inner, own_outer, other_outer, active, slope,
    keep_inner, send_inner, keep_outer, send_outer, hidden_grad,
    up, inner_weight, outer_weight, made, columns,
):
    step, steps, side = pl.program_id(0), pl.num_programs(0), spots[1]
    block = inner_weight.shape[1]

    @pl.when(step == 0)
    def _():
        upstream = widen(cotangent[...])
        normed = normed_two[...]
        hidden_grad[...] = norm_back(upstream, normed, inverse_two[...], rows_two[1:2])
        up[...] = narrow(hidden_grad[...])
        columns[...] = as_columns(
            (row_sum(widen(up[...])), row_sum(upstream * normed), row_sum(upstream))
        )

    unite(inner_weight, own_inner, other_inner, side)
    unite(outer_weight, own_outer, other_outer, side)
    inner_grad = narrow(dot(up[...], outer_weight[...], NT) * widen(slope[...]))
    made[...] = narrow(dot(low[...], inner_grad, TN))
    at = pl.ds(pl.multiple_of(step * block, block), block)
    divide(made, keep_inner, send_inner, side, at)
    hidden_grad[...] += dot(inner_grad, inner_weight[...], NT)
    outer_weight[...] = narrow(dot(active[...], up[...], TN))
    divide(outer_weight, keep_outer, send_outer, side, slice(None))

    bias = row_sum(widen(inner_grad))
    share_rows = columns.shape[0] // STEPS
    per = block // share_rows
    lane = lax.broadcasted_iota(jnp.int32, (1, LANES), 1)
    total = 0.0
    for column in range(per):
        value = jnp.sum(
            jnp.where(spread_mask(share_rows, per, column), bias, 0.0), axis=1, keepdims=True
        )
        total = total + jnp.where(lane == 3 + column, value, 0.0)
    columns[pl.ds(pl.multiple_of(step * share_rows, share_rows), share_rows), :] += total

    @pl.when(step == steps - 1)
    def _():
        made[:, :LANES] = narrow(columns[...])
        count, rows, wide = keep_inner.shape
        for index in range(count):
            for half, target in ((side, keep_inner), (1 - side, send_inner)):
                start = pl.multiple_of((2 * index + half) * rows, rows)
                target[index, :, wide - LANES :] = made[pl.ds(start, rows), :LANES]


def feed_back(spots, cotangent, normed_two, inverse_two, rows_two, low, inner, outer, active, slope):
    count, width = low.shape
    block, right, down = feed_specs(width, inner, outer)
    wide = block * STEPS
    all_of = fixed((count, width))
    across = pl.BlockSpec((count, block), lambda f: (0, f))
    return kernel(
        feed_back_body,
        "feed_back",
        8 * count * width * wide,
        12 * count * wide,
        grid=(STEPS,),
        in_specs=[SCALARS, all_of, all_of, fixed((count, 1)), fixed((8, width)), all_of]
        + [right, right, down, down, across, across],
        out_specs=[fixed(inner[0].shape), fixed(inner[0].shape), down, down, all_of],
        out_shape=[like(inner[0]), like(inner[0]), like(outer[0]), like(outer[0])]
        + [shape((count, width), F32)],
        scratch_shapes=[
            pltpu.VMEM((count, width), BF16),
            pltpu.VMEM((width, block), BF16),
            pltpu.VMEM((block, width), BF16),
            pltpu.VMEM((width, block), BF16),
            pltpu.VMEM((width, LANES), F32),
        ],
    )(spots, cotangent, normed_two, inverse_two, rows_two, low, *inner, *outer, active, slope)


def settle_back_body(
    spots, hidden_grad, normed, inverse, rows, context, own, other,
    first_up, context_grad, keep, send, sums, total, weight,
):
    step, steps = pl.program_id(0), pl.num_programs(0)

    @pl.when(step == 0)
    def _():
        unite(weight, own, other, spots[1])
        sums[...] = jnp.zeros_like(sums)
        total[...] = jnp.zeros_like(total)

    upstream = hidden_grad[...]
    up = norm_back(upstream, normed[...], inverse[...], rows[3:4])
    first_up[...] = up
    low = narrow(up)
    context_grad[...] = narrow(dot(low, weight[...], NT))
    total[...] += dot(context[...], low, TN)
    sums[0:1] += row_sum(widen(low))
    sums[1:2] += row_sum(upstream * normed[...])
    sums[2:3] += row_sum(upstream)

    @pl.when(step == steps - 1)
    def _():
        weight[...] = narrow(total[...])
        divide(weight, keep, send, spots[1], slice(None))


def settle_back(spots, hidden_grad, normed, inverse, rows, context, second):
    count, width = context.shape
    block = count // 4
    tall = pl.BlockSpec((block, width), lambda i: (i, 0))
    dims = second[0].shape[:2] + (width,)
    return kernel(
        settle_back_body,
        "settle_back",
        4 * count * width * width,
        16 * count * width,
        grid=(4,),
        in_specs=[SCALARS, tall, tall, pl.BlockSpec((block, 1), lambda i: (i, 0))]
        + [fixed(rows.shape), tall, fixed(dims, 0, 0, 1), fixed(dims, 0, 0, 1)],
        out_specs=[tall, tall, fixed(dims), fixed(dims), fixed((8, width))],
        out_shape=[
            shape((count, width), F32),
            shape((count, width)),
            shape(dims),
            shape(dims),
            shape((8, width), F32),
        ],
        scratch_shapes=[pltpu.VMEM((width, width), F32), pltpu.VMEM((width, width), BF16)],
    )(spots, hidden_grad, normed, inverse, rows, context, *second)


def tokens_back_body(
    spots, packed_grad, own_first, other_first, own_second, other_second, first_up, grad, total, weight
):
    part, side = pl.program_id(0), spots[1]

    @pl.when(part < 2)
    def _():
        unite(weight, own_first, other_first, side)

    @pl.when(part == 2)
    def _():
        unite(weight, own_second, other_second, side)

    added = dot(packed_grad[...], weight[...], NT)

    @pl.when(part == 0)
    def _():
        total[...] = first_up[...] + added

    @pl.when(part == 1)
    def _():
        total[...] += added

    @pl.when(part == 2)
    def _():
        grad[...] = narrow(total[...] + added)


def tokens_back(spots, packed_grad, first, second, first_up):
    count, width = first_up.shape
    dims = first[0].shape[:2] + (width,)
    pick = pl.BlockSpec(dims, lambda i: (0, 0, jnp.minimum(i, 1)))
    return kernel(
        tokens_back_body,
        "tokens_back",
        6 * count * width * width,
        8 * count * width,
        grid=(3,),
        in_specs=[SCALARS, pl.BlockSpec((count, width), lambda i: (0, i)), pick, pick]
        + [fixed(dims), fixed(dims), fixed((count, width))],
        out_specs=fixed((count, width)),
        out_shape=shape((count, width)),
        scratch_shapes=[pltpu.VMEM((count, width), F32), pltpu.VMEM((width, width), BF16)],
    )(spots, packed_grad, *first, *second, first_up)


def weights_back_body(
    spots, packed_grad, tokens, packed_sums, sums, keep_first, send_first, keep_second, send_second, made
):
    part, side = pl.program_id(0), spots[1]
    width = tokens.shape[1]
    half = width // 2
    made[...] = narrow(dot(tokens[...], packed_grad[...], TN))
    low, high = made.at[:, :half], made.at[:, half:]

    @pl.when(part == 0)
    def _():
        divide(made, keep_first, send_first, side, slice(0, width))

    @pl.when(part == 1)
    def _():
        divide(low, keep_first, send_first, side, slice(width, width + half))
        divide(high, keep_second, send_second, side, slice(0, half))

    @pl.when(part == 2)
    def _():
        divide(made, keep_second, send_second, side, slice(half, half + width))
        packed = jnp.sum(packed_sums[...], axis=0)
        made[:, :LANES] = narrow(
            as_columns(
                (packed[:, :width], packed[:, 2 * width :], sums[0:1], sums[1:2], sums[2:3])
            )
        )
        divide(
            made.at[:, :LANES],
            keep_first,
            send_first,
            side,
            slice(width + half, width + half + LANES),
        )


def weights_back(spots, packed_grad, tokens, packed_sums, sums, dims):
    count, width = tokens.shape
    one, two = dims + (width + width // 2 + LANES,), dims + (width + width // 2,)
    return kernel(
        weights_back_body,
        "weights_back",
        6 * count * width * width,
        8 * count * width,
        grid=(3,),
        in_specs=[SCALARS, pl.BlockSpec((count, width), lambda i: (0, i)), fixed(tokens.shape)]
        + [fixed(packed_sums.shape), fixed(sums.shape)],
        out_specs=[fixed(one), fixed(one), fixed(two), fixed(two)],
        out_shape=[shape(one), shape(one), shape(two), shape(two)],
        scratch_shapes=[pltpu.VMEM((width, width), BF16)],
    )(spots, packed_grad, tokens, packed_sums, sums)


def move(name, spots, sources, outs, moves):
    def body(spots, *refs):
        ins, results, sems = refs[: len(sources)], refs[len(sources) : -1], refs[-1]
        copies = []
        for number, (source, source_at, out, out_at) in enumerate(moves):
            taken = ins[source].at[source_at(spots)] if source_at else ins[source]
            put = results[out].at[out_at(spots)] if out_at else results[out]
            copies.append(pltpu.make_async_copy(taken, put, sems.at[number]))
        for copy in copies:
            copy.start()
        for copy in copies:
            copy.wait()

    return kernel(
        body,
        name,
        0,
        4 * sum(math.prod(out.shape) for out in outs),
        in_specs=[SCALARS] + [ANYWHERE] * len(sources),
        out_specs=[pl.BlockSpec(memory_space=pltpu.VMEM)] * len(outs),
        out_shape=outs,
        scratch_shapes=[pltpu.SemaphoreType.DMA((len(moves),))],
    )(spots, *sources)


def combine(name, spots, groups, seq):
    operands, in_specs, out_specs, out_shape, plan = [], [], [], [], []
    for members, axis, spot in groups:
        first = members[0][0].shape
        rest = first[:axis] + first[axis + 1 : -3]
        rows = sum(kept.shape[-2] for kept, _ in members)
        for flip in range(2):
            for kept, came in members:
                dims = kept.shape
                block = dims[:axis] + (None,) + dims[axis + 1 : -3] + (None,) + dims[-2:]

                def index(i, spots, axis=axis, spot=spot, flip=flip, count=len(dims)):
                    at = [0] * count
                    at[axis] = spots[spot] if flip == 0 else 1 - spots[spot]
                    at[count - 3] = i
                    return tuple(at)

                operands += [kept, came]
                in_specs += [pl.BlockSpec(block, index)] * 2
            dims = rest + (seq, rows, first[-1])
            out_shape.append(shape(dims))
            out_specs.append(
                pl.BlockSpec(
                    rest + (None,) + dims[-2:],
                    lambda i, spots, count=len(rest): (0,) * count + (i, 0, 0),
                )
            )
            plan.append([kept.shape[-2] for kept, _ in members])

    def body(spots, *refs):
        ins, outs = iter(refs[: len(operands)]), refs[len(operands) :]
        for out, heights in zip(outs, plan):
            start = 0
            for height in heights:
                total = narrow(widen(next(ins)[...]) + widen(next(ins)[...]))
                out[..., start : start + height, :] = total
                start += height

    outs = kernel(
        body,
        name,
        0,
        3 * sum(2 * math.prod(out.shape) for out in out_shape),
        grid_spec=pltpu.PrefetchScalarGridSpec(
            num_scalar_prefetch=1, grid=(seq,), in_specs=in_specs, out_specs=out_specs
        ),
        out_shape=out_shape,
    )(spots, *operands)
    return [tuple(outs[2 * i : 2 * i + 2]) for i in range(len(groups))]


def total_of(kept, came):
    return narrow(widen(kept) + widen(came))


def block_at(blocks, index, axis=0):
    return lax.dynamic_index_in_dim(blocks, index, axis, keepdims=False)


class Links:
    def __init__(self, mesh):
        self.dp, self.seq = mesh.shape["dp"], mesh.shape["seq"]
        self.bits = self.dp.bit_length() - 1
        assert self.dp == 1 << self.bits
        upward = list(range(1, self.bits))
        self.orders = (upward, upward[::-1])
        self.direct = self.bits == 3

    def turn(self, blocks):
        return lax.all_to_all(blocks, "seq", split_axis=0, concat_axis=0, tiled=True)

    def gather_seq(self, shard):
        return self.turn(jnp.broadcast_to(shard, (self.seq,) + shard.shape))

    def reduce_seq(self, blocks):
        return jnp.sum(widen(self.turn(blocks)), axis=0)

    def by_seq(self, value):
        return value.reshape(self.seq, value.shape[0] // self.seq, *value.shape[1:])

    def across(self, value, bit):
        pairs = [
            (d * self.seq + s, (d ^ (1 << bit)) * self.seq + s)
            for d in range(self.dp)
            for s in range(self.seq)
        ]
        return lax.ppermute(value, AXES, pairs)

    def digit(self, bit):
        return (lax.axis_index("dp") >> bit) & 1

    def spots(self):
        digits = [self.digit(bit) for bit in range(self.bits)]
        if not self.direct:
            digits[0] = jnp.zeros_like(digits[0])
        return jnp.stack([lax.axis_index("seq")] + digits).astype(jnp.int32)


    def gather_digits(self, name, spots, arrays, bits, done, wait=()):
        others = [after(self.across(held, bit), *wait) for held, bit in zip(arrays, bits)]
        outs, moves = [], []
        for out, (held, bit) in enumerate(zip(arrays, bits)):
            axis = sum(other > bit for other in done[out])
            outs.append(shape(held.shape[:axis] + (2,) + held.shape[axis:]))
            for flip in range(2):

                def at(spots, axis=axis, bit=bit, flip=flip):
                    mine = spots[1 + bit]
                    return (slice(None),) * axis + (1 - mine if flip else mine,)

                moves.append((2 * out + flip, None, out, at))
        sources = [value for pair in zip(arrays, others) for value in pair]
        return move(name, spots, sources, outs, moves)

    def halves(self, held):
        if self.direct:
            held = held.reshape(STEPS, -1, held.shape[-1])
            return held, self.across(held, 0)
        whole = self.gather_rest(held)
        whole = whole.reshape(STEPS, 2, -1, whole.shape[-1])
        return whole[:, 0], whole[:, 1]

    def gather_rest(self, held):
        done = []
        for bit in self.orders[0] + [0]:
            axis = sum(other > bit for other in done)
            other, mine = self.across(held, bit), self.digit(bit)
            held = jnp.where(
                mine == 0, jnp.stack([held, other], axis=axis), jnp.stack([other, held], axis=axis)
            )
            done.append(bit)
        return held


    def swapped(self, keep, send, wait=()):
        return keep, after(self.across(send, 0), *wait)

    def reduce_whole(self, keep, send):
        rows = keep.shape[0] * keep.shape[1] * 2 // (self.dp * self.seq)
        whole = jnp.stack([keep, send], axis=1)
        held = whole.reshape((2,) * self.bits + (self.seq, rows, keep.shape[-1]))
        left = list(range(self.bits))[::-1]
        for bit in [0] + self.orders[0]:
            axis = left.index(bit)
            mine = self.digit(bit)
            other = self.across(block_at(held, 1 - mine, axis), bit)
            held = narrow(widen(block_at(held, mine, axis)) + widen(other))
            left.remove(bit)
        return self.reduce_seq(held)

    def by_digits(self, value):
        return value.reshape(2, 2, self.seq, -1, value.shape[-1])


def columns(vectors, rows):
    block = jnp.concatenate([vector.reshape(rows, -1) for vector in vectors], axis=1)
    return jnp.pad(block, ((0, 0), (0, LANES - block.shape[1])))


def shards(
    links,
    tokens,
    cotangent,
    lengths,
    packed_weight,
    query_bias,
    value_bias,
    output_weight,
    output_bias,
    first_gain,
    first_shift,
    inner_weight,
    inner_bias,
    outer_weight,
    outer_bias,
    second_gain,
    second_shift,
):
    width = tokens.shape[-1]
    seq, direct = links.seq, links.direct
    small = packed_weight.shape[0]
    feed_width = inner_weight.shape[1]
    wide = feed_width // width
    spots = links.spots()

    attention_vectors = columns(
        [narrow(v) for v in (query_bias, value_bias, output_bias, first_gain, first_shift)], small
    )
    held = [
        links.gather_seq(
            jnp.concatenate([narrow(packed_weight[:, : 2 * width]), attention_vectors], axis=1)
        ),
        links.gather_seq(
            jnp.concatenate([narrow(packed_weight[:, 2 * width :]), narrow(output_weight)], axis=1)
        ),
    ]
    feed_vectors = columns(
        [narrow(v) for v in (outer_bias, second_gain, second_shift, inner_bias)], small
    )
    feed_shard = jnp.concatenate([narrow(inner_weight), feed_vectors], axis=1)
    feed_held = [
        links.gather_seq(after(feed_shard, *held)),
        links.gather_seq(after(narrow(outer_weight), *held)),
    ]
    if direct:
        held = links.gather_digits("attention_one", spots, held, (1, 2), ([], []))
        held = links.gather_digits("attention_two", spots, held, (2, 1), ([1], [2]))
        feed_held = [after(value, *held) for value in feed_held]
    first, second = (links.halves(value) for value in held)
    came = links.turn(after(links.by_seq(tokens), *feed_held))
    if direct:
        feed_held = links.gather_digits("feed_one", spots, feed_held, (1, 2), ([], []))
    came = after(came, *feed_held)
    cotangent_mine = links.turn(after(links.by_seq(cotangent), came))
    dims = came.shape
    flat = came.reshape(-1, width)

    packed, rows_one = project(spots, flat, first, second)
    packed = packed.reshape(dims[:-1] + (3 * width,))
    context, probs = attend(spots, lengths, packed)
    context = context.reshape(-1, width)
    if direct:
        feed_held = links.gather_digits("feed_two", spots, feed_held, (2, 1), ([1], [2]), [context])
    context = after(context, *feed_held)
    normed_one, inverse_one, low = settle(spots, context, second, flat, rows_one)
    inner, outer = (links.halves(value) for value in feed_held)
    active, slope, normed_two, inverse_two, rows_two, output = feed(
        spots, low, inner, outer, normed_one, rows_one
    )
    cotangent_mine = after(cotangent_mine, slope)
    output = after(output, cotangent_mine)
    cotangent_mine = after(cotangent_mine, output)
    keep_inner, send_inner, keep_outer, send_outer, hidden_grad = feed_back(
        spots,
        cotangent_mine.reshape(-1, width),
        normed_two,
        inverse_two,
        rows_two,
        low,
        inner,
        outer,
        active,
        slope,
    )
    output = after(links.turn(output.reshape(dims)), hidden_grad)
    send_inner, send_outer = after(send_inner, output), after(send_outer, output)
    hidden_grad = after(hidden_grad, send_inner, send_outer)
    first_up, context_grad, keep_output, send_output, sums = settle_back(
        spots, hidden_grad, normed_one, inverse_one, rows_one, context, second
    )
    if direct:
        feed_pair = [links.by_digits(x) for x in links.swapped(keep_inner, send_inner, [sums])]
        outer_pair = [links.by_digits(x) for x in links.swapped(keep_outer, send_outer, [sums])]
        output_pair = [links.by_digits(x) for x in links.swapped(keep_output, send_output)]
        feed_sum, outer_sum = combine(
            "feed_sum_one", spots, [([feed_pair], 1, 2), ([outer_pair, output_pair], 0, 3)], seq
        )
        context_grad = after(context_grad, feed_sum[1], outer_sum[1])
    packed_grad, packed_sums = attend_back(packed, probs, context_grad.reshape(dims))
    packed_grad = packed_grad.reshape(-1, 3 * width)
    tokens_grad = tokens_back(spots, packed_grad, first, second, first_up)
    if direct:
        feed_came = after(links.across(feed_sum[1], 1), tokens_grad)
        outer_came = after(links.across(outer_sum[1], 2), tokens_grad)
        feed_sum, outer_sum = combine(
            "feed_sum_two",
            spots,
            [
                ([(feed_sum[0], feed_came)], 0, 3),
                ([(outer_sum[0], outer_came)], 0, 2),
            ],
            seq,
        )
        packed_grad = after(packed_grad, feed_sum[1], outer_sum[1])
    tokens_grad = links.turn(tokens_grad.reshape(dims))
    keep_first, send_first, keep_second, send_second = weights_back(
        spots, packed_grad, flat, packed_sums, sums, first[0].shape[:2]
    )
    if direct:
        first_pair = [links.by_digits(x) for x in links.swapped(keep_first, send_first)]
        second_pair = [links.by_digits(x) for x in links.swapped(keep_second, send_second)]
        first_sum, second_sum = combine(
            "first_sum_one", spots, [([first_pair], 1, 2), ([second_pair], 0, 3)], seq
        )
        first_came, second_came = links.across(first_sum[1], 1), links.across(second_sum[1], 2)
        feed_came = after(links.across(feed_sum[1], 2), first_sum[1])
        outer_came = after(links.across(outer_sum[1], 1), second_sum[1])
        feed_total, outer_total = total_of(feed_sum[0], feed_came), total_of(outer_sum[0], outer_came)
        first_came, second_came = after(first_came, feed_total), after(second_came, outer_total)
        first_sum, second_sum = combine(
            "first_sum_two",
            spots,
            [([(first_sum[0], first_came)], 0, 3), ([(second_sum[0], second_came)], 0, 2)],
            seq,
        )
        first_came, second_came = links.across(first_sum[1], 2), links.across(second_sum[1], 1)
        feed_share, outer_share = links.reduce_seq(feed_total), links.reduce_seq(outer_total)
        first = links.reduce_seq(total_of(first_sum[0], first_came))
        second = links.reduce_seq(total_of(second_sum[0], second_came))
        output_share = outer_share[outer_weight.shape[0] :]
        outer_share = outer_share[: outer_weight.shape[0]]
    else:
        feed_share = links.reduce_whole(keep_inner, send_inner)
        outer_share = links.reduce_whole(keep_outer, send_outer)
        output_share = links.reduce_whole(keep_output, send_output)
        first = links.reduce_whole(keep_first, send_first)
        second = links.reduce_whole(keep_second, send_second)
    tokens_grad = widen(tokens_grad)
    half = width + width // 2
    return (
        output.reshape(tokens.shape),
        tokens_grad.reshape(tokens.shape),
        jnp.concatenate([first[:, :half], second], axis=1),
        first[:, half],
        first[:, half + 1],
        output_share,
        first[:, half + 2],
        first[:, half + 3],
        first[:, half + 4],
        feed_share[:, :feed_width],
        feed_share[:, feed_width + 3 : feed_width + 3 + wide].reshape(-1),
        outer_share,
        feed_share[:, feed_width],
        feed_share[:, feed_width + 1],
        feed_share[:, feed_width + 2],
    )


def solution(mesh):
    split = P(AXES)
    split_rows = P(AXES, None)
    packed_rows = P("dp", "seq", None)
    return jax.shard_map(
        partial(shards, Links(mesh)),
        mesh=mesh,
        in_specs=(
            packed_rows,
            packed_rows,
            P("dp", None),
            split_rows,
            split,
            split,
            split_rows,
            split,
            split,
            split,
            split_rows,
            split,
            split_rows,
            split,
            split,
            split,
        ),
        out_specs=(
            packed_rows,
            packed_rows,
            split_rows,
            split,
            split,
            split_rows,
            split,
            split,
            split,
            split_rows,
            split,
            split_rows,
            split,
            split,
            split,
        ),
        check_vma=False,
    )
```

time: 491 us -> 400 us (0.81)
  waiting for transfers between devices: 167 us -> 110 us
  Pallas kernels: 129 us -> 178 us
  other arithmetic: 55 us -> 14.9 us
  starting transfers between devices: 101 us -> 63.3 us
  local copies, waits for them, and re-layouts: 35.4 us -> 18.5 us
  blocking collectives: 0 us -> 11.7 us
    ppermute x33 -> x0, waiting for transfers between devices: 133 us -> none  [along(): return lax.ppermute(value, AXES, pairs)]
    ppermute x33 -> x0, starting transfers between devices: 79.7 us -> none  [along(): return lax.ppermute(value, AXES, pairs)]
    all_to_all x0 -> x11, waiting for transfers between devices: none -> 60.9 us  [turn(): lax.all_to_all(blocks, 'seq', split_axis=0, concat_axis=0, tiled=True)]
    all_to_all x0 -> x11, starting transfers between devices: none -> 44.4 us  [turn(): lax.all_to_all(blocks, 'seq', split_axis=0, concat_axis=0, tiled=True)]
    pallas_call x1 -> x10, Pallas kernels: 13.7 us -> 56.7 us  [the longest x4 22.3 us: combine(): kernel(body, name, 0, 3 * sum((2 * math.prod(out.shape) for out in out_sh...]
    select_n x16 -> x0, other arithmetic: 20.2 us -> none  [gather_digit(): jnp.where(mine == 0, jnp.stack([held, other], axis=axis), jnp.stack([othe...]
    ppermute x24 -> x25, waiting for transfers between devices: 33.8 us -> 49.2 us  [across(): return lax.ppermute(value, AXES, pairs)]
    all_to_all x0 -> x1, blocking collectives: none -> 11.7 us  [turn(): lax.all_to_all(blocks, 'seq', split_axis=0, concat_axis=0, tiled=True)]
  transfers between devices with their start and end apart: 57 -> 36, of which waited for: 27 -> 19; matrix products, arithmetic and copies ran while one was open for 14% -> 4% of each run, Pallas kernels for 14% -> 41%
where the time goes in v3:
time: 400 us; the launch traced here: 397 us
  Pallas kernels  178 us (44%)
  waiting for transfers between devices  110 us (28%)
  starting transfers between devices  63.3 us (16%)
  local copies, waits for them, and re-layouts  18.5 us (5%)
  other arithmetic  14.9 us (4%)
  blocking collectives  11.7 us (3%)
    all_to_all x11, waiting for transfers between devices, turn(): lax.all_to_all(blocks, 'seq', split_axis=0, concat_axis=0, tiled=True)  60.9 us
    ppermute x25, waiting for transfers between devices, across(): return lax.ppermute(value, AXES, pairs)  49.2 us
    all_to_all x11, starting transfers between devices, turn(): lax.all_to_all(blocks, 'seq', split_axis=0, concat_axis=0, tiled=True)  44.4 us
    pallas_call x1, Pallas kernels, feed_back(): kernel(feed_back_body, 'feed_back', 8 * count * width * wide, 12 * count...  32.1 us
    pallas_call x1, Pallas kernels, feed(): kernel(feed_body, 'feed', 4 * count * width * wide, 12 * count * wide, gr...  24.2 us
    pallas_call x4, Pallas kernels, combine(): kernel(body, name, 0, 3 * sum((2 * math.prod(out.shape) for out in out_sh...  22.3 us
    pallas_call x1, Pallas kernels, attend_back(): kernel(attend_back_body, 'attend_back', rows * pairs * 16 * length * leng...  21.1 us
    pallas_call x1, Pallas kernels, attend(): kernel(attend_body, 'attend', rows * pairs * 16 * length * length * LANES...  19.3 us
  transfers between devices with their start and end apart: 36, of which 19 were waited for; matrix products, arithmetic and copies ran while one was open for 4% of the time, Pallas kernels for 41%

profile of v3, /device:TPU:0, one launch (start us, length us, event | category | flops | bytes accessed | tf_op | source)
XLA Modules:
  0.0 397.2 jit_solution(4124478139016529310)
XLA Ops:
  3.4 6.3 %all-to-all-start.1 = ((bf16[4,24,1536]{2,1,0:T(8,128)(2,1)}), bf16[4,24,1536]{2,1,0:T(8,128)(2,1)S(1)}, u32[]{:S(2)}, u32[]{:S(2)}) async-start(bf16[4,24,1536]{2,1,0:T(8,128)(2,1)} %broadcast_in_dim.13), calls=%async_computation.1 | async-start | bytes 589824 | tf_op jit(solution)/shard_map/all_to_all | solution.py:712
  9.9 9.4 %all-to-all-done.1.refs_2_ = bf16[4,24,1536]{2,1,0:T(8,128)(2,1)S(1)} async-done(((bf16[4,24,1536]{2,1,0:T(8,128)(2,1)}), bf16[4,24,1536]{2,1,0:T(8,128)(2,1)S(1)}, u32[]{:S(2)}, u32[]{:S(2)}) %all-to-all-start.1) | async-done | bytes 294944 | tf_op jit(solution)/shard_map/all_to_all | solution.py:712
  23.8 8.5 %all-to-all-done.refs_0_ = bf16[4,24,1664]{2,1,0:T(8,128)(2,1)S(1)} async-done(((bf16[4,24,1664]{2,1,0:T(8,128)(2,1)}), bf16[4,24,1664]{2,1,0:T(8,128)(2,1)S(1)}, u32[]{:S(2)}, u32[]{:S(2)}) %all-to-all-start) | async-done | bytes 319520 | tf_op jit(solution)/shard_map/all_to_all | solution.py:712
  40.2 10.2 %all-to-all-done.3.refs_2_ = bf16[4,96,768]{2,1,0:T(8,128)(2,1)S(1)} async-done(((bf16[4,96,768]{2,1,0:T(8,128)(2,1)}), bf16[4,96,768]{2,1,0:T(8,128)(2,1)S(1)}, u32[]{:S(2)}, u32[]{:S(2)}) %all-to-all-start.3) | async-done | bytes 589856 | tf_op jit(solution)/shard_map/all_to_all | solution.py:712
  63.0 11.5 %collective-permute-done.3.refs_3_ = bf16[2,4,24,1536]{3,2,1,0:T(8,128)(2,1)S(1)} collective-permute-done((bf16[2,4,24,1536]{3,2,1,0:T(8,128)(2,1)}, bf16[2,4,24,1536]{3,2,1,0:T(8,128)(2,1)S(1)}, u32[]{:S(2)}, u32[]{:S(2)}) %collective-permute-start.3) | collective-permute-done | bytes 589856 | tf_op jit(solution)/shard_map/ppermute | solution.py:729
  76.1 3.7 attention_two.1
  79.9 4.9 %all-to-all-start.4 = ((bf16[4,2,128,768]{3,2,1,0:T(8,128)(2,1)}), bf16[4,2,128,768]{3,2,1,0:T(8,128)(2,1)}, u32[]{:S(2)}, u32[]{:S(2)}) async-start(bf16[4,2,128,768]{3,2,1,0:T(8,128)(2,1)} %bitcast.80), calls=%async_computation.4 | async-start | bytes 3145728 | tf_op jit(solution)/shard_map/all_to_all | solution.py:712
  87.3 14.8 %collective-permute-done.5.refs_3_ = bf16[4,96,768]{2,1,0:T(8,128)(2,1)} collective-permute-done((bf16[4,96,768]{2,1,0:T(8,128)(2,1)}, bf16[4,96,768]{2,1,0:T(8,128)(2,1)}, u32[]{:S(2)}, u32[]{:S(2)}) %collective-permute-start.5) | collective-permute-done | bytes 589856 | tf_op jit(solution)/shard_map/ppermute | solution.py:729
  102.1 3.8 feed_one.1
  107.8 10.6 %all-to-all-done.4 = bf16[4,2,128,768]{3,2,1,0:T(8,128)(2,1)} async-done(((bf16[4,2,128,768]{3,2,1,0:T(8,128)(2,1)}), bf16[4,2,128,768]{3,2,1,0:T(8,128)(2,1)}, u32[]{:S(2)}, u32[]{:S(2)}) %all-to-all-start.4) | async-done | bytes 1572896 | tf_op jit(solution)/shard_map/all_to_all | solution.py:712
  119.4 8.0 %project.1 = (bf16[1024,2304]{1,0:T(8,128)(2,1)}, f32[8,768]{1,0:T(8,128)}) custom-call(s32[4]{0:T(128)} %pad_add_fusion.spots, bf16[1024,768]{1,0:T(8,128)(2,1)} %bitcast.13.tokens, bf16[4,96,1664]{2,1,0:T(8,128)(2,1)} %bitcast.84, bf16[4,96,1664]{2,1,0:T(8,128)(2,1)} %collective-permute-done.6.other_first.other_vectors, bf16[4,96,1536]{2,1,0:T(8,128)(2,1)} %bitcast.54, ...), custom_call_target="tpu_custom_call" | custom-call | flops 3623878656 | bytes 6291456 | tf_op jit(solution)/shard_map/project/pallas_call | solution.py:122
  127.4 19.3 %attend.1 = (bf16[4,2,128,768]{3,2,1,0:T(8,128)(2,1)}, bf16[2,12,512,512]{3,2,1,0:T(8,128)(2,1)}) custom-call(s32[4]{0:T(128)} %pad_add_fusion.spots, s32[8,4]{1,0:T(8,128)} %copy.44.lengths, bf16[4,2,128,2304]{3,2,1,0:T(8,128)(2,1)} %bitcast.48, bf16[4,2,128,2304]{3,2,1,0:T(8,128)(2,1)} %bitcast.49, bf16[4,2,128,2304]{3,2,1,0:T(8,128)(2,1)} %bitcast.50), custom_call_target="tpu_custom_call" | custom-call | flops 6442450944 | bytes 25165824 | tf_op jit(solution)/shard_map/attend/pallas_call | solution.py:180
  147.8 5.3 %feed_two.1 = (bf16[2,2,4,24,3200]{4,3,2,1,0:T(8,128)(2,1)}, bf16[2,2,4,96,768]{4,3,2,1,0:T(8,128)(2,1)}) custom-call(s32[4]{0:T(128)} %pad_add_fusion.spots, bf16[2,4,24,3200]{3,2,1,0:T(8,128)(2,1)} %get-tuple-element.104.refs_0_, bf16[2,4,24,3200]{3,2,1,0:T(8,128)(2,1)} %collective-permute-done.8.refs_1_, ...), custom_call_target="tpu_custom_call" | custom-call | bytes 9633792 | tf_op jit(solution)/shard_map/feed_two/pallas_call | solution.py:631
  157.2 6.5 %settle.1 = (f32[1024,768]{1,0:T(8,128)}, f32[1024,1]{1,0:T(8,128)}, bf16[1024,768]{1,0:T(8,128)(2,1)}) custom-call(s32[4]{0:T(128)} %pad_add_fusion.spots, bf16[1024,768]{1,0:T(8,128)(2,1)} %bitcast.66, bf16[4,96,1536]{2,1,0:T(8,128)(2,1)} %bitcast.55, bf16[4,96,1536]{2,1,0:T(8,128)(2,1)} %copy-done.1, bf16[1024,768]{1,0:T(8,128)(2,1)} %bitcast.13.tokens, ...), custom_call_target="tpu_custom_call" | custom-call | flops 1207959552 | bytes 7864320 | tf_op jit(solution)/shard_map/settle/pallas_call | solution.py:282
  163.7 24.2 %feed.1 = (bf16[1024,3072]{1,0:T(8,128)(2,1)}, bf16[1024,3072]{1,0:T(8,128)(2,1)}, f32[1024,768]{1,0:T(8,128)}, f32[1024,1]{1,0:T(8,128)}, f32[8,768]{1,0:T(8,128)}, /*index=5*/bf16[1024,768]{1,0:T(8,128)(2,1)}) custom-call(s32[4]{0:T(128)} %pad_add_fusion.spots, bf16[1024,768]{1,0:T(8,128)(2,1)} %get-tuple-element.115.low, bf16[4,96,3200]{2,1,0:T(8,128)(2,1)} %bitcast.88, ...), custom_call_target="tpu_custom_call" | custom-call | flops 9663676416 | bytes 37748736 | tf_op jit(solution)/shard_map/feed/pallas_call | solution.py:362
  187.9 6.7 %all-to-all-done.5 = bf16[4,2,128,768]{3,2,1,0:T(8,128)(2,1)S(1)} async-done(((bf16[4,2,128,768]{3,2,1,0:T(8,128)(2,1)}), bf16[4,2,128,768]{3,2,1,0:T(8,128)(2,1)S(1)}, u32[]{:S(2)}, u32[]{:S(2)}) %all-to-all-start.5) | async-done | bytes 1572896 | tf_op jit(solution)/shard_map/all_to_all | solution.py:712
  199.6 32.1 %feed_back.1 = (bf16[4,96,3200]{2,1,0:T(8,128)(2,1)}, bf16[4,96,3200]{2,1,0:T(8,128)(2,1)}, bf16[4,384,768]{2,1,0:T(8,128)(2,1)}, bf16[4,384,768]{2,1,0:T(8,128)(2,1)}, f32[1024,768]{1,0:T(8,128)}) custom-call(s32[4]{0:T(128)} %pad_add_fusion.spots, bf16[1024,768]{1,0:T(8,128)(2,1)} %bitcast.81, f32[1024,768]{1,0:T(8,128)} %get-tuple-element.123.normed_two, ...), custom_call_target="tpu_custom_call" | custom-call | flops 19327352832 | bytes 37748736 | tf_op jit(solution)/shard_map/feed_back/pallas_call | solution.py:445
  231.7 4.3 %all-to-all-done.6 = bf16[4,2,128,768]{3,2,1,0:T(8,128)(2,1)S(1)} async-done(((bf16[4,2,128,768]{3,2,1,0:T(8,128)(2,1)}), bf16[4,2,128,768]{3,2,1,0:T(8,128)(2,1)S(1)}, u32[]{:S(2)}, u32[]{:S(2)}) %all-to-all-start.6) | async-done | bytes 1572896 | tf_op jit(solution)/shard_map/all_to_all | solution.py:712
  236.5 9.7 %settle_back.1 = (f32[1024,768]{1,0:T(8,128)}, bf16[1024,768]{1,0:T(8,128)(2,1)}, bf16[4,96,768]{2,1,0:T(8,128)(2,1)}, bf16[4,96,768]{2,1,0:T(8,128)(2,1)}, f32[8,768]{1,0:T(8,128)}) custom-call(s32[4]{0:T(128)} %pad_add_fusion.spots, f32[1024,768]{1,0:T(8,128)} %get-tuple-element.133.hidden_grad, f32[1024,768]{1,0:T(8,128)} %get-tuple-element.116.normed_one.normed, ...), custom_call_target="tpu_custom_call" | custom-call | flops 2415919104 | bytes 12582912 | tf_op jit(solution)/shard_map/settle_back/pallas_call | solution.py:499
  250.7 7.8 %feed_sum_one.1 = (bf16[2,4,24,3200]{3,2,1,0:T(8,128)(2,1)}, bf16[2,4,24,3200]{3,2,1,0:T(8,128)(2,1)}, bf16[2,4,120,768]{3,2,1,0:T(8,128)(2,1)}, bf16[2,4,120,768]{3,2,1,0:T(8,128)(2,1)}) custom-call(s32[4]{0:T(128)} %pad_add_fusion.spots, bf16[2,2,4,24,3200]{4,3,2,1,0:T(8,128)(2,1)} %bitcast.59, bf16[2,2,4,24,3200]{4,3,2,1,0:T(8,128)(2,1)} %bitcast.61, ...), custom_call_target="tpu_custom_call" | custom-call | bytes 16220160 | tf_op jit(solution)/shard_map/feed_sum_one/pallas_call | solution.py:681
  260.8 21.1 %attend_back.1 = (bf16[4,2,128,2304]{3,2,1,0:T(8,128)(2,1)}, f32[2,1,2304]{2,1,0:T(1,128)}) custom-call(bf16[4,2,128,2304]{3,2,1,0:T(8,128)(2,1)} %bitcast.51, bf16[4,2,128,2304]{3,2,1,0:T(8,128)(2,1)} %bitcast.52, bf16[4,2,128,2304]{3,2,1,0:T(8,128)(2,1)} %bitcast.53, bf16[4,2,128,768]{3,2,1,0:T(8,128)(2,1)} %bitcast.79, ...), custom_call_target="tpu_custom_call" | custom-call | flops 6442450944 | bytes 25165824 | tf_op jit(solution)/shard_map/attend_back/pallas_call | solution.py:232
  281.9 10.0 %tokens_back.1 = bf16[1024,768]{1,0:T(8,128)(2,1)} custom-call(s32[4]{0:T(128)} %pad_add_fusion.spots, bf16[1024,2304]{1,0:T(8,128)(2,1)} %bitcast.69, bf16[4,96,1664]{2,1,0:T(8,128)(2,1)} %bitcast.86, bf16[4,96,1664]{2,1,0:T(8,128)(2,1)} %collective-permute-done.6.other_first.other_vectors, bf16[4,96,1536]{2,1,0:T(8,128)(2,1)} %bitcast.57, ...), custom_call_target="tpu_custom_call" | custom-call | flops 3623878656 | bytes 6291456 | tf_op jit(solution)/shard_map/tokens_back/pallas_call | solution.py:551
  295.5 5.4 %feed_sum_two.1 = (bf16[4,24,3200]{2,1,0:T(8,128)(2,1)}, bf16[4,24,3200]{2,1,0:T(8,128)(2,1)}, bf16[4,120,768]{2,1,0:T(8,128)(2,1)}, bf16[4,120,768]{2,1,0:T(8,128)(2,1)}) custom-call(s32[4]{0:T(128)} %pad_add_fusion.spots, bf16[2,4,24,3200]{3,2,1,0:T(8,128)(2,1)} %get-tuple-element.149.refs_0_.refs_2_, ...), custom_call_target="tpu_custom_call" | custom-call | bytes 8110080 | tf_op jit(solution)/shard_map/feed_sum_two/pallas_call | solution.py:681
  300.9 8.6 %weights_back.1 = (bf16[4,96,1280]{2,1,0:T(8,128)(2,1)}, bf16[4,96,1280]{2,1,0:T(8,128)(2,1)}, bf16[4,96,1152]{2,1,0:T(8,128)(2,1)}, bf16[4,96,1152]{2,1,0:T(8,128)(2,1)}) custom-call(s32[4]{0:T(128)} %pad_add_fusion.spots, bf16[1024,2304]{1,0:T(8,128)(2,1)} %bitcast.70, bf16[1024,768]{1,0:T(8,128)(2,1)} %bitcast.13.tokens, ...), custom_call_target="tpu_custom_call" | custom-call | flops 3623878656 | bytes 6291456 | tf_op jit(solution)/shard_map/weights_back/pallas_call | solution.py:604
  313.7 5.0 %first_sum_one.1 = (bf16[2,4,24,1280]{3,2,1,0:T(8,128)(2,1)}, bf16[2,4,24,1280]{3,2,1,0:T(8,128)(2,1)}, bf16[2,4,24,1152]{3,2,1,0:T(8,128)(2,1)}, bf16[2,4,24,1152]{3,2,1,0:T(8,128)(2,1)}) custom-call(s32[4]{0:T(128)} %pad_add_fusion.spots, bf16[2,2,4,24,1280]{4,3,2,1,0:T(8,128)(2,1)} %bitcast.71, bf16[2,2,4,24,1280]{4,3,2,1,0:T(8,128)(2,1)} %bitcast.35.refs_1_.refs_3_, ...), custom_call_target="tpu_custom_call" | custom-call | bytes 5603328 | tf_op jit(solution)/shard_map/first_sum_one/pallas_call | solution.py:681
  319.3 6.8 %collective-permute-done.20 = bf16[4,24,3200]{2,1,0:T(8,128)(2,1)} collective-permute-done((bf16[4,24,3200]{2,1,0:T(8,128)(2,1)}, bf16[4,24,3200]{2,1,0:T(8,128)(2,1)}, u32[]{:S(2)}, u32[]{:S(2)}) %collective-permute-start.20) | collective-permute-done | bytes 614432 | tf_op jit(solution)/shard_map/ppermute | solution.py:729
  332.5 4.2 %all-to-all-start.11 = ((bf16[4,24,3200]{2,1,0:T(8,128)(2,1)}), bf16[4,24,3200]{2,1,0:T(8,128)(2,1)}, u32[]{:S(2)}, u32[]{:S(2)}) async-start(bf16[4,24,3200]{2,1,0:T(8,128)(2,1)} %add_convert_fusion.1), calls=%async_computation.11 | async-start | bytes 1228800 | tf_op jit(solution)/shard_map/all_to_all | solution.py:712
  340.2 4.1 %first_sum_two.1 = (bf16[4,24,1280]{2,1,0:T(8,128)(2,1)}, bf16[4,24,1280]{2,1,0:T(8,128)(2,1)}, bf16[4,24,1152]{2,1,0:T(8,128)(2,1)}, bf16[4,24,1152]{2,1,0:T(8,128)(2,1)}) custom-call(s32[4]{0:T(128)} %pad_add_fusion.spots, bf16[2,4,24,1280]{3,2,1,0:T(8,128)(2,1)} %get-tuple-element.161.refs_0_.refs_2_, ...), custom_call_target="tpu_custom_call" | custom-call | bytes 2801664 | tf_op jit(solution)/shard_map/first_sum_two/pallas_call | solution.py:681
  344.9 5.8 %collective-permute-done.24 = bf16[4,24,1152]{2,1,0:T(8,128)(2,1)S(1)} collective-permute-done((bf16[4,24,1152]{2,1,0:T(8,128)(2,1)}, bf16[4,24,1152]{2,1,0:T(8,128)(2,1)S(1)}, u32[]{:S(2)}, u32[]{:S(2)}) %collective-permute-start.24) | collective-permute-done | bytes 221216 | tf_op jit(solution)/shard_map/ppermute | solution.py:729
  352.6 11.7 %all_to_all.60 = bf16[4,24,1152]{2,1,0:T(8,128)(2,1)S(1)} all-to-all(bf16[4,24,1152]{2,1,0:T(8,128)(2,1)} %add_convert_fusion.3), channel_id=1, replica_groups=mesh['dp'=8,'seq'=4] {'seq'}, dimensions={0} | all-to-all | bytes 442368 | tf_op jit(solution)/shard_map/all_to_all | solution.py:712
  364.3 4.2 %all-to-all-start.10 = ((bf16[4,120,768]{2,1,0:T(8,128)(2,1)}), bf16[4,120,768]{2,1,0:T(8,128)(2,1)}, u32[]{:S(2)}, u32[]{:S(2)}) async-start(bf16[4,120,768]{2,1,0:T(8,128)(2,1)} %add_convert_fusion), calls=%async_computation.10 | async-start | bytes 1474560 | tf_op jit(solution)/shard_map/all_to_all | solution.py:712
  378.3 6.2 %all-to-all-done.10 = bf16[4,120,768]{2,1,0:T(8,128)(2,1)} async-done(((bf16[4,120,768]{2,1,0:T(8,128)(2,1)}), bf16[4,120,768]{2,1,0:T(8,128)(2,1)}, u32[]{:S(2)}, u32[]{:S(2)}) %all-to-all-start.10) | async-done | bytes 737312 | tf_op jit(solution)/shard_map/all_to_all | solution.py:712
  (158 shorter events, 95.3 us)
Async XLA Ops:
  3.4 15.9 %all-to-all-start.1 = ((bf16[4,24,1536]{2,1,0:T(8,128)(2,1)}), bf16[4,24,1536]{2,1,0:T(8,128)(2,1)S(1)}, u32[]{:S(2)}, u32[]{:S(2)}) async-start(bf16[4,24,1536]{2,1,0:T(8,128)(2,1)} %broadcast_in_dim.13), calls=%async_computation.1 | async-start | bytes 589824 | tf_op jit(solution)/shard_map/all_to_all | solution.py:712
  20.1 12.1 %all-to-all-start = ((bf16[4,24,1664]{2,1,0:T(8,128)(2,1)}), bf16[4,24,1664]{2,1,0:T(8,128)(2,1)S(1)}, u32[]{:S(2)}, u32[]{:S(2)}) async-start(bf16[4,24,1664]{2,1,0:T(8,128)(2,1)} %broadcast_in_dim.12), calls=%async_computation | async-start | bytes 638976 | tf_op jit(solution)/shard_map/all_to_all | solution.py:712
  33.2 17.2 %all-to-all-start.3 = ((bf16[4,96,768]{2,1,0:T(8,128)(2,1)}), bf16[4,96,768]{2,1,0:T(8,128)(2,1)S(1)}, u32[]{:S(2)}, u32[]{:S(2)}) async-start(bf16[4,96,768]{2,1,0:T(8,128)(2,1)} %broadcast_in_dim.15), calls=%async_computation.3 | async-start | bytes 1179648 | tf_op jit(solution)/shard_map/all_to_all | solution.py:712
  37.1 18.4 %collective-permute-start.1 = (bf16[4,24,1536]{2,1,0:T(8,128)(2,1)S(1)}, bf16[4,24,1536]{2,1,0:T(8,128)(2,1)S(1)}, u32[]{:S(2)}, u32[]{:S(2)}) collective-permute-start(bf16[4,24,1536]{2,1,0:T(8,128)(2,1)S(1)} %all-to-all-done.1.refs_2_), channel_id=1, source_target_pairs={{0,16},{1,17},{2,18},{3,19},{4,20},{5,21},{6,22},{7,23},{8,24},{9,... | collective-permute-start | bytes 884744 | tf_op jit(solution)/shard_map/ppermute | solution.py:729
  38.7 16.8 %collective-permute-start = (bf16[4,24,1664]{2,1,0:T(8,128)(2,1)S(1)}, bf16[4,24,1664]{2,1,0:T(8,128)(2,1)S(1)}, u32[]{:S(2)}, u32[]{:S(2)}) collective-permute-start(bf16[4,24,1664]{2,1,0:T(8,128)(2,1)S(1)} %all-to-all-done.refs_0_), channel_id=1, source_target_pairs={{0,8},{1,9},{2,10},{3,11},{4,12},{5,13},{6,14},{7,15},{8,0},{9,1},... | collective-permute-start | bytes 958472 | tf_op jit(solution)/shard_map/ppermute | solution.py:729
  51.3 28.5 %all-to-all-start.2 = ((bf16[4,24,3200]{2,1,0:T(8,128)(2,1)}), bf16[4,24,3200]{2,1,0:T(8,128)(2,1)S(1)}, u32[]{:S(2)}, u32[]{:S(2)}) async-start(bf16[4,24,3200]{2,1,0:T(8,128)(2,1)} %broadcast_in_dim.14), calls=%async_computation.2 | async-start | bytes 1228800 | tf_op jit(solution)/shard_map/all_to_all | solution.py:712
  59.9 14.5 %collective-permute-start.2 = (bf16[2,4,24,1664]{3,2,1,0:T(8,128)(2,1)}, bf16[2,4,24,1664]{3,2,1,0:T(8,128)(2,1)S(1)}, u32[]{:S(2)}, u32[]{:S(2)}) collective-permute-start(bf16[2,4,24,1664]{3,2,1,0:T(8,128)(2,1)} %get-tuple-element.96.refs_0_), channel_id=1, source_target_pairs={{0,16},{1,17},{2,18},{3,19},{4,20},{5,21},{6,22},{7,23},{8,24},{9,... | collective-permute-start | bytes 1916936 | tf_op jit(solution)/shard_map/ppermute | solution.py:729
  61.5 12.9 %collective-permute-start.3 = (bf16[2,4,24,1536]{3,2,1,0:T(8,128)(2,1)}, bf16[2,4,24,1536]{3,2,1,0:T(8,128)(2,1)S(1)}, u32[]{:S(2)}, u32[]{:S(2)}) collective-permute-start(bf16[2,4,24,1536]{3,2,1,0:T(8,128)(2,1)} %get-tuple-element.97.refs_2_), channel_id=1, source_target_pairs={{0,8},{1,9},{2,10},{3,11},{4,12},{5,13},{6,14},{7,15},{8,0},{9,1},... | collective-permute-start | bytes 1769480 | tf_op jit(solution)/shard_map/ppermute | solution.py:729
  79.9 38.5 %all-to-all-start.4 = ((bf16[4,2,128,768]{3,2,1,0:T(8,128)(2,1)}), bf16[4,2,128,768]{3,2,1,0:T(8,128)(2,1)}, u32[]{:S(2)}, u32[]{:S(2)}) async-start(bf16[4,2,128,768]{3,2,1,0:T(8,128)(2,1)} %bitcast.80), calls=%async_computation.4 | async-start | bytes 3145728 | tf_op jit(solution)/shard_map/all_to_all | solution.py:712
  84.8 33.6 %collective-permute-start.6 = (bf16[4,96,1664]{2,1,0:T(8,128)(2,1)}, bf16[4,96,1664]{2,1,0:T(8,128)(2,1)}, u32[]{:S(2)}, u32[]{:S(2)}) collective-permute-start(bf16[4,96,1664]{2,1,0:T(8,128)(2,1)} %bitcast.83), channel_id=1, source_target_pairs={{0,4},{1,5},{2,6},{3,7},{4,0},{5,1},{6,2},{7,3},{8,12},{9,13},{10,... | collective-permute-start | bytes 3833864 | tf_op jit(solution)/shard_map/ppermute | solution.py:729
  84.8 33.6 %collective-permute-start.7 = (bf16[4,96,1536]{2,1,0:T(8,128)(2,1)S(1)}, bf16[4,96,1536]{2,1,0:T(8,128)(2,1)S(1)}, u32[]{:S(2)}, u32[]{:S(2)}) collective-permute-start(bf16[4,96,1536]{2,1,0:T(8,128)(2,1)S(1)} %bitcast.58), channel_id=1, source_target_pairs={{0,4},{1,5},{2,6},{3,7},{4,0},{5,1},{6,2},{7,3},{8,12},{9,13},{10,... | collective-permute-start | bytes 3538952 | tf_op jit(solution)/shard_map/ppermute | solution.py:729
  85.3 16.8 %collective-permute-start.4 = (bf16[4,24,3200]{2,1,0:T(8,128)(2,1)S(1)}, bf16[4,24,3200]{2,1,0:T(8,128)(2,1)}, u32[]{:S(2)}, u32[]{:S(2)}) collective-permute-start(bf16[4,24,3200]{2,1,0:T(8,128)(2,1)S(1)} %all-to-all-done.2.refs_0_), channel_id=1, source_target_pairs={{0,8},{1,9},{2,10},{3,11},{4,12},{5,13},{6,14},{7,15},{8,0},{9,1},... | collective-permute-start | bytes 1843208 | tf_op jit(solution)/shard_map/ppermute | solution.py:729
  86.8 15.3 %collective-permute-start.5 = (bf16[4,96,768]{2,1,0:T(8,128)(2,1)}, bf16[4,96,768]{2,1,0:T(8,128)(2,1)}, u32[]{:S(2)}, u32[]{:S(2)}) collective-permute-start(bf16[4,96,768]{2,1,0:T(8,128)(2,1)} %copy-done.5), channel_id=1, source_target_pairs={{0,16},{1,17},{2,18},{3,19},{4,20},{5,21},{6,22},{7,23},{8,24},{9,... | collective-permute-start | bytes 1769480 | tf_op jit(solution)/shard_map/ppermute | solution.py:729
  106.0 40.8 %collective-permute-start.8 = (bf16[2,4,24,3200]{3,2,1,0:T(8,128)(2,1)}, bf16[2,4,24,3200]{3,2,1,0:T(8,128)(2,1)}, u32[]{:S(2)}, u32[]{:S(2)}) collective-permute-start(bf16[2,4,24,3200]{3,2,1,0:T(8,128)(2,1)} %get-tuple-element.104.refs_0_), channel_id=1, source_target_pairs={{0,16},{1,17},{2,18},{3,19},{4,20},{5,21},{6,22},{7,23},{8,24},{9,... | collective-permute-start | bytes 3686408 | tf_op jit(solution)/shard_map/ppermute | solution.py:729
  106.5 40.2 %collective-permute-start.9 = (bf16[2,4,96,768]{3,2,1,0:T(8,128)(2,1)}, bf16[2,4,96,768]{3,2,1,0:T(8,128)(2,1)S(1)}, u32[]{:S(2)}, u32[]{:S(2)}) collective-permute-start(bf16[2,4,96,768]{3,2,1,0:T(8,128)(2,1)} %get-tuple-element.105.refs_2_), channel_id=1, source_target_pairs={{0,8},{1,9},{2,10},{3,11},{4,12},{5,13},{6,14},{7,15},{8,0},{9,1},... | collective-permute-start | bytes 3538952 | tf_op jit(solution)/shard_map/ppermute | solution.py:729
  153.0 10.6 %collective-permute-start.10 = (bf16[4,96,3200]{2,1,0:T(8,128)(2,1)}, bf16[4,96,3200]{2,1,0:T(8,128)(2,1)}, u32[]{:S(2)}, u32[]{:S(2)}) collective-permute-start(bf16[4,96,3200]{2,1,0:T(8,128)(2,1)} %bitcast.87), channel_id=1, source_target_pairs={{0,4},{1,5},{2,6},{3,7},{4,0},{5,1},{6,2},{7,3},{8,12},{9,13},{10,... | collective-permute-start | bytes 7372808 | tf_op jit(solution)/shard_map/ppermute | solution.py:729
  153.1 10.5 %collective-permute-start.11 = (bf16[4,384,768]{2,1,0:T(8,128)(2,1)}, bf16[4,384,768]{2,1,0:T(8,128)(2,1)}, u32[]{:S(2)}, u32[]{:S(2)}) collective-permute-start(bf16[4,384,768]{2,1,0:T(8,128)(2,1)} %bitcast.91), channel_id=1, source_target_pairs={{0,4},{1,5},{2,6},{3,7},{4,0},{5,1},{6,2},{7,3},{8,12},{9,13},{10,... | collective-permute-start | bytes 7077896 | tf_op jit(solution)/shard_map/ppermute | solution.py:729
  153.6 41.0 %all-to-all-start.5 = ((bf16[4,2,128,768]{3,2,1,0:T(8,128)(2,1)}), bf16[4,2,128,768]{3,2,1,0:T(8,128)(2,1)S(1)}, u32[]{:S(2)}, u32[]{:S(2)}) async-start(bf16[4,2,128,768]{3,2,1,0:T(8,128)(2,1)} %bitcast.20), calls=%async_computation.5 | async-start | bytes 3145728 | tf_op jit(solution)/shard_map/all_to_all | solution.py:712
  195.8 40.2 %all-to-all-start.6 = ((bf16[4,2,128,768]{3,2,1,0:T(8,128)(2,1)}), bf16[4,2,128,768]{3,2,1,0:T(8,128)(2,1)S(1)}, u32[]{:S(2)}, u32[]{:S(2)}) async-start(bf16[4,2,128,768]{3,2,1,0:T(8,128)(2,1)} %bitcast.82), calls=%async_computation.6 | async-start | bytes 3145728 | tf_op jit(solution)/shard_map/all_to_all | solution.py:712
  236.0 12.5 %collective-permute-start.12 = (bf16[4,96,3200]{2,1,0:T(8,128)(2,1)}, bf16[4,96,3200]{2,1,0:T(8,128)(2,1)S(1)}, u32[]{:S(2)}, u32[]{:S(2)}) collective-permute-start(bf16[4,96,3200]{2,1,0:T(8,128)(2,1)} %get-tuple-element.130), channel_id=1, source_target_pairs={{0,4},{1,5},{2,6},{3,7},{4,0},{5,1},{6,2},{7,3},{8,12},{9,13},{10,... | collective-permute-start | bytes 7372808 | tf_op jit(solution)/shard_map/ppermute | solution.py:729
  236.0 12.5 %collective-permute-start.13 = (bf16[4,384,768]{2,1,0:T(8,128)(2,1)}, bf16[4,384,768]{2,1,0:T(8,128)(2,1)}, u32[]{:S(2)}, u32[]{:S(2)}) collective-permute-start(bf16[4,384,768]{2,1,0:T(8,128)(2,1)} %get-tuple-element.132), channel_id=1, source_target_pairs={{0,4},{1,5},{2,6},{3,7},{4,0},{5,1},{6,2},{7,3},{8,12},{9,13},{10,... | collective-permute-start | bytes 7077896 | tf_op jit(solution)/shard_map/ppermute | solution.py:729
  258.5 37.1 %collective-permute-start.16 = (bf16[2,4,120,768]{3,2,1,0:T(8,128)(2,1)}, bf16[2,4,120,768]{3,2,1,0:T(8,128)(2,1)}, u32[]{:S(2)}, u32[]{:S(2)}) collective-permute-start(bf16[2,4,120,768]{3,2,1,0:T(8,128)(2,1)} %get-tuple-element.144), channel_id=1, source_target_pairs={{0,16},{1,17},{2,18},{3,19},{4,20},{5,21},{6,22},{7,23},{8,24},{9,... | collective-permute-start | bytes 4423688 | tf_op jit(solution)/shard_map/ppermute | solution.py:729
  259.3 36.2 %collective-permute-start.15 = (bf16[2,4,24,3200]{3,2,1,0:T(8,128)(2,1)}, bf16[2,4,24,3200]{3,2,1,0:T(8,128)(2,1)}, u32[]{:S(2)}, u32[]{:S(2)}) collective-permute-start(bf16[2,4,24,3200]{3,2,1,0:T(8,128)(2,1)} %get-tuple-element.143), channel_id=1, source_target_pairs={{0,8},{1,9},{2,10},{3,11},{4,12},{5,13},{6,14},{7,15},{8,0},{9,1},... | collective-permute-start | bytes 3686408 | tf_op jit(solution)/shard_map/ppermute | solution.py:729
  291.9 40.5 %all-to-all-start.7 = ((bf16[4,2,128,768]{3,2,1,0:T(8,128)(2,1)}), bf16[4,2,128,768]{3,2,1,0:T(8,128)(2,1)S(1)}, u32[]{:S(2)}, u32[]{:S(2)}) async-start(bf16[4,2,128,768]{3,2,1,0:T(8,128)(2,1)} %bitcast.68), calls=%async_computation.7 | async-start | bytes 3145728 | tf_op jit(solution)/shard_map/all_to_all | solution.py:712
  310.0 16.1 %collective-permute-start.20 = (bf16[4,24,3200]{2,1,0:T(8,128)(2,1)}, bf16[4,24,3200]{2,1,0:T(8,128)(2,1)}, u32[]{:S(2)}, u32[]{:S(2)}) collective-permute-start(bf16[4,24,3200]{2,1,0:T(8,128)(2,1)} %get-tuple-element.153), channel_id=1, source_target_pairs={{0,16},{1,17},{2,18},{3,19},{4,20},{5,21},{6,22},{7,23},{8,24},{9,... | collective-permute-start | bytes 1843208 | tf_op jit(solution)/shard_map/ppermute | solution.py:729
  311.2 19.7 %collective-permute-start.22 = (bf16[4,120,768]{2,1,0:T(8,128)(2,1)}, bf16[4,120,768]{2,1,0:T(8,128)(2,1)}, u32[]{:S(2)}, u32[]{:S(2)}) collective-permute-start(bf16[4,120,768]{2,1,0:T(8,128)(2,1)} %get-tuple-element.154), channel_id=1, source_target_pairs={{0,8},{1,9},{2,10},{3,11},{4,12},{5,13},{6,14},{7,15},{8,0},{9,1},... | collective-permute-start | bytes 2211848 | tf_op jit(solution)/shard_map/ppermute | solution.py:729
  318.7 21.5 %collective-permute-start.19 = (bf16[2,4,24,1280]{3,2,1,0:T(8,128)(2,1)}, bf16[2,4,24,1280]{3,2,1,0:T(8,128)(2,1)}, u32[]{:S(2)}, u32[]{:S(2)}) collective-permute-start(bf16[2,4,24,1280]{3,2,1,0:T(8,128)(2,1)} %get-tuple-element.162), channel_id=1, source_target_pairs={{0,8},{1,9},{2,10},{3,11},{4,12},{5,13},{6,14},{7,15},{8,0},{9,1},... | collective-permute-start | bytes 1474568 | tf_op jit(solution)/shard_map/ppermute | solution.py:729
  326.1 12.9 %collective-permute-start.21 = (bf16[2,4,24,1152]{3,2,1,0:T(8,128)(2,1)}, bf16[2,4,24,1152]{3,2,1,0:T(8,128)(2,1)}, u32[]{:S(2)}, u32[]{:S(2)}) collective-permute-start(bf16[2,4,24,1152]{3,2,1,0:T(8,128)(2,1)} %get-tuple-element.167), channel_id=1, source_target_pairs={{0,16},{1,17},{2,18},{3,19},{4,20},{5,21},{6,22},{7,23},{8,24},{9,... | collective-permute-start | bytes 1327112 | tf_op jit(solution)/shard_map/ppermute | solution.py:729
  332.5 20.2 %all-to-all-start.11 = ((bf16[4,24,3200]{2,1,0:T(8,128)(2,1)}), bf16[4,24,3200]{2,1,0:T(8,128)(2,1)}, u32[]{:S(2)}, u32[]{:S(2)}) async-start(bf16[4,24,3200]{2,1,0:T(8,128)(2,1)} %add_convert_fusion.1), calls=%async_computation.11 | async-start | bytes 1228800 | tf_op jit(solution)/shard_map/all_to_all | solution.py:712
  364.3 20.2 %all-to-all-start.10 = ((bf16[4,120,768]{2,1,0:T(8,128)(2,1)}), bf16[4,120,768]{2,1,0:T(8,128)(2,1)}, u32[]{:S(2)}, u32[]{:S(2)}) async-start(bf16[4,120,768]{2,1,0:T(8,128)(2,1)} %add_convert_fusion), calls=%async_computation.10 | async-start | bytes 1474560 | tf_op jit(solution)/shard_map/all_to_all | solution.py:712
  368.5 6.5 %collective-permute-start.23 = (bf16[4,24,1280]{2,1,0:T(8,128)(2,1)}, bf16[4,24,1280]{2,1,0:T(8,128)(2,1)S(1)}, u32[]{:S(2)}, u32[]{:S(2)}) collective-permute-start(bf16[4,24,1280]{2,1,0:T(8,128)(2,1)} %get-tuple-element.172), channel_id=1, source_target_pairs={{0,16},{1,17},{2,18},{3,19},{4,20},{5,21},{6,22},{7,23},{8,24},{9,... | collective-permute-start | bytes 737288 | tf_op jit(solution)/shard_map/ppermute | solution.py:729
  384.5 10.0 %all-to-all-start.8 = ((bf16[4,24,1280]{2,1,0:T(8,128)(2,1)}), bf16[4,24,1280]{2,1,0:T(8,128)(2,1)S(1)}, u32[]{:S(2)}, u32[]{:S(2)}) async-start(bf16[4,24,1280]{2,1,0:T(8,128)(2,1)} %add_convert_fusion.2), calls=%async_computation.8 | async-start | bytes 491520 | tf_op jit(solution)/shard_map/all_to_all | solution.py:712
  (31 other events, 283.1 us)

commit v4 on v3

v4 whole, which is shorter than its diff:
```python
from functools import partial
import math

import jax
import jax.numpy as jnp
from jax import lax
from jax.experimental import pallas as pl
from jax.experimental.pallas import tpu as pltpu
from jax.sharding import PartitionSpec as P

HEAD_DIM = 64
LANES = 128
PARTS = 4
EPSILON = 1e-06
AXES = ("dp", "seq")
BF16, F32 = jnp.bfloat16, jnp.float32

NN = (((1,), (0,)), ((), ()))
NT = (((1,), (1,)), ((), ()))
TN = (((0,), (0,)), ((), ()))


def narrow(value):
    return value.astype(BF16)


def widen(value):
    return value.astype(F32)


def after(value, *others):
    return lax.optimization_barrier((value,) + others)[0]


def dot(left, right, dims=NN):
    return lax.dot_general(left, right, dims, preferred_element_type=F32)


def shape(dims, dtype=BF16):
    return jax.ShapeDtypeStruct(dims, dtype)


def like(value):
    return jax.ShapeDtypeStruct(value.shape, value.dtype)


def fixed(dims, *index):
    at = tuple(index) or (0,) * len(dims)
    return pl.BlockSpec(dims, lambda *_: at)


SCALARS = pl.BlockSpec(memory_space=pltpu.SMEM)
ANYWHERE = pl.BlockSpec(memory_space=pl.ANY)


def row_sum(value):
    return jnp.sum(value, axis=0, keepdims=True)


def kernel(body, name, flops, touched, **options):
    return pl.pallas_call(
        body,
        name=name,
        compiler_params=pltpu.CompilerParams(vmem_limit_bytes=60 << 20),
        cost_estimate=pl.CostEstimate(flops=flops, bytes_accessed=touched, transcendentals=0),
        **options,
    )


def unite(target, own, other, spots):
    side, chip = spots[1], spots[2]
    rows = own[0].shape[0]
    for index in range(PARTS):
        for half, value in ((side, own[index]), (1 - side, other[index])):
            start = pl.multiple_of((2 * (chip ^ index) + half) * rows, rows)
            target[pl.ds(start, rows), :] = value[...]


def divide(source, keep, send, side, columns):
    count, rows = keep.shape[:2]
    for index in range(count):
        for half, target in ((side, keep), (1 - side, send)):
            start = pl.multiple_of((2 * index + half) * rows, rows)
            target[index, :, columns] = source[pl.ds(start, rows), :]


def gathered_specs(gathered, columns, index):
    block = (gathered[0].shape[0], columns)
    return [pl.BlockSpec(block, lambda *at: (0, index(*at)))] * len(gathered)


def as_columns(rows):
    width = rows[0].shape[1]
    padding = jnp.zeros((LANES - len(rows), width), F32)
    return jnp.concatenate(list(rows) + [padding], axis=0).T


def prepare_attention_body(packed_weight, output_weight, *rest):
    *vectors, out = rest
    seq, small, _ = out.shape
    lane = lax.broadcasted_iota(jnp.int32, (1, LANES), 1)
    block, column = 0.0, 0
    for vector in vectors:
        per = vector.shape[1] // small
        for part in range(per):
            value = jnp.where(spread_mask(small, per, part), vector[...], 0.0)
            value = jnp.sum(value, axis=1, keepdims=True)
            block = block + jnp.where(lane == column, value, 0.0)
            column += 1
    shard = jnp.concatenate(
        [narrow(packed_weight[...]), narrow(output_weight[...]), narrow(block)], axis=1
    )
    for index in range(seq):
        out[index] = shard


def prepare_attention(seq, packed_weight, output_weight, vectors):
    small, wide = packed_weight.shape
    vectors = [vector.reshape(1, -1) for vector in vectors]
    return kernel(
        prepare_attention_body,
        "prepare_attention",
        0,
        16 * small * wide,
        out_shape=shape((seq, small, wide + LANES + output_weight.shape[1])),
    )(packed_weight, output_weight, *vectors)


def prepare_feed_body(inner_weight, outer_weight, out):
    seq, small, _ = out.shape
    wide, width = inner_weight.shape[1], outer_weight.shape[1]
    out[0, :, :wide] = narrow(inner_weight[...])
    for index in range(outer_weight.shape[0] // small):
        start = wide + index * width
        block = outer_weight[index * small : (index + 1) * small]
        out[0, :, start : start + width] = narrow(block)
    for index in range(1, seq):
        out[index] = out[0]


def prepare_feed(seq, inner_weight, outer_weight):
    small, wide = inner_weight.shape
    return kernel(
        prepare_feed_body,
        "prepare_feed",
        0,
        16 * small * wide,
        out_shape=shape((seq, small, 2 * wide)),
    )(inner_weight, outer_weight)


def project_body(spots, tokens, *refs):
    weights, columns = refs[: 2 * PARTS], refs[2 * PARTS : 4 * PARTS]
    packed, flat, weight, rows, vectors = refs[4 * PARTS :]
    part = pl.program_id(0)
    seq, count, places, width = tokens.shape
    length = seq * places

    @pl.when(part == 0)
    def _():
        unite(vectors, columns[:PARTS], columns[PARTS:], spots)
        rows[...] = widen(vectors[...]).T[:8]
        for row in range(count):
            flat[row * length : (row + 1) * length] = tokens[:, row].reshape(length, width)

    unite(weight, weights[:PARTS], weights[PARTS:], spots)
    query, value = rows[0:1], rows[1:2]
    bias = jnp.where(part == 0, query, jnp.where(part == 2, value, jnp.zeros_like(query)))
    result = narrow(dot(flat[...], weight[...]) + bias)
    packed[...] = result.reshape(packed.shape)


def project(spots, tokens, gathered):
    seq, rows, places, width = tokens.shape
    length = seq * places
    return kernel(
        project_body,
        "project",
        6 * rows * length * width * width,
        8 * rows * length * width,
        grid=(3,),
        in_specs=[SCALARS, fixed(tokens.shape)]
        + gathered_specs(gathered, width, lambda i: i)
        + gathered_specs(gathered, LANES, lambda i: 4 * width // LANES),
        out_specs=[
            pl.BlockSpec((rows, length, width), lambda i: (0, 0, i)),
            fixed((rows * length, width)),
            pl.BlockSpec((width, width), lambda i: (0, i)),
            fixed((8, width)),
            fixed((width, LANES)),
        ],
        out_shape=[
            shape((rows, length, 3 * width)),
            shape((rows * length, width)),
            shape((width, 3 * width)),
            shape((8, width), F32),
            shape((width, LANES)),
        ],
    )(spots, tokens, *gathered, *gathered)


def pair_labels(places, lengths, row):
    label, bound = jnp.zeros_like(places), 0
    for pair in range(lengths.shape[1] - 1):
        bound = bound + lengths[row, pair]
        label = label + (places >= bound).astype(jnp.int32)
    return label


def attend_body(spots, lengths, query, key, value, context, probs, bias):
    length = bias.shape[0]

    @pl.when(pl.program_id(1) == 0)
    def _():
        at = spots[0] * pl.num_programs(0) + pl.program_id(0)
        down = pair_labels(lax.broadcasted_iota(jnp.int32, (length, 1), 0), lengths, at)
        along = pair_labels(lax.broadcasted_iota(jnp.int32, (1, length), 1), lengths, at)
        bias[...] = jnp.where(down == along, 0.0, -1e30)

    lane = lax.broadcasted_iota(jnp.int32, (1, LANES), 1)
    keys, values = key[0], value[0]
    queries = query[0] * BF16(HEAD_DIM**-0.5)
    parts = []
    for head in range(2):
        mine = (lane >= HEAD_DIM) == bool(head)
        scores = dot(jnp.where(mine, queries, BF16(0)), keys, NT) + bias[...]
        raised = jnp.exp(scores - jnp.max(scores, axis=-1, keepdims=True))
        total = jnp.sum(raised, axis=-1, keepdims=True)
        low = narrow(raised * (1.0 / total))
        probs[0, head] = low
        parts.append(dot(low, values))
    context[0] = narrow(jnp.where(lane < HEAD_DIM, parts[0], parts[1]))


def head_pair(length, offset):
    return pl.BlockSpec((1, length, LANES), lambda r, p: (r, 0, offset + p))


def attend(spots, lengths, packed):
    rows, length, wide = packed.shape
    pairs = wide // 3 // LANES
    return kernel(
        attend_body,
        "attend",
        rows * pairs * 16 * length * length * LANES,
        rows * pairs * 8 * length * length,
        grid=(rows, pairs),
        in_specs=[SCALARS, SCALARS] + [head_pair(length, part * pairs) for part in range(3)],
        out_specs=[
            head_pair(length, 0),
            pl.BlockSpec((1, 2, length, length), lambda r, p: (r, p, 0, 0)),
        ],
        out_shape=[shape((rows, length, wide // 3)), shape((rows, 2 * pairs, length, length))],
        scratch_shapes=[pltpu.VMEM((length, length), F32)],
    )(spots, lengths, packed, packed, packed)


def attend_back_body(query, key, value, upstream, probs, grads, sums):
    pair, pairs = pl.program_id(1), pl.num_programs(1)
    lane = lax.broadcasted_iota(jnp.int32, (1, LANES), 1)
    scale = BF16(HEAD_DIM**-0.5)
    queries, keys, values, up = query[0] * scale, key[0], value[0], upstream[0]
    scaled_keys = keys * scale
    query_parts, key_grad, value_grad = [], 0.0, 0.0
    for head in range(2):
        mine = (lane >= HEAD_DIM) == bool(head)
        up_mine = jnp.where(mine, up, BF16(0))
        queries_mine = jnp.where(mine, queries, BF16(0))
        low = probs[0, head]
        prob_grad = dot(up_mine, values, NT)
        softmaxed = widen(low)
        weighted = jnp.sum(softmaxed * prob_grad, axis=-1, keepdims=True)
        score_grad = narrow(softmaxed * (prob_grad - weighted))
        query_parts.append(dot(score_grad, scaled_keys))
        key_grad = key_grad + dot(queries_mine, score_grad, TN)
        value_grad = value_grad + dot(up_mine, low, TN)
    query_grad = jnp.where(lane < HEAD_DIM, query_parts[0], query_parts[1])
    for part, grad in enumerate((query_grad, key_grad.T, value_grad.T)):
        at = pl.ds(pl.multiple_of((part * pairs + pair) * LANES, LANES), LANES)
        rounded = narrow(grad)
        grads[0, :, at] = rounded
        sums[0, :, at] = row_sum(widen(rounded))


def attend_back(packed, probs, upstream):
    rows, length, wide = packed.shape
    pairs = wide // 3 // LANES
    return kernel(
        attend_back_body,
        "attend_back",
        rows * pairs * 16 * length * length * LANES,
        rows * pairs * 8 * length * length,
        grid=(rows, pairs),
        in_specs=[head_pair(length, part * pairs) for part in range(3)]
        + [
            head_pair(length, 0),
            pl.BlockSpec((1, 2, length, length), lambda r, p: (r, p, 0, 0)),
        ],
        out_specs=[
            pl.BlockSpec((1, length, wide), lambda r, p: (r, 0, 0)),
            pl.BlockSpec((1, 1, wide), lambda r, p: (r, 0, 0)),
        ],
        out_shape=[shape(packed.shape), shape((rows, 1, wide), F32)],
    )(packed, packed, packed, upstream, probs)


def normed_of(summed):
    centred = summed - jnp.mean(summed, axis=-1, keepdims=True)
    variance = jnp.mean(centred * centred, axis=-1, keepdims=True)
    inverse = lax.rsqrt(variance + EPSILON)
    return centred * inverse, inverse


def norm_back(upstream, normed, inverse, gain):
    scaled = upstream * gain
    first_mean = jnp.mean(scaled, axis=-1, keepdims=True)
    second_mean = jnp.mean(scaled * normed, axis=-1, keepdims=True)
    return inverse * (scaled - first_mean - normed * second_mean)


def settle_body(spots, context, tokens, rows, *refs):
    parts, (normed, inverse, low, weight) = refs[: 2 * PARTS], refs[2 * PARTS :]

    @pl.when(pl.program_id(0) == 0)
    def _():
        unite(weight, parts[:PARTS], parts[PARTS:], spots)

    summed = widen(tokens[...]) + dot(context[...], weight[...]) + rows[2:3]
    normed[...], inverse[...] = normed_of(summed)
    low[...] = narrow(normed[...] * rows[3:4] + rows[4:5])


def settle(spots, context, tokens, rows, gathered):
    count, width = context.shape
    block = count // 4
    tall = pl.BlockSpec((block, width), lambda i: (i, 0))
    return kernel(
        settle_body,
        "settle",
        2 * count * width * width,
        10 * count * width,
        grid=(4,),
        in_specs=[SCALARS, tall, tall, fixed(rows.shape)]
        + gathered_specs(gathered, width, lambda i: 3),
        out_specs=[tall, pl.BlockSpec((block, 1), lambda i: (i, 0)), tall, fixed((width, width))],
        out_shape=[
            shape((count, width), F32),
            shape((count, 1), F32),
            shape((count, width)),
            shape((width, width)),
        ],
    )(spots, context, tokens, rows, *gathered)


def spread_mask(rows, per, column):
    down = lax.broadcasted_iota(jnp.int32, (rows, rows * per), 0)
    along = lax.broadcasted_iota(jnp.int32, (rows, rows * per), 1)
    return along == down * per + column


def stack_blocks(part):
    seq, rows, wide = part.shape
    width = wide // PARTS
    blocks = [
        widen(part[place, :, index * width : (index + 1) * width])
        for place in range(seq)
        for index in range(PARTS)
    ]
    return narrow(jnp.concatenate(blocks, axis=0))


def feed_body(spots, low, vectors, normed_one, rows, *refs):
    inners, outers = refs[: 2 * PARTS], refs[2 * PARTS : 4 * PARTS]
    (
        active, slope, normed_two, inverse_two, output, inner_weight, outer_weight, branch,
    ) = refs[4 * PARTS :]
    step, steps = pl.program_id(0), pl.num_programs(0)
    unite(inner_weight, inners[:PARTS], inners[PARTS:], spots)
    for index in range(PARTS):

        @pl.when(step == spots[2] ^ index)
        def _():
            half = outer_weight.shape[0] // 2
            for side, part in ((spots[1], outers[index]), (1 - spots[1], outers[PARTS + index])):
                start = pl.multiple_of(side * half, half)
                outer_weight[pl.ds(start, half), :] = stack_blocks(part)

    block = inner_weight.shape[-1]
    share_rows = vectors.shape[0] // PARTS
    per = block // share_rows
    own_rows = vectors[pl.ds(pl.multiple_of(step * share_rows, share_rows), share_rows), :]
    bias = 0.0
    for column in range(per):
        value = widen(own_rows[:, 8 + column : 9 + column])
        bias = bias + jnp.where(spread_mask(share_rows, per, column), value, 0.0)
    inner = dot(low[...], inner_weight[...]) + row_sum(bias)
    share = 0.5 * (1.0 + lax.erf(inner * math.sqrt(0.5)))
    raised = jnp.exp(-0.5 * inner * inner) * (1.0 / math.sqrt(2.0 * math.pi))
    acted = narrow(inner * share)
    active[...] = acted
    slope[...] = narrow(share + inner * raised)
    part = dot(acted, outer_weight[...])

    @pl.when(step == 0)
    def _():
        branch[...] = part

    @pl.when(step > 0)
    def _():
        branch[...] += part

    @pl.when(step == steps - 1)
    def _():
        hidden = normed_one[...] * rows[3:4] + rows[4:5]
        normed_two[...], inverse_two[...] = normed_of(hidden + branch[...] + rows[5:6])
        result = narrow(normed_two[...] * rows[6:7] + rows[7:8])
        seq, count, places, width = output.shape
        result = result.reshape(count, seq, places, width)
        for row in range(count):
            output[:, row] = result[row]


def feed(spots, low, vectors, normed_one, rows, gathered, dims):
    count, width = low.shape
    wide = gathered[0].shape[1] // 2
    block = wide // PARTS
    deep = [part.reshape(dims[0], -1, 2 * wide) for part in gathered]
    all_of = fixed((count, width))
    across = pl.BlockSpec((count, block), lambda f: (0, f))
    outer = pl.BlockSpec(
        deep[0].shape[:2] + (wide,), lambda f: (0, 0, 1), pipeline_mode=pl.Buffered(1)
    )
    return kernel(
        feed_body,
        "feed",
        4 * count * width * wide,
        12 * count * wide,
        grid=(PARTS,),
        in_specs=[SCALARS, all_of, fixed(vectors.shape), all_of, fixed(rows.shape)]
        + gathered_specs(gathered, block, lambda f: f)
        + [outer] * len(deep),
        out_specs=[
            across,
            across,
            all_of,
            fixed((count, 1)),
            fixed(dims),
            pl.BlockSpec((width, block), lambda f: (0, f)),
            pl.BlockSpec((block, width), lambda f: (f, 0)),
        ],
        out_shape=[
            shape((count, wide)),
            shape((count, wide)),
            shape((count, width), F32),
            shape((count, 1), F32),
            shape(dims),
            shape((width, wide)),
            shape((wide, width)),
        ],
        scratch_shapes=[pltpu.VMEM((count, width), F32)],
    )(spots, low, vectors, normed_one, rows, *gathered, *deep)


def feed_back_body(
    spots, cotangent, normed_two, inverse_two, rows_one, low, inner_weight, outer_weight, active, slope,
    keep_inner, send_inner, keep_outer, send_outer, hidden_grad,
    up, made, columns,
):
    step, steps, side = pl.program_id(0), pl.num_programs(0), spots[1]
    block = inner_weight.shape[-1]

    @pl.when(step == 0)
    def _():
        rows, width = cotangent.shape[1], cotangent.shape[-1]
        upstream = jnp.concatenate(
            [widen(cotangent[:, row]).reshape(-1, width) for row in range(rows)], axis=0
        )
        normed = normed_two[...]
        hidden_grad[...] = norm_back(upstream, normed, inverse_two[...], rows_one[6:7])
        up[...] = narrow(hidden_grad[...])
        columns[...] = as_columns(
            (row_sum(widen(up[...])), row_sum(upstream * normed), row_sum(upstream))
        )

    inner_grad = narrow(dot(up[...], outer_weight[...], NT) * widen(slope[...]))
    made[...] = narrow(dot(low[...], inner_grad, TN))
    at = pl.ds(pl.multiple_of(step * block, block), block)
    divide(made, keep_inner, send_inner, side, at)
    hidden_grad[...] += dot(inner_grad, inner_weight[...], NT)
    made[...] = narrow(dot(active[...], up[...], TN))
    divide(made, keep_outer, send_outer, side, slice(None))

    bias = row_sum(widen(inner_grad))
    share_rows = columns.shape[0] // PARTS
    per = block // share_rows
    lane = lax.broadcasted_iota(jnp.int32, (1, LANES), 1)
    total = 0.0
    for column in range(per):
        value = jnp.sum(
            jnp.where(spread_mask(share_rows, per, column), bias, 0.0), axis=1, keepdims=True
        )
        total = total + jnp.where(lane == 3 + column, value, 0.0)
    columns[pl.ds(pl.multiple_of(step * share_rows, share_rows), share_rows), :] += total

    @pl.when(step == steps - 1)
    def _():
        made[:, :LANES] = narrow(columns[...])
        count, rows, wide = keep_inner.shape
        for index in range(count):
            for half, target in ((side, keep_inner), (1 - side, send_inner)):
                start = pl.multiple_of((2 * index + half) * rows, rows)
                target[index, :, wide - LANES :] = made[pl.ds(start, rows), :LANES]


def feed_back(spots, cotangent, normed_two, inverse_two, rows, low, inner, outer, active, slope):
    count, width = low.shape
    wide = inner.shape[1]
    block = wide // PARTS
    all_of = fixed((count, width))
    across = pl.BlockSpec((count, block), lambda f: (0, f))
    first = (PARTS, width // PARTS // 2, wide + LANES)
    second = (PARTS, block // 2, width)
    down = pl.BlockSpec((1,) + second[1:], lambda f: (f, 0, 0))
    return kernel(
        feed_back_body,
        "feed_back",
        8 * count * width * wide,
        12 * count * wide,
        grid=(PARTS,),
        in_specs=[SCALARS, fixed(cotangent.shape), all_of, fixed((count, 1)), fixed(rows.shape), all_of]
        + [
            pl.BlockSpec((width, block), lambda f: (0, f)),
            pl.BlockSpec((block, width), lambda f: (f, 0)),
            across,
            across,
        ],
        out_specs=[fixed(first), fixed(first), down, down, all_of],
        out_shape=[shape(first), shape(first), shape(second), shape(second)]
        + [shape((count, width), F32)],
        scratch_shapes=[
            pltpu.VMEM((count, width), BF16),
            pltpu.VMEM((width, block), BF16),
            pltpu.VMEM((width, LANES), F32),
        ],
    )(spots, cotangent, normed_two, inverse_two, rows, low, inner, outer, active, slope)


def settle_back_body(
    spots, hidden_grad, normed, inverse, rows, context, weight,
    first_up, context_grad, keep, send, sums, total, made,
):
    step, steps = pl.program_id(0), pl.num_programs(0)

    @pl.when(step == 0)
    def _():
        sums[...] = jnp.zeros_like(sums)
        total[...] = jnp.zeros_like(total)

    upstream = hidden_grad[...]
    up = norm_back(upstream, normed[...], inverse[...], rows[3:4])
    first_up[...] = up
    low = narrow(up)
    context_grad[...] = narrow(dot(low, weight[...], NT))
    total[...] += dot(context[...], low, TN)
    sums[0:1] += row_sum(widen(low))
    sums[1:2] += row_sum(upstream * normed[...])
    sums[2:3] += row_sum(upstream)

    @pl.when(step == steps - 1)
    def _():
        made[...] = narrow(total[...])
        divide(made, keep, send, spots[1], slice(None))


def settle_back(spots, hidden_grad, normed, inverse, rows, context, weight):
    count, width = context.shape
    block = count // 4
    tall = pl.BlockSpec((block, width), lambda i: (i, 0))
    dims = (PARTS, width // PARTS // 2, width)
    return kernel(
        settle_back_body,
        "settle_back",
        4 * count * width * width,
        16 * count * width,
        grid=(4,),
        in_specs=[SCALARS, tall, tall, pl.BlockSpec((block, 1), lambda i: (i, 0))]
        + [fixed(rows.shape), tall, fixed((width, width))],
        out_specs=[tall, tall, fixed(dims), fixed(dims), fixed((8, width))],
        out_shape=[
            shape((count, width), F32),
            shape((count, width)),
            shape(dims),
            shape(dims),
            shape((8, width), F32),
        ],
        scratch_shapes=[pltpu.VMEM((width, width), F32), pltpu.VMEM((width, width), BF16)],
    )(spots, hidden_grad, normed, inverse, rows, context, weight)


def tokens_back_body(packed_grad, weight, first_up, grad, total):
    part = pl.program_id(0)
    added = dot(packed_grad[...], weight[...], NT)

    @pl.when(part == 0)
    def _():
        total[...] = first_up[...] + added

    @pl.when(part == 1)
    def _():
        total[...] += added

    @pl.when(part == 2)
    def _():
        seq, rows, places, width = grad.shape
        result = narrow(total[...] + added).reshape(rows, seq, places, width)
        for row in range(rows):
            grad[:, row] = result[row]


def tokens_back(packed_grad, weight, first_up, dims):
    count, width = first_up.shape
    return kernel(
        tokens_back_body,
        "tokens_back",
        6 * count * width * width,
        8 * count * width,
        grid=(3,),
        in_specs=[
            pl.BlockSpec((count, width), lambda i: (0, i)),
            pl.BlockSpec((width, width), lambda i: (0, i)),
            fixed((count, width)),
        ],
        out_specs=fixed(dims),
        out_shape=shape(dims),
        scratch_shapes=[pltpu.VMEM((count, width), F32)],
    )(packed_grad, weight, first_up)


def weights_back_body(spots, packed_grad, tokens, packed_sums, sums, keep, send, made):
    part, side = pl.program_id(0), spots[1]
    width = tokens.shape[1]
    made[...] = narrow(dot(tokens[...], packed_grad[...], TN))
    divide(made, keep, send, side, pl.ds(pl.multiple_of(part * width, width), width))

    @pl.when(part == 2)
    def _():
        packed = jnp.sum(packed_sums[...], axis=0)
        made[:, :LANES] = narrow(
            as_columns(
                (packed[:, :width], packed[:, 2 * width :], sums[0:1], sums[1:2], sums[2:3])
            )
        )
        divide(made.at[:, :LANES], keep, send, side, slice(3 * width, 3 * width + LANES))


def weights_back(spots, packed_grad, tokens, packed_sums, sums):
    count, width = tokens.shape
    dims = (PARTS, width // PARTS // 2, 3 * width + LANES)
    return kernel(
        weights_back_body,
        "weights_back",
        6 * count * width * width,
        8 * count * width,
        grid=(3,),
        in_specs=[SCALARS, pl.BlockSpec((count, width), lambda i: (0, i)), fixed(tokens.shape)]
        + [fixed(packed_sums.shape), fixed(sums.shape)],
        out_specs=[fixed(dims), fixed(dims)],
        out_shape=[shape(dims), shape(dims)],
        scratch_shapes=[pltpu.VMEM((width, width), BF16)],
    )(spots, packed_grad, tokens, packed_sums, sums)


def side_by_side(out, start, total):
    small, width = out.shape[0], total.shape[1]
    for height in range(0, total.shape[0], small):
        out[:, start : start + width] = narrow(total[height : height + small])
        start += width
    return start


def chip_sums(name, spots, pairs, seq, small):
    operands, in_specs = [], []
    wide = sum(kept.shape[1] // (seq * small) * kept.shape[2] for kept, _ in pairs)
    for kept, came in pairs:
        height = kept.shape[1] // seq
        for part in range(PARTS):
            block = pl.BlockSpec(
                (None, None, height, kept.shape[2]),
                lambda i, spots, part=part: (spots[2] ^ part, i, 0, 0),
            )
            for value in (kept, came):
                operands.append(value.reshape(PARTS, seq, height, value.shape[2]))
                in_specs.append(block)

    def body(spots, *refs):
        ins, outs = refs[: len(operands)], refs[len(operands) :]
        for part, out in enumerate(outs):
            start = 0
            for pair in range(len(pairs)):
                at = 2 * (pair * PARTS + part)
                start = side_by_side(out, start, widen(ins[at][...]) + widen(ins[at + 1][...]))

    return kernel(
        body,
        name,
        0,
        6 * PARTS * seq * small * wide,
        grid_spec=pltpu.PrefetchScalarGridSpec(
            num_scalar_prefetch=1,
            grid=(seq,),
            in_specs=in_specs,
            out_specs=[pl.BlockSpec((None, small, wide), lambda i, spots: (i, 0, 0))] * PARTS,
        ),
        out_shape=[shape((seq, small, wide))] * PARTS,
    )(spots, *operands)


def total_body(*refs):
    total = widen(refs[0][...])
    for ref in refs[1:-1]:
        total = total + widen(ref[...])
    refs[-1][...] = narrow(total)


def total_of(name, values, flops=0):
    seq, small, wide = values[0].shape
    block = pl.BlockSpec((None, small, wide), lambda i: (i, 0, 0))
    return kernel(
        total_body,
        name,
        flops,
        2 * (len(values) + 1) * seq * small * wide,
        grid=(seq,),
        in_specs=[block] * len(values),
        out_specs=block,
        out_shape=shape(values[0].shape),
    )(*values)


def finish_body(vectors, blocks, came, *outs):
    seq, small, wide = came.shape
    total = widen(came[0])
    for index in range(1, seq):
        total = total + widen(came[index])
    start = 0
    for out, (count, width) in zip(outs, blocks):
        for index in range(count):
            out[index * small : (index + 1) * small] = total[:, start : start + width]
            start += width
    at = wide - LANES
    for out, (column, per) in zip(outs[len(blocks) :], vectors):
        line = 0.0
        for part in range(per):
            value = total[:, at + column + part : at + column + part + 1]
            line = line + jnp.where(spread_mask(small, per, part), value, 0.0)
        out[...] = row_sum(line)


def finish(name, came, blocks, vectors):
    seq, small, wide = came.shape
    return kernel(
        partial(finish_body, vectors, blocks),
        name,
        0,
        4 * seq * small * wide,
        out_shape=[shape((count * small, width), F32) for count, width in blocks]
        + [shape((1, small * per), F32) for _, per in vectors],
    )(came)


def block_at(blocks, index, axis=0):
    return lax.dynamic_index_in_dim(blocks, index, axis, keepdims=False)


class Links:
    def __init__(self, mesh):
        self.dp, self.seq = mesh.shape["dp"], mesh.shape["seq"]
        self.bits = self.dp.bit_length() - 1
        assert self.dp == 1 << self.bits
        self.direct = self.dp == 2 * PARTS

    def across(self, value, flip):
        pairs = [
            (d * self.seq + s, (d ^ flip) * self.seq + s)
            for d in range(self.dp)
            for s in range(self.seq)
        ]
        return lax.ppermute(value, AXES, pairs)

    def digit(self, bit):
        return (lax.axis_index("dp") >> bit) & 1

    def spots(self):
        place, dp = lax.axis_index("seq"), lax.axis_index("dp")
        side, chip = (dp & 1, dp >> 1) if self.direct else (0 * dp, 0 * dp)
        return jnp.stack([place, side, chip]).astype(jnp.int32)

    def turn(self, blocks):
        return lax.all_to_all(blocks, "seq", split_axis=0, concat_axis=0, tiled=True)

    def spread(self, held):
        return [held] + [self.across(held, 2 * part) for part in range(1, PARTS)]

    def swap(self, parts):
        parts = [part.reshape(-1, part.shape[-1]) for part in parts]
        return parts + [self.across(part, 1) for part in parts]

    def gather_whole(self, held):
        done = []
        for bit in range(self.bits):
            other, mine = self.across(held, 1 << bit), self.digit(bit)
            held = jnp.where(mine == 0, jnp.stack([held, other]), jnp.stack([other, held]))
        return held.reshape(self.dp * self.seq, *held.shape[self.bits + 1 :])

    def cut(self, whole):
        whole = whole.reshape(PARTS, 2, -1, whole.shape[-1])
        return [whole[part, side] for side in range(2) for part in range(PARTS)]

    def reduce_whole(self, keep, send):
        rows = keep.shape[0] * keep.shape[1] * 2 // (self.dp * self.seq)
        whole = jnp.stack([keep, send], axis=1)
        held = whole.reshape((2,) * self.bits + (self.seq, rows, keep.shape[-1]))
        for bit in reversed(range(self.bits)):
            mine = self.digit(bit)
            other = self.across(block_at(held, 1 - mine), 1 << bit)
            held = narrow(widen(block_at(held, mine)) + widen(other))
        return held


def shards(
    links,
    tokens,
    cotangent,
    lengths,
    packed_weight,
    query_bias,
    value_bias,
    output_weight,
    output_bias,
    first_gain,
    first_shift,
    inner_weight,
    inner_bias,
    outer_weight,
    outer_bias,
    second_gain,
    second_shift,
):
    row_count, places, width = tokens.shape
    seq, direct = links.seq, links.direct
    rows = row_count // seq
    dims = (seq, rows, places, width)
    small, tall = packed_weight.shape[0], outer_weight.shape[0]
    wide = inner_weight.shape[1]
    per = wide // width
    spots = links.spots()

    vectors = (
        query_bias, value_bias, output_bias, first_gain, first_shift,
        outer_bias, second_gain, second_shift, inner_bias,
    )
    held = links.turn(prepare_attention(seq, packed_weight, output_weight, vectors))
    feed_held = links.turn(after(prepare_feed(seq, inner_weight, outer_weight), held))
    if direct:
        held = links.spread(held)
        came = links.turn(after(tokens.reshape(dims), feed_held, *held))
        gathered = links.swap(held)
        feed_held = links.spread(feed_held)
    else:
        came = links.turn(after(tokens.reshape(dims), feed_held))
        gathered = links.cut(links.gather_whole(held))
        whole = links.gather_whole(feed_held)
        inner, outer = whole[..., :wide], whole[..., wide:]
        outer = outer.reshape(-1, small, per, width).swapaxes(1, 2)
        outer = outer.reshape(2 * PARTS * seq, per, -1, width).swapaxes(1, 2)
        inner, outer = inner.reshape(width, wide), outer.reshape(width, wide)
        feed_gathered = links.cut(jnp.concatenate([inner, outer], axis=1))
    cotangent_mine = links.turn(after(cotangent.reshape(dims), came))
    packed, flat, packed_whole, rows_one, vectors = project(spots, came, gathered)
    context, probs = attend(spots, lengths, packed)
    context = context.reshape(-1, width)
    if direct:
        feed_held = [feed_held[0]] + [after(value, context) for value in feed_held[1:]]
        context = after(context, *feed_held)
        feed_gathered = links.swap(feed_held)
    normed_one, inverse_one, low, output_whole = settle(spots, context, flat, rows_one, gathered)
    active, slope, normed_two, inverse_two, output, inner_whole, outer_whole = feed(
        spots, low, vectors, normed_one, rows_one, feed_gathered, dims
    )
    cotangent_mine = after(cotangent_mine, slope)
    output = after(output, cotangent_mine)
    cotangent_mine = after(cotangent_mine, output)
    keep_inner, send_inner, keep_outer, send_outer, hidden_grad = feed_back(
        spots,
        cotangent_mine,
        normed_two,
        inverse_two,
        rows_one,
        low,
        inner_whole,
        outer_whole,
        active,
        slope,
    )
    output = after(links.turn(output), hidden_grad)
    send_inner, send_outer = after(send_inner, output), after(send_outer, output)
    hidden_grad = after(hidden_grad, send_inner, send_outer)
    first_up, context_grad, keep_output, send_output, sums = settle_back(
        spots, hidden_grad, normed_one, inverse_one, rows_one, context, output_whole
    )
    if direct:
        inner_came = after(links.across(send_inner, 1), sums)
        outer_came = after(links.across(send_outer, 1), sums)
        output_came = links.across(send_output, 1)
        pairs = [(keep_outer, outer_came), (keep_output, output_came), (keep_inner, inner_came)]
        feed_sums = list(chip_sums("feed_chip_sums", spots, pairs, seq, small))
        context_grad = after(context_grad, *feed_sums[1:])
        feed_sums[1:] = [links.across(feed_sums[part], 2 * part) for part in range(1, PARTS)]
    packed_grad, packed_sums = attend_back(
        packed, probs, context_grad.reshape(rows, seq * places, width)
    )
    packed_grad = packed_grad.reshape(-1, 3 * width)
    grad = tokens_back(packed_grad, packed_whole, first_up, dims)
    tokens_grad = links.turn(grad)
    packed_grad = after(packed_grad, grad)
    keep, send = weights_back(spots, packed_grad, flat, packed_sums, sums)
    if direct:
        feed_sums[1:] = [after(value, keep) for value in feed_sums[1:]]
        feed_total = total_of("feed_total", feed_sums, 10**12)
        came = after(links.across(send, 1), feed_total)
        attention_sums = list(
            chip_sums("attention_chip_sums", spots, [(keep, came)], seq, small)
        )
        feed_total = after(feed_total, tokens_grad, *attention_sums[1:])
        attention_sums[1:] = [
            links.across(attention_sums[part], 2 * part) for part in range(1, PARTS)
        ]
        attention_total = total_of("attention_total", attention_sums)
    else:
        reduced = [
            links.reduce_whole(*pair)
            for pair in ((keep_outer, send_outer), (keep_output, send_output), (keep_inner, send_inner))
        ]
        reduced[0] = reduced[0].reshape(seq, per, small, width).swapaxes(1, 2)
        reduced[0] = reduced[0].reshape(seq, small, per * width)
        feed_total = jnp.concatenate(reduced, axis=2)
        attention_total = links.reduce_whole(keep, send)
    feed_total = links.turn(feed_total)
    attention_total = links.turn(after(attention_total, feed_total))
    (
        outer_grad, output_grad, inner_grad,
        outer_bias_grad, second_gain_grad, second_shift_grad, inner_bias_grad,
    ) = finish(
        "finish_feed",
        feed_total,
        [(per, width), (1, width), (1, wide)],
        [(0, 1), (1, 1), (2, 1), (3, per)],
    )
    (
        packed_weight_grad,
        query_bias_grad, value_bias_grad, output_bias_grad, first_gain_grad, first_shift_grad,
    ) = finish(
        "finish_attention", attention_total, [(1, 3 * width)], [(i, 1) for i in range(5)]
    )
    tokens_grad = widen(tokens_grad)
    return (
        output.reshape(tokens.shape),
        tokens_grad.reshape(tokens.shape),
        packed_weight_grad,
        query_bias_grad.reshape(-1),
        value_bias_grad.reshape(-1),
        output_grad,
        output_bias_grad.reshape(-1),
        first_gain_grad.reshape(-1),
        first_shift_grad.reshape(-1),
        inner_grad,
        inner_bias_grad.reshape(-1),
        outer_grad,
        outer_bias_grad.reshape(-1),
        second_gain_grad.reshape(-1),
        second_shift_grad.reshape(-1),
    )


def solution(mesh):
    split = P(AXES)
    split_rows = P(AXES, None)
    packed_rows = P("dp", "seq", None)
    return jax.shard_map(
        partial(shards, Links(mesh)),
        mesh=mesh,
        in_specs=(
            packed_rows,
            packed_rows,
            P("dp", None),
            split_rows,
            split,
            split,
            split_rows,
            split,
            split,
            split,
            split_rows,
            split,
            split_rows,
            split,
            split,
            split,
        ),
        out_specs=(
            packed_rows,
            packed_rows,
            split_rows,
            split,
            split,
            split_rows,
            split,
            split,
            split,
            split_rows,
            split,
            split_rows,
            split,
            split,
            split,
        ),
        check_vma=False,
    )
```

time: 400 us -> 364 us (0.910)
  waiting for transfers between devices: 110 us -> 125 us
  blocking collectives: 11.7 us -> 0 us
  starting transfers between devices: 63.3 us -> 52.1 us
  other arithmetic: 14.9 us -> 3.94 us
  Pallas kernels: 178 us -> 170 us
  local copies, waits for them, and re-layouts: 18.5 us -> 10.5 us
    ppermute x25 -> x24, waiting for transfers between devices: 49.2 us -> 62.3 us  [across(): return lax.ppermute(value, AXES, pairs)]
    all_to_all x1 -> x0, blocking collectives: 11.7 us -> none  [turn(): lax.all_to_all(blocks, 'seq', split_axis=0, concat_axis=0, tiled=True)]
    all_to_all x11 -> x8, starting transfers between devices: 44.4 us -> 34.5 us  [turn(): lax.all_to_all(blocks, 'seq', split_axis=0, concat_axis=0, tiled=True)]
    pallas_call x9, Pallas kernels: 46.1 us -> 37.3 us  [the longest x2 12.6 us: chip_sums(): kernel(body, name, 0, 6 * PARTS * seq * small * wide, grid_spec=pltpu.Pre...]
    convert_element_type x8 -> x0, other arithmetic: 7.99 us -> none  [narrow(): return value.astype(BF16)]
    all_to_all x11 -> x8, waiting for transfers between devices: 60.9 us -> 62.6 us  [turn(): lax.all_to_all(blocks, 'seq', split_axis=0, concat_axis=0, tiled=True)]
    ppermute x25 -> x24, starting transfers between devices: 18.9 us -> 17.7 us  [across(): return lax.ppermute(value, AXES, pairs)]
    unnamed x58 -> x46, local copies, waits for them, and re-layouts: 10.6 us -> 10.5 us
  transfers between devices with their start and end apart: 36 -> 32, of which waited for: 19 -> 12; matrix products, arithmetic and copies ran while one was open for 4% -> 1% of each run, Pallas kernels for 41% -> 44%
where the time goes in v4:
time: 364 us; the launch traced here: 362 us
  Pallas kernels  170 us (47%)
  waiting for transfers between devices  125 us (34%)
  starting transfers between devices  52.1 us (14%)
  local copies, waits for them, and re-layouts  10.5 us (3%)
  other arithmetic  3.94 us (1%)
    all_to_all x8, waiting for transfers between devices, turn(): lax.all_to_all(blocks, 'seq', split_axis=0, concat_axis=0, tiled=True)  62.6 us
    ppermute x24, waiting for transfers between devices, across(): return lax.ppermute(value, AXES, pairs)  62.3 us
    all_to_all x8, starting transfers between devices, turn(): lax.all_to_all(blocks, 'seq', split_axis=0, concat_axis=0, tiled=True)  34.5 us
    pallas_call x1, Pallas kernels, feed_back(): kernel(feed_back_body, 'feed_back', 8 * count * width * wide, 12 * count...  32.3 us
    pallas_call x1, Pallas kernels, feed(): kernel(feed_body, 'feed', 4 * count * width * wide, 12 * count * wide, gr...  26.4 us
    pallas_call x1, Pallas kernels, attend_back(): kernel(attend_back_body, 'attend_back', rows * pairs * 16 * length * leng...  21 us
    pallas_call x1, Pallas kernels, attend(): kernel(attend_body, 'attend', rows * pairs * 16 * length * length * LANES...  18.7 us
    ppermute x24, starting transfers between devices, across(): return lax.ppermute(value, AXES, pairs)  17.7 us
  transfers between devices with their start and end apart: 32, of which 12 were waited for; matrix products, arithmetic and copies ran while one was open for 1% of the time, Pallas kernels for 44%

profile of v4, /device:TPU:0, one launch (start us, length us, event | category | flops | bytes accessed | tf_op | source)
XLA Modules:
  0.0 362.3 jit_solution(7654764785420129994)
XLA Ops:
  2.6 6.3 %all-to-all-start = ((bf16[4,24,3200]{2,1,0:T(8,128)(2,1)}), bf16[4,24,3200]{2,1,0:T(8,128)(2,1)S(1)}, u32[]{:S(2)}, u32[]{:S(2)}) async-start(bf16[4,24,3200]{2,1,0:T(8,128)(2,1)} %prepare_attention.1), calls=%async_computation | async-start | bytes 1228800 | tf_op jit(solution)/shard_map/all_to_all | solution.py:799
  11.1 14.3 %all-to-all-done = bf16[4,24,3200]{2,1,0:T(8,128)(2,1)S(1)} async-done(((bf16[4,24,3200]{2,1,0:T(8,128)(2,1)}), bf16[4,24,3200]{2,1,0:T(8,128)(2,1)S(1)}, u32[]{:S(2)}, u32[]{:S(2)}) %all-to-all-start) | async-done | bytes 614432 | tf_op jit(solution)/shard_map/all_to_all | solution.py:799
  25.4 3.5 all-to-all-start.1
  32.5 14.2 %collective-permute-done.2 = bf16[4,24,3200]{2,1,0:T(8,128)(2,1)S(1)} collective-permute-done((bf16[4,24,3200]{2,1,0:T(8,128)(2,1)S(1)}, bf16[4,24,3200]{2,1,0:T(8,128)(2,1)S(1)}, u32[]{:S(2)}, u32[]{:S(2)}) %collective-permute-start.2) | collective-permute-done | bytes 614432 | tf_op jit(solution)/shard_map/ppermute | solution.py:788
  46.7 11.2 %collective-permute-done.1 = bf16[4,24,3200]{2,1,0:T(8,128)(2,1)S(1)} collective-permute-done((bf16[4,24,3200]{2,1,0:T(8,128)(2,1)S(1)}, bf16[4,24,3200]{2,1,0:T(8,128)(2,1)S(1)}, u32[]{:S(2)}, u32[]{:S(2)}) %collective-permute-start.1) | collective-permute-done | bytes 614432 | tf_op jit(solution)/shard_map/ppermute | solution.py:788
  58.7 4.7 %all-to-all-start.2 = ((bf16[4,2,128,768]{3,2,1,0:T(8,128)(2,1)}), bf16[4,2,128,768]{3,2,1,0:T(8,128)(2,1)S(1)}, u32[]{:S(2)}, u32[]{:S(2)}) async-start(bf16[4,2,128,768]{3,2,1,0:T(8,128)(2,1)} %bitcast.3), calls=%async_computation.2 | async-start | bytes 3145728 | tf_op jit(solution)/shard_map/all_to_all | solution.py:799
  70.9 29.8 %all-to-all-done.2.tokens = bf16[4,2,128,768]{3,2,1,0:T(8,128)(2,1)S(1)} async-done(((bf16[4,2,128,768]{3,2,1,0:T(8,128)(2,1)}), bf16[4,2,128,768]{3,2,1,0:T(8,128)(2,1)S(1)}, u32[]{:S(2)}, u32[]{:S(2)}) %all-to-all-start.2) | async-done | bytes 1572896 | tf_op jit(solution)/shard_map/all_to_all | solution.py:799
  101.8 3.6 all-to-all-start.3
  105.5 8.3 %project.1 = (bf16[2,512,2304]{2,1,0:T(8,128)(2,1)}, bf16[1024,768]{1,0:T(8,128)(2,1)}, bf16[768,2304]{1,0:T(8,128)(2,1)}, f32[8,768]{1,0:T(8,128)}, bf16[768,128]{1,0:T(8,128)(2,1)}) custom-call(s32[3]{0:T(128)} %pad_add_fusion.spots, bf16[4,2,128,768]{3,2,1,0:T(8,128)(2,1)} %copy-done.8, bf16[96,3200]{1,0:T(8,128)(2,1)} %bitcast.78, ...), custom_call_target="tpu_custom_call" | custom-call | flops 3623878656 | bytes 6291456 | tf_op jit(solution)/shard_map/project/pallas_call | solution.py:176
  113.8 18.7 %attend.1 = (bf16[2,512,768]{2,1,0:T(8,128)(2,1)}, bf16[2,12,512,512]{3,2,1,0:T(8,128)(2,1)}) custom-call(s32[3]{0:T(128)} %pad_add_fusion.spots, s32[8,4]{1,0:T(8,128)} %copy.31.lengths, bf16[2,512,2304]{2,1,0:T(8,128)(2,1)} %get-tuple-element.94.query.key.value, bf16[2,512,2304]{2,1,0:T(8,128)(2,1)} %get-tuple-element.94.query.key.value, ...), custom_call_target="tpu_custom_call" | custom-call | flops 6442450944 | bytes 25165824 | tf_op jit(solution)/shard_map/attend/pallas_call | solution.py:242
  133.6 6.6 %settle.1 = (f32[1024,768]{1,0:T(8,128)}, f32[1024,1]{1,0:T(8,128)}, bf16[1024,768]{1,0:T(8,128)(2,1)}, bf16[768,768]{1,0:T(8,128)(2,1)}) custom-call(s32[3]{0:T(128)} %pad_add_fusion.spots, bf16[1024,768]{1,0:T(8,128)(2,1)} %bitcast.75, bf16[1024,768]{1,0:T(8,128)(2,1)} %get-tuple-element.100.tokens, f32[8,768]{1,0:T(8,128)} %get-tuple-element.101.rows.rows_one, ...), custom_call_target="tpu_custom_call" | custom-call | flops 1207959552 | bytes 7864320 | tf_op jit(solution)/shard_map/settle/pallas_call | solution.py:337
  140.3 26.4 %feed.1 = (bf16[1024,3072]{1,0:T(8,128)(2,1)}, bf16[1024,3072]{1,0:T(8,128)(2,1)}, f32[1024,768]{1,0:T(8,128)}, f32[1024,1]{1,0:T(8,128)}, bf16[4,2,128,768]{3,2...) custom-call(s32[3]{0:T(128)} %pad_add_fusion.spots, bf16[1024,768]{1,0:T(8,128)(2,1)} %get-tuple-element.102.low, ...), custom_call_target="tpu_custom_call" | custom-call | flops 9663676416 | bytes 37748736 | tf_op jit(solution)/shard_map/feed/pallas_call | solution.py:433
  167.8 5.0 %all-to-all-start.4 = ((bf16[4,2,128,768]{3,2,1,0:T(8,128)(2,1)}), bf16[4,2,128,768]{3,2,1,0:T(8,128)(2,1)S(1)}, u32[]{:S(2)}, u32[]{:S(2)}) async-start(bf16[4,2,128,768]{3,2,1,0:T(8,128)(2,1)} %get-tuple-element.109), calls=%async_computation.4 | async-start | bytes 3145728 | tf_op jit(solution)/shard_map/all_to_all | solution.py:799
  172.8 32.3 %feed_back.1 = (bf16[4,96,3200]{2,1,0:T(8,128)(2,1)}, bf16[4,96,3200]{2,1,0:T(8,128)(2,1)}, bf16[4,384,768]{2,1,0:T(8,128)(2,1)}, bf16[4,384,768]{2,1,0:T(8,128)(2,1)}, f32[1024,768]{1,0:T(8,128)}) custom-call(s32[3]{0:T(128)} %pad_add_fusion.spots, bf16[4,2,128,768]{3,2,1,0:T(8,128)(2,1)} %copy-done.7, f32[1024,768]{1,0:T(8,128)} %get-tuple-element.111.normed_two, ...), custom_call_target="tpu_custom_call" | custom-call | flops 19327352832 | bytes 37748736 | tf_op jit(solution)/shard_map/feed_back/pallas_call | solution.py:524
  205.1 4.9 %all-to-all-done.4 = bf16[4,2,128,768]{3,2,1,0:T(8,128)(2,1)S(1)} async-done(((bf16[4,2,128,768]{3,2,1,0:T(8,128)(2,1)}), bf16[4,2,128,768]{3,2,1,0:T(8,128)(2,1)S(1)}, u32[]{:S(2)}, u32[]{:S(2)}) %all-to-all-start.4) | async-done | bytes 1572896 | tf_op jit(solution)/shard_map/all_to_all | solution.py:799
  211.7 9.6 %settle_back.1 = (f32[1024,768]{1,0:T(8,128)}, bf16[1024,768]{1,0:T(8,128)(2,1)}, bf16[4,96,768]{2,1,0:T(8,128)(2,1)}, bf16[4,96,768]{2,1,0:T(8,128)(2,1)}, f32[8,768]{1,0:T(8,128)}) custom-call(s32[3]{0:T(128)} %pad_add_fusion.spots, f32[1024,768]{1,0:T(8,128)} %get-tuple-element.122.hidden_grad, f32[1024,768]{1,0:T(8,128)} %get-tuple-element.104.normed_one.normed, ...), custom_call_target="tpu_custom_call" | custom-call | flops 2415919104 | bytes 12582912 | tf_op jit(solution)/shard_map/settle_back/pallas_call | solution.py:580
  224.4 7.8 %feed_chip_sums.1 = (bf16[4,24,7040]{2,1,0:T(8,128)(2,1)}, bf16[4,24,7040]{2,1,0:T(8,128)(2,1)}, bf16[4,24,7040]{2,1,0:T(8,128)(2,1)}, bf16[4,24,7040]{2,1,0:T(8,128)(2,1)}) custom-call(s32[3]{0:T(128)} %pad_add_fusion.spots, bf16[4,4,96,768]{3,2,1,0:T(8,128)(2,1)} %bitcast.58, bf16[4,4,96,768]{3,2,1,0:T(8,128)(2,1)} %bitcast.29.refs_1_.refs_3_.refs_5_.refs_7_, ...), custom_call_target="tpu_custom_call" | custom-call | bytes 16220160 | tf_op jit(solution)/shard_map/feed_chip_sums/pallas_call | solution.py:703
  235.8 21.0 %attend_back.1 = (bf16[2,512,2304]{2,1,0:T(8,128)(2,1)}, f32[2,1,2304]{2,1,0:T(1,128)}) custom-call(bf16[2,512,2304]{2,1,0:T(8,128)(2,1)} %get-tuple-element.94.query.key.value, bf16[2,512,2304]{2,1,0:T(8,128)(2,1)} %get-tuple-element.94.query.key.value, bf16[2,512,2304]{2,1,0:T(8,128)(2,1)} %get-tuple-element.94.query.key.value, ...), custom_call_target="tpu_custom_call" | custom-call | flops 6442450944 | bytes 25165824 | tf_op jit(solution)/shard_map/attend_back/pallas_call | solution.py:288
  256.8 9.3 %tokens_back.1 = bf16[4,2,128,768]{3,2,1,0:T(8,128)(2,1)} custom-call(bf16[1024,2304]{1,0:T(8,128)(2,1)} %bitcast.101, bf16[768,2304]{1,0:T(8,128)(2,1)} %get-tuple-element.139.weight, f32[1024,768]{1,0:T(8,128)} %get-tuple-element.140.first_up), custom_call_target="tpu_custom_call" | custom-call | flops 3623878656 | bytes 6291456 | tf_op jit(solution)/shard_map/tokens_back/pallas_call | solution.py:622
  266.1 4.4 %all-to-all-start.5 = ((bf16[4,2,128,768]{3,2,1,0:T(8,128)(2,1)}), bf16[4,2,128,768]{3,2,1,0:T(8,128)(2,1)}, u32[]{:S(2)}, u32[]{:S(2)}) async-start(bf16[4,2,128,768]{3,2,1,0:T(8,128)(2,1)} %tokens_back.1), calls=%async_computation.5 | async-start | bytes 3145728 | tf_op jit(solution)/shard_map/all_to_all | solution.py:799
  270.4 8.6 %weights_back.1 = (bf16[4,96,2432]{2,1,0:T(8,128)(2,1)}, bf16[4,96,2432]{2,1,0:T(8,128)(2,1)}) custom-call(s32[3]{0:T(128)} %pad_add_fusion.spots, bf16[1024,2304]{1,0:T(8,128)(2,1)} %bitcast.102, bf16[1024,768]{1,0:T(8,128)(2,1)} %get-tuple-element.100.tokens, f32[2,1,2304]{2,1,0:T(1,128)} %get-tuple-element.142.packed_sums, f32[8,768]{1,0:T(8,128)} %get-tuple-element.127.sums), custom_call_target="tpu_custom_call" | custom-call | flops 3623878656 | bytes 6291456 | tf_op jit(solution)/shard_map/weights_back/pallas_call | solution.py:659
  279.0 15.3 %collective-permute-done.19.refs_2_ = bf16[4,24,7040]{2,1,0:T(8,128)(2,1)S(1)} collective-permute-done((bf16[4,24,7040]{2,1,0:T(8,128)(2,1)}, bf16[4,24,7040]{2,1,0:T(8,128)(2,1)S(1)}, u32[]{:S(2)}, u32[]{:S(2)}) %collective-permute-start.19) | collective-permute-done | bytes 1351712 | tf_op jit(solution)/shard_map/ppermute | solution.py:788
  295.4 4.5 %feed_total.1 = bf16[4,24,7040]{2,1,0:T(8,128)(2,1)} custom-call(bf16[4,24,7040]{2,1,0:T(8,128)(2,1)} %get-tuple-element.145.refs_0_, bf16[4,24,7040]{2,1,0:T(8,128)(2,1)} %copy-done.18, bf16[4,24,7040]{2,1,0:T(8,128)(2,1)} %copy-done.19, bf16[4,24,7040]{2,1,0:T(8,128)(2,1)} %collective-permute-done.20.refs_3_), custom_call_target="tpu_custom_call" | custom-call | flops 999999995904 | bytes 6758400 | tf_op jit(solution)/shard_map/feed_total/pallas_call | solution.py:728
  299.9 4.8 %attention_chip_sums.1 = (bf16[4,24,2432]{2,1,0:T(8,128)(2,1)}, bf16[4,24,2432]{2,1,0:T(8,128)(2,1)}, bf16[4,24,2432]{2,1,0:T(8,128)(2,1)}, bf16[4,24,2432]{2,1,0:T(8,128)(2,1)}) custom-call(s32[3]{0:T(128)} %pad_add_fusion.spots, bf16[4,4,24,2432]{3,2,1,0:T(8,128)(2,1)} %bitcast.62, bf16[4,4,24,2432]{3,2,1,0:T(8,128)(2,1)} %bitcast.38.refs_1_.refs_3_.refs_5_.refs_7_, ...), custom_call_target="tpu_custom_call" | custom-call | bytes 5603328 | tf_op jit(solution)/shard_map/attention_chip_sums/pallas_call | solution.py:703
  307.2 3.5 all-to-all-start.6
  314.3 10.3 %collective-permute-done.21.refs_1_ = bf16[4,24,2432]{2,1,0:T(8,128)(2,1)S(1)} collective-permute-done((bf16[4,24,2432]{2,1,0:T(8,128)(2,1)}, bf16[4,24,2432]{2,1,0:T(8,128)(2,1)S(1)}, u32[]{:S(2)}, u32[]{:S(2)}) %collective-permute-start.21) | collective-permute-done | bytes 466976 | tf_op jit(solution)/shard_map/ppermute | solution.py:788
  324.6 9.0 %collective-permute-done.22.refs_2_ = bf16[4,24,2432]{2,1,0:T(8,128)(2,1)S(1)} collective-permute-done((bf16[4,24,2432]{2,1,0:T(8,128)(2,1)S(1)}, bf16[4,24,2432]{2,1,0:T(8,128)(2,1)S(1)}, u32[]{:S(2)}, u32[]{:S(2)}) %collective-permute-start.22) | collective-permute-done | bytes 466976 | tf_op jit(solution)/shard_map/ppermute | solution.py:788
  334.6 3.6 attention_total.1
  338.2 4.3 %all-to-all-done.6.came = bf16[4,24,7040]{2,1,0:T(8,128)(2,1)S(1)} async-done(((bf16[4,24,7040]{2,1,0:T(8,128)(2,1)}), bf16[4,24,7040]{2,1,0:T(8,128)(2,1)S(1)}, u32[]{:S(2)}, u32[]{:S(2)}) %all-to-all-start.6) | async-done | bytes 1351712 | tf_op jit(solution)/shard_map/all_to_all | solution.py:799
  342.4 3.5 all-to-all-start.7
  345.9 3.4 bitcast_convert_fusion
  351.7 6.9 %all-to-all-done.7.came = bf16[4,24,2432]{2,1,0:T(8,128)(2,1)S(1)} async-done(((bf16[4,24,2432]{2,1,0:T(8,128)(2,1)}), bf16[4,24,2432]{2,1,0:T(8,128)(2,1)S(1)}, u32[]{:S(2)}, u32[]{:S(2)}) %all-to-all-start.7) | async-done | bytes 466976 | tf_op jit(solution)/shard_map/all_to_all | solution.py:799
  (97 shorter events, 41.8 us)
Async XLA Ops:
  2.6 22.7 %all-to-all-start = ((bf16[4,24,3200]{2,1,0:T(8,128)(2,1)}), bf16[4,24,3200]{2,1,0:T(8,128)(2,1)S(1)}, u32[]{:S(2)}, u32[]{:S(2)}) async-start(bf16[4,24,3200]{2,1,0:T(8,128)(2,1)} %prepare_attention.1), calls=%async_computation | async-start | bytes 1228800 | tf_op jit(solution)/shard_map/all_to_all | solution.py:799
  25.4 33.3 %all-to-all-start.1 = ((bf16[4,24,6144]{2,1,0:T(8,128)(2,1)}), bf16[4,24,6144]{2,1,0:T(8,128)(2,1)S(1)}, u32[]{:S(2)}, u32[]{:S(2)}) async-start(bf16[4,24,6144]{2,1,0:T(8,128)(2,1)} %prepare_feed.1), calls=%async_computation.1 | async-start | bytes 2359296 | tf_op jit(solution)/shard_map/all_to_all | solution.py:799
  28.9 17.8 %collective-permute-start.2 = (bf16[4,24,3200]{2,1,0:T(8,128)(2,1)S(1)}, bf16[4,24,3200]{2,1,0:T(8,128)(2,1)S(1)}, u32[]{:S(2)}, u32[]{:S(2)}) collective-permute-start(bf16[4,24,3200]{2,1,0:T(8,128)(2,1)S(1)} %all-to-all-done), channel_id=1, source_target_pairs={{0,24},{1,25},{2,26},{3,27},{4,28},{5,29},{6,30},{7,31},{8,16},{9,... | collective-permute-start | bytes 1843208 | tf_op jit(solution)/shard_map/ppermute | solution.py:788
  31.4 26.4 %collective-permute-start.1 = (bf16[4,24,3200]{2,1,0:T(8,128)(2,1)S(1)}, bf16[4,24,3200]{2,1,0:T(8,128)(2,1)S(1)}, u32[]{:S(2)}, u32[]{:S(2)}) collective-permute-start(bf16[4,24,3200]{2,1,0:T(8,128)(2,1)S(1)} %all-to-all-done), channel_id=1, source_target_pairs={{0,16},{1,17},{2,18},{3,19},{4,20},{5,21},{6,22},{7,23},{8,24},{9,... | collective-permute-start | bytes 1843208 | tf_op jit(solution)/shard_map/ppermute | solution.py:788
  31.9 26.8 %collective-permute-start = (bf16[4,24,3200]{2,1,0:T(8,128)(2,1)S(1)}, bf16[4,24,3200]{2,1,0:T(8,128)(2,1)}, u32[]{:S(2)}, u32[]{:S(2)}) collective-permute-start(bf16[4,24,3200]{2,1,0:T(8,128)(2,1)S(1)} %all-to-all-done), channel_id=1, source_target_pairs={{0,8},{1,9},{2,10},{3,11},{4,12},{5,13},{6,14},{7,15},{8,0},{9,1},... | collective-permute-start | bytes 1843208 | tf_op jit(solution)/shard_map/ppermute | solution.py:788
  58.7 42.0 %all-to-all-start.2 = ((bf16[4,2,128,768]{3,2,1,0:T(8,128)(2,1)}), bf16[4,2,128,768]{3,2,1,0:T(8,128)(2,1)S(1)}, u32[]{:S(2)}, u32[]{:S(2)}) async-start(bf16[4,2,128,768]{3,2,1,0:T(8,128)(2,1)} %bitcast.3), calls=%async_computation.2 | async-start | bytes 3145728 | tf_op jit(solution)/shard_map/all_to_all | solution.py:799
  63.5 2.8 collective-permute-start.3
  63.5 4.0 %collective-permute-start.6 = (bf16[96,3200]{1,0:T(8,128)(2,1)}, bf16[96,3200]{1,0:T(8,128)(2,1)S(1)}, u32[]{:S(2)}, u32[]{:S(2)}) collective-permute-start(bf16[96,3200]{1,0:T(8,128)(2,1)} %bitcast.84), channel_id=1, source_target_pairs={{0,4},{1,5},{2,6},{3,7},{4,0},{5,1},{6,2},{7,3},{8,12},{9,13},{10,... | collective-permute-start | bytes 1843208 | tf_op jit(solution)/shard_map/ppermute | solution.py:788
  64.0 41.5 %collective-permute-start.5 = (bf16[96,3200]{1,0:T(8,128)(2,1)}, bf16[96,3200]{1,0:T(8,128)(2,1)}, u32[]{:S(2)}, u32[]{:S(2)}) collective-permute-start(bf16[96,3200]{1,0:T(8,128)(2,1)} %bitcast.88), channel_id=1, source_target_pairs={{0,4},{1,5},{2,6},{3,7},{4,0},{5,1},{6,2},{7,3},{8,12},{9,13},{10,... | collective-permute-start | bytes 1843208 | tf_op jit(solution)/shard_map/ppermute | solution.py:788
  64.0 41.5 %collective-permute-start.4 = (bf16[96,3200]{1,0:T(8,128)(2,1)}, bf16[96,3200]{1,0:T(8,128)(2,1)}, u32[]{:S(2)}, u32[]{:S(2)}) collective-permute-start(bf16[96,3200]{1,0:T(8,128)(2,1)} %bitcast.14.refs_1_.refs_9_), channel_id=1, source_target_pairs={{0,4},{1,5},{2,6},{3,7},{4,0},{5,1},{6,2},{7,3},{8,12},{9,13},{10,... | collective-permute-start | bytes 1843208 | tf_op jit(solution)/shard_map/ppermute | solution.py:788
  64.5 68.1 %collective-permute-start.9 = (bf16[4,24,6144]{2,1,0:T(8,128)(2,1)S(1)}, bf16[4,24,6144]{2,1,0:T(8,128)(2,1)}, u32[]{:S(2)}, u32[]{:S(2)}) collective-permute-start(bf16[4,24,6144]{2,1,0:T(8,128)(2,1)S(1)} %all-to-all-done.1.refs_8_), channel_id=1, source_target_pairs={{0,24},{1,25},{2,26},{3,27},{4,28},{5,29},{6,30},{7,31},{8,16},{9,... | collective-permute-start | bytes 3538952 | tf_op jit(solution)/shard_map/ppermute | solution.py:788
  66.2 66.3 %collective-permute-start.8 = (bf16[4,24,6144]{2,1,0:T(8,128)(2,1)S(1)}, bf16[4,24,6144]{2,1,0:T(8,128)(2,1)}, u32[]{:S(2)}, u32[]{:S(2)}) collective-permute-start(bf16[4,24,6144]{2,1,0:T(8,128)(2,1)S(1)} %all-to-all-done.1.refs_8_), channel_id=1, source_target_pairs={{0,16},{1,17},{2,18},{3,19},{4,20},{5,21},{6,22},{7,23},{8,24},{9,... | collective-permute-start | bytes 3538952 | tf_op jit(solution)/shard_map/ppermute | solution.py:788
  68.3 64.3 %collective-permute-start.7 = (bf16[4,24,6144]{2,1,0:T(8,128)(2,1)S(1)}, bf16[4,24,6144]{2,1,0:T(8,128)(2,1)}, u32[]{:S(2)}, u32[]{:S(2)}) collective-permute-start(bf16[4,24,6144]{2,1,0:T(8,128)(2,1)S(1)} %all-to-all-done.1.refs_8_), channel_id=1, source_target_pairs={{0,8},{1,9},{2,10},{3,11},{4,12},{5,13},{6,14},{7,15},{8,0},{9,1},... | collective-permute-start | bytes 3538952 | tf_op jit(solution)/shard_map/ppermute | solution.py:788
  101.8 64.8 %all-to-all-start.3 = ((bf16[4,2,128,768]{3,2,1,0:T(8,128)(2,1)}), bf16[4,2,128,768]{3,2,1,0:T(8,128)(2,1)S(1)}, u32[]{:S(2)}, u32[]{:S(2)}) async-start(bf16[4,2,128,768]{3,2,1,0:T(8,128)(2,1)} %bitcast.26), calls=%async_computation.3 | async-start | bytes 3145728 | tf_op jit(solution)/shard_map/all_to_all | solution.py:799
  105.4 34.8 %collective-permute-start.10 = (bf16[96,6144]{1,0:T(8,128)(2,1)S(1)}, bf16[96,6144]{1,0:T(8,128)(2,1)}, u32[]{:S(2)}, u32[]{:S(2)}) collective-permute-start(bf16[96,6144]{1,0:T(8,128)(2,1)S(1)} %bitcast.82), channel_id=1, source_target_pairs={{0,4},{1,5},{2,6},{3,7},{4,0},{5,1},{6,2},{7,3},{8,12},{9,13},{10,... | collective-permute-start | bytes 3538952 | tf_op jit(solution)/shard_map/ppermute | solution.py:788
  132.5 7.7 %collective-permute-start.11 = (bf16[96,6144]{1,0:T(8,128)(2,1)}, bf16[96,6144]{1,0:T(8,128)(2,1)}, u32[]{:S(2)}, u32[]{:S(2)}) collective-permute-start(bf16[96,6144]{1,0:T(8,128)(2,1)} %bitcast.19.refs_1_), channel_id=1, source_target_pairs={{0,4},{1,5},{2,6},{3,7},{4,0},{5,1},{6,2},{7,3},{8,12},{9,13},{10,... | collective-permute-start | bytes 3538952 | tf_op jit(solution)/shard_map/ppermute | solution.py:788
  133.1 7.2 %collective-permute-start.12 = (bf16[96,6144]{1,0:T(8,128)(2,1)}, bf16[96,6144]{1,0:T(8,128)(2,1)}, u32[]{:S(2)}, u32[]{:S(2)}) collective-permute-start(bf16[96,6144]{1,0:T(8,128)(2,1)} %bitcast.20.refs_2_), channel_id=1, source_target_pairs={{0,4},{1,5},{2,6},{3,7},{4,0},{5,1},{6,2},{7,3},{8,12},{9,13},{10,... | collective-permute-start | bytes 3538952 | tf_op jit(solution)/shard_map/ppermute | solution.py:788
  133.2 7.1 %collective-permute-start.13 = (bf16[96,6144]{1,0:T(8,128)(2,1)}, bf16[96,6144]{1,0:T(8,128)(2,1)}, u32[]{:S(2)}, u32[]{:S(2)}) collective-permute-start(bf16[96,6144]{1,0:T(8,128)(2,1)} %bitcast.21.refs_3_), channel_id=1, source_target_pairs={{0,4},{1,5},{2,6},{3,7},{4,0},{5,1},{6,2},{7,3},{8,12},{9,13},{10,... | collective-permute-start | bytes 3538952 | tf_op jit(solution)/shard_map/ppermute | solution.py:788
  167.8 42.2 %all-to-all-start.4 = ((bf16[4,2,128,768]{3,2,1,0:T(8,128)(2,1)}), bf16[4,2,128,768]{3,2,1,0:T(8,128)(2,1)S(1)}, u32[]{:S(2)}, u32[]{:S(2)}) async-start(bf16[4,2,128,768]{3,2,1,0:T(8,128)(2,1)} %get-tuple-element.109), calls=%async_computation.4 | async-start | bytes 3145728 | tf_op jit(solution)/shard_map/all_to_all | solution.py:799
  211.2 10.2 %collective-permute-start.16 = (bf16[4,96,3200]{2,1,0:T(8,128)(2,1)}, bf16[4,96,3200]{2,1,0:T(8,128)(2,1)S(1)}, u32[]{:S(2)}, u32[]{:S(2)}) collective-permute-start(bf16[4,96,3200]{2,1,0:T(8,128)(2,1)} %get-tuple-element.119), channel_id=1, source_target_pairs={{0,4},{1,5},{2,6},{3,7},{4,0},{5,1},{6,2},{7,3},{8,12},{9,13},{10,... | collective-permute-start | bytes 7372808 | tf_op jit(solution)/shard_map/ppermute | solution.py:788
  211.2 10.2 %collective-permute-start.14 = (bf16[4,384,768]{2,1,0:T(8,128)(2,1)}, bf16[4,384,768]{2,1,0:T(8,128)(2,1)}, u32[]{:S(2)}, u32[]{:S(2)}) collective-permute-start(bf16[4,384,768]{2,1,0:T(8,128)(2,1)} %get-tuple-element.121), channel_id=1, source_target_pairs={{0,4},{1,5},{2,6},{3,7},{4,0},{5,1},{6,2},{7,3},{8,12},{9,13},{10,... | collective-permute-start | bytes 7077896 | tf_op jit(solution)/shard_map/ppermute | solution.py:788
  221.3 2.3 collective-permute-start.15
  232.2 46.8 %collective-permute-start.18 = (bf16[4,24,7040]{2,1,0:T(8,128)(2,1)}, bf16[4,24,7040]{2,1,0:T(8,128)(2,1)S(1)}, u32[]{:S(2)}, u32[]{:S(2)}) collective-permute-start(bf16[4,24,7040]{2,1,0:T(8,128)(2,1)} %get-tuple-element.133), channel_id=1, source_target_pairs={{0,8},{1,9},{2,10},{3,11},{4,12},{5,13},{6,14},{7,15},{8,0},{9,1},... | collective-permute-start | bytes 4055048 | tf_op jit(solution)/shard_map/ppermute | solution.py:788
  233.8 60.6 %collective-permute-start.19 = (bf16[4,24,7040]{2,1,0:T(8,128)(2,1)}, bf16[4,24,7040]{2,1,0:T(8,128)(2,1)S(1)}, u32[]{:S(2)}, u32[]{:S(2)}) collective-permute-start(bf16[4,24,7040]{2,1,0:T(8,128)(2,1)} %get-tuple-element.134), channel_id=1, source_target_pairs={{0,16},{1,17},{2,18},{3,19},{4,20},{5,21},{6,22},{7,23},{8,24},{9,... | collective-permute-start | bytes 4055048 | tf_op jit(solution)/shard_map/ppermute | solution.py:788
  233.8 60.5 %collective-permute-start.20 = (bf16[4,24,7040]{2,1,0:T(8,128)(2,1)}, bf16[4,24,7040]{2,1,0:T(8,128)(2,1)}, u32[]{:S(2)}, u32[]{:S(2)}) collective-permute-start(bf16[4,24,7040]{2,1,0:T(8,128)(2,1)} %get-tuple-element.135), channel_id=1, source_target_pairs={{0,24},{1,25},{2,26},{3,27},{4,28},{5,29},{6,30},{7,31},{8,16},{9,... | collective-permute-start | bytes 4055048 | tf_op jit(solution)/shard_map/ppermute | solution.py:788
  266.1 41.1 %all-to-all-start.5 = ((bf16[4,2,128,768]{3,2,1,0:T(8,128)(2,1)}), bf16[4,2,128,768]{3,2,1,0:T(8,128)(2,1)}, u32[]{:S(2)}, u32[]{:S(2)}) async-start(bf16[4,2,128,768]{3,2,1,0:T(8,128)(2,1)} %tokens_back.1), calls=%async_computation.5 | async-start | bytes 3145728 | tf_op jit(solution)/shard_map/all_to_all | solution.py:799
  279.0 20.9 %collective-permute-start.17 = (bf16[4,96,2432]{2,1,0:T(8,128)(2,1)}, bf16[4,96,2432]{2,1,0:T(8,128)(2,1)}, u32[]{:S(2)}, u32[]{:S(2)}) collective-permute-start(bf16[4,96,2432]{2,1,0:T(8,128)(2,1)} %get-tuple-element.144), channel_id=1, source_target_pairs={{0,4},{1,5},{2,6},{3,7},{4,0},{5,1},{6,2},{7,3},{8,12},{9,13},{10,... | collective-permute-start | bytes 5603336 | tf_op jit(solution)/shard_map/ppermute | solution.py:788
  307.2 35.2 %all-to-all-start.6 = ((bf16[4,24,7040]{2,1,0:T(8,128)(2,1)}), bf16[4,24,7040]{2,1,0:T(8,128)(2,1)S(1)}, u32[]{:S(2)}, u32[]{:S(2)}) async-start(bf16[4,24,7040]{2,1,0:T(8,128)(2,1)} %feed_total.1), calls=%async_computation.6 | async-start | bytes 2703360 | tf_op jit(solution)/shard_map/all_to_all | solution.py:799
  310.7 13.9 %collective-permute-start.21 = (bf16[4,24,2432]{2,1,0:T(8,128)(2,1)}, bf16[4,24,2432]{2,1,0:T(8,128)(2,1)S(1)}, u32[]{:S(2)}, u32[]{:S(2)}) collective-permute-start(bf16[4,24,2432]{2,1,0:T(8,128)(2,1)} %get-tuple-element.151), channel_id=1, source_target_pairs={{0,8},{1,9},{2,10},{3,11},{4,12},{5,13},{6,14},{7,15},{8,0},{9,1},... | collective-permute-start | bytes 1400840 | tf_op jit(solution)/shard_map/ppermute | solution.py:788
  312.3 21.4 %collective-permute-start.22 = (bf16[4,24,2432]{2,1,0:T(8,128)(2,1)S(1)}, bf16[4,24,2432]{2,1,0:T(8,128)(2,1)S(1)}, u32[]{:S(2)}, u32[]{:S(2)}) collective-permute-start(bf16[4,24,2432]{2,1,0:T(8,128)(2,1)S(1)} %copy-done.21), channel_id=1, source_target_pairs={{0,16},{1,17},{2,18},{3,19},{4,20},{5,21},{6,22},{7,23},{8,24},{9,... | collective-permute-start | bytes 1400840 | tf_op jit(solution)/shard_map/ppermute | solution.py:788
  312.6 21.1 %collective-permute-start.23 = (bf16[4,24,2432]{2,1,0:T(8,128)(2,1)S(1)}, bf16[4,24,2432]{2,1,0:T(8,128)(2,1)S(1)}, u32[]{:S(2)}, u32[]{:S(2)}) collective-permute-start(bf16[4,24,2432]{2,1,0:T(8,128)(2,1)S(1)} %copy-done.20), channel_id=1, source_target_pairs={{0,24},{1,25},{2,26},{3,27},{4,28},{5,29},{6,30},{7,31},{8,16},{9,... | collective-permute-start | bytes 1400840 | tf_op jit(solution)/shard_map/ppermute | solution.py:788
  342.4 16.2 %all-to-all-start.7 = ((bf16[4,24,2432]{2,1,0:T(8,128)(2,1)}), bf16[4,24,2432]{2,1,0:T(8,128)(2,1)S(1)}, u32[]{:S(2)}, u32[]{:S(2)}) async-start(bf16[4,24,2432]{2,1,0:T(8,128)(2,1)} %attention_total.1), calls=%async_computation.7 | async-start | bytes 933888 | tf_op jit(solution)/shard_map/all_to_all | solution.py:799
  (22 other events, 178.2 us)

commit v5 on v4

--- a/solution.py
+++ b/solution.py
@@ -10,6 +10,7 @@
 
 HEAD_DIM = 64
 LANES = 128
+CHUNK = 64
 PARTS = 4
 EPSILON = 1e-06
 AXES = ("dp", "seq")
@@ -149,54 +150,80 @@
     )(inner_weight, outer_weight)
 
 
-def project_body(spots, tokens, *refs):
-    weights, columns = refs[: 2 * PARTS], refs[2 * PARTS : 4 * PARTS]
-    packed, flat, weight, rows, vectors = refs[4 * PARTS :]
+def unite_attention_body(spots, *refs):
+    parts, (packed, output, rows, bias, vectors) = refs[: 2 * PARTS], refs[2 * PARTS :]
+    width, wide = packed.shape
+    for target, start in ((packed, 0), (output, wide), (vectors, wide + width)):
+        views = [part.at[:, start : start + target.shape[1]] for part in parts]
+        unite(target, views[:PARTS], views[PARTS:], spots)
+    rows[...] = widen(vectors[...]).T[:8]
+    share, block = width // PARTS, bias.shape[1] // PARTS
+    per = block // share
+    for index in range(PARTS):
+        line = 0.0
+        for column in range(per):
+            value = widen(vectors[index * share : (index + 1) * share, 8 + column : 9 + column])
+            line = line + jnp.where(spread_mask(share, per, column), value, 0.0)
+        bias[:, index * block : (index + 1) * block] = row_sum(line)
+
+
+def unite_attention(spots, gathered, wide):
+    rows, columns = gathered[0].shape
+    width = 2 * PARTS * rows
+    whole = pl.BlockSpec(memory_space=pltpu.VMEM)
+    return kernel(
+        unite_attention_body,
+        "unite_attention",
+        0,
+        4 * width * columns,
+        in_specs=[SCALARS] + [whole] * len(gathered),
+        out_specs=[whole] * 4,
+        out_shape=[
+            shape((width, 3 * width)),
+            shape((width, width)),
+            shape((8, width), F32),
+            shape((1, wide), F32),
+        ],
+        scratch_shapes=[pltpu.VMEM((width, LANES), BF16)],
+    )(spots, *gathered)
+
+
+def project_body(tokens, weight, rows, packed, flat):
     part = pl.program_id(0)
     seq, count, places, width = tokens.shape
     length = seq * places
 
     @pl.when(part == 0)
     def _():
-        unite(vectors, columns[:PARTS], columns[PARTS:], spots)
-        rows[...] = widen(vectors[...]).T[:8]
         for row in range(count):
             flat[row * length : (row + 1) * length] = tokens[:, row].reshape(length, width)
 
-    unite(weight, weights[:PARTS], weights[PARTS:], spots)
     query, value = rows[0:1], rows[1:2]
     bias = jnp.where(part == 0, query, jnp.where(part == 2, value, jnp.zeros_like(query)))
     result = narrow(dot(flat[...], weight[...]) + bias)
     packed[...] = result.reshape(packed.shape)
 
 
-def project(spots, tokens, gathered):
-    seq, rows, places, width = tokens.shape
+def project(tokens, weight, rows):
+    seq, count, places, width = tokens.shape
     length = seq * places
     return kernel(
         project_body,
         "project",
-        6 * rows * length * width * width,
-        8 * rows * length * width,
+        6 * count * length * width * width,
+        8 * count * length * width,
         grid=(3,),
-        in_specs=[SCALARS, fixed(tokens.shape)]
-        + gathered_specs(gathered, width, lambda i: i)
-        + gathered_specs(gathered, LANES, lambda i: 4 * width // LANES),
+        in_specs=[
+            fixed(tokens.shape),
+            pl.BlockSpec((width, width), lambda i: (0, i)),
+            fixed(rows.shape),
+        ],
         out_specs=[
-            pl.BlockSpec((rows, length, width), lambda i: (0, 0, i)),
-            fixed((rows * length, width)),
-            pl.BlockSpec((width, width), lambda i: (0, i)),
-            fixed((8, width)),
-            fixed((width, LANES)),
-        ],
-        out_shape=[
-            shape((rows, length, 3 * width)),
-            shape((rows * length, width)),
-            shape((width, 3 * width)),
-            shape((8, width), F32),
-            shape((width, LANES)),
-        ],
-    )(spots, tokens, *gathered, *gathered)
+            pl.BlockSpec((count, length, width), lambda i: (0, 0, i)),
+            fixed((count * length, width)),
+        ],
+        out_shape=[shape((count, length, 3 * width)), shape((count * length, width))],
+    )(tokens, weight, rows)
 
 
 def pair_labels(places, lengths, row):
@@ -207,7 +234,7 @@
     return label
 
 
-def attend_body(spots, lengths, query, key, value, context, probs, bias):
+def attend_body(spots, lengths, query, key, value, context, probs, bias, scores):
     length = bias.shape[0]
 
     @pl.when(pl.program_id(1) == 0)
@@ -218,17 +245,20 @@
         bias[...] = jnp.where(down == along, 0.0, -1e30)
 
     lane = lax.broadcasted_iota(jnp.int32, (1, LANES), 1)
-    keys, values = key[0], value[0]
+    values = value[0]
     queries = query[0] * BF16(HEAD_DIM**-0.5)
+    for head in range(2):
+        mine = (lane >= HEAD_DIM) == bool(head)
+        scores[head] = dot(jnp.where(mine, queries, BF16(0)), key[0], NT)
     parts = []
     for head in range(2):
-        mine = (lane >= HEAD_DIM) == bool(head)
-        scores = dot(jnp.where(mine, queries, BF16(0)), keys, NT) + bias[...]
-        raised = jnp.exp(scores - jnp.max(scores, axis=-1, keepdims=True))
-        total = jnp.sum(raised, axis=-1, keepdims=True)
-        low = narrow(raised * (1.0 / total))
-        probs[0, head] = low
-        parts.append(dot(low, values))
+        for start in range(0, length, CHUNK):
+            rows = slice(start, start + CHUNK)
+            masked = scores[head, rows] + bias[rows]
+            raised = jnp.exp(masked - jnp.max(masked, axis=-1, keepdims=True))
+            total = jnp.sum(raised, axis=-1, keepdims=True)
+            probs[0, head, rows] = narrow(raised * (1.0 / total))
+        parts.append(dot(probs[0, head], values))
     context[0] = narrow(jnp.where(lane < HEAD_DIM, parts[0], parts[1]))
 
 
@@ -251,29 +281,34 @@
             pl.BlockSpec((1, 2, length, length), lambda r, p: (r, p, 0, 0)),
         ],
         out_shape=[shape((rows, length, wide // 3)), shape((rows, 2 * pairs, length, length))],
-        scratch_shapes=[pltpu.VMEM((length, length), F32)],
+        scratch_shapes=[pltpu.VMEM((length, length), F32), pltpu.VMEM((2, length, length), F32)],
     )(spots, lengths, packed, packed, packed)
 
 
-def attend_back_body(query, key, value, upstream, probs, grads, sums):
+def attend_back_body(query, key, value, upstream, probs, grads, sums, prob_grad, score_grad):
     pair, pairs = pl.program_id(1), pl.num_programs(1)
     lane = lax.broadcasted_iota(jnp.int32, (1, LANES), 1)
     scale = BF16(HEAD_DIM**-0.5)
     queries, keys, values, up = query[0] * scale, key[0], value[0], upstream[0]
     scaled_keys = keys * scale
+    length = keys.shape[0]
     query_parts, key_grad, value_grad = [], 0.0, 0.0
+    mine = [(lane >= HEAD_DIM) == bool(head) for head in range(2)]
+    ups = [jnp.where(lanes, up, BF16(0)) for lanes in mine]
     for head in range(2):
-        mine = (lane >= HEAD_DIM) == bool(head)
-        up_mine = jnp.where(mine, up, BF16(0))
-        queries_mine = jnp.where(mine, queries, BF16(0))
-        low = probs[0, head]
-        prob_grad = dot(up_mine, values, NT)
-        softmaxed = widen(low)
-        weighted = jnp.sum(softmaxed * prob_grad, axis=-1, keepdims=True)
-        score_grad = narrow(softmaxed * (prob_grad - weighted))
-        query_parts.append(dot(score_grad, scaled_keys))
-        key_grad = key_grad + dot(queries_mine, score_grad, TN)
-        value_grad = value_grad + dot(up_mine, low, TN)
+        prob_grad[head] = dot(ups[head], values, NT)
+    for head in range(2):
+        for start in range(0, length, CHUNK):
+            rows = slice(start, start + CHUNK)
+            softmaxed = widen(probs[0, head, rows])
+            product = softmaxed * prob_grad[head, rows]
+            weighted = jnp.sum(product, axis=-1, keepdims=True)
+            score_grad[head, rows] = narrow(product - softmaxed * weighted)
+    for head in range(2):
+        queries_mine = jnp.where(mine[head], queries, BF16(0))
+        query_parts.append(dot(score_grad[head], scaled_keys))
+        key_grad = key_grad + dot(queries_mine, score_grad[head], TN)
+        value_grad = value_grad + dot(ups[head], probs[0, head], TN)
     query_grad = jnp.where(lane < HEAD_DIM, query_parts[0], query_parts[1])
     for part, grad in enumerate((query_grad, key_grad.T, value_grad.T)):
         at = pl.ds(pl.multiple_of((part * pairs + pair) * LANES, LANES), LANES)
@@ -301,6 +336,10 @@
             pl.BlockSpec((1, 1, wide), lambda r, p: (r, 0, 0)),
         ],
         out_shape=[shape(packed.shape), shape((rows, 1, wide), F32)],
+        scratch_shapes=[
+            pltpu.VMEM((2, length, length), F32),
+            pltpu.VMEM((2, length, length), BF16),
+        ],
     )(packed, packed, packed, upstream, probs)
 
 
@@ -318,38 +357,26 @@
     return inverse * (scaled - first_mean - normed * second_mean)
 
 
-def settle_body(spots, context, tokens, rows, *refs):
-    parts, (normed, inverse, low, weight) = refs[: 2 * PARTS], refs[2 * PARTS :]
-
-    @pl.when(pl.program_id(0) == 0)
-    def _():
-        unite(weight, parts[:PARTS], parts[PARTS:], spots)
-
+def settle_body(context, tokens, rows, weight, normed, inverse, low):
     summed = widen(tokens[...]) + dot(context[...], weight[...]) + rows[2:3]
     normed[...], inverse[...] = normed_of(summed)
     low[...] = narrow(normed[...] * rows[3:4] + rows[4:5])
 
 
-def settle(spots, context, tokens, rows, gathered):
+def settle(context, tokens, rows, weight):
     count, width = context.shape
-    block = count // 4
+    block = count // 2
     tall = pl.BlockSpec((block, width), lambda i: (i, 0))
     return kernel(
         settle_body,
         "settle",
         2 * count * width * width,
         10 * count * width,
-        grid=(4,),
-        in_specs=[SCALARS, tall, tall, fixed(rows.shape)]
-        + gathered_specs(gathered, width, lambda i: 3),
-        out_specs=[tall, pl.BlockSpec((block, 1), lambda i: (i, 0)), tall, fixed((width, width))],
-        out_shape=[
-            shape((count, width), F32),
-            shape((count, 1), F32),
-            shape((count, width)),
-            shape((width, width)),
-        ],
-    )(spots, context, tokens, rows, *gathered)
+        grid=(2,),
+        in_specs=[tall, tall, fixed(rows.shape), fixed(weight.shape)],
+        out_specs=[tall, pl.BlockSpec((block, 1), lambda i: (i, 0)), tall],
+        out_shape=[shape((count, width), F32), shape((count, 1), F32), shape((count, width))],
+    )(context, tokens, rows, weight)
 
 
 def spread_mask(rows, per, column):
@@ -369,36 +396,44 @@
     return narrow(jnp.concatenate(blocks, axis=0))
 
 
-def feed_body(spots, low, vectors, normed_one, rows, *refs):
+def feed_body(spots, low, bias, normed_one, rows, *refs):
     inners, outers = refs[: 2 * PARTS], refs[2 * PARTS : 4 * PARTS]
     (
-        active, slope, normed_two, inverse_two, output, inner_weight, outer_weight, branch,
+        active, slope, normed_two, inverse_two, output, inner_weight, outer_weight,
+        branch, staged, sems,
     ) = refs[4 * PARTS :]
     step, steps = pl.program_id(0), pl.num_programs(0)
+    wide = staged.shape[-1]
+    copies = [
+        pltpu.make_async_copy(
+            outer.at[:, :, pl.ds(wide, wide)], staged.at[index], sems.at[index]
+        )
+        for index, outer in enumerate(outers)
+    ]
+
+    @pl.when(step == 0)
+    def _():
+        for copy in copies:
+            copy.start()
+
     unite(inner_weight, inners[:PARTS], inners[PARTS:], spots)
-    for index in range(PARTS):
-
-        @pl.when(step == spots[2] ^ index)
-        def _():
-            half = outer_weight.shape[0] // 2
-            for side, part in ((spots[1], outers[index]), (1 - spots[1], outers[PARTS + index])):
-                start = pl.multiple_of(side * half, half)
-                outer_weight[pl.ds(start, half), :] = stack_blocks(part)
-
-    block = inner_weight.shape[-1]
-    share_rows = vectors.shape[0] // PARTS
-    per = block // share_rows
-    own_rows = vectors[pl.ds(pl.multiple_of(step * share_rows, share_rows), share_rows), :]
-    bias = 0.0
-    for column in range(per):
-        value = widen(own_rows[:, 8 + column : 9 + column])
-        bias = bias + jnp.where(spread_mask(share_rows, per, column), value, 0.0)
-    inner = dot(low[...], inner_weight[...]) + row_sum(bias)
+    inner = dot(low[...], inner_weight[...]) + bias[...]
     share = 0.5 * (1.0 + lax.erf(inner * math.sqrt(0.5)))
     raised = jnp.exp(-0.5 * inner * inner) * (1.0 / math.sqrt(2.0 * math.pi))
     acted = narrow(inner * share)
     active[...] = acted
     slope[...] = narrow(share + inner * raised)
+    for index in range(PARTS):
+
+        @pl.when(step == spots[2] ^ index)
+        def _():
+            copies[index].wait()
+            copies[PARTS + index].wait()
+            half = outer_weight.shape[0] // 2
+            for side, at in ((spots[1], index), (1 - spots[1], PARTS + index)):
+                start = pl.multiple_of(side * half, half)
+                outer_weight[pl.ds(start, half), :] = stack_blocks(staged.at[at])
+
     part = dot(acted, outer_weight[...])
 
     @pl.when(step == 0)
@@ -409,10 +444,13 @@
     def _():
         branch[...] += part
 
+    height = normed_one.shape[0]
+    at = pl.ds(pl.multiple_of(step * height, height), height)
+    branch[at, :] += normed_one[...] * rows[3:4] + (rows[4:5] + rows[5:6])
+
     @pl.when(step == steps - 1)
     def _():
-        hidden = normed_one[...] * rows[3:4] + rows[4:5]
-        normed_two[...], inverse_two[...] = normed_of(hidden + branch[...] + rows[5:6])
+        normed_two[...], inverse_two[...] = normed_of(branch[...])
         result = narrow(normed_two[...] * rows[6:7] + rows[7:8])
         seq, count, places, width = output.shape
         result = result.reshape(count, seq, places, width)
@@ -420,25 +458,28 @@
             output[:, row] = result[row]
 
 
-def feed(spots, low, vectors, normed_one, rows, gathered, dims):
+def feed(spots, low, bias, normed_one, rows, gathered, dims):
     count, width = low.shape
     wide = gathered[0].shape[1] // 2
     block = wide // PARTS
     deep = [part.reshape(dims[0], -1, 2 * wide) for part in gathered]
     all_of = fixed((count, width))
     across = pl.BlockSpec((count, block), lambda f: (0, f))
-    outer = pl.BlockSpec(
-        deep[0].shape[:2] + (wide,), lambda f: (0, 0, 1), pipeline_mode=pl.Buffered(1)
-    )
     return kernel(
         feed_body,
         "feed",
         4 * count * width * wide,
         12 * count * wide,
         grid=(PARTS,),
-        in_specs=[SCALARS, all_of, fixed(vectors.shape), all_of, fixed(rows.shape)]
+        in_specs=[
+            SCALARS,
+            all_of,
+            pl.BlockSpec((1, block), lambda f: (0, f)),
+            pl.BlockSpec((count // PARTS, width), lambda f: (f, 0)),
+            fixed(rows.shape),
+        ]
         + gathered_specs(gathered, block, lambda f: f)
-        + [outer] * len(deep),
+        + [ANYWHERE] * len(deep),
         out_specs=[
             across,
             across,
@@ -457,13 +498,17 @@
             shape((width, wide)),
             shape((wide, width)),
         ],
-        scratch_shapes=[pltpu.VMEM((count, width), F32)],
-    )(spots, low, vectors, normed_one, rows, *gathered, *deep)
+        scratch_shapes=[
+            pltpu.VMEM((count, width), F32),
+            pltpu.VMEM((len(deep),) + deep[0].shape[:2] + (wide,), BF16),
+            pltpu.SemaphoreType.DMA((len(deep),)),
+        ],
+    )(spots, low, bias, normed_one, rows, *gathered, *deep)
 
 
 def feed_back_body(
     spots, cotangent, normed_two, inverse_two, rows_one, low, inner_weight, outer_weight, active, slope,
-    keep_inner, send_inner, keep_outer, send_outer, hidden_grad,
+    keep_inner, send_inner, keep_outer, send_outer, keep_vectors, send_vectors, hidden_grad,
     up, made, columns,
 ):
     step, steps, side = pl.program_id(0), pl.num_programs(0), spots[1]
@@ -484,8 +529,7 @@
 
     inner_grad = narrow(dot(up[...], outer_weight[...], NT) * widen(slope[...]))
     made[...] = narrow(dot(low[...], inner_grad, TN))
-    at = pl.ds(pl.multiple_of(step * block, block), block)
-    divide(made, keep_inner, send_inner, side, at)
+    divide(made, keep_inner, send_inner, side, slice(None))
     hidden_grad[...] += dot(inner_grad, inner_weight[...], NT)
     made[...] = narrow(dot(active[...], up[...], TN))
     divide(made, keep_outer, send_outer, side, slice(None))
@@ -505,11 +549,7 @@
     @pl.when(step == steps - 1)
     def _():
         made[:, :LANES] = narrow(columns[...])
-        count, rows, wide = keep_inner.shape
-        for index in range(count):
-            for half, target in ((side, keep_inner), (1 - side, send_inner)):
-                start = pl.multiple_of((2 * index + half) * rows, rows)
-                target[index, :, wide - LANES :] = made[pl.ds(start, rows), :LANES]
+        divide(made.at[:, :LANES], keep_vectors, send_vectors, side, slice(None))
 
 
 def feed_back(spots, cotangent, normed_two, inverse_two, rows, low, inner, outer, active, slope):
@@ -518,8 +558,9 @@
     block = wide // PARTS
     all_of = fixed((count, width))
     across = pl.BlockSpec((count, block), lambda f: (0, f))
-    first = (PARTS, width // PARTS // 2, wide + LANES)
-    second = (PARTS, block // 2, width)
+    first, second = (PARTS, width // PARTS // 2, wide), (PARTS, block // 2, width)
+    third = first[:2] + (LANES,)
+    right = pl.BlockSpec(first[:2] + (block,), lambda f: (0, 0, f))
     down = pl.BlockSpec((1,) + second[1:], lambda f: (f, 0, 0))
     return kernel(
         feed_back_body,
@@ -534,8 +575,8 @@
             across,
             across,
         ],
-        out_specs=[fixed(first), fixed(first), down, down, all_of],
-        out_shape=[shape(first), shape(first), shape(second), shape(second)]
+        out_specs=[right, right, down, down, fixed(third), fixed(third), all_of],
+        out_shape=[shape(dims) for dims in (first, first, second, second, third, third)]
         + [shape((count, width), F32)],
         scratch_shapes=[
             pltpu.VMEM((count, width), BF16),
@@ -574,15 +615,15 @@
 
 def settle_back(spots, hidden_grad, normed, inverse, rows, context, weight):
     count, width = context.shape
-    block = count // 4
+    block = count // 2
     tall = pl.BlockSpec((block, width), lambda i: (i, 0))
     dims = (PARTS, width // PARTS // 2, width)
     return kernel(
         settle_back_body,
         "settle_back",
-        4 * count * width * width,
+        10**12,
         16 * count * width,
-        grid=(4,),
+        grid=(2,),
         in_specs=[SCALARS, tall, tall, pl.BlockSpec((block, 1), lambda i: (i, 0))]
         + [fixed(rows.shape), tall, fixed((width, width))],
         out_specs=[tall, tall, fixed(dims), fixed(dims), fixed((8, width))],
@@ -597,42 +638,29 @@
     )(spots, hidden_grad, normed, inverse, rows, context, weight)
 
 
-def tokens_back_body(packed_grad, weight, first_up, grad, total):
-    part = pl.program_id(0)
-    added = dot(packed_grad[...], weight[...], NT)
-
-    @pl.when(part == 0)
-    def _():
-        total[...] = first_up[...] + added
-
-    @pl.when(part == 1)
-    def _():
-        total[...] += added
-
-    @pl.when(part == 2)
-    def _():
-        seq, rows, places, width = grad.shape
-        result = narrow(total[...] + added).reshape(rows, seq, places, width)
-        for row in range(rows):
-            grad[:, row] = result[row]
+def tokens_back_body(packed_grad, weight, first_up, grad):
+    total = first_up[...] + dot(packed_grad[...], weight[...], NT)
+    seq, _, places, width = grad.shape
+    grad[:, 0] = narrow(total).reshape(seq, places, width)
 
 
 def tokens_back(packed_grad, weight, first_up, dims):
     count, width = first_up.shape
+    seq, rows, places, _ = dims
+    length = seq * places
     return kernel(
         tokens_back_body,
         "tokens_back",
         6 * count * width * width,
         8 * count * width,
-        grid=(3,),
+        grid=(rows,),
         in_specs=[
-            pl.BlockSpec((count, width), lambda i: (0, i)),
-            pl.BlockSpec((width, width), lambda i: (0, i)),
-            fixed((count, width)),
-        ],
-        out_specs=fixed(dims),
+            pl.BlockSpec((length, 3 * width), lambda r: (r, 0)),
+            fixed((width, 3 * width)),
+            pl.BlockSpec((length, width), lambda r: (r, 0)),
+        ],
+        out_specs=pl.BlockSpec((seq, 1, places, width), lambda r: (0, r, 0, 0)),
         out_shape=shape(dims),
-        scratch_shapes=[pltpu.VMEM((count, width), F32)],
     )(packed_grad, weight, first_up)
 
 
@@ -737,11 +765,41 @@
     )(*values)
 
 
-def finish_body(vectors, blocks, came, *outs):
-    seq, small, wide = came.shape
-    total = widen(came[0])
-    for index in range(1, seq):
-        total = total + widen(came[index])
+def total_pieces(name, spots, values):
+    seq, small, wide = values[0].shape
+    blocks = [
+        pl.BlockSpec((None, small, wide), lambda i, spots, step=step: (lax.rem(spots[0] + step, seq), 0, 0))
+        for step in range(seq)
+    ]
+
+    def body(spots, *refs):
+        for step in range(seq):
+            part = refs[step * len(values) : (step + 1) * len(values)]
+            total_body(*part, refs[seq * len(values) + step])
+
+    return kernel(
+        body,
+        name,
+        0,
+        2 * (len(values) + 1) * seq * small * wide,
+        grid_spec=pltpu.PrefetchScalarGridSpec(
+            num_scalar_prefetch=1,
+            grid=(1,),
+            in_specs=[block for block in blocks for _ in values],
+            out_specs=[pl.BlockSpec((small, wide), lambda i, spots: (0, 0))] * seq,
+        ),
+        out_shape=[shape((small, wide))] * seq,
+    )(spots, *(list(values) * seq))
+
+
+def finish_body(count, vectors, blocks, *refs):
+    pieces, outs = refs[:count], refs[count:]
+    if count == 1:
+        pieces = [pieces[0].at[index] for index in range(pieces[0].shape[0])]
+    total = widen(pieces[0][...])
+    for piece in pieces[1:]:
+        total = total + widen(piece[...])
+    small, wide = total.shape
     start = 0
     for out, (count, width) in zip(outs, blocks):
         for index in range(count):
@@ -756,16 +814,16 @@
         out[...] = row_sum(line)
 
 
-def finish(name, came, blocks, vectors):
-    seq, small, wide = came.shape
-    return kernel(
-        partial(finish_body, vectors, blocks),
+def finish(name, pieces, blocks, vectors):
+    small, wide = pieces[0].shape[-2:]
+    return kernel(
+        partial(finish_body, len(pieces), vectors, blocks),
         name,
         0,
-        4 * seq * small * wide,
+        8 * small * wide,
         out_shape=[shape((count * small, width), F32) for count, width in blocks]
         + [shape((1, small * per), F32) for _, per in vectors],
-    )(came)
+    )(*pieces)
 
 
 def block_at(blocks, index, axis=0):
@@ -782,6 +840,14 @@
     def across(self, value, flip):
         pairs = [
             (d * self.seq + s, (d ^ flip) * self.seq + s)
+            for d in range(self.dp)
+            for s in range(self.seq)
+        ]
+        return lax.ppermute(value, AXES, pairs)
+
+    def along(self, value, step):
+        pairs = [
+            (d * self.seq + s, d * self.seq + (s + step) % self.seq)
             for d in range(self.dp)
             for s in range(self.seq)
         ]
@@ -876,21 +942,24 @@
         inner, outer = inner.reshape(width, wide), outer.reshape(width, wide)
         feed_gathered = links.cut(jnp.concatenate([inner, outer], axis=1))
     cotangent_mine = links.turn(after(cotangent.reshape(dims), came))
-    packed, flat, packed_whole, rows_one, vectors = project(spots, came, gathered)
+    packed_whole, output_whole, rows_one, inner_bias_row = unite_attention(spots, gathered, wide)
+    packed, flat = project(came, packed_whole, rows_one)
     context, probs = attend(spots, lengths, packed)
     context = context.reshape(-1, width)
     if direct:
         feed_held = [feed_held[0]] + [after(value, context) for value in feed_held[1:]]
         context = after(context, *feed_held)
         feed_gathered = links.swap(feed_held)
-    normed_one, inverse_one, low, output_whole = settle(spots, context, flat, rows_one, gathered)
+    normed_one, inverse_one, low = settle(context, flat, rows_one, output_whole)
     active, slope, normed_two, inverse_two, output, inner_whole, outer_whole = feed(
-        spots, low, vectors, normed_one, rows_one, feed_gathered, dims
+        spots, low, inner_bias_row, normed_one, rows_one, feed_gathered, dims
     )
     cotangent_mine = after(cotangent_mine, slope)
     output = after(output, cotangent_mine)
     cotangent_mine = after(cotangent_mine, output)
-    keep_inner, send_inner, keep_outer, send_outer, hidden_grad = feed_back(
+    (
+        keep_inner, send_inner, keep_outer, send_outer, keep_vectors, send_vectors, hidden_grad,
+    ) = feed_back(
         spots,
         cotangent_mine,
         normed_two,
@@ -902,17 +971,23 @@
         active,
         slope,
     )
-    output = after(links.turn(output), hidden_grad)
-    send_inner, send_outer = after(send_inner, output), after(send_outer, output)
-    hidden_grad = after(hidden_grad, send_inner, send_outer)
+    hidden_grad = after(hidden_grad, send_inner, send_outer, send_vectors)
     first_up, context_grad, keep_output, send_output, sums = settle_back(
         spots, hidden_grad, normed_one, inverse_one, rows_one, context, output_whole
     )
+    output = after(links.turn(output), sums)
+    context_grad = after(context_grad, output)
     if direct:
         inner_came = after(links.across(send_inner, 1), sums)
         outer_came = after(links.across(send_outer, 1), sums)
         output_came = links.across(send_output, 1)
-        pairs = [(keep_outer, outer_came), (keep_output, output_came), (keep_inner, inner_came)]
+        vectors_came = after(links.across(send_vectors, 1), sums)
+        pairs = [
+            (keep_outer, outer_came),
+            (keep_output, output_came),
+            (keep_inner, inner_came),
+            (keep_vectors, vectors_came),
+        ]
         feed_sums = list(chip_sums("feed_chip_sums", spots, pairs, seq, small))
         context_grad = after(context_grad, *feed_sums[1:])
         feed_sums[1:] = [links.across(feed_sums[part], 2 * part) for part in range(1, PARTS)]
@@ -935,34 +1010,43 @@
         attention_sums[1:] = [
             links.across(attention_sums[part], 2 * part) for part in range(1, PARTS)
         ]
-        attention_total = total_of("attention_total", attention_sums)
+        attention_total = total_pieces("attention_total", spots, attention_sums)
     else:
         reduced = [
             links.reduce_whole(*pair)
-            for pair in ((keep_outer, send_outer), (keep_output, send_output), (keep_inner, send_inner))
+            for pair in (
+                (keep_outer, send_outer),
+                (keep_output, send_output),
+                (keep_inner, send_inner),
+                (keep_vectors, send_vectors),
+            )
         ]
         reduced[0] = reduced[0].reshape(seq, per, small, width).swapaxes(1, 2)
         reduced[0] = reduced[0].reshape(seq, small, per * width)
         feed_total = jnp.concatenate(reduced, axis=2)
         attention_total = links.reduce_whole(keep, send)
+        attention_total = [block_at(attention_total, (spots[0] + i) % seq) for i in range(seq)]
     feed_total = links.turn(feed_total)
-    attention_total = links.turn(after(attention_total, feed_total))
+    attention_total = [
+        links.along(piece, step) if step else piece for step, piece in enumerate(attention_total)
+    ]
     (
         outer_grad, output_grad, inner_grad,
         outer_bias_grad, second_gain_grad, second_shift_grad, inner_bias_grad,
     ) = finish(
         "finish_feed",
-        feed_total,
+        [feed_total],
         [(per, width), (1, width), (1, wide)],
         [(0, 1), (1, 1), (2, 1), (3, per)],
     )
+    tokens_grad = widen(tokens_grad)
+    attention_total[1:] = [after(piece, inner_grad, tokens_grad) for piece in attention_total[1:]]
     (
         packed_weight_grad,
         query_bias_grad, value_bias_grad, output_bias_grad, first_gain_grad, first_shift_grad,
     ) = finish(
         "finish_attention", attention_total, [(1, 3 * width)], [(i, 1) for i in range(5)]
     )
-    tokens_grad = widen(tokens_grad)
     return (
         output.reshape(tokens.shape),
         tokens_grad.reshape(tokens.shape),

time: 364 us -> 349 us (0.959)
  waiting for transfers between devices: 125 us -> 106 us
    all_to_all x8 -> x7, waiting for transfers between devices: 62.6 us -> 43 us  [turn(): lax.all_to_all(blocks, 'seq', split_axis=0, concat_axis=0, tiled=True)]
    pallas_call x4 -> x6, Pallas kernels: 22.1 us -> 30.3 us  [the longest x1 9.33 us: settle_back(): kernel(settle_back_body, 'settle_back', 10 ** 12, 16 * count * width, gri...]
    ppermute x0 -> x3, starting transfers between devices: none -> 4.57 us  [along(): return lax.ppermute(value, AXES, pairs)]
    pallas_call x2 -> x1, Pallas kernels: 8.04 us -> 4.45 us  [total_of(): kernel(total_body, name, flops, 2 * (len(values) + 1) * seq * small * wid...]
    all_to_all x8 -> x7, starting transfers between devices: 34.5 us -> 32.6 us  [turn(): lax.all_to_all(blocks, 'seq', split_axis=0, concat_axis=0, tiled=True)]
    unnamed x46 -> x50, local copies, waits for them, and re-layouts: 10.5 us -> 11.9 us
    ppermute x24 -> x25, starting transfers between devices: 17.7 us -> 17.8 us  [across(): return lax.ppermute(value, AXES, pairs)]
    ppermute x24 -> x25, waiting for transfers between devices: 62.3 us -> 62.3 us  [across(): return lax.ppermute(value, AXES, pairs)]
  transfers between devices with their start and end apart: 32 -> 35, of which waited for: 12 -> 14; matrix products, arithmetic and copies ran while one was open for 1% -> 1% of each run, Pallas kernels for 44% -> 48%
where the time goes in v5:
time: 349 us; the launch traced here: 347 us
  Pallas kernels  169 us (48%)
  waiting for transfers between devices  106 us (30%)
  starting transfers between devices  55 us (16%)
  local copies, waits for them, and re-layouts  11.9 us (3%)
  other arithmetic  3.94 us (1%)
    ppermute x25, waiting for transfers between devices, across(): return lax.ppermute(value, AXES, pairs)  62.3 us
    all_to_all x7, waiting for transfers between devices, turn(): lax.all_to_all(blocks, 'seq', split_axis=0, concat_axis=0, tiled=True)  43 us
    all_to_all x7, starting transfers between devices, turn(): lax.all_to_all(blocks, 'seq', split_axis=0, concat_axis=0, tiled=True)  32.6 us
    pallas_call x1, Pallas kernels, feed_back(): kernel(feed_back_body, 'feed_back', 8 * count * width * wide, 12 * count...  31.2 us
    pallas_call x1, Pallas kernels, feed(): kernel(feed_body, 'feed', 4 * count * width * wide, 12 * count * wide, gr...  26.6 us
    pallas_call x1, Pallas kernels, attend_back(): kernel(attend_back_body, 'attend_back', rows * pairs * 16 * length * leng...  20.9 us
    ppermute x25, starting transfers between devices, across(): return lax.ppermute(value, AXES, pairs)  17.8 us
    pallas_call x1, Pallas kernels, attend(): kernel(attend_body, 'attend', rows * pairs * 16 * length * length * LANES...  16.2 us
  transfers between devices with their start and end apart: 35, of which 14 were waited for; matrix products, arithmetic and copies ran while one was open for 1% of the time, Pallas kernels for 48%

profile of v5, /device:TPU:0, one launch (start us, length us, event | category | flops | bytes accessed | tf_op | source)
XLA Modules:
  0.0 346.9 jit_solution(10497245079894185935)
XLA Ops:
  2.6 6.3 %all-to-all-start = ((bf16[4,24,3200]{2,1,0:T(8,128)(2,1)}), bf16[4,24,3200]{2,1,0:T(8,128)(2,1)S(1)}, u32[]{:S(2)}, u32[]{:S(2)}) async-start(bf16[4,24,3200]{2,1,0:T(8,128)(2,1)} %prepare_attention.1), calls=%async_computation | async-start | bytes 1228800 | tf_op jit(solution)/shard_map/all_to_all | solution.py:865
  11.1 14.3 %all-to-all-done = bf16[4,24,3200]{2,1,0:T(8,128)(2,1)S(1)} async-done(((bf16[4,24,3200]{2,1,0:T(8,128)(2,1)}), bf16[4,24,3200]{2,1,0:T(8,128)(2,1)S(1)}, u32[]{:S(2)}, u32[]{:S(2)}) %all-to-all-start) | async-done | bytes 614432 | tf_op jit(solution)/shard_map/all_to_all | solution.py:865
  25.4 3.5 %all-to-all-start.1 = ((bf16[4,24,6144]{2,1,0:T(8,128)(2,1)}), bf16[4,24,6144]{2,1,0:T(8,128)(2,1)S(1)}, u32[]{:S(2)}, u32[]{:S(2)}) async-start(bf16[4,24,6144]{2,1,0:T(8,128)(2,1)} %prepare_feed.1), calls=%async_computation.1 | async-start | bytes 2359296 | tf_op jit(solution)/shard_map/all_to_all | solution.py:865
  32.5 14.2 %collective-permute-done.2 = bf16[4,24,3200]{2,1,0:T(8,128)(2,1)S(1)} collective-permute-done((bf16[4,24,3200]{2,1,0:T(8,128)(2,1)S(1)}, bf16[4,24,3200]{2,1,0:T(8,128)(2,1)S(1)}, u32[]{:S(2)}, u32[]{:S(2)}) %collective-permute-start.2) | collective-permute-done | bytes 614432 | tf_op jit(solution)/shard_map/ppermute | solution.py:846
  46.7 11.2 %collective-permute-done.1 = bf16[4,24,3200]{2,1,0:T(8,128)(2,1)S(1)} collective-permute-done((bf16[4,24,3200]{2,1,0:T(8,128)(2,1)S(1)}, bf16[4,24,3200]{2,1,0:T(8,128)(2,1)S(1)}, u32[]{:S(2)}, u32[]{:S(2)}) %collective-permute-start.1) | collective-permute-done | bytes 614432 | tf_op jit(solution)/shard_map/ppermute | solution.py:846
  58.7 4.7 %all-to-all-start.2 = ((bf16[4,2,128,768]{3,2,1,0:T(8,128)(2,1)}), bf16[4,2,128,768]{3,2,1,0:T(8,128)(2,1)S(1)}, u32[]{:S(2)}, u32[]{:S(2)}) async-start(bf16[4,2,128,768]{3,2,1,0:T(8,128)(2,1)} %bitcast.3), calls=%async_computation.2 | async-start | bytes 3145728 | tf_op jit(solution)/shard_map/all_to_all | solution.py:865
  70.9 5.9 %unite_attention.1 = (bf16[768,2304]{1,0:T(8,128)(2,1)}, bf16[768,768]{1,0:T(8,128)(2,1)}, f32[8,768]{1,0:T(8,128)}, f32[1,3072]{1,0:T(1,128)}) custom-call(s32[3]{0:T(128)} %pad_add_fusion.spots, bf16[96,3200]{1,0:T(8,128)(2,1)} %bitcast.72, bf16[96,3200]{1,0:T(8,128)(2,1)} %bitcast.14.refs_1_, bf16[96,3200]{1,0:T(8,128)(2,1)} %bitcast.87, ...), custom_call_target="tpu_custom_call" | custom-call | bytes 9830400 | tf_op jit(solution)/shard_map/unite_attention/pallas_call | solution.py:174
  76.9 23.8 %all-to-all-done.2.tokens = bf16[4,2,128,768]{3,2,1,0:T(8,128)(2,1)S(1)} async-done(((bf16[4,2,128,768]{3,2,1,0:T(8,128)(2,1)}), bf16[4,2,128,768]{3,2,1,0:T(8,128)(2,1)S(1)}, u32[]{:S(2)}, u32[]{:S(2)}) %all-to-all-start.2) | async-done | bytes 1572896 | tf_op jit(solution)/shard_map/all_to_all | solution.py:865
  101.8 4.5 %all-to-all-start.3 = ((bf16[4,2,128,768]{3,2,1,0:T(8,128)(2,1)}), bf16[4,2,128,768]{3,2,1,0:T(8,128)(2,1)}, u32[]{:S(2)}, u32[]{:S(2)}) async-start(bf16[4,2,128,768]{3,2,1,0:T(8,128)(2,1)} %bitcast.26), calls=%async_computation.3 | async-start | bytes 3145728 | tf_op jit(solution)/shard_map/all_to_all | solution.py:865
  106.4 7.8 %project.1 = (bf16[2,512,2304]{2,1,0:T(8,128)(2,1)}, bf16[1024,768]{1,0:T(8,128)(2,1)}) custom-call(bf16[4,2,128,768]{3,2,1,0:T(8,128)(2,1)} %copy-done.6, bf16[768,2304]{1,0:T(8,128)(2,1)} %get-tuple-element.102.weight, f32[8,768]{1,0:T(8,128)} %get-tuple-element.103.rows.rows_one), custom_call_target="tpu_custom_call" | custom-call | flops 3623878656 | bytes 6291456 | tf_op jit(solution)/shard_map/project/pallas_call | solution.py:210
  114.2 16.2 %attend.1 = (bf16[2,512,768]{2,1,0:T(8,128)(2,1)}, bf16[2,12,512,512]{3,2,1,0:T(8,128)(2,1)}) custom-call(s32[3]{0:T(128)} %pad_add_fusion.spots, s32[8,4]{1,0:T(8,128)} %copy.31.lengths, bf16[2,512,2304]{2,1,0:T(8,128)(2,1)} %get-tuple-element.104.query.key.value, bf16[2,512,2304]{2,1,0:T(8,128)(2,1)} %get-tuple-element.104.query.key.value, ...), custom_call_target="tpu_custom_call" | custom-call | flops 6442450944 | bytes 25165824 | tf_op jit(solution)/shard_map/attend/pallas_call | solution.py:272
  131.1 5.7 %settle.1 = (f32[1024,768]{1,0:T(8,128)}, f32[1024,1]{1,0:T(8,128)}, bf16[1024,768]{1,0:T(8,128)(2,1)}) custom-call(bf16[1024,768]{1,0:T(8,128)(2,1)} %bitcast.110, bf16[1024,768]{1,0:T(8,128)(2,1)} %get-tuple-element.110.tokens, f32[8,768]{1,0:T(8,128)} %get-tuple-element.103.rows.rows_one, bf16[768,768]{1,0:T(8,128)(2,1)} %get-tuple-element.111.weight), custom_call_target="tpu_custom_call" | custom-call | flops 1207959552 | bytes 7864320 | tf_op jit(solution)/shard_map/settle/pallas_call | solution.py:370
  138.2 26.6 %feed.1 = (bf16[1024,3072]{1,0:T(8,128)(2,1)}, bf16[1024,3072]{1,0:T(8,128)(2,1)}, f32[1024,768]{1,0:T(8,128)}, f32[1024,1]{1,0:T(8,128)}, bf16[4,2,128,768]{3,2...) custom-call(s32[3]{0:T(128)} %pad_add_fusion.spots, bf16[1024,768]{1,0:T(8,128)(2,1)} %get-tuple-element.112.low, ...), custom_call_target="tpu_custom_call" | custom-call | flops 9663676416 | bytes 37748736 | tf_op jit(solution)/shard_map/feed/pallas_call | solution.py:468
  164.8 4.9 %all-to-all-start.4 = ((bf16[4,2,128,768]{3,2,1,0:T(8,128)(2,1)}), bf16[4,2,128,768]{3,2,1,0:T(8,128)(2,1)}, u32[]{:S(2)}, u32[]{:S(2)}) async-start(bf16[4,2,128,768]{3,2,1,0:T(8,128)(2,1)} %get-tuple-element.119), calls=%async_computation.4 | async-start | bytes 3145728 | tf_op jit(solution)/shard_map/all_to_all | solution.py:865
  169.6 31.2 %feed_back.1 = (bf16[4,96,3072]{2,1,0:T(8,128)(2,1)}, bf16[4,96,3072]{2,1,0:T(8,128)(2,1)}, bf16[4,384,768]{2,1,0:T(8,128)(2,1)}, bf16[4,384,768]{2,1,0:T(8,128)...) custom-call(s32[3]{0:T(128)} %pad_add_fusion.spots, ...), custom_call_target="tpu_custom_call" | custom-call | flops 19327352832 | bytes 37748736 | tf_op jit(solution)/shard_map/feed_back/pallas_call | solution.py:565
  201.5 9.3 %settle_back.1 = (f32[1024,768]{1,0:T(8,128)}, bf16[1024,768]{1,0:T(8,128)(2,1)}, bf16[4,96,768]{2,1,0:T(8,128)(2,1)}, bf16[4,96,768]{2,1,0:T(8,128)(2,1)}, f32[8,768]{1,0:T(8,128)}) custom-call(s32[3]{0:T(128)} %pad_add_fusion.spots, f32[1024,768]{1,0:T(8,128)} %get-tuple-element.130.hidden_grad, f32[1024,768]{1,0:T(8,128)} %get-tuple-element.114.normed_one.normed, ...), custom_call_target="tpu_custom_call" | custom-call | flops 999999995904 | bytes 12582912 | tf_op jit(solution)/shard_map/settle_back/pallas_call | solution.py:621
  213.9 8.0 %feed_chip_sums.1 = (bf16[4,24,7040]{2,1,0:T(8,128)(2,1)}, bf16[4,24,7040]{2,1,0:T(8,128)(2,1)}, bf16[4,24,7040]{2,1,0:T(8,128)(2,1)}, bf16[4,24,7040]{2,1,0:T(8,128)(2,1)}) custom-call(s32[3]{0:T(128)} %pad_add_fusion.spots, bf16[4,4,96,768]{3,2,1,0:T(8,128)(2,1)} %bitcast.54, bf16[4,4,96,768]{3,2,1,0:T(8,128)(2,1)} %bitcast.29.refs_1_.refs_3_.refs_5_.refs_7_, ...), custom_call_target="tpu_custom_call" | custom-call | bytes 16220160 | tf_op jit(solution)/shard_map/feed_chip_sums/pallas_call | solution.py:731
  225.4 20.9 %attend_back.1 = (bf16[2,512,2304]{2,1,0:T(8,128)(2,1)}, f32[2,1,2304]{2,1,0:T(1,128)}) custom-call(bf16[2,512,2304]{2,1,0:T(8,128)(2,1)} %get-tuple-element.104.query.key.value, bf16[2,512,2304]{2,1,0:T(8,128)(2,1)} %get-tuple-element.104.query.key.value, bf16[2,512,2304]{2,1,0:T(8,128)(2,1)} %get-tuple-element.104.query.key.value, ...), custom_call_target="tpu_custom_call" | custom-call | flops 6442450944 | bytes 25165824 | tf_op jit(solution)/shard_map/attend_back/pallas_call | solution.py:323
  246.3 8.4 %tokens_back.1 = bf16[4,2,128,768]{3,2,1,0:T(8,128)(2,1)} custom-call(bf16[1024,2304]{1,0:T(8,128)(2,1)} %bitcast.97, bf16[768,2304]{1,0:T(8,128)(2,1)} %get-tuple-element.102.weight, f32[1024,768]{1,0:T(8,128)} %get-tuple-element.150.first_up), custom_call_target="tpu_custom_call" | custom-call | flops 3623878656 | bytes 6291456 | tf_op jit(solution)/shard_map/tokens_back/pallas_call | solution.py:651
  254.8 5.1 %all-to-all-start.5 = ((bf16[4,2,128,768]{3,2,1,0:T(8,128)(2,1)}), bf16[4,2,128,768]{3,2,1,0:T(8,128)(2,1)}, u32[]{:S(2)}, u32[]{:S(2)}) async-start(bf16[4,2,128,768]{3,2,1,0:T(8,128)(2,1)} %tokens_back.1), calls=%async_computation.5 | async-start | bytes 3145728 | tf_op jit(solution)/shard_map/all_to_all | solution.py:865
  259.9 8.6 %weights_back.1 = (bf16[4,96,2432]{2,1,0:T(8,128)(2,1)}, bf16[4,96,2432]{2,1,0:T(8,128)(2,1)}) custom-call(s32[3]{0:T(128)} %pad_add_fusion.spots, bf16[1024,2304]{1,0:T(8,128)(2,1)} %bitcast.98, bf16[1024,768]{1,0:T(8,128)(2,1)} %get-tuple-element.110.tokens, f32[2,1,2304]{2,1,0:T(1,128)} %get-tuple-element.152.packed_sums, f32[8,768]{1,0:T(8,128)} %get-tuple-element.132.sums), custom_call_target="tpu_custom_call" | custom-call | flops 3623878656 | bytes 6291456 | tf_op jit(solution)/shard_map/weights_back/pallas_call | solution.py:687
  268.5 15.6 %collective-permute-done.20.refs_2_ = bf16[4,24,7040]{2,1,0:T(8,128)(2,1)S(1)} collective-permute-done((bf16[4,24,7040]{2,1,0:T(8,128)(2,1)}, bf16[4,24,7040]{2,1,0:T(8,128)(2,1)S(1)}, u32[]{:S(2)}, u32[]{:S(2)}) %collective-permute-start.20) | collective-permute-done | bytes 1351712 | tf_op jit(solution)/shard_map/ppermute | solution.py:846
  285.2 4.5 %feed_total.1 = bf16[4,24,7040]{2,1,0:T(8,128)(2,1)} custom-call(bf16[4,24,7040]{2,1,0:T(8,128)(2,1)} %get-tuple-element.155.refs_0_, bf16[4,24,7040]{2,1,0:T(8,128)(2,1)} %copy-done.17, bf16[4,24,7040]{2,1,0:T(8,128)(2,1)} %copy-done.18, bf16[4,24,7040]{2,1,0:T(8,128)(2,1)} %collective-permute-done.21.refs_3_), custom_call_target="tpu_custom_call" | custom-call | flops 999999995904 | bytes 6758400 | tf_op jit(solution)/shard_map/feed_total/pallas_call | solution.py:756
  289.6 4.8 %attention_chip_sums.1 = (bf16[4,24,2432]{2,1,0:T(8,128)(2,1)}, bf16[4,24,2432]{2,1,0:T(8,128)(2,1)}, bf16[4,24,2432]{2,1,0:T(8,128)(2,1)}, bf16[4,24,2432]{2,1,0:T(8,128)(2,1)}) custom-call(s32[3]{0:T(128)} %pad_add_fusion.spots, bf16[4,4,24,2432]{3,2,1,0:T(8,128)(2,1)} %bitcast.58, bf16[4,4,24,2432]{3,2,1,0:T(8,128)(2,1)} %bitcast.40.refs_1_.refs_3_.refs_5_.refs_7_, ...), custom_call_target="tpu_custom_call" | custom-call | bytes 5603328 | tf_op jit(solution)/shard_map/attention_chip_sums/pallas_call | solution.py:731
  296.4 3.5 %all-to-all-start.6 = ((bf16[4,24,7040]{2,1,0:T(8,128)(2,1)}), bf16[4,24,7040]{2,1,0:T(8,128)(2,1)S(1)}, u32[]{:S(2)}, u32[]{:S(2)}) async-start(bf16[4,24,7040]{2,1,0:T(8,128)(2,1)} %feed_total.1), calls=%async_computation.6 | async-start | bytes 2703360 | tf_op jit(solution)/shard_map/all_to_all | solution.py:865
  303.5 10.3 %collective-permute-done.22.refs_1_.refs_5_.refs_9_.refs_13_ = bf16[4,24,2432]{2,1,0:T(8,128)(2,1)S(1)} collective-permute-done((bf16[4,24,2432]{2,1,0:T(8,128)(2,1)}, bf16[4,24,2432]{2,1,0:T(8,128)(2,1)S(1)}, u32[]{:S(2)}, u32[]{:S(2)}) %collective-permute-start.22) | collective-permute-done | bytes 466976 | tf_op jit(solution)/shard_map/ppermute | solution.py:846
  313.9 9.0 %collective-permute-done.23.refs_2_.refs_6_.refs_10_.refs_14_ = bf16[4,24,2432]{2,1,0:T(8,128)(2,1)S(1)} collective-permute-done((bf16[4,24,2432]{2,1,0:T(8,128)(2,1)S(1)}, bf16[4,24,2432]{2,1,0:T(8,128)(2,1)S(1)}, u32[]{:S(2)}, u32[]{:S(2)}) %collective-permute-start.23) | collective-permute-done | bytes 466976 | tf_op jit(solution)/shard_map/ppermute | solution.py:846
  323.8 3.1 attention_total.1
  326.9 3.4 collective-permute-start.27
  331.5 3.4 convert_element_type.3
  334.8 2.9 all-to-all-done.6.refs_0_
  344.2 2.7 copy.33
  (108 shorter events, 41.5 us)
Async XLA Ops:
  2.6 22.7 %all-to-all-start = ((bf16[4,24,3200]{2,1,0:T(8,128)(2,1)}), bf16[4,24,3200]{2,1,0:T(8,128)(2,1)S(1)}, u32[]{:S(2)}, u32[]{:S(2)}) async-start(bf16[4,24,3200]{2,1,0:T(8,128)(2,1)} %prepare_attention.1), calls=%async_computation | async-start | bytes 1228800 | tf_op jit(solution)/shard_map/all_to_all | solution.py:865
  25.4 33.3 %all-to-all-start.1 = ((bf16[4,24,6144]{2,1,0:T(8,128)(2,1)}), bf16[4,24,6144]{2,1,0:T(8,128)(2,1)S(1)}, u32[]{:S(2)}, u32[]{:S(2)}) async-start(bf16[4,24,6144]{2,1,0:T(8,128)(2,1)} %prepare_feed.1), calls=%async_computation.1 | async-start | bytes 2359296 | tf_op jit(solution)/shard_map/all_to_all | solution.py:865
  28.9 17.8 %collective-permute-start.2 = (bf16[4,24,3200]{2,1,0:T(8,128)(2,1)S(1)}, bf16[4,24,3200]{2,1,0:T(8,128)(2,1)S(1)}, u32[]{:S(2)}, u32[]{:S(2)}) collective-permute-start(bf16[4,24,3200]{2,1,0:T(8,128)(2,1)S(1)} %all-to-all-done), channel_id=1, source_target_pairs={{0,24},{1,25},{2,26},{3,27},{4,28},{5,29},{6,30},{7,31},{8,16},{9,... | collective-permute-start | bytes 1843208 | tf_op jit(solution)/shard_map/ppermute | solution.py:846
  31.4 26.4 %collective-permute-start.1 = (bf16[4,24,3200]{2,1,0:T(8,128)(2,1)S(1)}, bf16[4,24,3200]{2,1,0:T(8,128)(2,1)S(1)}, u32[]{:S(2)}, u32[]{:S(2)}) collective-permute-start(bf16[4,24,3200]{2,1,0:T(8,128)(2,1)S(1)} %all-to-all-done), channel_id=1, source_target_pairs={{0,16},{1,17},{2,18},{3,19},{4,20},{5,21},{6,22},{7,23},{8,24},{9,... | collective-permute-start | bytes 1843208 | tf_op jit(solution)/shard_map/ppermute | solution.py:846
  31.9 26.8 %collective-permute-start = (bf16[4,24,3200]{2,1,0:T(8,128)(2,1)S(1)}, bf16[4,24,3200]{2,1,0:T(8,128)(2,1)}, u32[]{:S(2)}, u32[]{:S(2)}) collective-permute-start(bf16[4,24,3200]{2,1,0:T(8,128)(2,1)S(1)} %all-to-all-done), channel_id=1, source_target_pairs={{0,8},{1,9},{2,10},{3,11},{4,12},{5,13},{6,14},{7,15},{8,0},{9,1},... | collective-permute-start | bytes 1843208 | tf_op jit(solution)/shard_map/ppermute | solution.py:846
  58.7 42.0 %all-to-all-start.2 = ((bf16[4,2,128,768]{3,2,1,0:T(8,128)(2,1)}), bf16[4,2,128,768]{3,2,1,0:T(8,128)(2,1)S(1)}, u32[]{:S(2)}, u32[]{:S(2)}) async-start(bf16[4,2,128,768]{3,2,1,0:T(8,128)(2,1)} %bitcast.3), calls=%async_computation.2 | async-start | bytes 3145728 | tf_op jit(solution)/shard_map/all_to_all | solution.py:865
  63.4 4.0 %collective-permute-start.6 = (bf16[96,3200]{1,0:T(8,128)(2,1)}, bf16[96,3200]{1,0:T(8,128)(2,1)S(1)}, u32[]{:S(2)}, u32[]{:S(2)}) collective-permute-start(bf16[96,3200]{1,0:T(8,128)(2,1)} %bitcast.84), channel_id=1, source_target_pairs={{0,4},{1,5},{2,6},{3,7},{4,0},{5,1},{6,2},{7,3},{8,12},{9,13},{10,... | collective-permute-start | bytes 1843208 | tf_op jit(solution)/shard_map/ppermute | solution.py:846
  64.0 6.9 %collective-permute-start.5 = (bf16[96,3200]{1,0:T(8,128)(2,1)}, bf16[96,3200]{1,0:T(8,128)(2,1)}, u32[]{:S(2)}, u32[]{:S(2)}) collective-permute-start(bf16[96,3200]{1,0:T(8,128)(2,1)} %bitcast.86), channel_id=1, source_target_pairs={{0,4},{1,5},{2,6},{3,7},{4,0},{5,1},{6,2},{7,3},{8,12},{9,13},{10,... | collective-permute-start | bytes 1843208 | tf_op jit(solution)/shard_map/ppermute | solution.py:846
  64.0 6.8 %collective-permute-start.4 = (bf16[96,3200]{1,0:T(8,128)(2,1)}, bf16[96,3200]{1,0:T(8,128)(2,1)}, u32[]{:S(2)}, u32[]{:S(2)}) collective-permute-start(bf16[96,3200]{1,0:T(8,128)(2,1)} %bitcast.14.refs_1_), channel_id=1, source_target_pairs={{0,4},{1,5},{2,6},{3,7},{4,0},{5,1},{6,2},{7,3},{8,12},{9,13},{10,... | collective-permute-start | bytes 1843208 | tf_op jit(solution)/shard_map/ppermute | solution.py:846
  64.5 65.9 %collective-permute-start.9 = (bf16[4,24,6144]{2,1,0:T(8,128)(2,1)S(1)}, bf16[4,24,6144]{2,1,0:T(8,128)(2,1)}, u32[]{:S(2)}, u32[]{:S(2)}) collective-permute-start(bf16[4,24,6144]{2,1,0:T(8,128)(2,1)S(1)} %all-to-all-done.1.refs_8_), channel_id=1, source_target_pairs={{0,24},{1,25},{2,26},{3,27},{4,28},{5,29},{6,30},{7,31},{8,16},{9,... | collective-permute-start | bytes 3538952 | tf_op jit(solution)/shard_map/ppermute | solution.py:846
  66.2 64.2 %collective-permute-start.8 = (bf16[4,24,6144]{2,1,0:T(8,128)(2,1)S(1)}, bf16[4,24,6144]{2,1,0:T(8,128)(2,1)}, u32[]{:S(2)}, u32[]{:S(2)}) collective-permute-start(bf16[4,24,6144]{2,1,0:T(8,128)(2,1)S(1)} %all-to-all-done.1.refs_8_), channel_id=1, source_target_pairs={{0,16},{1,17},{2,18},{3,19},{4,20},{5,21},{6,22},{7,23},{8,24},{9,... | collective-permute-start | bytes 3538952 | tf_op jit(solution)/shard_map/ppermute | solution.py:846
  68.3 62.2 %collective-permute-start.7 = (bf16[4,24,6144]{2,1,0:T(8,128)(2,1)S(1)}, bf16[4,24,6144]{2,1,0:T(8,128)(2,1)}, u32[]{:S(2)}, u32[]{:S(2)}) collective-permute-start(bf16[4,24,6144]{2,1,0:T(8,128)(2,1)S(1)} %all-to-all-done.1.refs_8_), channel_id=1, source_target_pairs={{0,8},{1,9},{2,10},{3,11},{4,12},{5,13},{6,14},{7,15},{8,0},{9,1},... | collective-permute-start | bytes 3538952 | tf_op jit(solution)/shard_map/ppermute | solution.py:846
  76.8 60.0 %collective-permute-start.10 = (bf16[96,6144]{1,0:T(8,128)(2,1)S(1)}, bf16[96,6144]{1,0:T(8,128)(2,1)}, u32[]{:S(2)}, u32[]{:S(2)}) collective-permute-start(bf16[96,6144]{1,0:T(8,128)(2,1)S(1)} %bitcast.82), channel_id=1, source_target_pairs={{0,4},{1,5},{2,6},{3,7},{4,0},{5,1},{6,2},{7,3},{8,12},{9,13},{10,... | collective-permute-start | bytes 3538952 | tf_op jit(solution)/shard_map/ppermute | solution.py:846
  101.8 62.9 %all-to-all-start.3 = ((bf16[4,2,128,768]{3,2,1,0:T(8,128)(2,1)}), bf16[4,2,128,768]{3,2,1,0:T(8,128)(2,1)}, u32[]{:S(2)}, u32[]{:S(2)}) async-start(bf16[4,2,128,768]{3,2,1,0:T(8,128)(2,1)} %bitcast.26), calls=%async_computation.3 | async-start | bytes 3145728 | tf_op jit(solution)/shard_map/all_to_all | solution.py:865
  130.4 6.4 %collective-permute-start.11 = (bf16[96,6144]{1,0:T(8,128)(2,1)}, bf16[96,6144]{1,0:T(8,128)(2,1)S(1)}, u32[]{:S(2)}, u32[]{:S(2)}) collective-permute-start(bf16[96,6144]{1,0:T(8,128)(2,1)} %bitcast.19.refs_1_), channel_id=1, source_target_pairs={{0,4},{1,5},{2,6},{3,7},{4,0},{5,1},{6,2},{7,3},{8,12},{9,13},{10,... | collective-permute-start | bytes 3538952 | tf_op jit(solution)/shard_map/ppermute | solution.py:846
  130.5 6.4 %collective-permute-start.12 = (bf16[96,6144]{1,0:T(8,128)(2,1)}, bf16[96,6144]{1,0:T(8,128)(2,1)S(1)}, u32[]{:S(2)}, u32[]{:S(2)}) collective-permute-start(bf16[96,6144]{1,0:T(8,128)(2,1)} %bitcast.20.refs_2_), channel_id=1, source_target_pairs={{0,4},{1,5},{2,6},{3,7},{4,0},{5,1},{6,2},{7,3},{8,12},{9,13},{10,... | collective-permute-start | bytes 3538952 | tf_op jit(solution)/shard_map/ppermute | solution.py:846
  131.0 6.1 %collective-permute-start.13 = (bf16[96,6144]{1,0:T(8,128)(2,1)}, bf16[96,6144]{1,0:T(8,128)(2,1)}, u32[]{:S(2)}, u32[]{:S(2)}) collective-permute-start(bf16[96,6144]{1,0:T(8,128)(2,1)} %bitcast.21.refs_3_), channel_id=1, source_target_pairs={{0,4},{1,5},{2,6},{3,7},{4,0},{5,1},{6,2},{7,3},{8,12},{9,13},{10,... | collective-permute-start | bytes 3538952 | tf_op jit(solution)/shard_map/ppermute | solution.py:846
  164.8 60.7 %all-to-all-start.4 = ((bf16[4,2,128,768]{3,2,1,0:T(8,128)(2,1)}), bf16[4,2,128,768]{3,2,1,0:T(8,128)(2,1)}, u32[]{:S(2)}, u32[]{:S(2)}) async-start(bf16[4,2,128,768]{3,2,1,0:T(8,128)(2,1)} %get-tuple-element.119), calls=%async_computation.4 | async-start | bytes 3145728 | tf_op jit(solution)/shard_map/all_to_all | solution.py:865
  200.9 12.1 %collective-permute-start.16 = (bf16[4,96,3072]{2,1,0:T(8,128)(2,1)}, bf16[4,96,3072]{2,1,0:T(8,128)(2,1)}, u32[]{:S(2)}, u32[]{:S(2)}) collective-permute-start(bf16[4,96,3072]{2,1,0:T(8,128)(2,1)} %get-tuple-element.127), channel_id=1, source_target_pairs={{0,4},{1,5},{2,6},{3,7},{4,0},{5,1},{6,2},{7,3},{8,12},{9,13},{10,... | collective-permute-start | bytes 7077896 | tf_op jit(solution)/shard_map/ppermute | solution.py:846
  201.1 11.9 %collective-permute-start.14 = (bf16[4,384,768]{2,1,0:T(8,128)(2,1)}, bf16[4,384,768]{2,1,0:T(8,128)(2,1)}, u32[]{:S(2)}, u32[]{:S(2)}) collective-permute-start(bf16[4,384,768]{2,1,0:T(8,128)(2,1)} %get-tuple-element.128), channel_id=1, source_target_pairs={{0,4},{1,5},{2,6},{3,7},{4,0},{5,1},{6,2},{7,3},{8,12},{9,13},{10,... | collective-permute-start | bytes 7077896 | tf_op jit(solution)/shard_map/ppermute | solution.py:846
  221.9 46.6 %collective-permute-start.19 = (bf16[4,24,7040]{2,1,0:T(8,128)(2,1)}, bf16[4,24,7040]{2,1,0:T(8,128)(2,1)S(1)}, u32[]{:S(2)}, u32[]{:S(2)}) collective-permute-start(bf16[4,24,7040]{2,1,0:T(8,128)(2,1)} %get-tuple-element.144), channel_id=1, source_target_pairs={{0,8},{1,9},{2,10},{3,11},{4,12},{5,13},{6,14},{7,15},{8,0},{9,1},... | collective-permute-start | bytes 4055048 | tf_op jit(solution)/shard_map/ppermute | solution.py:846
  223.4 60.6 %collective-permute-start.20 = (bf16[4,24,7040]{2,1,0:T(8,128)(2,1)}, bf16[4,24,7040]{2,1,0:T(8,128)(2,1)S(1)}, u32[]{:S(2)}, u32[]{:S(2)}) collective-permute-start(bf16[4,24,7040]{2,1,0:T(8,128)(2,1)} %get-tuple-element.145), channel_id=1, source_target_pairs={{0,16},{1,17},{2,18},{3,19},{4,20},{5,21},{6,22},{7,23},{8,24},{9,... | collective-permute-start | bytes 4055048 | tf_op jit(solution)/shard_map/ppermute | solution.py:846
  223.5 60.6 %collective-permute-start.21 = (bf16[4,24,7040]{2,1,0:T(8,128)(2,1)}, bf16[4,24,7040]{2,1,0:T(8,128)(2,1)}, u32[]{:S(2)}, u32[]{:S(2)}) collective-permute-start(bf16[4,24,7040]{2,1,0:T(8,128)(2,1)} %get-tuple-element.146), channel_id=1, source_target_pairs={{0,24},{1,25},{2,26},{3,27},{4,28},{5,29},{6,30},{7,31},{8,16},{9,... | collective-permute-start | bytes 4055048 | tf_op jit(solution)/shard_map/ppermute | solution.py:846
  254.8 41.6 %all-to-all-start.5 = ((bf16[4,2,128,768]{3,2,1,0:T(8,128)(2,1)}), bf16[4,2,128,768]{3,2,1,0:T(8,128)(2,1)}, u32[]{:S(2)}, u32[]{:S(2)}) async-start(bf16[4,2,128,768]{3,2,1,0:T(8,128)(2,1)} %tokens_back.1), calls=%async_computation.5 | async-start | bytes 3145728 | tf_op jit(solution)/shard_map/all_to_all | solution.py:865
  268.4 21.2 %collective-permute-start.18 = (bf16[4,96,2432]{2,1,0:T(8,128)(2,1)}, bf16[4,96,2432]{2,1,0:T(8,128)(2,1)}, u32[]{:S(2)}, u32[]{:S(2)}) collective-permute-start(bf16[4,96,2432]{2,1,0:T(8,128)(2,1)} %get-tuple-element.154), channel_id=1, source_target_pairs={{0,4},{1,5},{2,6},{3,7},{4,0},{5,1},{6,2},{7,3},{8,12},{9,13},{10,... | collective-permute-start | bytes 5603336 | tf_op jit(solution)/shard_map/ppermute | solution.py:846
  296.4 41.3 %all-to-all-start.6 = ((bf16[4,24,7040]{2,1,0:T(8,128)(2,1)}), bf16[4,24,7040]{2,1,0:T(8,128)(2,1)S(1)}, u32[]{:S(2)}, u32[]{:S(2)}) async-start(bf16[4,24,7040]{2,1,0:T(8,128)(2,1)} %feed_total.1), calls=%async_computation.6 | async-start | bytes 2703360 | tf_op jit(solution)/shard_map/all_to_all | solution.py:865
  299.9 13.9 %collective-permute-start.22 = (bf16[4,24,2432]{2,1,0:T(8,128)(2,1)}, bf16[4,24,2432]{2,1,0:T(8,128)(2,1)S(1)}, u32[]{:S(2)}, u32[]{:S(2)}) collective-permute-start(bf16[4,24,2432]{2,1,0:T(8,128)(2,1)} %get-tuple-element.161), channel_id=1, source_target_pairs={{0,8},{1,9},{2,10},{3,11},{4,12},{5,13},{6,14},{7,15},{8,0},{9,1},... | collective-permute-start | bytes 1400840 | tf_op jit(solution)/shard_map/ppermute | solution.py:846
  301.5 21.4 %collective-permute-start.23 = (bf16[4,24,2432]{2,1,0:T(8,128)(2,1)S(1)}, bf16[4,24,2432]{2,1,0:T(8,128)(2,1)S(1)}, u32[]{:S(2)}, u32[]{:S(2)}) collective-permute-start(bf16[4,24,2432]{2,1,0:T(8,128)(2,1)S(1)} %copy-done.22), channel_id=1, source_target_pairs={{0,16},{1,17},{2,18},{3,19},{4,20},{5,21},{6,22},{7,23},{8,24},{9,... | collective-permute-start | bytes 1400840 | tf_op jit(solution)/shard_map/ppermute | solution.py:846
  301.8 21.1 %collective-permute-start.24 = (bf16[4,24,2432]{2,1,0:T(8,128)(2,1)S(1)}, bf16[4,24,2432]{2,1,0:T(8,128)(2,1)S(1)}, u32[]{:S(2)}, u32[]{:S(2)}) collective-permute-start(bf16[4,24,2432]{2,1,0:T(8,128)(2,1)S(1)} %copy-done.21), channel_id=1, source_target_pairs={{0,24},{1,25},{2,26},{3,27},{4,28},{5,29},{6,30},{7,31},{8,16},{9,... | collective-permute-start | bytes 1400840 | tf_op jit(solution)/shard_map/ppermute | solution.py:846
  326.9 14.2 %collective-permute-start.27 = (bf16[24,2432]{1,0:T(8,128)(2,1)}, bf16[24,2432]{1,0:T(8,128)(2,1)S(1)}, u32[]{:S(2)}, u32[]{:S(2)}) collective-permute-start(bf16[24,2432]{1,0:T(8,128)(2,1)} %get-tuple-element.171), channel_id=1, source_target_pairs={{0,3},{1,0},{2,1},{3,2},{4,7},{5,4},{6,5},{7,6},{8,11},{9,8},{10,9... | collective-permute-start | bytes 350216 | tf_op jit(solution)/shard_map/ppermute | solution.py:854
  330.3 11.3 %collective-permute-start.26 = (bf16[24,2432]{1,0:T(8,128)(2,1)}, bf16[24,2432]{1,0:T(8,128)(2,1)S(1)}, u32[]{:S(2)}, u32[]{:S(2)}) collective-permute-start(bf16[24,2432]{1,0:T(8,128)(2,1)} %get-tuple-element.169), channel_id=1, source_target_pairs={{0,2},{1,3},{2,0},{3,1},{4,6},{5,7},{6,4},{7,5},{8,10},{9,11},{10,... | collective-permute-start | bytes 350216 | tf_op jit(solution)/shard_map/ppermute | solution.py:854
  330.3 11.3 %collective-permute-start.25 = (bf16[24,2432]{1,0:T(8,128)(2,1)}, bf16[24,2432]{1,0:T(8,128)(2,1)S(1)}, u32[]{:S(2)}, u32[]{:S(2)}) collective-permute-start(bf16[24,2432]{1,0:T(8,128)(2,1)} %get-tuple-element.165), channel_id=1, source_target_pairs={{0,1},{1,2},{2,3},{3,0},{4,5},{5,6},{6,7},{7,4},{8,9},{9,10},{10,1... | collective-permute-start | bytes 350216 | tf_op jit(solution)/shard_map/ppermute | solution.py:854
  (27 other events, 147.5 us)

commit v6 on v5

--- a/solution.py
+++ b/solution.py
@@ -509,7 +509,7 @@
 def feed_back_body(
     spots, cotangent, normed_two, inverse_two, rows_one, low, inner_weight, outer_weight, active, slope,
     keep_inner, send_inner, keep_outer, send_outer, keep_vectors, send_vectors, hidden_grad,
-    up, made, columns,
+    up, made, columns, pre, grads,
 ):
     step, steps, side = pl.program_id(0), pl.num_programs(0), spots[1]
     block = inner_weight.shape[-1]
@@ -527,7 +527,11 @@
             (row_sum(widen(up[...])), row_sum(upstream * normed), row_sum(upstream))
         )
 
-    inner_grad = narrow(dot(up[...], outer_weight[...], NT) * widen(slope[...]))
+    pre[...] = dot(up[...], outer_weight[...], NT)
+    for start in range(0, pre.shape[0], 4 * CHUNK):
+        down = slice(start, start + 4 * CHUNK)
+        grads[down] = narrow(pre[down] * widen(slope[down]))
+    inner_grad = grads[...]
     made[...] = narrow(dot(low[...], inner_grad, TN))
     divide(made, keep_inner, send_inner, side, slice(None))
     hidden_grad[...] += dot(inner_grad, inner_weight[...], NT)
@@ -582,6 +586,8 @@
             pltpu.VMEM((count, width), BF16),
             pltpu.VMEM((width, block), BF16),
             pltpu.VMEM((width, LANES), F32),
+            pltpu.VMEM((count, block), F32),
+            pltpu.VMEM((count, block), BF16),
         ],
     )(spots, cotangent, normed_two, inverse_two, rows, low, inner, outer, active, slope)
 
@@ -790,6 +796,23 @@
         ),
         out_shape=[shape((small, wide))] * seq,
     )(spots, *(list(values) * seq))
+
+
+def copied(value, *others):
+    def body(source, target):
+        target[...] = source[...]
+
+    block = pl.BlockSpec((1,) + value.shape[1:], lambda i: (i,) + (0,) * (value.ndim - 1))
+    return kernel(
+        body,
+        "copied",
+        0,
+        4 * math.prod(value.shape),
+        grid=value.shape[:1],
+        in_specs=[block],
+        out_specs=block,
+        out_shape=like(value),
+    )(after(value, *others))
 
 
 def finish_body(count, vectors, blocks, *refs):
@@ -999,8 +1022,9 @@
     tokens_grad = links.turn(grad)
     packed_grad = after(packed_grad, grad)
     keep, send = weights_back(spots, packed_grad, flat, packed_sums, sums)
+    output = copied(output, keep)
     if direct:
-        feed_sums[1:] = [after(value, keep) for value in feed_sums[1:]]
+        feed_sums[1:] = [after(value, keep, output) for value in feed_sums[1:]]
         feed_total = total_of("feed_total", feed_sums, 10**12)
         came = after(links.across(send, 1), feed_total)
         attention_sums = list(

time: 349 us -> 346 us (level)
  Pallas kernels: 169 us -> 173 us
  waiting for transfers between devices: 106 us -> 102 us
    ppermute x25, waiting for transfers between devices: 62.3 us -> 58.7 us  [across(): return lax.ppermute(value, AXES, pairs)]
    pallas_call x0 -> x1, Pallas kernels: none -> 3.56 us  [copied(): kernel(body, 'copied', 0, 4 * math.prod(value.shape), grid=value.shape[:1...]
    unnamed x50 -> x49, local copies, waits for them, and re-layouts: 11.9 us -> 9.34 us
  transfers between devices with their start and end apart: 35 -> 35, of which waited for: 14 -> 14; matrix products, arithmetic and copies ran while one was open for 1% -> 1% of each run, Pallas kernels for 48% -> 49%
where the time goes in v6:
time: 346 us; the launch traced here: 344 us
  Pallas kernels  173 us (50%)
  waiting for transfers between devices  102 us (29%)
  starting transfers between devices  55 us (16%)
  local copies, waits for them, and re-layouts  9.34 us (3%)
  other arithmetic  3.94 us (1%)
    ppermute x25, waiting for transfers between devices, across(): return lax.ppermute(value, AXES, pairs)  58.7 us
    all_to_all x7, waiting for transfers between devices, turn(): lax.all_to_all(blocks, 'seq', split_axis=0, concat_axis=0, tiled=True)  42.9 us
    all_to_all x7, starting transfers between devices, turn(): lax.all_to_all(blocks, 'seq', split_axis=0, concat_axis=0, tiled=True)  32.6 us
    pallas_call x1, Pallas kernels, feed_back(): kernel(feed_back_body, 'feed_back', 8 * count * width * wide, 12 * count...  31.3 us
    pallas_call x1, Pallas kernels, feed(): kernel(feed_body, 'feed', 4 * count * width * wide, 12 * count * wide, gr...  26.6 us
    pallas_call x1, Pallas kernels, attend_back(): kernel(attend_back_body, 'attend_back', rows * pairs * 16 * length * leng...  20.9 us
    ppermute x25, starting transfers between devices, across(): return lax.ppermute(value, AXES, pairs)  17.8 us
    pallas_call x1, Pallas kernels, attend(): kernel(attend_body, 'attend', rows * pairs * 16 * length * length * LANES...  16.2 us
  transfers between devices with their start and end apart: 35, of which 14 were waited for; matrix products, arithmetic and copies ran while one was open for 1% of the time, Pallas kernels for 49%

profile of v6, /device:TPU:0, one launch (start us, length us, event | category | flops | bytes accessed | tf_op | source)
XLA Modules:
  0.0 344.4 jit_solution(12181542771302567093)
XLA Ops:
  2.6 6.3 %all-to-all-start = ((bf16[4,24,3200]{2,1,0:T(8,128)(2,1)}), bf16[4,24,3200]{2,1,0:T(8,128)(2,1)S(1)}, u32[]{:S(2)}, u32[]{:S(2)}) async-start(bf16[4,24,3200]{2,1,0:T(8,128)(2,1)} %prepare_attention.1), calls=%async_computation | async-start | bytes 1228800 | tf_op jit(solution)/shard_map/all_to_all | solution.py:888
  11.1 14.3 %all-to-all-done = bf16[4,24,3200]{2,1,0:T(8,128)(2,1)S(1)} async-done(((bf16[4,24,3200]{2,1,0:T(8,128)(2,1)}), bf16[4,24,3200]{2,1,0:T(8,128)(2,1)S(1)}, u32[]{:S(2)}, u32[]{:S(2)}) %all-to-all-start) | async-done | bytes 614432 | tf_op jit(solution)/shard_map/all_to_all | solution.py:888
  25.4 3.5 %all-to-all-start.1 = ((bf16[4,24,6144]{2,1,0:T(8,128)(2,1)}), bf16[4,24,6144]{2,1,0:T(8,128)(2,1)S(1)}, u32[]{:S(2)}, u32[]{:S(2)}) async-start(bf16[4,24,6144]{2,1,0:T(8,128)(2,1)} %prepare_feed.1), calls=%async_computation.1 | async-start | bytes 2359296 | tf_op jit(solution)/shard_map/all_to_all | solution.py:888
  32.5 14.2 %collective-permute-done.2 = bf16[4,24,3200]{2,1,0:T(8,128)(2,1)S(1)} collective-permute-done((bf16[4,24,3200]{2,1,0:T(8,128)(2,1)S(1)}, bf16[4,24,3200]{2,1,0:T(8,128)(2,1)S(1)}, u32[]{:S(2)}, u32[]{:S(2)}) %collective-permute-start.2) | collective-permute-done | bytes 614432 | tf_op jit(solution)/shard_map/ppermute | solution.py:869
  46.7 11.2 %collective-permute-done.1 = bf16[4,24,3200]{2,1,0:T(8,128)(2,1)S(1)} collective-permute-done((bf16[4,24,3200]{2,1,0:T(8,128)(2,1)S(1)}, bf16[4,24,3200]{2,1,0:T(8,128)(2,1)S(1)}, u32[]{:S(2)}, u32[]{:S(2)}) %collective-permute-start.1) | collective-permute-done | bytes 614432 | tf_op jit(solution)/shard_map/ppermute | solution.py:869
  58.7 4.7 %all-to-all-start.2 = ((bf16[4,2,128,768]{3,2,1,0:T(8,128)(2,1)}), bf16[4,2,128,768]{3,2,1,0:T(8,128)(2,1)S(1)}, u32[]{:S(2)}, u32[]{:S(2)}) async-start(bf16[4,2,128,768]{3,2,1,0:T(8,128)(2,1)} %bitcast.3), calls=%async_computation.2 | async-start | bytes 3145728 | tf_op jit(solution)/shard_map/all_to_all | solution.py:888
  70.9 5.9 %unite_attention.1 = (bf16[768,2304]{1,0:T(8,128)(2,1)}, bf16[768,768]{1,0:T(8,128)(2,1)}, f32[8,768]{1,0:T(8,128)}, f32[1,3072]{1,0:T(1,128)}) custom-call(s32[3]{0:T(128)} %pad_add_fusion.spots, bf16[96,3200]{1,0:T(8,128)(2,1)} %bitcast.72, bf16[96,3200]{1,0:T(8,128)(2,1)} %bitcast.14.refs_1_, bf16[96,3200]{1,0:T(8,128)(2,1)} %bitcast.88, ...), custom_call_target="tpu_custom_call" | custom-call | bytes 9830400 | tf_op jit(solution)/shard_map/unite_attention/pallas_call | solution.py:174
  76.9 23.8 %all-to-all-done.2.tokens = bf16[4,2,128,768]{3,2,1,0:T(8,128)(2,1)S(1)} async-done(((bf16[4,2,128,768]{3,2,1,0:T(8,128)(2,1)}), bf16[4,2,128,768]{3,2,1,0:T(8,128)(2,1)S(1)}, u32[]{:S(2)}, u32[]{:S(2)}) %all-to-all-start.2) | async-done | bytes 1572896 | tf_op jit(solution)/shard_map/all_to_all | solution.py:888
  101.8 4.5 %all-to-all-start.3 = ((bf16[4,2,128,768]{3,2,1,0:T(8,128)(2,1)}), bf16[4,2,128,768]{3,2,1,0:T(8,128)(2,1)}, u32[]{:S(2)}, u32[]{:S(2)}) async-start(bf16[4,2,128,768]{3,2,1,0:T(8,128)(2,1)} %bitcast.26), calls=%async_computation.3 | async-start | bytes 3145728 | tf_op jit(solution)/shard_map/all_to_all | solution.py:888
  106.4 7.8 %project.1 = (bf16[2,512,2304]{2,1,0:T(8,128)(2,1)}, bf16[1024,768]{1,0:T(8,128)(2,1)}) custom-call(bf16[4,2,128,768]{3,2,1,0:T(8,128)(2,1)} %copy-done.6, bf16[768,2304]{1,0:T(8,128)(2,1)} %get-tuple-element.103.weight, f32[8,768]{1,0:T(8,128)} %get-tuple-element.104.rows.rows_one), custom_call_target="tpu_custom_call" | custom-call | flops 3623878656 | bytes 6291456 | tf_op jit(solution)/shard_map/project/pallas_call | solution.py:210
  114.2 16.2 %attend.1 = (bf16[2,512,768]{2,1,0:T(8,128)(2,1)}, bf16[2,12,512,512]{3,2,1,0:T(8,128)(2,1)}) custom-call(s32[3]{0:T(128)} %pad_add_fusion.spots, s32[8,4]{1,0:T(8,128)} %copy.31.lengths, bf16[2,512,2304]{2,1,0:T(8,128)(2,1)} %get-tuple-element.105.query.key.value, bf16[2,512,2304]{2,1,0:T(8,128)(2,1)} %get-tuple-element.105.query.key.value, ...), custom_call_target="tpu_custom_call" | custom-call | flops 6442450944 | bytes 25165824 | tf_op jit(solution)/shard_map/attend/pallas_call | solution.py:272
  131.1 5.7 %settle.1 = (f32[1024,768]{1,0:T(8,128)}, f32[1024,1]{1,0:T(8,128)}, bf16[1024,768]{1,0:T(8,128)(2,1)}) custom-call(bf16[1024,768]{1,0:T(8,128)(2,1)} %bitcast.111, bf16[1024,768]{1,0:T(8,128)(2,1)} %get-tuple-element.111.tokens, f32[8,768]{1,0:T(8,128)} %get-tuple-element.104.rows.rows_one, bf16[768,768]{1,0:T(8,128)(2,1)} %get-tuple-element.112.weight), custom_call_target="tpu_custom_call" | custom-call | flops 1207959552 | bytes 7864320 | tf_op jit(solution)/shard_map/settle/pallas_call | solution.py:370
  138.3 26.6 %feed.1 = (bf16[1024,3072]{1,0:T(8,128)(2,1)}, bf16[1024,3072]{1,0:T(8,128)(2,1)}, f32[1024,768]{1,0:T(8,128)}, f32[1024,1]{1,0:T(8,128)}, bf16[4,2,128,768]{3,2...) custom-call(s32[3]{0:T(128)} %pad_add_fusion.spots, bf16[1024,768]{1,0:T(8,128)(2,1)} %get-tuple-element.113.low, ...), custom_call_target="tpu_custom_call" | custom-call | flops 9663676416 | bytes 37748736 | tf_op jit(solution)/shard_map/feed/pallas_call | solution.py:468
  164.9 4.9 %all-to-all-start.4 = ((bf16[4,2,128,768]{3,2,1,0:T(8,128)(2,1)}), bf16[4,2,128,768]{3,2,1,0:T(8,128)(2,1)}, u32[]{:S(2)}, u32[]{:S(2)}) async-start(bf16[4,2,128,768]{3,2,1,0:T(8,128)(2,1)} %get-tuple-element.120), calls=%async_computation.4 | async-start | bytes 3145728 | tf_op jit(solution)/shard_map/all_to_all | solution.py:888
  169.7 31.3 %feed_back.1 = (bf16[4,96,3072]{2,1,0:T(8,128)(2,1)}, bf16[4,96,3072]{2,1,0:T(8,128)(2,1)}, bf16[4,384,768]{2,1,0:T(8,128)(2,1)}, bf16[4,384,768]{2,1,0:T(8,128)...) custom-call(s32[3]{0:T(128)} %pad_add_fusion.spots, ...), custom_call_target="tpu_custom_call" | custom-call | flops 19327352832 | bytes 37748736 | tf_op jit(solution)/shard_map/feed_back/pallas_call | solution.py:569
  201.6 9.3 %settle_back.1 = (f32[1024,768]{1,0:T(8,128)}, bf16[1024,768]{1,0:T(8,128)(2,1)}, bf16[4,96,768]{2,1,0:T(8,128)(2,1)}, bf16[4,96,768]{2,1,0:T(8,128)(2,1)}, f32[8,768]{1,0:T(8,128)}) custom-call(s32[3]{0:T(128)} %pad_add_fusion.spots, f32[1024,768]{1,0:T(8,128)} %get-tuple-element.131.hidden_grad, f32[1024,768]{1,0:T(8,128)} %get-tuple-element.115.normed_one.normed, ...), custom_call_target="tpu_custom_call" | custom-call | flops 999999995904 | bytes 12582912 | tf_op jit(solution)/shard_map/settle_back/pallas_call | solution.py:627
  214.1 8.0 %feed_chip_sums.1 = (bf16[4,24,7040]{2,1,0:T(8,128)(2,1)}, bf16[4,24,7040]{2,1,0:T(8,128)(2,1)}, bf16[4,24,7040]{2,1,0:T(8,128)(2,1)}, bf16[4,24,7040]{2,1,0:T(8,128)(2,1)}) custom-call(s32[3]{0:T(128)} %pad_add_fusion.spots, bf16[4,4,96,768]{3,2,1,0:T(8,128)(2,1)} %bitcast.54, bf16[4,4,96,768]{3,2,1,0:T(8,128)(2,1)} %bitcast.28.refs_1_.refs_3_.refs_5_.refs_7_, ...), custom_call_target="tpu_custom_call" | custom-call | bytes 16220160 | tf_op jit(solution)/shard_map/feed_chip_sums/pallas_call | solution.py:737
  225.6 20.9 %attend_back.1 = (bf16[2,512,2304]{2,1,0:T(8,128)(2,1)}, f32[2,1,2304]{2,1,0:T(1,128)}) custom-call(bf16[2,512,2304]{2,1,0:T(8,128)(2,1)} %get-tuple-element.105.query.key.value, bf16[2,512,2304]{2,1,0:T(8,128)(2,1)} %get-tuple-element.105.query.key.value, bf16[2,512,2304]{2,1,0:T(8,128)(2,1)} %get-tuple-element.105.query.key.value, ...), custom_call_target="tpu_custom_call" | custom-call | flops 6442450944 | bytes 25165824 | tf_op jit(solution)/shard_map/attend_back/pallas_call | solution.py:323
  246.5 8.5 %tokens_back.1 = bf16[4,2,128,768]{3,2,1,0:T(8,128)(2,1)} custom-call(bf16[1024,2304]{1,0:T(8,128)(2,1)} %bitcast.98, bf16[768,2304]{1,0:T(8,128)(2,1)} %get-tuple-element.103.weight, f32[1024,768]{1,0:T(8,128)} %get-tuple-element.151.first_up), custom_call_target="tpu_custom_call" | custom-call | flops 3623878656 | bytes 6291456 | tf_op jit(solution)/shard_map/tokens_back/pallas_call | solution.py:657
  255.0 5.1 %all-to-all-start.5 = ((bf16[4,2,128,768]{3,2,1,0:T(8,128)(2,1)}), bf16[4,2,128,768]{3,2,1,0:T(8,128)(2,1)}, u32[]{:S(2)}, u32[]{:S(2)}) async-start(bf16[4,2,128,768]{3,2,1,0:T(8,128)(2,1)} %tokens_back.1), calls=%async_computation.5 | async-start | bytes 3145728 | tf_op jit(solution)/shard_map/all_to_all | solution.py:888
  260.1 8.6 %weights_back.1 = (bf16[4,96,2432]{2,1,0:T(8,128)(2,1)}, bf16[4,96,2432]{2,1,0:T(8,128)(2,1)}) custom-call(s32[3]{0:T(128)} %pad_add_fusion.spots, bf16[1024,2304]{1,0:T(8,128)(2,1)} %bitcast.99, bf16[1024,768]{1,0:T(8,128)(2,1)} %get-tuple-element.111.tokens, f32[2,1,2304]{2,1,0:T(1,128)} %get-tuple-element.153.packed_sums, f32[8,768]{1,0:T(8,128)} %get-tuple-element.133.sums), custom_call_target="tpu_custom_call" | custom-call | flops 3623878656 | bytes 6291456 | tf_op jit(solution)/shard_map/weights_back/pallas_call | solution.py:693
  268.6 3.6 %copied.1 = bf16[4,2,128,768]{3,2,1,0:T(8,128)(2,1)} custom-call(bf16[4,2,128,768]{3,2,1,0:T(8,128)(2,1)} %all-to-all-done.4.source), custom_call_target="tpu_custom_call" | custom-call | bytes 3145728 | tf_op jit(solution)/shard_map/copied/pallas_call | solution.py:806
  272.2 12.0 %collective-permute-done.20.refs_2_ = bf16[4,24,7040]{2,1,0:T(8,128)(2,1)S(1)} collective-permute-done((bf16[4,24,7040]{2,1,0:T(8,128)(2,1)}, bf16[4,24,7040]{2,1,0:T(8,128)(2,1)S(1)}, u32[]{:S(2)}, u32[]{:S(2)}) %collective-permute-start.20) | collective-permute-done | bytes 1351712 | tf_op jit(solution)/shard_map/ppermute | solution.py:869
  285.3 4.5 %feed_total.1 = bf16[4,24,7040]{2,1,0:T(8,128)(2,1)} custom-call(bf16[4,24,7040]{2,1,0:T(8,128)(2,1)} %get-tuple-element.157.refs_0_, bf16[4,24,7040]{2,1,0:T(8,128)(2,1)} %copy-done.17, bf16[4,24,7040]{2,1,0:T(8,128)(2,1)} %copy-done.18, bf16[4,24,7040]{2,1,0:T(8,128)(2,1)} %collective-permute-done.21.refs_3_), custom_call_target="tpu_custom_call" | custom-call | flops 999999995904 | bytes 6758400 | tf_op jit(solution)/shard_map/feed_total/pallas_call | solution.py:762
  289.9 4.8 %attention_chip_sums.1 = (bf16[4,24,2432]{2,1,0:T(8,128)(2,1)}, bf16[4,24,2432]{2,1,0:T(8,128)(2,1)}, bf16[4,24,2432]{2,1,0:T(8,128)(2,1)}, bf16[4,24,2432]{2,1,0:T(8,128)(2,1)}) custom-call(s32[3]{0:T(128)} %pad_add_fusion.spots, bf16[4,4,24,2432]{3,2,1,0:T(8,128)(2,1)} %bitcast.58, bf16[4,4,24,2432]{3,2,1,0:T(8,128)(2,1)} %bitcast.40.refs_1_.refs_3_.refs_5_.refs_7_, ...), custom_call_target="tpu_custom_call" | custom-call | bytes 5603328 | tf_op jit(solution)/shard_map/attention_chip_sums/pallas_call | solution.py:737
  296.6 3.5 %all-to-all-start.6 = ((bf16[4,24,7040]{2,1,0:T(8,128)(2,1)}), bf16[4,24,7040]{2,1,0:T(8,128)(2,1)S(1)}, u32[]{:S(2)}, u32[]{:S(2)}) async-start(bf16[4,24,7040]{2,1,0:T(8,128)(2,1)} %feed_total.1), calls=%async_computation.6 | async-start | bytes 2703360 | tf_op jit(solution)/shard_map/all_to_all | solution.py:888
  303.7 10.3 %collective-permute-done.22.refs_1_.refs_5_.refs_9_.refs_13_ = bf16[4,24,2432]{2,1,0:T(8,128)(2,1)S(1)} collective-permute-done((bf16[4,24,2432]{2,1,0:T(8,128)(2,1)}, bf16[4,24,2432]{2,1,0:T(8,128)(2,1)S(1)}, u32[]{:S(2)}, u32[]{:S(2)}) %collective-permute-start.22) | collective-permute-done | bytes 466976 | tf_op jit(solution)/shard_map/ppermute | solution.py:869
  314.1 9.0 %collective-permute-done.23.refs_2_.refs_6_.refs_10_.refs_14_ = bf16[4,24,2432]{2,1,0:T(8,128)(2,1)S(1)} collective-permute-done((bf16[4,24,2432]{2,1,0:T(8,128)(2,1)S(1)}, bf16[4,24,2432]{2,1,0:T(8,128)(2,1)S(1)}, u32[]{:S(2)}, u32[]{:S(2)}) %collective-permute-start.23) | collective-permute-done | bytes 466976 | tf_op jit(solution)/shard_map/ppermute | solution.py:869
  324.0 3.1 attention_total.1
  327.1 3.4 collective-permute-start.27
  331.7 3.4 convert_element_type.3
  335.0 2.9 all-to-all-done.6.refs_0_
  (108 shorter events, 41.6 us)
Async XLA Ops:
  2.6 22.7 %all-to-all-start = ((bf16[4,24,3200]{2,1,0:T(8,128)(2,1)}), bf16[4,24,3200]{2,1,0:T(8,128)(2,1)S(1)}, u32[]{:S(2)}, u32[]{:S(2)}) async-start(bf16[4,24,3200]{2,1,0:T(8,128)(2,1)} %prepare_attention.1), calls=%async_computation | async-start | bytes 1228800 | tf_op jit(solution)/shard_map/all_to_all | solution.py:888
  25.4 33.3 %all-to-all-start.1 = ((bf16[4,24,6144]{2,1,0:T(8,128)(2,1)}), bf16[4,24,6144]{2,1,0:T(8,128)(2,1)S(1)}, u32[]{:S(2)}, u32[]{:S(2)}) async-start(bf16[4,24,6144]{2,1,0:T(8,128)(2,1)} %prepare_feed.1), calls=%async_computation.1 | async-start | bytes 2359296 | tf_op jit(solution)/shard_map/all_to_all | solution.py:888
  28.9 17.8 %collective-permute-start.2 = (bf16[4,24,3200]{2,1,0:T(8,128)(2,1)S(1)}, bf16[4,24,3200]{2,1,0:T(8,128)(2,1)S(1)}, u32[]{:S(2)}, u32[]{:S(2)}) collective-permute-start(bf16[4,24,3200]{2,1,0:T(8,128)(2,1)S(1)} %all-to-all-done), channel_id=1, source_target_pairs={{0,24},{1,25},{2,26},{3,27},{4,28},{5,29},{6,30},{7,31},{8,16},{9,... | collective-permute-start | bytes 1843208 | tf_op jit(solution)/shard_map/ppermute | solution.py:869
  31.4 26.4 %collective-permute-start.1 = (bf16[4,24,3200]{2,1,0:T(8,128)(2,1)S(1)}, bf16[4,24,3200]{2,1,0:T(8,128)(2,1)S(1)}, u32[]{:S(2)}, u32[]{:S(2)}) collective-permute-start(bf16[4,24,3200]{2,1,0:T(8,128)(2,1)S(1)} %all-to-all-done), channel_id=1, source_target_pairs={{0,16},{1,17},{2,18},{3,19},{4,20},{5,21},{6,22},{7,23},{8,24},{9,... | collective-permute-start | bytes 1843208 | tf_op jit(solution)/shard_map/ppermute | solution.py:869
  31.9 26.8 %collective-permute-start = (bf16[4,24,3200]{2,1,0:T(8,128)(2,1)S(1)}, bf16[4,24,3200]{2,1,0:T(8,128)(2,1)}, u32[]{:S(2)}, u32[]{:S(2)}) collective-permute-start(bf16[4,24,3200]{2,1,0:T(8,128)(2,1)S(1)} %all-to-all-done), channel_id=1, source_target_pairs={{0,8},{1,9},{2,10},{3,11},{4,12},{5,13},{6,14},{7,15},{8,0},{9,1},... | collective-permute-start | bytes 1843208 | tf_op jit(solution)/shard_map/ppermute | solution.py:869
  58.7 42.0 %all-to-all-start.2 = ((bf16[4,2,128,768]{3,2,1,0:T(8,128)(2,1)}), bf16[4,2,128,768]{3,2,1,0:T(8,128)(2,1)S(1)}, u32[]{:S(2)}, u32[]{:S(2)}) async-start(bf16[4,2,128,768]{3,2,1,0:T(8,128)(2,1)} %bitcast.3), calls=%async_computation.2 | async-start | bytes 3145728 | tf_op jit(solution)/shard_map/all_to_all | solution.py:888
  63.4 4.0 %collective-permute-start.6 = (bf16[96,3200]{1,0:T(8,128)(2,1)}, bf16[96,3200]{1,0:T(8,128)(2,1)S(1)}, u32[]{:S(2)}, u32[]{:S(2)}) collective-permute-start(bf16[96,3200]{1,0:T(8,128)(2,1)} %bitcast.85), channel_id=1, source_target_pairs={{0,4},{1,5},{2,6},{3,7},{4,0},{5,1},{6,2},{7,3},{8,12},{9,13},{10,... | collective-permute-start | bytes 1843208 | tf_op jit(solution)/shard_map/ppermute | solution.py:869
  64.0 6.9 %collective-permute-start.5 = (bf16[96,3200]{1,0:T(8,128)(2,1)}, bf16[96,3200]{1,0:T(8,128)(2,1)}, u32[]{:S(2)}, u32[]{:S(2)}) collective-permute-start(bf16[96,3200]{1,0:T(8,128)(2,1)} %bitcast.87), channel_id=1, source_target_pairs={{0,4},{1,5},{2,6},{3,7},{4,0},{5,1},{6,2},{7,3},{8,12},{9,13},{10,... | collective-permute-start | bytes 1843208 | tf_op jit(solution)/shard_map/ppermute | solution.py:869
  64.0 6.9 %collective-permute-start.4 = (bf16[96,3200]{1,0:T(8,128)(2,1)}, bf16[96,3200]{1,0:T(8,128)(2,1)}, u32[]{:S(2)}, u32[]{:S(2)}) collective-permute-start(bf16[96,3200]{1,0:T(8,128)(2,1)} %bitcast.14.refs_1_), channel_id=1, source_target_pairs={{0,4},{1,5},{2,6},{3,7},{4,0},{5,1},{6,2},{7,3},{8,12},{9,13},{10,... | collective-permute-start | bytes 1843208 | tf_op jit(solution)/shard_map/ppermute | solution.py:869
  64.5 65.9 %collective-permute-start.9 = (bf16[4,24,6144]{2,1,0:T(8,128)(2,1)S(1)}, bf16[4,24,6144]{2,1,0:T(8,128)(2,1)}, u32[]{:S(2)}, u32[]{:S(2)}) collective-permute-start(bf16[4,24,6144]{2,1,0:T(8,128)(2,1)S(1)} %all-to-all-done.1.refs_8_), channel_id=1, source_target_pairs={{0,24},{1,25},{2,26},{3,27},{4,28},{5,29},{6,30},{7,31},{8,16},{9,... | collective-permute-start | bytes 3538952 | tf_op jit(solution)/shard_map/ppermute | solution.py:869
  66.2 64.2 %collective-permute-start.8 = (bf16[4,24,6144]{2,1,0:T(8,128)(2,1)S(1)}, bf16[4,24,6144]{2,1,0:T(8,128)(2,1)}, u32[]{:S(2)}, u32[]{:S(2)}) collective-permute-start(bf16[4,24,6144]{2,1,0:T(8,128)(2,1)S(1)} %all-to-all-done.1.refs_8_), channel_id=1, source_target_pairs={{0,16},{1,17},{2,18},{3,19},{4,20},{5,21},{6,22},{7,23},{8,24},{9,... | collective-permute-start | bytes 3538952 | tf_op jit(solution)/shard_map/ppermute | solution.py:869
  68.3 62.1 %collective-permute-start.7 = (bf16[4,24,6144]{2,1,0:T(8,128)(2,1)S(1)}, bf16[4,24,6144]{2,1,0:T(8,128)(2,1)}, u32[]{:S(2)}, u32[]{:S(2)}) collective-permute-start(bf16[4,24,6144]{2,1,0:T(8,128)(2,1)S(1)} %all-to-all-done.1.refs_8_), channel_id=1, source_target_pairs={{0,8},{1,9},{2,10},{3,11},{4,12},{5,13},{6,14},{7,15},{8,0},{9,1},... | collective-permute-start | bytes 3538952 | tf_op jit(solution)/shard_map/ppermute | solution.py:869
  76.8 60.0 %collective-permute-start.10 = (bf16[96,6144]{1,0:T(8,128)(2,1)S(1)}, bf16[96,6144]{1,0:T(8,128)(2,1)}, u32[]{:S(2)}, u32[]{:S(2)}) collective-permute-start(bf16[96,6144]{1,0:T(8,128)(2,1)S(1)} %bitcast.83), channel_id=1, source_target_pairs={{0,4},{1,5},{2,6},{3,7},{4,0},{5,1},{6,2},{7,3},{8,12},{9,13},{10,... | collective-permute-start | bytes 3538952 | tf_op jit(solution)/shard_map/ppermute | solution.py:869
  101.8 63.0 %all-to-all-start.3 = ((bf16[4,2,128,768]{3,2,1,0:T(8,128)(2,1)}), bf16[4,2,128,768]{3,2,1,0:T(8,128)(2,1)}, u32[]{:S(2)}, u32[]{:S(2)}) async-start(bf16[4,2,128,768]{3,2,1,0:T(8,128)(2,1)} %bitcast.26), calls=%async_computation.3 | async-start | bytes 3145728 | tf_op jit(solution)/shard_map/all_to_all | solution.py:888
  130.4 6.4 %collective-permute-start.11 = (bf16[96,6144]{1,0:T(8,128)(2,1)}, bf16[96,6144]{1,0:T(8,128)(2,1)S(1)}, u32[]{:S(2)}, u32[]{:S(2)}) collective-permute-start(bf16[96,6144]{1,0:T(8,128)(2,1)} %bitcast.19.refs_1_), channel_id=1, source_target_pairs={{0,4},{1,5},{2,6},{3,7},{4,0},{5,1},{6,2},{7,3},{8,12},{9,13},{10,... | collective-permute-start | bytes 3538952 | tf_op jit(solution)/shard_map/ppermute | solution.py:869
  130.5 6.4 %collective-permute-start.12 = (bf16[96,6144]{1,0:T(8,128)(2,1)}, bf16[96,6144]{1,0:T(8,128)(2,1)S(1)}, u32[]{:S(2)}, u32[]{:S(2)}) collective-permute-start(bf16[96,6144]{1,0:T(8,128)(2,1)} %bitcast.20.refs_2_), channel_id=1, source_target_pairs={{0,4},{1,5},{2,6},{3,7},{4,0},{5,1},{6,2},{7,3},{8,12},{9,13},{10,... | collective-permute-start | bytes 3538952 | tf_op jit(solution)/shard_map/ppermute | solution.py:869
  131.0 6.1 %collective-permute-start.13 = (bf16[96,6144]{1,0:T(8,128)(2,1)}, bf16[96,6144]{1,0:T(8,128)(2,1)}, u32[]{:S(2)}, u32[]{:S(2)}) collective-permute-start(bf16[96,6144]{1,0:T(8,128)(2,1)} %bitcast.21.refs_3_), channel_id=1, source_target_pairs={{0,4},{1,5},{2,6},{3,7},{4,0},{5,1},{6,2},{7,3},{8,12},{9,13},{10,... | collective-permute-start | bytes 3538952 | tf_op jit(solution)/shard_map/ppermute | solution.py:869
  164.9 60.8 %all-to-all-start.4 = ((bf16[4,2,128,768]{3,2,1,0:T(8,128)(2,1)}), bf16[4,2,128,768]{3,2,1,0:T(8,128)(2,1)}, u32[]{:S(2)}, u32[]{:S(2)}) async-start(bf16[4,2,128,768]{3,2,1,0:T(8,128)(2,1)} %get-tuple-element.120), calls=%async_computation.4 | async-start | bytes 3145728 | tf_op jit(solution)/shard_map/all_to_all | solution.py:888
  201.0 12.1 %collective-permute-start.16 = (bf16[4,96,3072]{2,1,0:T(8,128)(2,1)}, bf16[4,96,3072]{2,1,0:T(8,128)(2,1)}, u32[]{:S(2)}, u32[]{:S(2)}) collective-permute-start(bf16[4,96,3072]{2,1,0:T(8,128)(2,1)} %get-tuple-element.128), channel_id=1, source_target_pairs={{0,4},{1,5},{2,6},{3,7},{4,0},{5,1},{6,2},{7,3},{8,12},{9,13},{10,... | collective-permute-start | bytes 7077896 | tf_op jit(solution)/shard_map/ppermute | solution.py:869
  201.3 11.9 %collective-permute-start.14 = (bf16[4,384,768]{2,1,0:T(8,128)(2,1)}, bf16[4,384,768]{2,1,0:T(8,128)(2,1)}, u32[]{:S(2)}, u32[]{:S(2)}) collective-permute-start(bf16[4,384,768]{2,1,0:T(8,128)(2,1)} %get-tuple-element.129), channel_id=1, source_target_pairs={{0,4},{1,5},{2,6},{3,7},{4,0},{5,1},{6,2},{7,3},{8,12},{9,13},{10,... | collective-permute-start | bytes 7077896 | tf_op jit(solution)/shard_map/ppermute | solution.py:869
  222.1 50.1 %collective-permute-start.19 = (bf16[4,24,7040]{2,1,0:T(8,128)(2,1)}, bf16[4,24,7040]{2,1,0:T(8,128)(2,1)S(1)}, u32[]{:S(2)}, u32[]{:S(2)}) collective-permute-start(bf16[4,24,7040]{2,1,0:T(8,128)(2,1)} %get-tuple-element.145), channel_id=1, source_target_pairs={{0,8},{1,9},{2,10},{3,11},{4,12},{5,13},{6,14},{7,15},{8,0},{9,1},... | collective-permute-start | bytes 4055048 | tf_op jit(solution)/shard_map/ppermute | solution.py:869
  223.6 60.6 %collective-permute-start.20 = (bf16[4,24,7040]{2,1,0:T(8,128)(2,1)}, bf16[4,24,7040]{2,1,0:T(8,128)(2,1)S(1)}, u32[]{:S(2)}, u32[]{:S(2)}) collective-permute-start(bf16[4,24,7040]{2,1,0:T(8,128)(2,1)} %get-tuple-element.146), channel_id=1, source_target_pairs={{0,16},{1,17},{2,18},{3,19},{4,20},{5,21},{6,22},{7,23},{8,24},{9,... | collective-permute-start | bytes 4055048 | tf_op jit(solution)/shard_map/ppermute | solution.py:869
  223.7 60.6 %collective-permute-start.21 = (bf16[4,24,7040]{2,1,0:T(8,128)(2,1)}, bf16[4,24,7040]{2,1,0:T(8,128)(2,1)}, u32[]{:S(2)}, u32[]{:S(2)}) collective-permute-start(bf16[4,24,7040]{2,1,0:T(8,128)(2,1)} %get-tuple-element.147), channel_id=1, source_target_pairs={{0,24},{1,25},{2,26},{3,27},{4,28},{5,29},{6,30},{7,31},{8,16},{9,... | collective-permute-start | bytes 4055048 | tf_op jit(solution)/shard_map/ppermute | solution.py:869
  255.0 41.6 %all-to-all-start.5 = ((bf16[4,2,128,768]{3,2,1,0:T(8,128)(2,1)}), bf16[4,2,128,768]{3,2,1,0:T(8,128)(2,1)}, u32[]{:S(2)}, u32[]{:S(2)}) async-start(bf16[4,2,128,768]{3,2,1,0:T(8,128)(2,1)} %tokens_back.1), calls=%async_computation.5 | async-start | bytes 3145728 | tf_op jit(solution)/shard_map/all_to_all | solution.py:888
  272.2 17.7 %collective-permute-start.18 = (bf16[4,96,2432]{2,1,0:T(8,128)(2,1)}, bf16[4,96,2432]{2,1,0:T(8,128)(2,1)}, u32[]{:S(2)}, u32[]{:S(2)}) collective-permute-start(bf16[4,96,2432]{2,1,0:T(8,128)(2,1)} %get-tuple-element.156), channel_id=1, source_target_pairs={{0,4},{1,5},{2,6},{3,7},{4,0},{5,1},{6,2},{7,3},{8,12},{9,13},{10,... | collective-permute-start | bytes 5603336 | tf_op jit(solution)/shard_map/ppermute | solution.py:869
  296.6 41.3 %all-to-all-start.6 = ((bf16[4,24,7040]{2,1,0:T(8,128)(2,1)}), bf16[4,24,7040]{2,1,0:T(8,128)(2,1)S(1)}, u32[]{:S(2)}, u32[]{:S(2)}) async-start(bf16[4,24,7040]{2,1,0:T(8,128)(2,1)} %feed_total.1), calls=%async_computation.6 | async-start | bytes 2703360 | tf_op jit(solution)/shard_map/all_to_all | solution.py:888
  300.1 13.9 %collective-permute-start.22 = (bf16[4,24,2432]{2,1,0:T(8,128)(2,1)}, bf16[4,24,2432]{2,1,0:T(8,128)(2,1)S(1)}, u32[]{:S(2)}, u32[]{:S(2)}) collective-permute-start(bf16[4,24,2432]{2,1,0:T(8,128)(2,1)} %get-tuple-element.163), channel_id=1, source_target_pairs={{0,8},{1,9},{2,10},{3,11},{4,12},{5,13},{6,14},{7,15},{8,0},{9,1},... | collective-permute-start | bytes 1400840 | tf_op jit(solution)/shard_map/ppermute | solution.py:869
  301.7 21.4 %collective-permute-start.23 = (bf16[4,24,2432]{2,1,0:T(8,128)(2,1)S(1)}, bf16[4,24,2432]{2,1,0:T(8,128)(2,1)S(1)}, u32[]{:S(2)}, u32[]{:S(2)}) collective-permute-start(bf16[4,24,2432]{2,1,0:T(8,128)(2,1)S(1)} %copy-done.22), channel_id=1, source_target_pairs={{0,16},{1,17},{2,18},{3,19},{4,20},{5,21},{6,22},{7,23},{8,24},{9,... | collective-permute-start | bytes 1400840 | tf_op jit(solution)/shard_map/ppermute | solution.py:869
  302.0 21.1 %collective-permute-start.24 = (bf16[4,24,2432]{2,1,0:T(8,128)(2,1)S(1)}, bf16[4,24,2432]{2,1,0:T(8,128)(2,1)S(1)}, u32[]{:S(2)}, u32[]{:S(2)}) collective-permute-start(bf16[4,24,2432]{2,1,0:T(8,128)(2,1)S(1)} %copy-done.21), channel_id=1, source_target_pairs={{0,24},{1,25},{2,26},{3,27},{4,28},{5,29},{6,30},{7,31},{8,16},{9,... | collective-permute-start | bytes 1400840 | tf_op jit(solution)/shard_map/ppermute | solution.py:869
  327.1 14.2 %collective-permute-start.27 = (bf16[24,2432]{1,0:T(8,128)(2,1)}, bf16[24,2432]{1,0:T(8,128)(2,1)S(1)}, u32[]{:S(2)}, u32[]{:S(2)}) collective-permute-start(bf16[24,2432]{1,0:T(8,128)(2,1)} %get-tuple-element.173), channel_id=1, source_target_pairs={{0,3},{1,0},{2,1},{3,2},{4,7},{5,4},{6,5},{7,6},{8,11},{9,8},{10,9... | collective-permute-start | bytes 350216 | tf_op jit(solution)/shard_map/ppermute | solution.py:877
  330.6 11.3 %collective-permute-start.26 = (bf16[24,2432]{1,0:T(8,128)(2,1)}, bf16[24,2432]{1,0:T(8,128)(2,1)S(1)}, u32[]{:S(2)}, u32[]{:S(2)}) collective-permute-start(bf16[24,2432]{1,0:T(8,128)(2,1)} %get-tuple-element.171), channel_id=1, source_target_pairs={{0,2},{1,3},{2,0},{3,1},{4,6},{5,7},{6,4},{7,5},{8,10},{9,11},{10,... | collective-permute-start | bytes 350216 | tf_op jit(solution)/shard_map/ppermute | solution.py:877
  330.6 11.3 %collective-permute-start.25 = (bf16[24,2432]{1,0:T(8,128)(2,1)}, bf16[24,2432]{1,0:T(8,128)(2,1)S(1)}, u32[]{:S(2)}, u32[]{:S(2)}) collective-permute-start(bf16[24,2432]{1,0:T(8,128)(2,1)} %get-tuple-element.167), channel_id=1, source_target_pairs={{0,1},{1,2},{2,3},{3,0},{4,5},{5,6},{6,7},{7,4},{8,9},{9,10},{10,1... | collective-permute-start | bytes 350216 | tf_op jit(solution)/shard_map/ppermute | solution.py:877
  (27 other events, 144.0 us)

commit v7 on v6

--- a/solution.py
+++ b/solution.py
@@ -285,8 +285,9 @@
     )(spots, lengths, packed, packed, packed)
 
 
-def attend_back_body(query, key, value, upstream, probs, grads, sums, prob_grad, score_grad):
-    pair, pairs = pl.program_id(1), pl.num_programs(1)
+def attend_back_body(query, key, value, upstream, probs, *rest):
+    grads, sums, prob_grad, score_grad = rest[-4:]
+    pair, pairs = pl.program_id(0), pl.num_programs(0)
     lane = lax.broadcasted_iota(jnp.int32, (1, LANES), 1)
     scale = BF16(HEAD_DIM**-0.5)
     queries, keys, values, up = query[0] * scale, key[0], value[0], upstream[0]
@@ -317,30 +318,33 @@
         sums[0, :, at] = row_sum(widen(rounded))
 
 
-def attend_back(packed, probs, upstream):
+def attend_back(packed, probs, upstream, row, prior=()):
     rows, length, wide = packed.shape
     pairs = wide // 3 // LANES
+
+    def columns(offset):
+        return pl.BlockSpec((1, length, LANES), lambda p: (row, 0, offset + p))
+
     return kernel(
         attend_back_body,
         "attend_back",
-        rows * pairs * 16 * length * length * LANES,
-        rows * pairs * 8 * length * length,
-        grid=(rows, pairs),
-        in_specs=[head_pair(length, part * pairs) for part in range(3)]
-        + [
-            head_pair(length, 0),
-            pl.BlockSpec((1, 2, length, length), lambda r, p: (r, p, 0, 0)),
-        ],
+        10**12 if row else 0,
+        pairs * 8 * length * length,
+        grid=(pairs,),
+        in_specs=[columns(part * pairs) for part in range(3)]
+        + [columns(0), pl.BlockSpec((1, 2, length, length), lambda p: (row, p, 0, 0))]
+        + [ANYWHERE] * len(prior),
         out_specs=[
-            pl.BlockSpec((1, length, wide), lambda r, p: (r, 0, 0)),
-            pl.BlockSpec((1, 1, wide), lambda r, p: (r, 0, 0)),
+            pl.BlockSpec((1, length, wide), lambda p: (row, 0, 0)),
+            pl.BlockSpec((1, 1, wide), lambda p: (row, 0, 0)),
         ],
         out_shape=[shape(packed.shape), shape((rows, 1, wide), F32)],
         scratch_shapes=[
             pltpu.VMEM((2, length, length), F32),
             pltpu.VMEM((2, length, length), BF16),
         ],
-    )(packed, packed, packed, upstream, probs)
+        input_output_aliases={5 + index: index for index in range(len(prior))},
+    )(packed, packed, packed, upstream, probs, *prior)
 
 
 def normed_of(summed):
@@ -645,28 +649,26 @@
 
 
 def tokens_back_body(packed_grad, weight, first_up, grad):
-    total = first_up[...] + dot(packed_grad[...], weight[...], NT)
-    seq, _, places, width = grad.shape
-    grad[:, 0] = narrow(total).reshape(seq, places, width)
-
-
-def tokens_back(packed_grad, weight, first_up, dims):
-    count, width = first_up.shape
-    seq, rows, places, _ = dims
-    length = seq * places
+    grad[...] = narrow(first_up[...] + dot(packed_grad[0], weight[...], NT))
+
+
+def tokens_back(packed_grad, weight, first_up, row):
+    _, length, wide = packed_grad.shape
+    width = wide // 3
+    half = length // 2
     return kernel(
         tokens_back_body,
         "tokens_back",
-        6 * count * width * width,
-        8 * count * width,
-        grid=(rows,),
+        2 * length * width * wide,
+        8 * length * width,
+        grid=(2,),
         in_specs=[
-            pl.BlockSpec((length, 3 * width), lambda r: (r, 0)),
-            fixed((width, 3 * width)),
-            pl.BlockSpec((length, width), lambda r: (r, 0)),
-        ],
-        out_specs=pl.BlockSpec((seq, 1, places, width), lambda r: (0, r, 0, 0)),
-        out_shape=shape(dims),
+            pl.BlockSpec((1, half, wide), lambda i: (row, i, 0)),
+            fixed((width, wide)),
+            pl.BlockSpec((half, width), lambda i: (2 * row + i, 0)),
+        ],
+        out_specs=pl.BlockSpec((half, width), lambda i: (i, 0)),
+        out_shape=shape((length, width)),
     )(packed_grad, weight, first_up)
 
 
@@ -717,22 +719,21 @@
     wide = sum(kept.shape[1] // (seq * small) * kept.shape[2] for kept, _ in pairs)
     for kept, came in pairs:
         height = kept.shape[1] // seq
-        for part in range(PARTS):
-            block = pl.BlockSpec(
-                (None, None, height, kept.shape[2]),
-                lambda i, spots, part=part: (spots[2] ^ part, i, 0, 0),
+        for value in (kept, came):
+            operands.append(value.reshape(PARTS, seq, height, value.shape[2]))
+            in_specs.append(
+                pl.BlockSpec(
+                    (PARTS, None, height, value.shape[2]), lambda i, spots: (0, i, 0, 0)
+                )
             )
-            for value in (kept, came):
-                operands.append(value.reshape(PARTS, seq, height, value.shape[2]))
-                in_specs.append(block)
 
     def body(spots, *refs):
         ins, outs = refs[: len(operands)], refs[len(operands) :]
         for part, out in enumerate(outs):
             start = 0
-            for pair in range(len(pairs)):
-                at = 2 * (pair * PARTS + part)
-                start = side_by_side(out, start, widen(ins[at][...]) + widen(ins[at + 1][...]))
+            chip = spots[2] ^ part
+            for kept, came in zip(ins[::2], ins[1::2]):
+                start = side_by_side(out, start, widen(kept[chip]) + widen(came[chip]))
 
     return kernel(
         body,
@@ -773,29 +774,21 @@
 
 def total_pieces(name, spots, values):
     seq, small, wide = values[0].shape
-    blocks = [
-        pl.BlockSpec((None, small, wide), lambda i, spots, step=step: (lax.rem(spots[0] + step, seq), 0, 0))
-        for step in range(seq)
-    ]
 
     def body(spots, *refs):
         for step in range(seq):
-            part = refs[step * len(values) : (step + 1) * len(values)]
-            total_body(*part, refs[seq * len(values) + step])
+            at = lax.rem(spots[0] + step, seq)
+            total_body(*[ref.at[at] for ref in refs[: len(values)]], refs[len(values) + step])
 
     return kernel(
         body,
         name,
         0,
         2 * (len(values) + 1) * seq * small * wide,
-        grid_spec=pltpu.PrefetchScalarGridSpec(
-            num_scalar_prefetch=1,
-            grid=(1,),
-            in_specs=[block for block in blocks for _ in values],
-            out_specs=[pl.BlockSpec((small, wide), lambda i, spots: (0, 0))] * seq,
-        ),
+        in_specs=[SCALARS] + [pl.BlockSpec(memory_space=pltpu.VMEM)] * len(values),
+        out_specs=[pl.BlockSpec(memory_space=pltpu.VMEM)] * seq,
         out_shape=[shape((small, wide))] * seq,
-    )(spots, *(list(values) * seq))
+    )(spots, *values)
 
 
 def copied(value, *others):
@@ -1014,23 +1007,26 @@
         feed_sums = list(chip_sums("feed_chip_sums", spots, pairs, seq, small))
         context_grad = after(context_grad, *feed_sums[1:])
         feed_sums[1:] = [links.across(feed_sums[part], 2 * part) for part in range(1, PARTS)]
-    packed_grad, packed_sums = attend_back(
-        packed, probs, context_grad.reshape(rows, seq * places, width)
-    )
-    packed_grad = packed_grad.reshape(-1, 3 * width)
-    grad = tokens_back(packed_grad, packed_whole, first_up, dims)
-    tokens_grad = links.turn(grad)
-    packed_grad = after(packed_grad, grad)
+    context_grad = context_grad.reshape(rows, seq * places, width)
+    prior, tokens_grad = (), []
+    for row in range(rows):
+        prior = attend_back(packed, probs, context_grad, row, prior)
+        grad = tokens_back(prior[0], packed_whole, first_up, row)
+        context_grad = after(context_grad, grad)
+        sent = after(grad, tokens_grad[-1]) if row else grad
+        tokens_grad.append(links.turn(sent.reshape(seq, places, width)))
+    packed_grad, packed_sums = prior
+    packed_grad = after(packed_grad, grad).reshape(-1, 3 * width)
     keep, send = weights_back(spots, packed_grad, flat, packed_sums, sums)
     output = copied(output, keep)
     if direct:
         feed_sums[1:] = [after(value, keep, output) for value in feed_sums[1:]]
-        feed_total = total_of("feed_total", feed_sums, 10**12)
+        feed_total = total_of("feed_total", feed_sums, 10**10)
         came = after(links.across(send, 1), feed_total)
         attention_sums = list(
             chip_sums("attention_chip_sums", spots, [(keep, came)], seq, small)
         )
-        feed_total = after(feed_total, tokens_grad, *attention_sums[1:])
+        feed_total = after(feed_total, *tokens_grad)
         attention_sums[1:] = [
             links.across(attention_sums[part], 2 * part) for part in range(1, PARTS)
         ]
@@ -1063,7 +1059,7 @@
         [(per, width), (1, width), (1, wide)],
         [(0, 1), (1, 1), (2, 1), (3, per)],
     )
-    tokens_grad = widen(tokens_grad)
+    tokens_grad = widen(jnp.stack(tokens_grad, axis=1))
     attention_total[1:] = [after(piece, inner_grad, tokens_grad) for piece in attention_total[1:]]
     (
         packed_weight_grad,

time: 346 us -> 341 us (0.986)
  waiting for transfers between devices: 102 us -> 90.7 us
  starting transfers between devices: 55 us -> 59.4 us
    ppermute x25, waiting for transfers between devices: 58.7 us -> 48.4 us  [across(): return lax.ppermute(value, AXES, pairs)]
    pallas_call x3 -> x5, Pallas kernels: 32.5 us -> 36.4 us  [the longest x2 22.8 us: attend_back(): kernel(attend_back_body, 'attend_back', 10 ** 12 if row else 0, pairs * 8...]
    all_to_all x7 -> x8, starting transfers between devices: 32.6 us -> 36.1 us  [turn(): lax.all_to_all(blocks, 'seq', split_axis=0, concat_axis=0, tiled=True)]
    unnamed x49 -> x41, local copies, waits for them, and re-layouts: 9.34 us -> 8.05 us
    all_to_all x7 -> x8, waiting for transfers between devices: 42.9 us -> 42.3 us  [turn(): lax.all_to_all(blocks, 'seq', split_axis=0, concat_axis=0, tiled=True)]
  transfers between devices with their start and end apart: 35 -> 36, of which waited for: 14 -> 14; matrix products, arithmetic and copies ran while one was open for 1% -> 1% of each run, Pallas kernels for 49% -> 49%
where the time goes in v7:
time: 341 us; the launch traced here: 339 us
  Pallas kernels  176 us (52%)
  waiting for transfers between devices  90.7 us (27%)
  starting transfers between devices  59.4 us (17%)
  local copies, waits for them, and re-layouts  10 us (3%)
    ppermute x25, waiting for transfers between devices, across(): return lax.ppermute(value, AXES, pairs)  48.4 us
    all_to_all x8, waiting for transfers between devices, turn(): lax.all_to_all(blocks, 'seq', split_axis=0, concat_axis=0, tiled=True)  42.3 us
    all_to_all x8, starting transfers between devices, turn(): lax.all_to_all(blocks, 'seq', split_axis=0, concat_axis=0, tiled=True)  36.1 us
    pallas_call x1, Pallas kernels, feed_back(): kernel(feed_back_body, 'feed_back', 8 * count * width * wide, 12 * count...  31.1 us
    pallas_call x1, Pallas kernels, feed(): kernel(feed_body, 'feed', 4 * count * width * wide, 12 * count * wide, gr...  26.5 us
    pallas_call x2, Pallas kernels, attend_back(): kernel(attend_back_body, 'attend_back', 10 ** 12 if row else 0, pairs * 8...  22.8 us
    ppermute x25, starting transfers between devices, across(): return lax.ppermute(value, AXES, pairs)  17.8 us
    pallas_call x1, Pallas kernels, attend(): kernel(attend_body, 'attend', rows * pairs * 16 * length * length * LANES...  16.2 us
  transfers between devices with their start and end apart: 36, of which 14 were waited for; matrix products, arithmetic and copies ran while one was open for 1% of the time, Pallas kernels for 49%

profile of v7, /device:TPU:0, one launch (start us, length us, event | category | flops | bytes accessed | tf_op | source)
XLA Modules:
  0.0 339.1 jit_solution(15467252712704784618)
XLA Ops:
  2.6 6.3 %all-to-all-start = ((bf16[4,24,3200]{2,1,0:T(8,128)(2,1)}), bf16[4,24,3200]{2,1,0:T(8,128)(2,1)S(1)}, u32[]{:S(2)}, u32[]{:S(2)}) async-start(bf16[4,24,3200]{2,1,0:T(8,128)(2,1)} %prepare_attention.1), calls=%async_computation | async-start | bytes 1228800 | tf_op jit(solution)/shard_map/all_to_all | solution.py:881
  11.1 14.3 %all-to-all-done = bf16[4,24,3200]{2,1,0:T(8,128)(2,1)S(1)} async-done(((bf16[4,24,3200]{2,1,0:T(8,128)(2,1)}), bf16[4,24,3200]{2,1,0:T(8,128)(2,1)S(1)}, u32[]{:S(2)}, u32[]{:S(2)}) %all-to-all-start) | async-done | bytes 614432 | tf_op jit(solution)/shard_map/all_to_all | solution.py:881
  25.4 3.5 %all-to-all-start.1 = ((bf16[4,24,6144]{2,1,0:T(8,128)(2,1)}), bf16[4,24,6144]{2,1,0:T(8,128)(2,1)S(1)}, u32[]{:S(2)}, u32[]{:S(2)}) async-start(bf16[4,24,6144]{2,1,0:T(8,128)(2,1)} %prepare_feed.1), calls=%async_computation.1 | async-start | bytes 2359296 | tf_op jit(solution)/shard_map/all_to_all | solution.py:881
  28.9 2.5 collective-permute-start.2
  32.5 14.2 %collective-permute-done.2 = bf16[4,24,3200]{2,1,0:T(8,128)(2,1)S(1)} collective-permute-done((bf16[4,24,3200]{2,1,0:T(8,128)(2,1)S(1)}, bf16[4,24,3200]{2,1,0:T(8,128)(2,1)S(1)}, u32[]{:S(2)}, u32[]{:S(2)}) %collective-permute-start.2) | collective-permute-done | bytes 614432 | tf_op jit(solution)/shard_map/ppermute | solution.py:862
  46.7 11.2 %collective-permute-done.1 = bf16[4,24,3200]{2,1,0:T(8,128)(2,1)S(1)} collective-permute-done((bf16[4,24,3200]{2,1,0:T(8,128)(2,1)S(1)}, bf16[4,24,3200]{2,1,0:T(8,128)(2,1)S(1)}, u32[]{:S(2)}, u32[]{:S(2)}) %collective-permute-start.1) | collective-permute-done | bytes 614432 | tf_op jit(solution)/shard_map/ppermute | solution.py:862
  58.7 4.7 %all-to-all-start.2 = ((bf16[4,2,128,768]{3,2,1,0:T(8,128)(2,1)}), bf16[4,2,128,768]{3,2,1,0:T(8,128)(2,1)S(1)}, u32[]{:S(2)}, u32[]{:S(2)}) async-start(bf16[4,2,128,768]{3,2,1,0:T(8,128)(2,1)} %bitcast.3), calls=%async_computation.2 | async-start | bytes 3145728 | tf_op jit(solution)/shard_map/all_to_all | solution.py:881
  70.8 6.0 %unite_attention.1 = (bf16[768,2304]{1,0:T(8,128)(2,1)}, bf16[768,768]{1,0:T(8,128)(2,1)}, f32[8,768]{1,0:T(8,128)}, f32[1,3072]{1,0:T(1,128)}) custom-call(s32[3]{0:T(128)} %pad_add_fusion.spots, bf16[96,3200]{1,0:T(8,128)(2,1)} %bitcast.60, bf16[96,3200]{1,0:T(8,128)(2,1)} %bitcast.14.refs_1_, bf16[96,3200]{1,0:T(8,128)(2,1)} %bitcast.72, ...), custom_call_target="tpu_custom_call" | custom-call | bytes 9830400 | tf_op jit(solution)/shard_map/unite_attention/pallas_call | solution.py:174
  76.9 23.8 %all-to-all-done.2.tokens = bf16[4,2,128,768]{3,2,1,0:T(8,128)(2,1)S(1)} async-done(((bf16[4,2,128,768]{3,2,1,0:T(8,128)(2,1)}), bf16[4,2,128,768]{3,2,1,0:T(8,128)(2,1)S(1)}, u32[]{:S(2)}, u32[]{:S(2)}) %all-to-all-start.2) | async-done | bytes 1572896 | tf_op jit(solution)/shard_map/all_to_all | solution.py:881
  101.8 4.5 %all-to-all-start.3 = ((bf16[4,2,128,768]{3,2,1,0:T(8,128)(2,1)}), bf16[4,2,128,768]{3,2,1,0:T(8,128)(2,1)}, u32[]{:S(2)}, u32[]{:S(2)}) async-start(bf16[4,2,128,768]{3,2,1,0:T(8,128)(2,1)} %bitcast.26), calls=%async_computation.3 | async-start | bytes 3145728 | tf_op jit(solution)/shard_map/all_to_all | solution.py:881
  106.3 7.7 %project.1 = (bf16[2,512,2304]{2,1,0:T(8,128)(2,1)}, bf16[1024,768]{1,0:T(8,128)(2,1)}) custom-call(bf16[4,2,128,768]{3,2,1,0:T(8,128)(2,1)} %copy-done.2, bf16[768,2304]{1,0:T(8,128)(2,1)} %get-tuple-element.107.weight, f32[8,768]{1,0:T(8,128)} %get-tuple-element.108.rows.rows_one), custom_call_target="tpu_custom_call" | custom-call | flops 3623878656 | bytes 6291456 | tf_op jit(solution)/shard_map/project/pallas_call | solution.py:210
  114.1 16.2 %attend.1 = (bf16[2,512,768]{2,1,0:T(8,128)(2,1)}, bf16[2,12,512,512]{3,2,1,0:T(8,128)(2,1)}) custom-call(s32[3]{0:T(128)} %pad_add_fusion.spots, s32[8,4]{1,0:T(8,128)} %copy.33.lengths, bf16[2,512,2304]{2,1,0:T(8,128)(2,1)} %get-tuple-element.109.query.key.value, bf16[2,512,2304]{2,1,0:T(8,128)(2,1)} %get-tuple-element.109.query.key.value, ...), custom_call_target="tpu_custom_call" | custom-call | flops 6442450944 | bytes 25165824 | tf_op jit(solution)/shard_map/attend/pallas_call | solution.py:272
  130.9 5.8 %settle.1 = (f32[1024,768]{1,0:T(8,128)}, f32[1024,1]{1,0:T(8,128)}, bf16[1024,768]{1,0:T(8,128)(2,1)}) custom-call(bf16[1024,768]{1,0:T(8,128)(2,1)} %bitcast.97, bf16[1024,768]{1,0:T(8,128)(2,1)} %get-tuple-element.115.tokens, f32[8,768]{1,0:T(8,128)} %get-tuple-element.108.rows.rows_one, bf16[768,768]{1,0:T(8,128)(2,1)} %get-tuple-element.116.weight), custom_call_target="tpu_custom_call" | custom-call | flops 1207959552 | bytes 7864320 | tf_op jit(solution)/shard_map/settle/pallas_call | solution.py:374
  138.1 26.5 %feed.1 = (bf16[1024,3072]{1,0:T(8,128)(2,1)}, bf16[1024,3072]{1,0:T(8,128)(2,1)}, f32[1024,768]{1,0:T(8,128)}, f32[1024,1]{1,0:T(8,128)}, bf16[4,2,128,768]{3,2...) custom-call(s32[3]{0:T(128)} %pad_add_fusion.spots, bf16[1024,768]{1,0:T(8,128)(2,1)} %get-tuple-element.117.low, ...), custom_call_target="tpu_custom_call" | custom-call | flops 9663676416 | bytes 37748736 | tf_op jit(solution)/shard_map/feed/pallas_call | solution.py:472
  164.7 4.9 %all-to-all-start.4 = ((bf16[4,2,128,768]{3,2,1,0:T(8,128)(2,1)}), bf16[4,2,128,768]{3,2,1,0:T(8,128)(2,1)}, u32[]{:S(2)}, u32[]{:S(2)}) async-start(bf16[4,2,128,768]{3,2,1,0:T(8,128)(2,1)} %get-tuple-element.124), calls=%async_computation.4 | async-start | bytes 3145728 | tf_op jit(solution)/shard_map/all_to_all | solution.py:881
  169.5 31.1 %feed_back.1 = (bf16[4,96,3072]{2,1,0:T(8,128)(2,1)}, bf16[4,96,3072]{2,1,0:T(8,128)(2,1)}, bf16[4,384,768]{2,1,0:T(8,128)(2,1)}, bf16[4,384,768]{2,1,0:T(8,128)...) custom-call(s32[3]{0:T(128)} %pad_add_fusion.spots, ...), custom_call_target="tpu_custom_call" | custom-call | flops 19327352832 | bytes 37748736 | tf_op jit(solution)/shard_map/feed_back/pallas_call | solution.py:573
  201.2 9.3 %settle_back.1 = (f32[1024,768]{1,0:T(8,128)}, bf16[1024,768]{1,0:T(8,128)(2,1)}, bf16[4,96,768]{2,1,0:T(8,128)(2,1)}, bf16[4,96,768]{2,1,0:T(8,128)(2,1)}, f32[8,768]{1,0:T(8,128)}) custom-call(s32[3]{0:T(128)} %pad_add_fusion.spots, f32[1024,768]{1,0:T(8,128)} %get-tuple-element.135.hidden_grad, f32[1024,768]{1,0:T(8,128)} %get-tuple-element.119.normed_one.normed, ...), custom_call_target="tpu_custom_call" | custom-call | flops 999999995904 | bytes 12582912 | tf_op jit(solution)/shard_map/settle_back/pallas_call | solution.py:631
  213.6 7.6 %feed_chip_sums.1 = (bf16[4,24,7040]{2,1,0:T(8,128)(2,1)}, bf16[4,24,7040]{2,1,0:T(8,128)(2,1)}, bf16[4,24,7040]{2,1,0:T(8,128)(2,1)}, bf16[4,24,7040]{2,1,0:T(8,128)(2,1)}) custom-call(s32[3]{0:T(128)} %pad_add_fusion.spots, bf16[4,4,96,768]{3,2,1,0:T(8,128)(2,1)} %bitcast.62, bf16[4,4,96,768]{3,2,1,0:T(8,128)(2,1)} %bitcast.28.refs_1_, ...), custom_call_target="tpu_custom_call" | custom-call | bytes 16220160 | tf_op jit(solution)/shard_map/feed_chip_sums/pallas_call | solution.py:738
  224.7 11.4 %attend_back.2 = (bf16[2,512,2304]{2,1,0:T(8,128)(2,1)}, f32[2,1,2304]{2,1,0:T(1,128)}) custom-call(bf16[2,512,2304]{2,1,0:T(8,128)(2,1)} %get-tuple-element.109.query.key.value, bf16[2,512,2304]{2,1,0:T(8,128)(2,1)} %get-tuple-element.109.query.key.value, bf16[2,512,2304]{2,1,0:T(8,128)(2,1)} %get-tuple-element.109.query.key.value, ...), custom_call_target="tpu_custom_call" | custom-call | bytes 12582912 | tf_op jit(solution)/shard_map/attend_back/pallas_call | solution.py:328
  236.2 5.6 %tokens_back.2 = bf16[512,768]{1,0:T(8,128)(2,1)} custom-call(bf16[2,512,2304]{2,1,0:T(8,128)(2,1)} %get-tuple-element.154.packed_grad.rest_0_, bf16[768,2304]{1,0:T(8,128)(2,1)} %get-tuple-element.107.weight, f32[1024,768]{1,0:T(8,128)} %get-tuple-element.155.first_up), custom_call_target="tpu_custom_call" | custom-call | flops 1811939328 | bytes 3145728 | tf_op jit(solution)/shard_map/tokens_back/pallas_call | solution.py:659
  241.8 5.1 %all-to-all-start.5 = ((bf16[4,128,768]{2,1,0:T(8,128)(2,1)}), bf16[4,128,768]{2,1,0:T(8,128)(2,1)}, u32[]{:S(2)}, u32[]{:S(2)}) async-start(bf16[4,128,768]{2,1,0:T(8,128)(2,1)} %bitcast.57), calls=%async_computation.5 | async-start | bytes 1572864 | tf_op jit(solution)/shard_map/all_to_all | solution.py:881
  246.9 11.4 %attend_back.3 = (bf16[2,512,2304]{2,1,0:T(8,128)(2,1)}, f32[2,1,2304]{2,1,0:T(1,128)}) custom-call(bf16[2,512,2304]{2,1,0:T(8,128)(2,1)} %get-tuple-element.109.query.key.value, bf16[2,512,2304]{2,1,0:T(8,128)(2,1)} %get-tuple-element.109.query.key.value, ...), custom_call_target="tpu_custom_call", output_to_operand_aliasing={{0}: (5, {}), {1}: (6, {})} | custom-call | flops 999999995904 | bytes 12582912 | tf_op jit(solution)/shard_map/attend_back/pallas_call | solution.py:328
  258.3 5.6 %tokens_back.3 = bf16[512,768]{1,0:T(8,128)(2,1)} custom-call(bf16[2,512,2304]{2,1,0:T(8,128)(2,1)} %get-tuple-element.159.packed_grad, bf16[768,2304]{1,0:T(8,128)(2,1)} %get-tuple-element.107.weight, f32[1024,768]{1,0:T(8,128)} %get-tuple-element.155.first_up), custom_call_target="tpu_custom_call" | custom-call | flops 1811939328 | bytes 3145728 | tf_op jit(solution)/shard_map/tokens_back/pallas_call | solution.py:659
  264.0 2.6 all-to-all-done.5
  266.6 3.5 %all-to-all-start.6 = ((bf16[4,128,768]{2,1,0:T(8,128)(2,1)}), bf16[4,128,768]{2,1,0:T(8,128)(2,1)S(1)}, u32[]{:S(2)}, u32[]{:S(2)}) async-start(bf16[4,128,768]{2,1,0:T(8,128)(2,1)} %bitcast.56), calls=%async_computation.6 | async-start | bytes 1572864 | tf_op jit(solution)/shard_map/all_to_all | solution.py:881
  270.1 8.6 %weights_back.1 = (bf16[4,96,2432]{2,1,0:T(8,128)(2,1)}, bf16[4,96,2432]{2,1,0:T(8,128)(2,1)}) custom-call(s32[3]{0:T(128)} %pad_add_fusion.spots, bf16[1024,2304]{1,0:T(8,128)(2,1)} %bitcast.54, bf16[1024,768]{1,0:T(8,128)(2,1)} %get-tuple-element.115.tokens, f32[2,1,2304]{2,1,0:T(1,128)} %get-tuple-element.160.packed_sums, f32[8,768]{1,0:T(8,128)} %get-tuple-element.137.sums), custom_call_target="tpu_custom_call" | custom-call | flops 3623878656 | bytes 6291456 | tf_op jit(solution)/shard_map/weights_back/pallas_call | solution.py:695
  278.7 3.6 %copied.1 = bf16[4,2,128,768]{3,2,1,0:T(8,128)(2,1)} custom-call(bf16[4,2,128,768]{3,2,1,0:T(8,128)(2,1)} %all-to-all-done.4.source), custom_call_target="tpu_custom_call" | custom-call | bytes 3145728 | tf_op jit(solution)/shard_map/copied/pallas_call | solution.py:799
  283.5 4.5 %feed_total.1 = bf16[4,24,7040]{2,1,0:T(8,128)(2,1)} custom-call(bf16[4,24,7040]{2,1,0:T(8,128)(2,1)} %get-tuple-element.165.refs_0_, bf16[4,24,7040]{2,1,0:T(8,128)(2,1)} %collective-permute-done.19.refs_1_, bf16[4,24,7040]{2,1,0:T(8,128)(2,1)} %collective-permute-done.20.refs_2_, bf16[4,24,7040]{2,1,0:T(8,128)(2,1)} %collective-permute-done.21.refs_3_), custom_call_target="tpu_custom_call" | custom-call | flops 10000000000 | bytes 6758400 | tf_op jit(solution)/shard_map/feed_total/pallas_call | solution.py:763
  289.6 3.5 %all-to-all-start.7 = ((bf16[4,24,7040]{2,1,0:T(8,128)(2,1)}), bf16[4,24,7040]{2,1,0:T(8,128)(2,1)S(1)}, u32[]{:S(2)}, u32[]{:S(2)}) async-start(bf16[4,24,7040]{2,1,0:T(8,128)(2,1)} %feed_total.1), calls=%async_computation.7 | async-start | bytes 2703360 | tf_op jit(solution)/shard_map/all_to_all | solution.py:881
  293.2 4.7 %attention_chip_sums.1 = (bf16[4,24,2432]{2,1,0:T(8,128)(2,1)}, bf16[4,24,2432]{2,1,0:T(8,128)(2,1)}, bf16[4,24,2432]{2,1,0:T(8,128)(2,1)}, bf16[4,24,2432]{2,1,0:T(8,128)(2,1)}) custom-call(s32[3]{0:T(128)} %pad_add_fusion.spots, bf16[4,4,24,2432]{3,2,1,0:T(8,128)(2,1)} %bitcast.63, bf16[4,4,24,2432]{3,2,1,0:T(8,128)(2,1)} %bitcast.44.refs_1_), custom_call_target="tpu_custom_call" | custom-call | bytes 5603328 | tf_op jit(solution)/shard_map/attention_chip_sums/pallas_call | solution.py:738
  301.4 10.4 %collective-permute-done.22.refs_1_ = bf16[4,24,2432]{2,1,0:T(8,128)(2,1)S(1)} collective-permute-done((bf16[4,24,2432]{2,1,0:T(8,128)(2,1)}, bf16[4,24,2432]{2,1,0:T(8,128)(2,1)S(1)}, u32[]{:S(2)}, u32[]{:S(2)}) %collective-permute-start.22) | collective-permute-done | bytes 466976 | tf_op jit(solution)/shard_map/ppermute | solution.py:862
  311.7 9.2 %collective-permute-done.23.refs_2_ = bf16[4,24,2432]{2,1,0:T(8,128)(2,1)S(1)} collective-permute-done((bf16[4,24,2432]{2,1,0:T(8,128)(2,1)}, bf16[4,24,2432]{2,1,0:T(8,128)(2,1)S(1)}, u32[]{:S(2)}, u32[]{:S(2)}) %collective-permute-start.23) | collective-permute-done | bytes 466976 | tf_op jit(solution)/shard_map/ppermute | solution.py:862
  (105 shorter events, 48.4 us)
Async XLA Ops:
  2.6 22.7 %all-to-all-start = ((bf16[4,24,3200]{2,1,0:T(8,128)(2,1)}), bf16[4,24,3200]{2,1,0:T(8,128)(2,1)S(1)}, u32[]{:S(2)}, u32[]{:S(2)}) async-start(bf16[4,24,3200]{2,1,0:T(8,128)(2,1)} %prepare_attention.1), calls=%async_computation | async-start | bytes 1228800 | tf_op jit(solution)/shard_map/all_to_all | solution.py:881
  25.4 32.7 %all-to-all-start.1 = ((bf16[4,24,6144]{2,1,0:T(8,128)(2,1)}), bf16[4,24,6144]{2,1,0:T(8,128)(2,1)S(1)}, u32[]{:S(2)}, u32[]{:S(2)}) async-start(bf16[4,24,6144]{2,1,0:T(8,128)(2,1)} %prepare_feed.1), calls=%async_computation.1 | async-start | bytes 2359296 | tf_op jit(solution)/shard_map/all_to_all | solution.py:881
  28.9 17.8 %collective-permute-start.2 = (bf16[4,24,3200]{2,1,0:T(8,128)(2,1)S(1)}, bf16[4,24,3200]{2,1,0:T(8,128)(2,1)S(1)}, u32[]{:S(2)}, u32[]{:S(2)}) collective-permute-start(bf16[4,24,3200]{2,1,0:T(8,128)(2,1)S(1)} %all-to-all-done), channel_id=1, source_target_pairs={{0,24},{1,25},{2,26},{3,27},{4,28},{5,29},{6,30},{7,31},{8,16},{9,... | collective-permute-start | bytes 1843208 | tf_op jit(solution)/shard_map/ppermute | solution.py:862
  31.4 26.4 %collective-permute-start.1 = (bf16[4,24,3200]{2,1,0:T(8,128)(2,1)S(1)}, bf16[4,24,3200]{2,1,0:T(8,128)(2,1)S(1)}, u32[]{:S(2)}, u32[]{:S(2)}) collective-permute-start(bf16[4,24,3200]{2,1,0:T(8,128)(2,1)S(1)} %all-to-all-done), channel_id=1, source_target_pairs={{0,16},{1,17},{2,18},{3,19},{4,20},{5,21},{6,22},{7,23},{8,24},{9,... | collective-permute-start | bytes 1843208 | tf_op jit(solution)/shard_map/ppermute | solution.py:862
  31.9 26.1 %collective-permute-start = (bf16[4,24,3200]{2,1,0:T(8,128)(2,1)S(1)}, bf16[4,24,3200]{2,1,0:T(8,128)(2,1)}, u32[]{:S(2)}, u32[]{:S(2)}) collective-permute-start(bf16[4,24,3200]{2,1,0:T(8,128)(2,1)S(1)} %all-to-all-done), channel_id=1, source_target_pairs={{0,8},{1,9},{2,10},{3,11},{4,12},{5,13},{6,14},{7,15},{8,0},{9,1},... | collective-permute-start | bytes 1843208 | tf_op jit(solution)/shard_map/ppermute | solution.py:862
  58.7 42.0 %all-to-all-start.2 = ((bf16[4,2,128,768]{3,2,1,0:T(8,128)(2,1)}), bf16[4,2,128,768]{3,2,1,0:T(8,128)(2,1)S(1)}, u32[]{:S(2)}, u32[]{:S(2)}) async-start(bf16[4,2,128,768]{3,2,1,0:T(8,128)(2,1)} %bitcast.3), calls=%async_computation.2 | async-start | bytes 3145728 | tf_op jit(solution)/shard_map/all_to_all | solution.py:881
  63.9 6.9 %collective-permute-start.5 = (bf16[96,3200]{1,0:T(8,128)(2,1)}, bf16[96,3200]{1,0:T(8,128)(2,1)}, u32[]{:S(2)}, u32[]{:S(2)}) collective-permute-start(bf16[96,3200]{1,0:T(8,128)(2,1)} %bitcast.71), channel_id=1, source_target_pairs={{0,4},{1,5},{2,6},{3,7},{4,0},{5,1},{6,2},{7,3},{8,12},{9,13},{10,... | collective-permute-start | bytes 1843208 | tf_op jit(solution)/shard_map/ppermute | solution.py:862
  64.0 6.9 %collective-permute-start.4 = (bf16[96,3200]{1,0:T(8,128)(2,1)}, bf16[96,3200]{1,0:T(8,128)(2,1)}, u32[]{:S(2)}, u32[]{:S(2)}) collective-permute-start(bf16[96,3200]{1,0:T(8,128)(2,1)} %bitcast.14.refs_1_), channel_id=1, source_target_pairs={{0,4},{1,5},{2,6},{3,7},{4,0},{5,1},{6,2},{7,3},{8,12},{9,13},{10,... | collective-permute-start | bytes 1843208 | tf_op jit(solution)/shard_map/ppermute | solution.py:862
  64.4 65.8 %collective-permute-start.9 = (bf16[4,24,6144]{2,1,0:T(8,128)(2,1)S(1)}, bf16[4,24,6144]{2,1,0:T(8,128)(2,1)}, u32[]{:S(2)}, u32[]{:S(2)}) collective-permute-start(bf16[4,24,6144]{2,1,0:T(8,128)(2,1)S(1)} %all-to-all-done.1.refs_8_), channel_id=1, source_target_pairs={{0,24},{1,25},{2,26},{3,27},{4,28},{5,29},{6,30},{7,31},{8,16},{9,... | collective-permute-start | bytes 3538952 | tf_op jit(solution)/shard_map/ppermute | solution.py:862
  66.2 64.1 %collective-permute-start.8 = (bf16[4,24,6144]{2,1,0:T(8,128)(2,1)S(1)}, bf16[4,24,6144]{2,1,0:T(8,128)(2,1)}, u32[]{:S(2)}, u32[]{:S(2)}) collective-permute-start(bf16[4,24,6144]{2,1,0:T(8,128)(2,1)S(1)} %all-to-all-done.1.refs_8_), channel_id=1, source_target_pairs={{0,16},{1,17},{2,18},{3,19},{4,20},{5,21},{6,22},{7,23},{8,24},{9,... | collective-permute-start | bytes 3538952 | tf_op jit(solution)/shard_map/ppermute | solution.py:862
  68.2 62.0 %collective-permute-start.7 = (bf16[4,24,6144]{2,1,0:T(8,128)(2,1)S(1)}, bf16[4,24,6144]{2,1,0:T(8,128)(2,1)}, u32[]{:S(2)}, u32[]{:S(2)}) collective-permute-start(bf16[4,24,6144]{2,1,0:T(8,128)(2,1)S(1)} %all-to-all-done.1.refs_8_), channel_id=1, source_target_pairs={{0,8},{1,9},{2,10},{3,11},{4,12},{5,13},{6,14},{7,15},{8,0},{9,1},... | collective-permute-start | bytes 3538952 | tf_op jit(solution)/shard_map/ppermute | solution.py:862
  76.8 59.9 %collective-permute-start.10 = (bf16[96,6144]{1,0:T(8,128)(2,1)S(1)}, bf16[96,6144]{1,0:T(8,128)(2,1)}, u32[]{:S(2)}, u32[]{:S(2)}) collective-permute-start(bf16[96,6144]{1,0:T(8,128)(2,1)S(1)} %bitcast.67), channel_id=1, source_target_pairs={{0,4},{1,5},{2,6},{3,7},{4,0},{5,1},{6,2},{7,3},{8,12},{9,13},{10,... | collective-permute-start | bytes 3538952 | tf_op jit(solution)/shard_map/ppermute | solution.py:862
  101.8 62.9 %all-to-all-start.3 = ((bf16[4,2,128,768]{3,2,1,0:T(8,128)(2,1)}), bf16[4,2,128,768]{3,2,1,0:T(8,128)(2,1)}, u32[]{:S(2)}, u32[]{:S(2)}) async-start(bf16[4,2,128,768]{3,2,1,0:T(8,128)(2,1)} %bitcast.26), calls=%async_computation.3 | async-start | bytes 3145728 | tf_op jit(solution)/shard_map/all_to_all | solution.py:881
  130.3 6.4 %collective-permute-start.11 = (bf16[96,6144]{1,0:T(8,128)(2,1)}, bf16[96,6144]{1,0:T(8,128)(2,1)S(1)}, u32[]{:S(2)}, u32[]{:S(2)}) collective-permute-start(bf16[96,6144]{1,0:T(8,128)(2,1)} %bitcast.19.refs_1_), channel_id=1, source_target_pairs={{0,4},{1,5},{2,6},{3,7},{4,0},{5,1},{6,2},{7,3},{8,12},{9,13},{10,... | collective-permute-start | bytes 3538952 | tf_op jit(solution)/shard_map/ppermute | solution.py:862
  130.3 6.4 %collective-permute-start.12 = (bf16[96,6144]{1,0:T(8,128)(2,1)}, bf16[96,6144]{1,0:T(8,128)(2,1)S(1)}, u32[]{:S(2)}, u32[]{:S(2)}) collective-permute-start(bf16[96,6144]{1,0:T(8,128)(2,1)} %bitcast.20.refs_2_), channel_id=1, source_target_pairs={{0,4},{1,5},{2,6},{3,7},{4,0},{5,1},{6,2},{7,3},{8,12},{9,13},{10,... | collective-permute-start | bytes 3538952 | tf_op jit(solution)/shard_map/ppermute | solution.py:862
  130.8 6.1 %collective-permute-start.13 = (bf16[96,6144]{1,0:T(8,128)(2,1)}, bf16[96,6144]{1,0:T(8,128)(2,1)}, u32[]{:S(2)}, u32[]{:S(2)}) collective-permute-start(bf16[96,6144]{1,0:T(8,128)(2,1)} %bitcast.21.refs_3_), channel_id=1, source_target_pairs={{0,4},{1,5},{2,6},{3,7},{4,0},{5,1},{6,2},{7,3},{8,12},{9,13},{10,... | collective-permute-start | bytes 3538952 | tf_op jit(solution)/shard_map/ppermute | solution.py:862
  164.7 48.0 %all-to-all-start.4 = ((bf16[4,2,128,768]{3,2,1,0:T(8,128)(2,1)}), bf16[4,2,128,768]{3,2,1,0:T(8,128)(2,1)}, u32[]{:S(2)}, u32[]{:S(2)}) async-start(bf16[4,2,128,768]{3,2,1,0:T(8,128)(2,1)} %get-tuple-element.124), calls=%async_computation.4 | async-start | bytes 3145728 | tf_op jit(solution)/shard_map/all_to_all | solution.py:881
  200.6 12.1 %collective-permute-start.16 = (bf16[4,96,3072]{2,1,0:T(8,128)(2,1)}, bf16[4,96,3072]{2,1,0:T(8,128)(2,1)}, u32[]{:S(2)}, u32[]{:S(2)}) collective-permute-start(bf16[4,96,3072]{2,1,0:T(8,128)(2,1)} %get-tuple-element.132), channel_id=1, source_target_pairs={{0,4},{1,5},{2,6},{3,7},{4,0},{5,1},{6,2},{7,3},{8,12},{9,13},{10,... | collective-permute-start | bytes 7077896 | tf_op jit(solution)/shard_map/ppermute | solution.py:862
  200.8 11.9 %collective-permute-start.14 = (bf16[4,384,768]{2,1,0:T(8,128)(2,1)}, bf16[4,384,768]{2,1,0:T(8,128)(2,1)}, u32[]{:S(2)}, u32[]{:S(2)}) collective-permute-start(bf16[4,384,768]{2,1,0:T(8,128)(2,1)} %get-tuple-element.133), channel_id=1, source_target_pairs={{0,4},{1,5},{2,6},{3,7},{4,0},{5,1},{6,2},{7,3},{8,12},{9,13},{10,... | collective-permute-start | bytes 7077896 | tf_op jit(solution)/shard_map/ppermute | solution.py:862
  221.2 62.3 %collective-permute-start.19 = (bf16[4,24,7040]{2,1,0:T(8,128)(2,1)}, bf16[4,24,7040]{2,1,0:T(8,128)(2,1)}, u32[]{:S(2)}, u32[]{:S(2)}) collective-permute-start(bf16[4,24,7040]{2,1,0:T(8,128)(2,1)} %get-tuple-element.149), channel_id=1, source_target_pairs={{0,8},{1,9},{2,10},{3,11},{4,12},{5,13},{6,14},{7,15},{8,0},{9,1},... | collective-permute-start | bytes 4055048 | tf_op jit(solution)/shard_map/ppermute | solution.py:862
  222.7 60.8 %collective-permute-start.20 = (bf16[4,24,7040]{2,1,0:T(8,128)(2,1)}, bf16[4,24,7040]{2,1,0:T(8,128)(2,1)}, u32[]{:S(2)}, u32[]{:S(2)}) collective-permute-start(bf16[4,24,7040]{2,1,0:T(8,128)(2,1)} %get-tuple-element.150), channel_id=1, source_target_pairs={{0,16},{1,17},{2,18},{3,19},{4,20},{5,21},{6,22},{7,23},{8,24},{9,... | collective-permute-start | bytes 4055048 | tf_op jit(solution)/shard_map/ppermute | solution.py:862
  222.8 60.4 %collective-permute-start.21 = (bf16[4,24,7040]{2,1,0:T(8,128)(2,1)}, bf16[4,24,7040]{2,1,0:T(8,128)(2,1)}, u32[]{:S(2)}, u32[]{:S(2)}) collective-permute-start(bf16[4,24,7040]{2,1,0:T(8,128)(2,1)} %get-tuple-element.151), channel_id=1, source_target_pairs={{0,24},{1,25},{2,26},{3,27},{4,28},{5,29},{6,30},{7,31},{8,16},{9,... | collective-permute-start | bytes 4055048 | tf_op jit(solution)/shard_map/ppermute | solution.py:862
  241.8 24.8 %all-to-all-start.5 = ((bf16[4,128,768]{2,1,0:T(8,128)(2,1)}), bf16[4,128,768]{2,1,0:T(8,128)(2,1)}, u32[]{:S(2)}, u32[]{:S(2)}) async-start(bf16[4,128,768]{2,1,0:T(8,128)(2,1)} %bitcast.57), calls=%async_computation.5 | async-start | bytes 1572864 | tf_op jit(solution)/shard_map/all_to_all | solution.py:881
  266.6 23.1 %all-to-all-start.6 = ((bf16[4,128,768]{2,1,0:T(8,128)(2,1)}), bf16[4,128,768]{2,1,0:T(8,128)(2,1)S(1)}, u32[]{:S(2)}, u32[]{:S(2)}) async-start(bf16[4,128,768]{2,1,0:T(8,128)(2,1)} %bitcast.56), calls=%async_computation.6 | async-start | bytes 1572864 | tf_op jit(solution)/shard_map/all_to_all | solution.py:881
  282.2 11.0 %collective-permute-start.18 = (bf16[4,96,2432]{2,1,0:T(8,128)(2,1)}, bf16[4,96,2432]{2,1,0:T(8,128)(2,1)}, u32[]{:S(2)}, u32[]{:S(2)}) collective-permute-start(bf16[4,96,2432]{2,1,0:T(8,128)(2,1)} %get-tuple-element.164), channel_id=1, source_target_pairs={{0,4},{1,5},{2,6},{3,7},{4,0},{5,1},{6,2},{7,3},{8,12},{9,13},{10,... | collective-permute-start | bytes 5603336 | tf_op jit(solution)/shard_map/ppermute | solution.py:862
  289.6 43.4 %all-to-all-start.7 = ((bf16[4,24,7040]{2,1,0:T(8,128)(2,1)}), bf16[4,24,7040]{2,1,0:T(8,128)(2,1)S(1)}, u32[]{:S(2)}, u32[]{:S(2)}) async-start(bf16[4,24,7040]{2,1,0:T(8,128)(2,1)} %feed_total.1), calls=%async_computation.7 | async-start | bytes 2703360 | tf_op jit(solution)/shard_map/all_to_all | solution.py:881
  297.9 13.8 %collective-permute-start.22 = (bf16[4,24,2432]{2,1,0:T(8,128)(2,1)}, bf16[4,24,2432]{2,1,0:T(8,128)(2,1)S(1)}, u32[]{:S(2)}, u32[]{:S(2)}) collective-permute-start(bf16[4,24,2432]{2,1,0:T(8,128)(2,1)} %get-tuple-element.171), channel_id=1, source_target_pairs={{0,8},{1,9},{2,10},{3,11},{4,12},{5,13},{6,14},{7,15},{8,0},{9,1},... | collective-permute-start | bytes 1400840 | tf_op jit(solution)/shard_map/ppermute | solution.py:862
  299.4 21.6 %collective-permute-start.23 = (bf16[4,24,2432]{2,1,0:T(8,128)(2,1)}, bf16[4,24,2432]{2,1,0:T(8,128)(2,1)S(1)}, u32[]{:S(2)}, u32[]{:S(2)}) collective-permute-start(bf16[4,24,2432]{2,1,0:T(8,128)(2,1)} %get-tuple-element.172), channel_id=1, source_target_pairs={{0,16},{1,17},{2,18},{3,19},{4,20},{5,21},{6,22},{7,23},{8,24},{9,... | collective-permute-start | bytes 1400840 | tf_op jit(solution)/shard_map/ppermute | solution.py:862
  299.7 21.3 %collective-permute-start.24 = (bf16[4,24,2432]{2,1,0:T(8,128)(2,1)}, bf16[4,24,2432]{2,1,0:T(8,128)(2,1)S(1)}, u32[]{:S(2)}, u32[]{:S(2)}) collective-permute-start(bf16[4,24,2432]{2,1,0:T(8,128)(2,1)} %get-tuple-element.173), channel_id=1, source_target_pairs={{0,24},{1,25},{2,26},{3,27},{4,28},{5,29},{6,30},{7,31},{8,16},{9,... | collective-permute-start | bytes 1400840 | tf_op jit(solution)/shard_map/ppermute | solution.py:862
  324.2 12.3 %collective-permute-start.25 = (bf16[24,2432]{1,0:T(8,128)(2,1)}, bf16[24,2432]{1,0:T(8,128)(2,1)S(1)}, u32[]{:S(2)}, u32[]{:S(2)}) collective-permute-start(bf16[24,2432]{1,0:T(8,128)(2,1)} %get-tuple-element.175), channel_id=1, source_target_pairs={{0,1},{1,2},{2,3},{3,0},{4,5},{5,6},{6,7},{7,4},{8,9},{9,10},{10,1... | collective-permute-start | bytes 350216 | tf_op jit(solution)/shard_map/ppermute | solution.py:870
  325.9 10.6 %collective-permute-start.26 = (bf16[24,2432]{1,0:T(8,128)(2,1)}, bf16[24,2432]{1,0:T(8,128)(2,1)S(1)}, u32[]{:S(2)}, u32[]{:S(2)}) collective-permute-start(bf16[24,2432]{1,0:T(8,128)(2,1)} %get-tuple-element.179), channel_id=1, source_target_pairs={{0,2},{1,3},{2,0},{3,1},{4,6},{5,7},{6,4},{7,5},{8,10},{9,11},{10,... | collective-permute-start | bytes 350216 | tf_op jit(solution)/shard_map/ppermute | solution.py:870
  328.3 8.2 %collective-permute-start.27 = (bf16[24,2432]{1,0:T(8,128)(2,1)}, bf16[24,2432]{1,0:T(8,128)(2,1)S(1)}, u32[]{:S(2)}, u32[]{:S(2)}) collective-permute-start(bf16[24,2432]{1,0:T(8,128)(2,1)} %get-tuple-element.181), channel_id=1, source_target_pairs={{0,3},{1,0},{2,1},{3,2},{4,7},{5,4},{6,5},{7,6},{8,11},{9,8},{10,9... | collective-permute-start | bytes 350216 | tf_op jit(solution)/shard_map/ppermute | solution.py:870
  (24 other events, 122.1 us)

commit v8 on v7

--- a/solution.py
+++ b/solution.py
@@ -733,7 +733,11 @@
             start = 0
             chip = spots[2] ^ part
             for kept, came in zip(ins[::2], ins[1::2]):
-                start = side_by_side(out, start, widen(kept[chip]) + widen(came[chip]))
+                if kept.shape[1] == small:
+                    out[:, start : start + kept.shape[2]] = kept[chip] + came[chip]
+                    start += kept.shape[2]
+                else:
+                    start = side_by_side(out, start, widen(kept[chip]) + widen(came[chip]))
 
     return kernel(
         body,

time: 341 us -> 341 us (level)
  no operation moved by 1% of the time
where the time goes in v8:
time: 341 us; the launch traced here: 339 us
  Pallas kernels  176 us (52%)
  waiting for transfers between devices  90.7 us (27%)
  starting transfers between devices  59.4 us (17%)
  local copies, waits for them, and re-layouts  10 us (3%)
    ppermute x25, waiting for transfers between devices, across(): return lax.ppermute(value, AXES, pairs)  48.4 us
    all_to_all x8, waiting for transfers between devices, turn(): lax.all_to_all(blocks, 'seq', split_axis=0, concat_axis=0, tiled=True)  42.3 us
    all_to_all x8, starting transfers between devices, turn(): lax.all_to_all(blocks, 'seq', split_axis=0, concat_axis=0, tiled=True)  36.1 us
    pallas_call x1, Pallas kernels, feed_back(): kernel(feed_back_body, 'feed_back', 8 * count * width * wide, 12 * count...  31.1 us
    pallas_call x1, Pallas kernels, feed(): kernel(feed_body, 'feed', 4 * count * width * wide, 12 * count * wide, gr...  26.5 us
    pallas_call x2, Pallas kernels, attend_back(): kernel(attend_back_body, 'attend_back', 10 ** 12 if row else 0, pairs * 8...  22.8 us
    ppermute x25, starting transfers between devices, across(): return lax.ppermute(value, AXES, pairs)  17.8 us
    pallas_call x1, Pallas kernels, attend(): kernel(attend_body, 'attend', rows * pairs * 16 * length * length * LANES...  16.2 us
  transfers between devices with their start and end apart: 36, of which 14 were waited for; matrix products, arithmetic and copies ran while one was open for 1% of the time, Pallas kernels for 49%

profile of v8, /device:TPU:0, one launch (start us, length us, event | category | flops | bytes accessed | tf_op | source)
XLA Modules:
  0.0 338.9 jit_solution(6977375703826914319)
XLA Ops:
  2.6 6.3 %all-to-all-start = ((bf16[4,24,3200]{2,1,0:T(8,128)(2,1)}), bf16[4,24,3200]{2,1,0:T(8,128)(2,1)S(1)}, u32[]{:S(2)}, u32[]{:S(2)}) async-start(bf16[4,24,3200]{2,1,0:T(8,128)(2,1)} %prepare_attention.1), calls=%async_computation | async-start | bytes 1228800 | tf_op jit(solution)/shard_map/all_to_all | solution.py:885
  11.1 14.3 %all-to-all-done = bf16[4,24,3200]{2,1,0:T(8,128)(2,1)S(1)} async-done(((bf16[4,24,3200]{2,1,0:T(8,128)(2,1)}), bf16[4,24,3200]{2,1,0:T(8,128)(2,1)S(1)}, u32[]{:S(2)}, u32[]{:S(2)}) %all-to-all-start) | async-done | bytes 614432 | tf_op jit(solution)/shard_map/all_to_all | solution.py:885
  25.4 3.5 %all-to-all-start.1 = ((bf16[4,24,6144]{2,1,0:T(8,128)(2,1)}), bf16[4,24,6144]{2,1,0:T(8,128)(2,1)S(1)}, u32[]{:S(2)}, u32[]{:S(2)}) async-start(bf16[4,24,6144]{2,1,0:T(8,128)(2,1)} %prepare_feed.1), calls=%async_computation.1 | async-start | bytes 2359296 | tf_op jit(solution)/shard_map/all_to_all | solution.py:885
  28.9 2.5 collective-permute-start.2
  32.5 14.2 %collective-permute-done.2 = bf16[4,24,3200]{2,1,0:T(8,128)(2,1)S(1)} collective-permute-done((bf16[4,24,3200]{2,1,0:T(8,128)(2,1)S(1)}, bf16[4,24,3200]{2,1,0:T(8,128)(2,1)S(1)}, u32[]{:S(2)}, u32[]{:S(2)}) %collective-permute-start.2) | collective-permute-done | bytes 614432 | tf_op jit(solution)/shard_map/ppermute | solution.py:866
  46.7 11.2 %collective-permute-done.1 = bf16[4,24,3200]{2,1,0:T(8,128)(2,1)S(1)} collective-permute-done((bf16[4,24,3200]{2,1,0:T(8,128)(2,1)S(1)}, bf16[4,24,3200]{2,1,0:T(8,128)(2,1)S(1)}, u32[]{:S(2)}, u32[]{:S(2)}) %collective-permute-start.1) | collective-permute-done | bytes 614432 | tf_op jit(solution)/shard_map/ppermute | solution.py:866
  58.7 4.7 %all-to-all-start.2 = ((bf16[4,2,128,768]{3,2,1,0:T(8,128)(2,1)}), bf16[4,2,128,768]{3,2,1,0:T(8,128)(2,1)S(1)}, u32[]{:S(2)}, u32[]{:S(2)}) async-start(bf16[4,2,128,768]{3,2,1,0:T(8,128)(2,1)} %bitcast.3), calls=%async_computation.2 | async-start | bytes 3145728 | tf_op jit(solution)/shard_map/all_to_all | solution.py:885
  70.8 6.0 %unite_attention.1 = (bf16[768,2304]{1,0:T(8,128)(2,1)}, bf16[768,768]{1,0:T(8,128)(2,1)}, f32[8,768]{1,0:T(8,128)}, f32[1,3072]{1,0:T(1,128)}) custom-call(s32[3]{0:T(128)} %pad_add_fusion.spots, bf16[96,3200]{1,0:T(8,128)(2,1)} %bitcast.60, bf16[96,3200]{1,0:T(8,128)(2,1)} %bitcast.14.refs_1_, bf16[96,3200]{1,0:T(8,128)(2,1)} %bitcast.72, ...), custom_call_target="tpu_custom_call" | custom-call | bytes 9830400 | tf_op jit(solution)/shard_map/unite_attention/pallas_call | solution.py:174
  76.9 23.8 %all-to-all-done.2.tokens = bf16[4,2,128,768]{3,2,1,0:T(8,128)(2,1)S(1)} async-done(((bf16[4,2,128,768]{3,2,1,0:T(8,128)(2,1)}), bf16[4,2,128,768]{3,2,1,0:T(8,128)(2,1)S(1)}, u32[]{:S(2)}, u32[]{:S(2)}) %all-to-all-start.2) | async-done | bytes 1572896 | tf_op jit(solution)/shard_map/all_to_all | solution.py:885
  101.8 4.5 %all-to-all-start.3 = ((bf16[4,2,128,768]{3,2,1,0:T(8,128)(2,1)}), bf16[4,2,128,768]{3,2,1,0:T(8,128)(2,1)}, u32[]{:S(2)}, u32[]{:S(2)}) async-start(bf16[4,2,128,768]{3,2,1,0:T(8,128)(2,1)} %bitcast.26), calls=%async_computation.3 | async-start | bytes 3145728 | tf_op jit(solution)/shard_map/all_to_all | solution.py:885
  106.3 7.7 %project.1 = (bf16[2,512,2304]{2,1,0:T(8,128)(2,1)}, bf16[1024,768]{1,0:T(8,128)(2,1)}) custom-call(bf16[4,2,128,768]{3,2,1,0:T(8,128)(2,1)} %copy-done.2, bf16[768,2304]{1,0:T(8,128)(2,1)} %get-tuple-element.107.weight, f32[8,768]{1,0:T(8,128)} %get-tuple-element.108.rows.rows_one), custom_call_target="tpu_custom_call" | custom-call | flops 3623878656 | bytes 6291456 | tf_op jit(solution)/shard_map/project/pallas_call | solution.py:210
  114.1 16.2 %attend.1 = (bf16[2,512,768]{2,1,0:T(8,128)(2,1)}, bf16[2,12,512,512]{3,2,1,0:T(8,128)(2,1)}) custom-call(s32[3]{0:T(128)} %pad_add_fusion.spots, s32[8,4]{1,0:T(8,128)} %copy.33.lengths, bf16[2,512,2304]{2,1,0:T(8,128)(2,1)} %get-tuple-element.109.query.key.value, bf16[2,512,2304]{2,1,0:T(8,128)(2,1)} %get-tuple-element.109.query.key.value, ...), custom_call_target="tpu_custom_call" | custom-call | flops 6442450944 | bytes 25165824 | tf_op jit(solution)/shard_map/attend/pallas_call | solution.py:272
  130.9 5.8 %settle.1 = (f32[1024,768]{1,0:T(8,128)}, f32[1024,1]{1,0:T(8,128)}, bf16[1024,768]{1,0:T(8,128)(2,1)}) custom-call(bf16[1024,768]{1,0:T(8,128)(2,1)} %bitcast.97, bf16[1024,768]{1,0:T(8,128)(2,1)} %get-tuple-element.115.tokens, f32[8,768]{1,0:T(8,128)} %get-tuple-element.108.rows.rows_one, bf16[768,768]{1,0:T(8,128)(2,1)} %get-tuple-element.116.weight), custom_call_target="tpu_custom_call" | custom-call | flops 1207959552 | bytes 7864320 | tf_op jit(solution)/shard_map/settle/pallas_call | solution.py:374
  138.1 26.5 %feed.1 = (bf16[1024,3072]{1,0:T(8,128)(2,1)}, bf16[1024,3072]{1,0:T(8,128)(2,1)}, f32[1024,768]{1,0:T(8,128)}, f32[1024,1]{1,0:T(8,128)}, bf16[4,2,128,768]{3,2...) custom-call(s32[3]{0:T(128)} %pad_add_fusion.spots, bf16[1024,768]{1,0:T(8,128)(2,1)} %get-tuple-element.117.low, ...), custom_call_target="tpu_custom_call" | custom-call | flops 9663676416 | bytes 37748736 | tf_op jit(solution)/shard_map/feed/pallas_call | solution.py:472
  164.7 4.9 %all-to-all-start.4 = ((bf16[4,2,128,768]{3,2,1,0:T(8,128)(2,1)}), bf16[4,2,128,768]{3,2,1,0:T(8,128)(2,1)}, u32[]{:S(2)}, u32[]{:S(2)}) async-start(bf16[4,2,128,768]{3,2,1,0:T(8,128)(2,1)} %get-tuple-element.124), calls=%async_computation.4 | async-start | bytes 3145728 | tf_op jit(solution)/shard_map/all_to_all | solution.py:885
  169.5 31.1 %feed_back.1 = (bf16[4,96,3072]{2,1,0:T(8,128)(2,1)}, bf16[4,96,3072]{2,1,0:T(8,128)(2,1)}, bf16[4,384,768]{2,1,0:T(8,128)(2,1)}, bf16[4,384,768]{2,1,0:T(8,128)...) custom-call(s32[3]{0:T(128)} %pad_add_fusion.spots, ...), custom_call_target="tpu_custom_call" | custom-call | flops 19327352832 | bytes 37748736 | tf_op jit(solution)/shard_map/feed_back/pallas_call | solution.py:573
  201.2 9.3 %settle_back.1 = (f32[1024,768]{1,0:T(8,128)}, bf16[1024,768]{1,0:T(8,128)(2,1)}, bf16[4,96,768]{2,1,0:T(8,128)(2,1)}, bf16[4,96,768]{2,1,0:T(8,128)(2,1)}, f32[8,768]{1,0:T(8,128)}) custom-call(s32[3]{0:T(128)} %pad_add_fusion.spots, f32[1024,768]{1,0:T(8,128)} %get-tuple-element.135.hidden_grad, f32[1024,768]{1,0:T(8,128)} %get-tuple-element.119.normed_one.normed, ...), custom_call_target="tpu_custom_call" | custom-call | flops 999999995904 | bytes 12582912 | tf_op jit(solution)/shard_map/settle_back/pallas_call | solution.py:631
  213.6 7.4 %feed_chip_sums.1 = (bf16[4,24,7040]{2,1,0:T(8,128)(2,1)}, bf16[4,24,7040]{2,1,0:T(8,128)(2,1)}, bf16[4,24,7040]{2,1,0:T(8,128)(2,1)}, bf16[4,24,7040]{2,1,0:T(8,128)(2,1)}) custom-call(s32[3]{0:T(128)} %pad_add_fusion.spots, bf16[4,4,96,768]{3,2,1,0:T(8,128)(2,1)} %bitcast.62, bf16[4,4,96,768]{3,2,1,0:T(8,128)(2,1)} %bitcast.28.refs_1_, ...), custom_call_target="tpu_custom_call" | custom-call | bytes 16220160 | tf_op jit(solution)/shard_map/feed_chip_sums/pallas_call | solution.py:742
  224.5 11.4 %attend_back.2 = (bf16[2,512,2304]{2,1,0:T(8,128)(2,1)}, f32[2,1,2304]{2,1,0:T(1,128)}) custom-call(bf16[2,512,2304]{2,1,0:T(8,128)(2,1)} %get-tuple-element.109.query.key.value, bf16[2,512,2304]{2,1,0:T(8,128)(2,1)} %get-tuple-element.109.query.key.value, bf16[2,512,2304]{2,1,0:T(8,128)(2,1)} %get-tuple-element.109.query.key.value, ...), custom_call_target="tpu_custom_call" | custom-call | bytes 12582912 | tf_op jit(solution)/shard_map/attend_back/pallas_call | solution.py:328
  236.0 5.6 %tokens_back.2 = bf16[512,768]{1,0:T(8,128)(2,1)} custom-call(bf16[2,512,2304]{2,1,0:T(8,128)(2,1)} %get-tuple-element.154.packed_grad.rest_0_, bf16[768,2304]{1,0:T(8,128)(2,1)} %get-tuple-element.107.weight, f32[1024,768]{1,0:T(8,128)} %get-tuple-element.155.first_up), custom_call_target="tpu_custom_call" | custom-call | flops 1811939328 | bytes 3145728 | tf_op jit(solution)/shard_map/tokens_back/pallas_call | solution.py:659
  241.6 5.1 %all-to-all-start.5 = ((bf16[4,128,768]{2,1,0:T(8,128)(2,1)}), bf16[4,128,768]{2,1,0:T(8,128)(2,1)}, u32[]{:S(2)}, u32[]{:S(2)}) async-start(bf16[4,128,768]{2,1,0:T(8,128)(2,1)} %bitcast.57), calls=%async_computation.5 | async-start | bytes 1572864 | tf_op jit(solution)/shard_map/all_to_all | solution.py:885
  246.7 11.4 %attend_back.3 = (bf16[2,512,2304]{2,1,0:T(8,128)(2,1)}, f32[2,1,2304]{2,1,0:T(1,128)}) custom-call(bf16[2,512,2304]{2,1,0:T(8,128)(2,1)} %get-tuple-element.109.query.key.value, bf16[2,512,2304]{2,1,0:T(8,128)(2,1)} %get-tuple-element.109.query.key.value, ...), custom_call_target="tpu_custom_call", output_to_operand_aliasing={{0}: (5, {}), {1}: (6, {})} | custom-call | flops 999999995904 | bytes 12582912 | tf_op jit(solution)/shard_map/attend_back/pallas_call | solution.py:328
  258.1 5.6 %tokens_back.3 = bf16[512,768]{1,0:T(8,128)(2,1)} custom-call(bf16[2,512,2304]{2,1,0:T(8,128)(2,1)} %get-tuple-element.159.packed_grad, bf16[768,2304]{1,0:T(8,128)(2,1)} %get-tuple-element.107.weight, f32[1024,768]{1,0:T(8,128)} %get-tuple-element.155.first_up), custom_call_target="tpu_custom_call" | custom-call | flops 1811939328 | bytes 3145728 | tf_op jit(solution)/shard_map/tokens_back/pallas_call | solution.py:659
  263.8 2.6 all-to-all-done.5
  266.4 3.5 %all-to-all-start.6 = ((bf16[4,128,768]{2,1,0:T(8,128)(2,1)}), bf16[4,128,768]{2,1,0:T(8,128)(2,1)S(1)}, u32[]{:S(2)}, u32[]{:S(2)}) async-start(bf16[4,128,768]{2,1,0:T(8,128)(2,1)} %bitcast.56), calls=%async_computation.6 | async-start | bytes 1572864 | tf_op jit(solution)/shard_map/all_to_all | solution.py:885
  269.9 8.6 %weights_back.1 = (bf16[4,96,2432]{2,1,0:T(8,128)(2,1)}, bf16[4,96,2432]{2,1,0:T(8,128)(2,1)}) custom-call(s32[3]{0:T(128)} %pad_add_fusion.spots, bf16[1024,2304]{1,0:T(8,128)(2,1)} %bitcast.54, bf16[1024,768]{1,0:T(8,128)(2,1)} %get-tuple-element.115.tokens, f32[2,1,2304]{2,1,0:T(1,128)} %get-tuple-element.160.packed_sums, f32[8,768]{1,0:T(8,128)} %get-tuple-element.137.sums), custom_call_target="tpu_custom_call" | custom-call | flops 3623878656 | bytes 6291456 | tf_op jit(solution)/shard_map/weights_back/pallas_call | solution.py:695
  278.4 3.6 %copied.1 = bf16[4,2,128,768]{3,2,1,0:T(8,128)(2,1)} custom-call(bf16[4,2,128,768]{3,2,1,0:T(8,128)(2,1)} %all-to-all-done.4.source), custom_call_target="tpu_custom_call" | custom-call | bytes 3145728 | tf_op jit(solution)/shard_map/copied/pallas_call | solution.py:803
  283.3 4.5 %feed_total.1 = bf16[4,24,7040]{2,1,0:T(8,128)(2,1)} custom-call(bf16[4,24,7040]{2,1,0:T(8,128)(2,1)} %get-tuple-element.165.refs_0_, bf16[4,24,7040]{2,1,0:T(8,128)(2,1)} %collective-permute-done.19.refs_1_, bf16[4,24,7040]{2,1,0:T(8,128)(2,1)} %collective-permute-done.20.refs_2_, bf16[4,24,7040]{2,1,0:T(8,128)(2,1)} %collective-permute-done.21.refs_3_), custom_call_target="tpu_custom_call" | custom-call | flops 10000000000 | bytes 6758400 | tf_op jit(solution)/shard_map/feed_total/pallas_call | solution.py:767
  289.4 3.5 %all-to-all-start.7 = ((bf16[4,24,7040]{2,1,0:T(8,128)(2,1)}), bf16[4,24,7040]{2,1,0:T(8,128)(2,1)S(1)}, u32[]{:S(2)}, u32[]{:S(2)}) async-start(bf16[4,24,7040]{2,1,0:T(8,128)(2,1)} %feed_total.1), calls=%async_computation.7 | async-start | bytes 2703360 | tf_op jit(solution)/shard_map/all_to_all | solution.py:885
  293.0 4.7 %attention_chip_sums.1 = (bf16[4,24,2432]{2,1,0:T(8,128)(2,1)}, bf16[4,24,2432]{2,1,0:T(8,128)(2,1)}, bf16[4,24,2432]{2,1,0:T(8,128)(2,1)}, bf16[4,24,2432]{2,1,0:T(8,128)(2,1)}) custom-call(s32[3]{0:T(128)} %pad_add_fusion.spots, bf16[4,4,24,2432]{3,2,1,0:T(8,128)(2,1)} %bitcast.63, bf16[4,4,24,2432]{3,2,1,0:T(8,128)(2,1)} %bitcast.44.refs_1_), custom_call_target="tpu_custom_call" | custom-call | bytes 5603328 | tf_op jit(solution)/shard_map/attention_chip_sums/pallas_call | solution.py:742
  301.2 10.4 %collective-permute-done.22.refs_1_ = bf16[4,24,2432]{2,1,0:T(8,128)(2,1)S(1)} collective-permute-done((bf16[4,24,2432]{2,1,0:T(8,128)(2,1)}, bf16[4,24,2432]{2,1,0:T(8,128)(2,1)S(1)}, u32[]{:S(2)}, u32[]{:S(2)}) %collective-permute-start.22) | collective-permute-done | bytes 466976 | tf_op jit(solution)/shard_map/ppermute | solution.py:866
  311.6 9.2 %collective-permute-done.23.refs_2_ = bf16[4,24,2432]{2,1,0:T(8,128)(2,1)S(1)} collective-permute-done((bf16[4,24,2432]{2,1,0:T(8,128)(2,1)}, bf16[4,24,2432]{2,1,0:T(8,128)(2,1)S(1)}, u32[]{:S(2)}, u32[]{:S(2)}) %collective-permute-start.23) | collective-permute-done | bytes 466976 | tf_op jit(solution)/shard_map/ppermute | solution.py:866
  (105 shorter events, 48.4 us)
Async XLA Ops:
  2.6 22.7 %all-to-all-start = ((bf16[4,24,3200]{2,1,0:T(8,128)(2,1)}), bf16[4,24,3200]{2,1,0:T(8,128)(2,1)S(1)}, u32[]{:S(2)}, u32[]{:S(2)}) async-start(bf16[4,24,3200]{2,1,0:T(8,128)(2,1)} %prepare_attention.1), calls=%async_computation | async-start | bytes 1228800 | tf_op jit(solution)/shard_map/all_to_all | solution.py:885
  25.4 32.7 %all-to-all-start.1 = ((bf16[4,24,6144]{2,1,0:T(8,128)(2,1)}), bf16[4,24,6144]{2,1,0:T(8,128)(2,1)S(1)}, u32[]{:S(2)}, u32[]{:S(2)}) async-start(bf16[4,24,6144]{2,1,0:T(8,128)(2,1)} %prepare_feed.1), calls=%async_computation.1 | async-start | bytes 2359296 | tf_op jit(solution)/shard_map/all_to_all | solution.py:885
  28.9 17.8 %collective-permute-start.2 = (bf16[4,24,3200]{2,1,0:T(8,128)(2,1)S(1)}, bf16[4,24,3200]{2,1,0:T(8,128)(2,1)S(1)}, u32[]{:S(2)}, u32[]{:S(2)}) collective-permute-start(bf16[4,24,3200]{2,1,0:T(8,128)(2,1)S(1)} %all-to-all-done), channel_id=1, source_target_pairs={{0,24},{1,25},{2,26},{3,27},{4,28},{5,29},{6,30},{7,31},{8,16},{9,... | collective-permute-start | bytes 1843208 | tf_op jit(solution)/shard_map/ppermute | solution.py:866
  31.4 26.4 %collective-permute-start.1 = (bf16[4,24,3200]{2,1,0:T(8,128)(2,1)S(1)}, bf16[4,24,3200]{2,1,0:T(8,128)(2,1)S(1)}, u32[]{:S(2)}, u32[]{:S(2)}) collective-permute-start(bf16[4,24,3200]{2,1,0:T(8,128)(2,1)S(1)} %all-to-all-done), channel_id=1, source_target_pairs={{0,16},{1,17},{2,18},{3,19},{4,20},{5,21},{6,22},{7,23},{8,24},{9,... | collective-permute-start | bytes 1843208 | tf_op jit(solution)/shard_map/ppermute | solution.py:866
  31.9 26.1 %collective-permute-start = (bf16[4,24,3200]{2,1,0:T(8,128)(2,1)S(1)}, bf16[4,24,3200]{2,1,0:T(8,128)(2,1)}, u32[]{:S(2)}, u32[]{:S(2)}) collective-permute-start(bf16[4,24,3200]{2,1,0:T(8,128)(2,1)S(1)} %all-to-all-done), channel_id=1, source_target_pairs={{0,8},{1,9},{2,10},{3,11},{4,12},{5,13},{6,14},{7,15},{8,0},{9,1},... | collective-permute-start | bytes 1843208 | tf_op jit(solution)/shard_map/ppermute | solution.py:866
  58.7 42.0 %all-to-all-start.2 = ((bf16[4,2,128,768]{3,2,1,0:T(8,128)(2,1)}), bf16[4,2,128,768]{3,2,1,0:T(8,128)(2,1)S(1)}, u32[]{:S(2)}, u32[]{:S(2)}) async-start(bf16[4,2,128,768]{3,2,1,0:T(8,128)(2,1)} %bitcast.3), calls=%async_computation.2 | async-start | bytes 3145728 | tf_op jit(solution)/shard_map/all_to_all | solution.py:885
  63.9 6.9 %collective-permute-start.5 = (bf16[96,3200]{1,0:T(8,128)(2,1)}, bf16[96,3200]{1,0:T(8,128)(2,1)}, u32[]{:S(2)}, u32[]{:S(2)}) collective-permute-start(bf16[96,3200]{1,0:T(8,128)(2,1)} %bitcast.71), channel_id=1, source_target_pairs={{0,4},{1,5},{2,6},{3,7},{4,0},{5,1},{6,2},{7,3},{8,12},{9,13},{10,... | collective-permute-start | bytes 1843208 | tf_op jit(solution)/shard_map/ppermute | solution.py:866
  64.0 6.9 %collective-permute-start.4 = (bf16[96,3200]{1,0:T(8,128)(2,1)}, bf16[96,3200]{1,0:T(8,128)(2,1)}, u32[]{:S(2)}, u32[]{:S(2)}) collective-permute-start(bf16[96,3200]{1,0:T(8,128)(2,1)} %bitcast.14.refs_1_), channel_id=1, source_target_pairs={{0,4},{1,5},{2,6},{3,7},{4,0},{5,1},{6,2},{7,3},{8,12},{9,13},{10,... | collective-permute-start | bytes 1843208 | tf_op jit(solution)/shard_map/ppermute | solution.py:866
  64.4 65.8 %collective-permute-start.9 = (bf16[4,24,6144]{2,1,0:T(8,128)(2,1)S(1)}, bf16[4,24,6144]{2,1,0:T(8,128)(2,1)}, u32[]{:S(2)}, u32[]{:S(2)}) collective-permute-start(bf16[4,24,6144]{2,1,0:T(8,128)(2,1)S(1)} %all-to-all-done.1.refs_8_), channel_id=1, source_target_pairs={{0,24},{1,25},{2,26},{3,27},{4,28},{5,29},{6,30},{7,31},{8,16},{9,... | collective-permute-start | bytes 3538952 | tf_op jit(solution)/shard_map/ppermute | solution.py:866
  66.2 64.1 %collective-permute-start.8 = (bf16[4,24,6144]{2,1,0:T(8,128)(2,1)S(1)}, bf16[4,24,6144]{2,1,0:T(8,128)(2,1)}, u32[]{:S(2)}, u32[]{:S(2)}) collective-permute-start(bf16[4,24,6144]{2,1,0:T(8,128)(2,1)S(1)} %all-to-all-done.1.refs_8_), channel_id=1, source_target_pairs={{0,16},{1,17},{2,18},{3,19},{4,20},{5,21},{6,22},{7,23},{8,24},{9,... | collective-permute-start | bytes 3538952 | tf_op jit(solution)/shard_map/ppermute | solution.py:866
  68.2 62.0 %collective-permute-start.7 = (bf16[4,24,6144]{2,1,0:T(8,128)(2,1)S(1)}, bf16[4,24,6144]{2,1,0:T(8,128)(2,1)}, u32[]{:S(2)}, u32[]{:S(2)}) collective-permute-start(bf16[4,24,6144]{2,1,0:T(8,128)(2,1)S(1)} %all-to-all-done.1.refs_8_), channel_id=1, source_target_pairs={{0,8},{1,9},{2,10},{3,11},{4,12},{5,13},{6,14},{7,15},{8,0},{9,1},... | collective-permute-start | bytes 3538952 | tf_op jit(solution)/shard_map/ppermute | solution.py:866
  76.8 59.9 %collective-permute-start.10 = (bf16[96,6144]{1,0:T(8,128)(2,1)S(1)}, bf16[96,6144]{1,0:T(8,128)(2,1)}, u32[]{:S(2)}, u32[]{:S(2)}) collective-permute-start(bf16[96,6144]{1,0:T(8,128)(2,1)S(1)} %bitcast.67), channel_id=1, source_target_pairs={{0,4},{1,5},{2,6},{3,7},{4,0},{5,1},{6,2},{7,3},{8,12},{9,13},{10,... | collective-permute-start | bytes 3538952 | tf_op jit(solution)/shard_map/ppermute | solution.py:866
  101.8 62.9 %all-to-all-start.3 = ((bf16[4,2,128,768]{3,2,1,0:T(8,128)(2,1)}), bf16[4,2,128,768]{3,2,1,0:T(8,128)(2,1)}, u32[]{:S(2)}, u32[]{:S(2)}) async-start(bf16[4,2,128,768]{3,2,1,0:T(8,128)(2,1)} %bitcast.26), calls=%async_computation.3 | async-start | bytes 3145728 | tf_op jit(solution)/shard_map/all_to_all | solution.py:885
  130.3 6.4 %collective-permute-start.11 = (bf16[96,6144]{1,0:T(8,128)(2,1)}, bf16[96,6144]{1,0:T(8,128)(2,1)S(1)}, u32[]{:S(2)}, u32[]{:S(2)}) collective-permute-start(bf16[96,6144]{1,0:T(8,128)(2,1)} %bitcast.19.refs_1_), channel_id=1, source_target_pairs={{0,4},{1,5},{2,6},{3,7},{4,0},{5,1},{6,2},{7,3},{8,12},{9,13},{10,... | collective-permute-start | bytes 3538952 | tf_op jit(solution)/shard_map/ppermute | solution.py:866
  130.3 6.4 %collective-permute-start.12 = (bf16[96,6144]{1,0:T(8,128)(2,1)}, bf16[96,6144]{1,0:T(8,128)(2,1)S(1)}, u32[]{:S(2)}, u32[]{:S(2)}) collective-permute-start(bf16[96,6144]{1,0:T(8,128)(2,1)} %bitcast.20.refs_2_), channel_id=1, source_target_pairs={{0,4},{1,5},{2,6},{3,7},{4,0},{5,1},{6,2},{7,3},{8,12},{9,13},{10,... | collective-permute-start | bytes 3538952 | tf_op jit(solution)/shard_map/ppermute | solution.py:866
  130.8 6.1 %collective-permute-start.13 = (bf16[96,6144]{1,0:T(8,128)(2,1)}, bf16[96,6144]{1,0:T(8,128)(2,1)}, u32[]{:S(2)}, u32[]{:S(2)}) collective-permute-start(bf16[96,6144]{1,0:T(8,128)(2,1)} %bitcast.21.refs_3_), channel_id=1, source_target_pairs={{0,4},{1,5},{2,6},{3,7},{4,0},{5,1},{6,2},{7,3},{8,12},{9,13},{10,... | collective-permute-start | bytes 3538952 | tf_op jit(solution)/shard_map/ppermute | solution.py:866
  164.7 48.0 %all-to-all-start.4 = ((bf16[4,2,128,768]{3,2,1,0:T(8,128)(2,1)}), bf16[4,2,128,768]{3,2,1,0:T(8,128)(2,1)}, u32[]{:S(2)}, u32[]{:S(2)}) async-start(bf16[4,2,128,768]{3,2,1,0:T(8,128)(2,1)} %get-tuple-element.124), calls=%async_computation.4 | async-start | bytes 3145728 | tf_op jit(solution)/shard_map/all_to_all | solution.py:885
  200.6 12.1 %collective-permute-start.16 = (bf16[4,96,3072]{2,1,0:T(8,128)(2,1)}, bf16[4,96,3072]{2,1,0:T(8,128)(2,1)}, u32[]{:S(2)}, u32[]{:S(2)}) collective-permute-start(bf16[4,96,3072]{2,1,0:T(8,128)(2,1)} %get-tuple-element.132), channel_id=1, source_target_pairs={{0,4},{1,5},{2,6},{3,7},{4,0},{5,1},{6,2},{7,3},{8,12},{9,13},{10,... | collective-permute-start | bytes 7077896 | tf_op jit(solution)/shard_map/ppermute | solution.py:866
  200.8 11.9 %collective-permute-start.14 = (bf16[4,384,768]{2,1,0:T(8,128)(2,1)}, bf16[4,384,768]{2,1,0:T(8,128)(2,1)}, u32[]{:S(2)}, u32[]{:S(2)}) collective-permute-start(bf16[4,384,768]{2,1,0:T(8,128)(2,1)} %get-tuple-element.133), channel_id=1, source_target_pairs={{0,4},{1,5},{2,6},{3,7},{4,0},{5,1},{6,2},{7,3},{8,12},{9,13},{10,... | collective-permute-start | bytes 7077896 | tf_op jit(solution)/shard_map/ppermute | solution.py:866
  221.0 62.3 %collective-permute-start.19 = (bf16[4,24,7040]{2,1,0:T(8,128)(2,1)}, bf16[4,24,7040]{2,1,0:T(8,128)(2,1)}, u32[]{:S(2)}, u32[]{:S(2)}) collective-permute-start(bf16[4,24,7040]{2,1,0:T(8,128)(2,1)} %get-tuple-element.149), channel_id=1, source_target_pairs={{0,8},{1,9},{2,10},{3,11},{4,12},{5,13},{6,14},{7,15},{8,0},{9,1},... | collective-permute-start | bytes 4055048 | tf_op jit(solution)/shard_map/ppermute | solution.py:866
  222.5 60.8 %collective-permute-start.20 = (bf16[4,24,7040]{2,1,0:T(8,128)(2,1)}, bf16[4,24,7040]{2,1,0:T(8,128)(2,1)}, u32[]{:S(2)}, u32[]{:S(2)}) collective-permute-start(bf16[4,24,7040]{2,1,0:T(8,128)(2,1)} %get-tuple-element.150), channel_id=1, source_target_pairs={{0,16},{1,17},{2,18},{3,19},{4,20},{5,21},{6,22},{7,23},{8,24},{9,... | collective-permute-start | bytes 4055048 | tf_op jit(solution)/shard_map/ppermute | solution.py:866
  222.6 60.4 %collective-permute-start.21 = (bf16[4,24,7040]{2,1,0:T(8,128)(2,1)}, bf16[4,24,7040]{2,1,0:T(8,128)(2,1)}, u32[]{:S(2)}, u32[]{:S(2)}) collective-permute-start(bf16[4,24,7040]{2,1,0:T(8,128)(2,1)} %get-tuple-element.151), channel_id=1, source_target_pairs={{0,24},{1,25},{2,26},{3,27},{4,28},{5,29},{6,30},{7,31},{8,16},{9,... | collective-permute-start | bytes 4055048 | tf_op jit(solution)/shard_map/ppermute | solution.py:866
  241.6 24.8 %all-to-all-start.5 = ((bf16[4,128,768]{2,1,0:T(8,128)(2,1)}), bf16[4,128,768]{2,1,0:T(8,128)(2,1)}, u32[]{:S(2)}, u32[]{:S(2)}) async-start(bf16[4,128,768]{2,1,0:T(8,128)(2,1)} %bitcast.57), calls=%async_computation.5 | async-start | bytes 1572864 | tf_op jit(solution)/shard_map/all_to_all | solution.py:885
  266.4 23.1 %all-to-all-start.6 = ((bf16[4,128,768]{2,1,0:T(8,128)(2,1)}), bf16[4,128,768]{2,1,0:T(8,128)(2,1)S(1)}, u32[]{:S(2)}, u32[]{:S(2)}) async-start(bf16[4,128,768]{2,1,0:T(8,128)(2,1)} %bitcast.56), calls=%async_computation.6 | async-start | bytes 1572864 | tf_op jit(solution)/shard_map/all_to_all | solution.py:885
  282.0 11.0 %collective-permute-start.18 = (bf16[4,96,2432]{2,1,0:T(8,128)(2,1)}, bf16[4,96,2432]{2,1,0:T(8,128)(2,1)}, u32[]{:S(2)}, u32[]{:S(2)}) collective-permute-start(bf16[4,96,2432]{2,1,0:T(8,128)(2,1)} %get-tuple-element.164), channel_id=1, source_target_pairs={{0,4},{1,5},{2,6},{3,7},{4,0},{5,1},{6,2},{7,3},{8,12},{9,13},{10,... | collective-permute-start | bytes 5603336 | tf_op jit(solution)/shard_map/ppermute | solution.py:866
  289.4 43.4 %all-to-all-start.7 = ((bf16[4,24,7040]{2,1,0:T(8,128)(2,1)}), bf16[4,24,7040]{2,1,0:T(8,128)(2,1)S(1)}, u32[]{:S(2)}, u32[]{:S(2)}) async-start(bf16[4,24,7040]{2,1,0:T(8,128)(2,1)} %feed_total.1), calls=%async_computation.7 | async-start | bytes 2703360 | tf_op jit(solution)/shard_map/all_to_all | solution.py:885
  297.7 13.8 %collective-permute-start.22 = (bf16[4,24,2432]{2,1,0:T(8,128)(2,1)}, bf16[4,24,2432]{2,1,0:T(8,128)(2,1)S(1)}, u32[]{:S(2)}, u32[]{:S(2)}) collective-permute-start(bf16[4,24,2432]{2,1,0:T(8,128)(2,1)} %get-tuple-element.171), channel_id=1, source_target_pairs={{0,8},{1,9},{2,10},{3,11},{4,12},{5,13},{6,14},{7,15},{8,0},{9,1},... | collective-permute-start | bytes 1400840 | tf_op jit(solution)/shard_map/ppermute | solution.py:866
  299.2 21.6 %collective-permute-start.23 = (bf16[4,24,2432]{2,1,0:T(8,128)(2,1)}, bf16[4,24,2432]{2,1,0:T(8,128)(2,1)S(1)}, u32[]{:S(2)}, u32[]{:S(2)}) collective-permute-start(bf16[4,24,2432]{2,1,0:T(8,128)(2,1)} %get-tuple-element.172), channel_id=1, source_target_pairs={{0,16},{1,17},{2,18},{3,19},{4,20},{5,21},{6,22},{7,23},{8,24},{9,... | collective-permute-start | bytes 1400840 | tf_op jit(solution)/shard_map/ppermute | solution.py:866
  299.5 21.3 %collective-permute-start.24 = (bf16[4,24,2432]{2,1,0:T(8,128)(2,1)}, bf16[4,24,2432]{2,1,0:T(8,128)(2,1)S(1)}, u32[]{:S(2)}, u32[]{:S(2)}) collective-permute-start(bf16[4,24,2432]{2,1,0:T(8,128)(2,1)} %get-tuple-element.173), channel_id=1, source_target_pairs={{0,24},{1,25},{2,26},{3,27},{4,28},{5,29},{6,30},{7,31},{8,16},{9,... | collective-permute-start | bytes 1400840 | tf_op jit(solution)/shard_map/ppermute | solution.py:866
  324.0 12.3 %collective-permute-start.25 = (bf16[24,2432]{1,0:T(8,128)(2,1)}, bf16[24,2432]{1,0:T(8,128)(2,1)S(1)}, u32[]{:S(2)}, u32[]{:S(2)}) collective-permute-start(bf16[24,2432]{1,0:T(8,128)(2,1)} %get-tuple-element.175), channel_id=1, source_target_pairs={{0,1},{1,2},{2,3},{3,0},{4,5},{5,6},{6,7},{7,4},{8,9},{9,10},{10,1... | collective-permute-start | bytes 350216 | tf_op jit(solution)/shard_map/ppermute | solution.py:874
  325.7 10.6 %collective-permute-start.26 = (bf16[24,2432]{1,0:T(8,128)(2,1)}, bf16[24,2432]{1,0:T(8,128)(2,1)S(1)}, u32[]{:S(2)}, u32[]{:S(2)}) collective-permute-start(bf16[24,2432]{1,0:T(8,128)(2,1)} %get-tuple-element.179), channel_id=1, source_target_pairs={{0,2},{1,3},{2,0},{3,1},{4,6},{5,7},{6,4},{7,5},{8,10},{9,11},{10,... | collective-permute-start | bytes 350216 | tf_op jit(solution)/shard_map/ppermute | solution.py:874
  328.1 8.2 %collective-permute-start.27 = (bf16[24,2432]{1,0:T(8,128)(2,1)}, bf16[24,2432]{1,0:T(8,128)(2,1)S(1)}, u32[]{:S(2)}, u32[]{:S(2)}) collective-permute-start(bf16[24,2432]{1,0:T(8,128)(2,1)} %get-tuple-element.181), channel_id=1, source_target_pairs={{0,3},{1,0},{2,1},{3,2},{4,7},{5,4},{6,5},{7,6},{8,11},{9,8},{10,9... | collective-permute-start | bytes 350216 | tf_op jit(solution)/shard_map/ppermute | solution.py:874
  (24 other events, 122.1 us)
